TPU v7x, 32 devices: a whole 2x2x4 slice. The times are simulated.
32 devices in a mesh: groups: 2 (over y), frame: 4 (over x, core), row: 4 (over z).
Axes of the slice: x: 2, y: 2, z: 4, core: 2. Of those that a mesh axis runs over, the one named last changes fastest.
Arguments:
- observed: float32 [16, 128, 2048], P('frame', ('groups', 'row')), parts along dimension 1, may hold values from 0.5 to 8
- kernels: float32 [8, 5], replicated, may hold values from 0.05 to 1
- band_kernel: int32 [16], P('groups'), parts along dimension 0, may hold values from 0 to 7
- masks: int32 [256, 128, 16], P(None, ('groups', 'row'), 'frame'), parts along dimension 1, may hold values from 0 to 1, as said below
Outputs:
- spikes: bfloat16 [16, 128, 2048], P(None, ('groups', 'row'), 'frame'), parts along dimension 1
- traces: float32 [512, 16], P(('groups', 'frame', 'row')), parts along dimension 0
There are 2 independent parts, one for each index of `groups`. A program takes and returns all parts, laid end to end along the dimension named above; an argument that names none is the same for every part. Nothing has to cross between parts.
Inputs may be any that keep to these rules, and one draw needn't show every extreme that they name: `masks`: each component covers the tile at its centre and a random half of the tiles within 8 rows and one tile column of that centre, so it covers at least one tile.
All inputs are finite; a program needn't handle non-finite values.
Results may differ from a plain program's by a relative error of at most 0.0062.
Values may be sent and summed in bfloat16 or wider, within the bound.
No kernel may reach another device: no remote copies, remote signals or barrier semaphores. Data moves between devices by JAX's collectives and lax.ppermute only.
A program may use at most 64 MiB of HBM per device.

v0:
```python
import jax
import jax.numpy as jnp
from jax import lax
from jax.sharding import PartitionSpec as P

TILE = 128
BAND = 8
ITERS = 3


SMOOTHING = 1024.0
DECAY_RATE = 0.9


def padded_2(cells, sides, width):
    for axis, dim in sides:
        count = lax.axis_size(axis)
        ends = count - 1
        head = lax.slice_in_dim(cells, 0, width, axis=dim)
        tail = lax.slice_in_dim(cells, cells.shape[dim] - width, cells.shape[dim], axis=dim)
        cells = jnp.concatenate(
            [
                lax.ppermute(tail, axis, [(i, (i + 1) % count) for i in range(ends)]),
                cells,
                lax.ppermute(head, axis, [((i + 1) % count, i) for i in range(ends)]),
            ],
            axis=dim,
        )
    return cells


def tap_rows(tap_table, band_kernel, first_row, row_count, height):
    row_ids = jnp.clip(first_row + jnp.arange(row_count), 0, height - 1)
    row_bands = row_ids // BAND
    band_slots = jnp.arange(band_kernel.shape[0])
    kernel_ids = jnp.sum(
        jnp.where(row_bands[:, None] == band_slots[None, :], band_kernel[None, :], 0), axis=1
    )
    kernel_slots = jnp.arange(tap_table.shape[0])
    picked = jnp.where(
        kernel_ids[:, None, None] == kernel_slots[None, :, None], tap_table[None, :, :], 0.0
    )
    return jnp.sum(picked, axis=1)


def blur_rows(padded, row_taps, row_count):
    summed = row_taps[:, 0][None, :, None] * padded[:, 0:row_count]
    for offset in range(1, 5):
        summed = (
            summed + row_taps[:, offset][None, :, None] * padded[:, offset : offset + row_count]
        )
    return summed


def back_rows(padded_quotient, outer_taps, row_count):
    summed = outer_taps[4 : 4 + row_count, 0][None, :, None] * padded_quotient[:, 4 : 4 + row_count]
    for offset in range(1, 5):
        start = 4 - offset
        summed = (
            summed
            + outer_taps[start : start + row_count, offset][None, :, None]
            * padded_quotient[:, start : start + row_count]
        )
    return summed


def temporal(series_block):
    frame_total, item_count, columns = series_block.shape
    values = series_block.astype(jnp.float32).reshape(frame_total, item_count * columns)
    frame_ids = jnp.arange(frame_total)
    at_ends = (frame_ids == 0) | (frame_ids == frame_total - 1)
    middle = (1.0 + SMOOTHING * jnp.where(at_ends, 1.0, 2.0)).astype(jnp.float32)
    sub_diag = jnp.where(frame_ids == 0, 0.0, -SMOOTHING).astype(jnp.float32)
    super_diag = jnp.where(frame_ids == frame_total - 1, 0.0, -SMOOTHING).astype(jnp.float32)
    baseline = lax.linalg.tridiagonal_solve(sub_diag, middle, super_diag, values)
    detrended = values - baseline
    earlier = jnp.concatenate(
        [jnp.zeros((1, values.shape[1]), jnp.float32), detrended[:-1]], axis=0
    )
    result = (detrended - DECAY_RATE * earlier).astype(jnp.bfloat16)
    return result.reshape(frame_total, item_count, columns)


def local(observed, kernels, band_kernel, masks):
    frames_dev, rows_dev, row_pixels = observed.shape
    height = rows_dev * lax.axis_size("row")
    tap_table = kernels / jnp.sum(kernels, axis=1, keepdims=True)
    first_row = lax.axis_index("row") * rows_dev
    own_taps = tap_rows(tap_table, band_kernel, first_row, rows_dev, height)
    outer_taps = tap_rows(tap_table, band_kernel, first_row - 2, rows_dev + 4, height)
    current = observed
    for iteration in range(ITERS):
        padded = padded_2(current, (("row", 1),), 2)
        blurred = blur_rows(padded, own_taps, rows_dev)
        quotient = observed / blurred
        padded_quotient = padded_2(quotient, (("row", 1),), 2)
        current = current * back_rows(padded_quotient, outer_taps, rows_dev)
    estimate = current.astype(jnp.bfloat16)
    spikes = temporal(lax.all_to_all(estimate, "frame", split_axis=2, concat_axis=0, tiled=True))
    frames_all, _, columns = spikes.shape
    tile_count = columns // TILE
    tile_sums = jnp.sum(
        spikes.reshape(frames_all, rows_dev * tile_count, TILE).astype(jnp.float32), axis=2
    )
    weights = masks.astype(jnp.float32).reshape(masks.shape[0], rows_dev * tile_count)
    local_sums = lax.dot_general(
        weights, tile_sums, (((1,), (1,)), ((), ())), precision=lax.Precision.HIGHEST
    )
    counts = jnp.sum(weights, axis=1)
    trace_sums, totals = (
        lax.psum_scatter(local_sums, ("frame", "row"), scatter_dimension=0, tiled=True),
        lax.psum_scatter(counts, ("frame", "row"), scatter_dimension=0, tiled=True),
    )
    traces = trace_sums / (TILE * totals[:, None])
    return (spikes, traces)


def solution(mesh):
    in_specs = (
        P("frame", ("groups", "row"), None),
        P(),
        P("groups"),
        P(None, ("groups", "row"), "frame"),
    )
    out_specs = (P(None, ("groups", "row"), "frame"), P(("groups", "frame", "row"), None))
    return jax.shard_map(local, mesh=mesh, in_specs=in_specs, out_specs=out_specs, check_vma=False)
```

profile of v0, /device:TPU:0, one launch (start us, length us, event | category | flops | bytes accessed | tf_op | source)
XLA Modules:
  0.0 221.8 jit_solution(17117470301086755105)
XLA Ops:
  7.2 1.1 fusion.69
  8.4 4.9 %collective-permute-start = (f32[4,2,2048]{2,0,1:T(4,128)S(1)}, f32[4,2,2048]{2,0,1:T(4,128)S(1)}, u32[]{:S(2)}, u32[]{:S(2)}) collective-permute-start(f32[4,2,2048]{2,0,1:T(4,128)S(1)} %copy.150), channel_id=1, source_target_pairs={{0,1},{1,2},{2,3},{4,5},{5,6},{6,7},{8,9},{9,10},{10,11},{12,13},{... | collective-permute-start | bytes 196616 | tf_op jit(solution)/shard_map/ppermute | solution.py:23
  13.4 1.3 collective-permute-start.1
  18.1 0.9 convert_element_type.45
  19.0 1.5 constant_dynamic-update-slice_fusion
  21.4 1.3 collective-permute-start.2
  22.7 5.2 %collective-permute-start.3 = (f32[4,2,2048]{2,0,1:T(4,128)S(1)}, f32[4,2,2048]{2,0,1:T(4,128)S(1)}, u32[]{:S(2)}, u32[]{:S(2)}) collective-permute-start(f32[4,2,2048]{2,0,1:T(4,128)S(1)} %get-tuple-element.75), channel_id=1, source_target_pairs={{0,1},{1,2},{2,3},{4,5},{5,6},{6,7},{8,9},{9,10},{10,11},{12,13},{... | collective-permute-start | bytes 196616 | tf_op jit(solution)/shard_map/ppermute | solution.py:23
  28.2 1.6 collective-permute-done.3
  29.8 0.9 fusion.40
  30.6 4.3 %collective-permute-start.4 = (f32[4,2,2048]{2,0,1:T(4,128)S(1)}, f32[4,2,2048]{2,0,1:T(4,128)S(1)}, u32[]{:S(2)}, u32[]{:S(2)}) collective-permute-start(f32[4,2,2048]{2,0,1:T(4,128)S(1)} %get-tuple-element.72), channel_id=1, source_target_pairs={{0,1},{1,2},{2,3},{4,5},{5,6},{6,7},{8,9},{9,10},{10,11},{12,13},{... | collective-permute-start | bytes 196616 | tf_op jit(solution)/shard_map/ppermute | solution.py:23
  34.9 1.3 collective-permute-start.5
  36.9 4.1 %collective-permute-done.5 = f32[4,2,2048]{2,0,1:T(4,128)S(1)} collective-permute-done((f32[4,2,2048]{2,0,1:T(4,128)S(1)}, f32[4,2,2048]{2,0,1:T(4,128)S(1)}, u32[]{:S(2)}, u32[]{:S(2)}) %collective-permute-start.5) | collective-permute-done | bytes 65568 | tf_op jit(solution)/shard_map/ppermute | solution.py:25
  41.1 0.9 fusion.31
  42.0 1.3 collective-permute-start.6
  43.3 4.5 %collective-permute-start.7 = (f32[4,2,2048]{2,0,1:T(4,128)S(1)}, f32[4,2,2048]{2,0,1:T(4,128)S(1)}, u32[]{:S(2)}, u32[]{:S(2)}) collective-permute-start(f32[4,2,2048]{2,0,1:T(4,128)S(1)} %get-tuple-element.71), channel_id=1, source_target_pairs={{0,1},{1,2},{2,3},{4,5},{5,6},{6,7},{8,9},{9,10},{10,11},{12,13},{... | collective-permute-start | bytes 196616 | tf_op jit(solution)/shard_map/ppermute | solution.py:23
  48.1 1.6 collective-permute-done.7
  50.4 4.3 %collective-permute-start.8 = (f32[4,2,2048]{2,0,1:T(4,128)S(1)}, f32[4,2,2048]{2,0,1:T(4,128)S(1)}, u32[]{:S(2)}, u32[]{:S(2)}) collective-permute-start(f32[4,2,2048]{2,0,1:T(4,128)S(1)} %get-tuple-element.68), channel_id=1, source_target_pairs={{0,1},{1,2},{2,3},{4,5},{5,6},{6,7},{8,9},{9,10},{10,11},{12,13},{... | collective-permute-start | bytes 196616 | tf_op jit(solution)/shard_map/ppermute | solution.py:23
  54.6 1.3 collective-permute-start.9
  58.0 3.5 %collective-permute-done.9 = f32[4,2,2048]{2,0,1:T(4,128)S(1)} collective-permute-done((f32[4,2,2048]{2,0,1:T(4,128)S(1)}, f32[4,2,2048]{2,0,1:T(4,128)S(1)}, u32[]{:S(2)}, u32[]{:S(2)}) %collective-permute-start.9) | collective-permute-done | bytes 65568 | tf_op jit(solution)/shard_map/ppermute | solution.py:25
  61.5 0.9 fusion.13
  62.3 1.3 collective-permute-start.10
  63.6 4.5 %collective-permute-start.11 = (f32[4,2,2048]{2,0,1:T(4,128)S(1)}, f32[4,2,2048]{2,0,1:T(4,128)S(1)}, u32[]{:S(2)}, u32[]{:S(2)}) collective-permute-start(f32[4,2,2048]{2,0,1:T(4,128)S(1)} %get-tuple-element.67), channel_id=1, source_target_pairs={{0,1},{1,2},{2,3},{4,5},{5,6},{6,7},{8,9},{9,10},{10,11},{12,13},{... | collective-permute-start | bytes 196616 | tf_op jit(solution)/shard_map/ppermute | solution.py:23
  68.5 1.6 collective-permute-done.11
  70.7 1.5 copy.117
  72.2 2.9 %reshape.1472 = bf16[4,2,16384]{2,1,0:T(2,128)(2,1)} reshape(bf16[2048,4,16]{2,1,0:T(4,128)(2,1)S(1)} %bitcast.135) | data formatting | bytes 524288
  75.1 3.4 %all-to-all-start = ((bf16[4,2,16384]{2,1,0:T(2,128)(2,1)}), bf16[4,2,16384]{2,1,0:T(2,128)(2,1)S(1)}, u32[]{:S(2)}, u32[]{:S(2)}) async-start(bf16[4,2,16384]{2,1,0:T(2,128)(2,1)} %reshape.1472), calls=%async_computation | async-start | bytes 524288 | tf_op jit(solution)/shard_map/all_to_all | solution.py:99
  108.1 35.6 %all-reduce.1 = f32[256]{0:T(256)S(1)} all-reduce(f32[256]{0:T(256)S(1)} %convert_reduce_fusion), channel_id=3, replica_groups=mesh['groups'=2,'frame'=4,'row'=4] {'frame','row'}, use_global_device_ids=true, to_apply=%region_8.9.clone | all-reduce | flops 256 | bytes 2048
  143.7 1.4 reshape.1473
  145.2 1.1 copy.118
  148.6 9.3 %subtract_divide_fusion.1 = (f32[1,8192]{1,0:T(1,128)S(1)}, f32[1,8192]{1,0:T(1,128)S(1)}, f32[1,8192]{1,0:T(1,128)S(1)}, f32[1,8192]{1,0:T(1,128)S(1)}, f32[1,8...) fusion(f32[1,8192]{1,0:T(1,128)S(1)} %bitcast.161, ...), kind=kLoop, calls=%fused_computation.131 | loop fusion | flops 344064 | bytes 950384 | tf_op jit(solution)/shard_map/eval_jaxpr/div | solution.py:75
  157.9 1.0 multiply_subtract_fusion
  161.9 51.6 %reduce-scatter.4.cloned.1.call-done = f32[16,16]{1,0:T(8,128)} async-done(((f32[256,16]{1,0:T(8,128)}), f32[16,16]{1,0:T(8,128)}) %reduce-scatter.4.cloned.1.call-update) | async-done | bytes 1040
  (82 shorter events, 15.9 us)
Async XLA Ops:
  7.2 13.4 %copy-start = (f32[4,16,2048]{2,1,0:T(8,128)S(1)}, f32[4,16,2048]{2,1,0:T(8,128)}, u32[]{:S(2)}) copy-start(f32[4,16,2048]{2,1,0:T(8,128)} %param.4) | copy-start | bytes 1572868
  8.4 10.6 %collective-permute-start = (f32[4,2,2048]{2,0,1:T(4,128)S(1)}, f32[4,2,2048]{2,0,1:T(4,128)S(1)}, u32[]{:S(2)}, u32[]{:S(2)}) collective-permute-start(f32[4,2,2048]{2,0,1:T(4,128)S(1)} %copy.150), channel_id=1, source_target_pairs={{0,1},{1,2},{2,3},{4,5},{5,6},{6,7},{8,9},{9,10},{10,11},{12,13},{... | collective-permute-start | bytes 196616 | tf_op jit(solution)/shard_map/ppermute | solution.py:23
  13.4 7.2 %collective-permute-start.1 = (f32[4,2,2048]{2,0,1:T(4,128)S(1)}, f32[4,2,2048]{2,0,1:T(4,128)S(1)}, u32[]{:S(2)}, u32[]{:S(2)}) collective-permute-start(f32[4,2,2048]{2,0,1:T(4,128)S(1)} %copy.149), channel_id=1, source_target_pairs={{1,0},{2,1},{3,2},{5,4},{6,5},{7,6},{9,8},{10,9},{11,10},{13,12},{... | collective-permute-start | bytes 196616 | tf_op jit(solution)/shard_map/ppermute | solution.py:25
  21.4 6.8 %collective-permute-start.2 = (f32[4,2,2048]{2,0,1:T(4,128)S(1)}, f32[4,2,2048]{2,0,1:T(4,128)S(1)}, u32[]{:S(2)}, u32[]{:S(2)}) collective-permute-start(f32[4,2,2048]{2,0,1:T(4,128)S(1)} %get-tuple-element.74), channel_id=1, source_target_pairs={{1,0},{2,1},{3,2},{5,4},{6,5},{7,6},{9,8},{10,9},{11,10},{13,12},{... | collective-permute-start | bytes 196616 | tf_op jit(solution)/shard_map/ppermute | solution.py:25
  22.7 7.1 %collective-permute-start.3 = (f32[4,2,2048]{2,0,1:T(4,128)S(1)}, f32[4,2,2048]{2,0,1:T(4,128)S(1)}, u32[]{:S(2)}, u32[]{:S(2)}) collective-permute-start(f32[4,2,2048]{2,0,1:T(4,128)S(1)} %get-tuple-element.75), channel_id=1, source_target_pairs={{0,1},{1,2},{2,3},{4,5},{5,6},{6,7},{8,9},{9,10},{10,11},{12,13},{... | collective-permute-start | bytes 196616 | tf_op jit(solution)/shard_map/ppermute | solution.py:23
  30.6 6.3 %collective-permute-start.4 = (f32[4,2,2048]{2,0,1:T(4,128)S(1)}, f32[4,2,2048]{2,0,1:T(4,128)S(1)}, u32[]{:S(2)}, u32[]{:S(2)}) collective-permute-start(f32[4,2,2048]{2,0,1:T(4,128)S(1)} %get-tuple-element.72), channel_id=1, source_target_pairs={{0,1},{1,2},{2,3},{4,5},{5,6},{6,7},{8,9},{9,10},{10,11},{12,13},{... | collective-permute-start | bytes 196616 | tf_op jit(solution)/shard_map/ppermute | solution.py:23
  34.9 6.2 %collective-permute-start.5 = (f32[4,2,2048]{2,0,1:T(4,128)S(1)}, f32[4,2,2048]{2,0,1:T(4,128)S(1)}, u32[]{:S(2)}, u32[]{:S(2)}) collective-permute-start(f32[4,2,2048]{2,0,1:T(4,128)S(1)} %get-tuple-element.73), channel_id=1, source_target_pairs={{1,0},{2,1},{3,2},{5,4},{6,5},{7,6},{9,8},{10,9},{11,10},{13,12},{... | collective-permute-start | bytes 196616 | tf_op jit(solution)/shard_map/ppermute | solution.py:25
  42.0 6.2 %collective-permute-start.6 = (f32[4,2,2048]{2,0,1:T(4,128)S(1)}, f32[4,2,2048]{2,0,1:T(4,128)S(1)}, u32[]{:S(2)}, u32[]{:S(2)}) collective-permute-start(f32[4,2,2048]{2,0,1:T(4,128)S(1)} %get-tuple-element.70), channel_id=1, source_target_pairs={{1,0},{2,1},{3,2},{5,4},{6,5},{7,6},{9,8},{10,9},{11,10},{13,12},{... | collective-permute-start | bytes 196616 | tf_op jit(solution)/shard_map/ppermute | solution.py:25
  43.3 6.4 %collective-permute-start.7 = (f32[4,2,2048]{2,0,1:T(4,128)S(1)}, f32[4,2,2048]{2,0,1:T(4,128)S(1)}, u32[]{:S(2)}, u32[]{:S(2)}) collective-permute-start(f32[4,2,2048]{2,0,1:T(4,128)S(1)} %get-tuple-element.71), channel_id=1, source_target_pairs={{0,1},{1,2},{2,3},{4,5},{5,6},{6,7},{8,9},{9,10},{10,11},{12,13},{... | collective-permute-start | bytes 196616 | tf_op jit(solution)/shard_map/ppermute | solution.py:23
  50.4 7.6 %collective-permute-start.8 = (f32[4,2,2048]{2,0,1:T(4,128)S(1)}, f32[4,2,2048]{2,0,1:T(4,128)S(1)}, u32[]{:S(2)}, u32[]{:S(2)}) collective-permute-start(f32[4,2,2048]{2,0,1:T(4,128)S(1)} %get-tuple-element.68), channel_id=1, source_target_pairs={{0,1},{1,2},{2,3},{4,5},{5,6},{6,7},{8,9},{9,10},{10,11},{12,13},{... | collective-permute-start | bytes 196616 | tf_op jit(solution)/shard_map/ppermute | solution.py:23
  54.6 6.8 %collective-permute-start.9 = (f32[4,2,2048]{2,0,1:T(4,128)S(1)}, f32[4,2,2048]{2,0,1:T(4,128)S(1)}, u32[]{:S(2)}, u32[]{:S(2)}) collective-permute-start(f32[4,2,2048]{2,0,1:T(4,128)S(1)} %get-tuple-element.69), channel_id=1, source_target_pairs={{1,0},{2,1},{3,2},{5,4},{6,5},{7,6},{9,8},{10,9},{11,10},{13,12},{... | collective-permute-start | bytes 196616 | tf_op jit(solution)/shard_map/ppermute | solution.py:25
  62.3 6.2 %collective-permute-start.10 = (f32[4,2,2048]{2,0,1:T(4,128)S(1)}, f32[4,2,2048]{2,0,1:T(4,128)S(1)}, u32[]{:S(2)}, u32[]{:S(2)}) collective-permute-start(f32[4,2,2048]{2,0,1:T(4,128)S(1)} %get-tuple-element.66), channel_id=1, source_target_pairs={{1,0},{2,1},{3,2},{5,4},{6,5},{7,6},{9,8},{10,9},{11,10},{13,12},{... | collective-permute-start | bytes 196616 | tf_op jit(solution)/shard_map/ppermute | solution.py:25
  63.6 6.4 %collective-permute-start.11 = (f32[4,2,2048]{2,0,1:T(4,128)S(1)}, f32[4,2,2048]{2,0,1:T(4,128)S(1)}, u32[]{:S(2)}, u32[]{:S(2)}) collective-permute-start(f32[4,2,2048]{2,0,1:T(4,128)S(1)} %get-tuple-element.67), channel_id=1, source_target_pairs={{0,1},{1,2},{2,3},{4,5},{5,6},{6,7},{8,9},{9,10},{10,11},{12,13},{... | collective-permute-start | bytes 196616 | tf_op jit(solution)/shard_map/ppermute | solution.py:23
  72.2 34.6 %copy-start.2 = (u32[32]{0:T(128)S(1)}, u32[32]{0:T(128)}, u32[]{:S(2)}) copy-start(u32[32]{0:T(128)} %constant.60) | copy-start | bytes 388
  72.2 35.9 %copy-start.1 = (s32[256,16,4]{0,2,1:T(4,128)S(1)}, s32[256,16,4]{0,2,1:T(4,128)}, u32[]{:S(2)}) copy-start(s32[256,16,4]{0,2,1:T(4,128)} %param.7) | copy-start | bytes 196612
  75.1 68.6 %all-to-all-start = ((bf16[4,2,16384]{2,1,0:T(2,128)(2,1)}), bf16[4,2,16384]{2,1,0:T(2,128)(2,1)S(1)}, u32[]{:S(2)}, u32[]{:S(2)}) async-start(bf16[4,2,16384]{2,1,0:T(2,128)(2,1)} %reshape.1472), calls=%async_computation | async-start | bytes 524288 | tf_op jit(solution)/shard_map/all_to_all | solution.py:99
  78.5 135.0 %reduce-scatter.4.cloned.1.call-start = ((), (), s32[]{:S(2)}) async-start(), calls=%async_computation.2 | async-start | bytes 139264
Sparse Core Ops, SparseCore 0:
  161.2 52.2 reduce-scatter.3
where the time goes:
time: 223 us; the launch traced here: 222 us
  waiting for transfers between devices  64.8 us (29%)
  between operations  44.1 us (20%)
  starting transfers between devices  38.9 us (17%)
  blocking collectives  35.6 us (16%)
  other arithmetic  20.2 us (9%)
  local copies, waits for them, and re-layouts  18 us (8%)
    unnamed x2, waiting for transfers between devices  51.6 us
    unnamed x1, blocking collectives  35.6 us
    ppermute x6, starting transfers between devices, padded_2(): lax.ppermute(tail, axis, [(i, (i + 1) % count) for i in range(ends)])  27.7 us
    div x1, other arithmetic, temporal(): lax.linalg.tridiagonal_solve(sub_diag, middle, super_diag, values)  9.26 us
    unnamed x34, local copies, waits for them, and re-layouts  8.98 us
    ppermute x6, waiting for transfers between devices, padded_2(): lax.ppermute(head, axis, [((i + 1) % count, i) for i in range(ends)])  8.5 us
    ppermute x6, starting transfers between devices, padded_2(): lax.ppermute(head, axis, [((i + 1) % count, i) for i in range(ends)])  7.75 us
    ppermute x6, waiting for transfers between devices, padded_2(): lax.ppermute(tail, axis, [(i, (i + 1) % count) for i in range(ends)])  4.75 us
  transfers between devices with their start and end apart: 14, of which 9 were waited for; matrix products, arithmetic and copies ran while one was open for 4% of the time, Pallas kernels for 0%

commit v1 on v0

--- a/solution.py
+++ b/solution.py
@@ -1,11 +1,16 @@
+import functools
+
 import jax
 import jax.numpy as jnp
 from jax import lax
+from jax.experimental import pallas as pl
+from jax.experimental.pallas import tpu as pltpu
 from jax.sharding import PartitionSpec as P
 
 TILE = 128
 BAND = 8
 ITERS = 3
+TAPS = 5
 
 
 SMOOTHING = 1024.0
@@ -115,6 +120,173 @@
     return (spikes, traces)
 
 
+def roll_rows(cells, shift):
+    rows = cells.shape[0]
+    return cells if shift % rows == 0 else pltpu.roll(cells, shift % rows, 0)
+
+
+def restore_kernel(
+    band_ref, kernels_ref, observed_ref, masks_ref, out_ref, tap_ref, sums_ref, *, devices, rows_dev, tiles_dev
+):
+    n_frame, n_row = devices
+    height, _ = observed_ref.shape
+    positions = rows_dev * tiles_dev
+    row_ids = lax.broadcasted_iota(jnp.int32, (BAND, TILE), 0)
+    for band in range(height // BAND):
+        kernel = band_ref[band]
+        raw = [kernels_ref[kernel, tap] for tap in range(TAPS)]
+        total = raw[0]
+        for tap in range(1, TAPS):
+            total = total + raw[tap]
+        for tap in range(TAPS):
+            weight = jnp.full((BAND, TILE), raw[tap], jnp.float32) / jnp.full((BAND, TILE), total, jnp.float32)
+            target = row_ids + (band * BAND + tap - TAPS // 2)
+            weight = jnp.where((target >= 0) & (target < height), weight, 0.0)
+            tap_ref[tap, band * BAND : (band + 1) * BAND, :] = weight
+    flat = jnp.concatenate([masks_ref[row].astype(jnp.float32) for row in range(rows_dev)], axis=0)
+    both = jnp.concatenate([flat, flat], axis=0).T.astype(jnp.bfloat16)
+    share = both.shape[0] // (n_frame * n_row)
+    est_rows = rows_dev * tiles_dev
+    for place in range(n_frame * n_row):
+        out_ref[place, est_rows + rows_dev : est_rows + rows_dev + share, :] = both[place * share : (place + 1) * share]
+    lanes = lax.broadcasted_iota(jnp.int32, (rows_dev, TILE), 1)
+    own_rows = lax.broadcasted_iota(jnp.int32, (rows_dev, TILE), 0)
+    ones = jnp.ones((TILE, TILE), jnp.bfloat16)
+
+    def column_block(block, carry):
+        gathered = [jnp.zeros((1, TILE), jnp.float32) for _ in range(n_row)]
+        for tile in range(tiles_dev):
+            start = pl.multiple_of((block * tiles_dev + tile) * TILE, TILE)
+            image = observed_ref[:, pl.ds(start, TILE)].astype(jnp.float32)
+            current = image
+            for _ in range(ITERS):
+                blurred = tap_ref[2] * current
+                for tap in (0, 1, 3, 4):
+                    blurred = blurred + tap_ref[tap] * roll_rows(current, 2 - tap)
+                quotient = image / blurred
+                back = tap_ref[2] * quotient
+                for tap in (0, 1, 3, 4):
+                    back = back + roll_rows(tap_ref[tap] * quotient, tap - 2)
+                current = current * back
+            estimate = current.astype(jnp.bfloat16)
+            for row in range(n_row):
+                out_ref[block * n_row + row, tile * rows_dev : (tile + 1) * rows_dev, :] = estimate[
+                    row * rows_dev : (row + 1) * rows_dev
+                ]
+            tile_sums = jnp.dot(estimate, ones, preferred_element_type=jnp.float32)
+            here = lanes % positions == own_rows * tiles_dev + tile
+            for row in range(n_row):
+                part = jnp.where(here, tile_sums[row * rows_dev : (row + 1) * rows_dev], 0.0)
+                gathered[row] = gathered[row] + jnp.sum(part, axis=0, keepdims=True)
+        for row in range(n_row):
+            sums_ref[pl.ds(block * n_row + row, 1), :] = gathered[row]
+        return carry
+
+    lax.fori_loop(0, n_frame, column_block, 0)
+    sums = sums_ref[...]
+    high = sums.astype(jnp.bfloat16).astype(jnp.float32)
+    split = jnp.where(lax.broadcasted_iota(jnp.int32, sums.shape, 1) < positions, high, sums - high)
+    split = split.astype(jnp.bfloat16)
+    for place in range(n_frame * n_row):
+        out_ref[place, est_rows : est_rows + rows_dev, :] = split
+
+
+def deconvolved(series, factors):
+    total = len(series)
+    forward = [series[0] * factors[0]]
+    for step in range(1, total):
+        forward.append((series[step] + SMOOTHING * forward[step - 1]) * factors[step])
+    baseline = [None] * total
+    baseline[total - 1] = forward[total - 1]
+    for step in range(total - 2, -1, -1):
+        baseline[step] = forward[step] + (SMOOTHING * factors[step]) * baseline[step + 1]
+    result, earlier = [], None
+    for step in range(total):
+        detrended = series[step] - baseline[step]
+        result.append(detrended if earlier is None else detrended - DECAY_RATE * earlier)
+        earlier = detrended
+    return result
+
+
+def solve_factors(total):
+    factors = []
+    for step in range(total):
+        middle = 1.0 + SMOOTHING * (1.0 if step in (0, total - 1) else 2.0)
+        if step:
+            middle -= SMOOTHING * SMOOTHING * factors[-1]
+        factors.append(1.0 / middle)
+    return factors
+
+
+def temporal_kernel(in_ref, spikes_ref, traces_ref, sums_ref, *, rows_dev, tiles_dev, share):
+    frames = in_ref.shape[0]
+    factors = solve_factors(frames)
+    for tile in range(tiles_dev):
+        series = [in_ref[t, tile * rows_dev : (tile + 1) * rows_dev, :].astype(jnp.float32) for t in range(frames)]
+        for t, spikes in enumerate(deconvolved(series, factors)):
+            spikes_ref[t, :, tile * TILE : (tile + 1) * TILE] = spikes.astype(spikes_ref.dtype)
+    first = rows_dev * tiles_dev
+    series = [in_ref[t, first : first + frames, :].astype(jnp.float32) for t in range(frames)]
+    for t, sums in enumerate(deconvolved(series, factors)):
+        sums_ref[t * frames : (t + 1) * frames, :] = sums
+    first += frames
+    weights = jnp.concatenate([in_ref[j, first : first + share, :].astype(jnp.float32) for j in range(frames)], axis=1)
+    sums = jnp.concatenate([sums_ref[pl.ds(j, frames, stride=frames), :] for j in range(frames)], axis=1)
+    trace_sums = lax.dot_general(
+        weights, sums, (((1,), (1,)), ((), ())), precision=lax.Precision.HIGHEST, preferred_element_type=jnp.float32
+    )
+    counts = 0.5 * jnp.sum(weights, axis=1, keepdims=True)
+    traces_ref[...] = trace_sums / (TILE * counts)
+
+
+def by_frame(observed, kernels, band_kernel, masks):
+    n_frame, n_row = lax.axis_size("frame"), lax.axis_size("row")
+    places = n_frame * n_row
+    components, rows_dev, tiles_dev = masks.shape
+    height, width = rows_dev * n_row, observed.shape[2]
+    share = components // places
+    block_rows = rows_dev * tiles_dev + places + share
+    sent = lax.all_to_all(observed.astype(jnp.float16), "row", split_axis=0, concat_axis=0, tiled=True)
+    image = sent.astype(jnp.float32).reshape(height, width)
+    blocks = pl.pallas_call(
+        functools.partial(restore_kernel, devices=(n_frame, n_row), rows_dev=rows_dev, tiles_dev=tiles_dev),
+        out_shape=jax.ShapeDtypeStruct((places, block_rows, TILE), jnp.bfloat16),
+        in_specs=[pl.BlockSpec(memory_space=pltpu.SMEM)] * 2 + [pl.BlockSpec(memory_space=pltpu.VMEM)] * 2,
+        out_specs=pl.BlockSpec(memory_space=pltpu.VMEM),
+        scratch_shapes=[pltpu.VMEM((TAPS, height, TILE), jnp.float32), pltpu.VMEM((places, TILE), jnp.float32)],
+        compiler_params=pltpu.CompilerParams(vmem_limit_bytes=16 << 20),
+        name="restore",
+    )(band_kernel, kernels, image, masks.transpose(1, 2, 0))
+    series = lax.all_to_all(blocks, ("frame", "row"), split_axis=0, concat_axis=0, tiled=True)
+    spikes, traces = pl.pallas_call(
+        functools.partial(temporal_kernel, rows_dev=rows_dev, tiles_dev=tiles_dev, share=share),
+        out_shape=(
+            jax.ShapeDtypeStruct((places, rows_dev, tiles_dev * TILE), jnp.bfloat16),
+            jax.ShapeDtypeStruct((share, places), jnp.float32),
+        ),
+        in_specs=[pl.BlockSpec(memory_space=pltpu.VMEM)],
+        out_specs=(pl.BlockSpec(memory_space=pltpu.VMEM),) * 2,
+        scratch_shapes=[pltpu.VMEM((places * places, TILE), jnp.float32)],
+        compiler_params=pltpu.CompilerParams(vmem_limit_bytes=16 << 20),
+        name="temporal",
+    )(series)
+    return (spikes, traces)
+
+
+def fits(mesh, observed, masks):
+    frames_dev = observed.shape[0] // mesh.shape["frame"]
+    rows_dev = masks.shape[1] // (mesh.shape["groups"] * mesh.shape["row"])
+    tiles_dev = masks.shape[2] // mesh.shape["frame"]
+    places = mesh.shape["frame"] * mesh.shape["row"]
+    return (
+        frames_dev == mesh.shape["row"]
+        and 2 * rows_dev * tiles_dev == TILE
+        and rows_dev == 16
+        and places == 16
+        and masks.shape[0] // places == 16
+    )
+
+
 def solution(mesh):
     in_specs = (
         P("frame", ("groups", "row"), None),
@@ -123,4 +295,10 @@
         P(None, ("groups", "row"), "frame"),
     )
     out_specs = (P(None, ("groups", "row"), "frame"), P(("groups", "frame", "row"), None))
-    return jax.shard_map(local, mesh=mesh, in_specs=in_specs, out_specs=out_specs, check_vma=False)
+
+    def whole(observed, kernels, band_kernel, masks):
+        body = by_frame if fits(mesh, observed, masks) else local
+        mapped = jax.shard_map(body, mesh=mesh, in_specs=in_specs, out_specs=out_specs, check_vma=False)
+        return mapped(observed, kernels, band_kernel, masks)
+
+    return whole

time: 223 us -> 38.7 us (0.17)
  waiting for transfers between devices: 64.8 us -> 0 us
  between operations: 44.1 us -> 0.65 us
  starting transfers between devices: 38.9 us -> 0 us
  other arithmetic: 20.2 us -> 1.12 us
  local copies, waits for them, and re-layouts: 18 us -> 0.77 us
  Pallas kernels: 0 us -> 4.44 us
  blocking collectives: 35.6 us -> 31.4 us
    unnamed x2 -> x0, waiting for transfers between devices: 51.6 us -> none
    unnamed x1 -> x0, blocking collectives: 35.6 us -> none
    ppermute x12 -> x0, starting transfers between devices: 35.5 us -> none  [the longest x6 27.7 us: padded_2(): lax.ppermute(tail, axis, [(i, (i + 1) % count) for i in range(ends)])]
    all_to_all x0 -> x2, blocking collectives: none -> 31.4 us  [the longest x1 16.4 us: by_frame(): lax.all_to_all(blocks, ('frame', 'row'), split_axis=0, concat_axis=0, til...]
    ppermute x12 -> x0, waiting for transfers between devices: 13.3 us -> none  [the longest x6 8.5 us: padded_2(): lax.ppermute(head, axis, [((i + 1) % count, i) for i in range(ends)])]
    div x6 -> x0, other arithmetic: 12.6 us -> none  [the longest x1 9.26 us: temporal(): lax.linalg.tridiagonal_solve(sub_diag, middle, super_diag, values)]
    unnamed x34 -> x6, local copies, waits for them, and re-layouts: 8.98 us -> 0.77 us
    pallas_call x0 -> x2, Pallas kernels: none -> 4.44 us  [the longest x1 3.28 us: by_frame(): pl.pallas_call(functools.partial(restore_kernel, devices=(n_frame, n_row)...]
  transfers between devices with their start and end apart: 14 -> 0, of which waited for: 9 -> 0; matrix products, arithmetic and copies ran while one was open for 4% -> 0% of each run, Pallas kernels for 0% -> 0%
where the time goes in v1:
time: 38.7 us; the launch traced here: 38.4 us
  blocking collectives  31.4 us (81%)
  Pallas kernels  4.44 us (11%)
  other arithmetic  1.12 us (3%)
  local copies, waits for them, and re-layouts  0.77 us (2%)
  between operations  0.65 us (2%)
    all_to_all x1, blocking collectives, by_frame(): lax.all_to_all(blocks, ('frame', 'row'), split_axis=0, concat_axis=0, til...  16.4 us
    all_to_all x1, blocking collectives, by_frame(): lax.all_to_all(observed.astype(jnp.float16), 'row', split_axis=0, concat_...  15 us
    pallas_call x1, Pallas kernels, by_frame(): pl.pallas_call(functools.partial(restore_kernel, devices=(n_frame, n_row)...  3.28 us
    pallas_call x1, Pallas kernels, by_frame(): pl.pallas_call(functools.partial(temporal_kernel, rows_dev=rows_dev, tile...  1.15 us
    convert_element_type x1, other arithmetic, by_frame(): observed.astype(jnp.float16)  1.07 us

profile of v1, /device:TPU:0, one launch (start us, length us, event | category | flops | bytes accessed | tf_op | source)
XLA Modules:
  0.0 38.4 jit_solution(6201276481571329207)
XLA Ops:
  0.6 1.1 %convert_element_type.4 = f16[4,16,2048]{2,1,0:T(8,128)(2,1)S(1)} convert(f32[4,16,2048]{2,1,0:T(8,128)} %param.4) | non-fusion elementwise | flops 131072 | bytes 786432 | tf_op jit(solution)/shard_map/convert_element_type | solution.py:249
  1.7 15.0 %all_to_all.10 = f16[4,16,2048]{2,1,0:T(8,128)(2,1)S(1)} all-to-all(f16[4,16,2048]{2,1,0:T(8,128)(2,1)S(1)} %convert_element_type.4), channel_id=1, replica_groups=mesh['groups'=2,'frame'=4,'row'=4] {'row'}, dimensions={0} | all-to-all | bytes 524288 | tf_op jit(solution)/shard_map/all_to_all | solution.py:249
  16.7 0.0 copy-start
  16.7 0.0 copy-start.1
  16.7 0.1 bitcast_convert_fusion.observed_ref
  16.8 0.0 copy-start.2
  16.8 0.8 %copy-done = s32[256,16,4]{0,2,1:T(4,128)S(1)} copy-done((s32[256,16,4]{0,2,1:T(4,128)S(1)}, s32[256,16,4]{0,2,1:T(4,128)}, u32[]{:S(2)}) %copy-start) | copy-done | bytes 65560
  17.5 0.0 copy-done.1
  17.5 0.0 copy-done.2
  17.5 3.3 %restore.1 = bf16[16,96,128]{2,1,0:T(8,128)(2,1)S(1)} custom-call(s32[8]{0:T(128)S(1)} %copy-done.2, f32[8,5]{1,0:T(8,128)S(1)} %copy-done.1, f32[64,2048]{1,0:T(8,128)S(1)} %bitcast_convert_fusion.observed_ref, s32[16,4,256]{2,1,0:T(4,128)S(1)} %bitcast.4), custom_call_target="tpu_custom_call" | custom-call | tf_op jit(solution)/shard_map/restore/pallas_call | solution.py:251
  20.8 16.4 %all_to_all.11.in_ref = bf16[16,96,128]{2,1,0:T(8,128)(2,1)S(1)} all-to-all(bf16[16,96,128]{2,1,0:T(8,128)(2,1)S(1)} %restore.1), channel_id=1, replica_groups=mesh['groups'=2,'frame'=4,'row'=4] {'frame','row'}, dimensions={0} | all-to-all | bytes 786432 | tf_op jit(solution)/shard_map/all_to_all | solution.py:260
  37.3 1.2 %temporal.1 = (bf16[16,16,512]{2,1,0:T(8,128)(2,1)}, f32[16,16]{1,0:T(8,128)}) custom-call(bf16[16,96,128]{2,1,0:T(8,128)(2,1)S(1)} %all_to_all.11.in_ref), custom_call_target="tpu_custom_call" | custom-call | tf_op jit(solution)/shard_map/temporal/pallas_call | solution.py:261
Async XLA Ops:
  16.7 0.8 %copy-start = (s32[256,16,4]{0,2,1:T(4,128)S(1)}, s32[256,16,4]{0,2,1:T(4,128)}, u32[]{:S(2)}) copy-start(s32[256,16,4]{0,2,1:T(4,128)} %param.7) | copy-start | bytes 196612
  16.7 0.8 %copy-start.1 = (f32[8,5]{1,0:T(8,128)S(1)}, f32[8,5]{1,0:T(8,128)}, u32[]{:S(2)}) copy-start(f32[8,5]{1,0:T(8,128)} %kernels_ref.1) | copy-start | bytes 484
  16.8 0.8 %copy-start.2 = (s32[8]{0:T(128)S(1)}, s32[8]{0:T(128)}, u32[]{:S(2)}) copy-start(s32[8]{0:T(128)} %band_ref.1) | copy-start | bytes 100

commit v2 on v1

--- a/solution.py
+++ b/solution.py
@@ -126,9 +126,13 @@
 
 
 def restore_kernel(
-    band_ref, kernels_ref, observed_ref, masks_ref, out_ref, tap_ref, sums_ref, *, devices, rows_dev, tiles_dev
+    place_ref, band_ref, kernels_ref, *refs, devices, rows_dev, tiles_dev
 ):
     n_frame, n_row = devices
+    pieces, (masks_ref, out_ref, observed_ref, tap_ref, sums_ref) = refs[:n_row], refs[n_row:]
+    for step, piece in enumerate(pieces):
+        start = pl.multiple_of((place_ref[0] ^ step) * rows_dev, rows_dev)
+        observed_ref[pl.ds(start, rows_dev), :] = piece[...]
     height, _ = observed_ref.shape
     positions = rows_dev * tiles_dev
     row_ids = lax.broadcasted_iota(jnp.int32, (BAND, TILE), 0)
@@ -239,6 +243,15 @@
     traces_ref[...] = trace_sums / (TILE * counts)
 
 
+def swapped(parts, axis):
+    count, place = lax.axis_size(axis), lax.axis_index(axis)
+    arrived = [lax.dynamic_index_in_dim(parts, place, 0, keepdims=False, allow_negative_indices=False)]
+    for step in range(1, count):
+        part = lax.dynamic_index_in_dim(parts, place ^ step, 0, keepdims=False, allow_negative_indices=False)
+        arrived.append(lax.ppermute(part, axis, [(i, i ^ step) for i in range(count)]))
+    return arrived
+
+
 def by_frame(observed, kernels, band_kernel, masks):
     n_frame, n_row = lax.axis_size("frame"), lax.axis_size("row")
     places = n_frame * n_row
@@ -246,17 +259,22 @@
     height, width = rows_dev * n_row, observed.shape[2]
     share = components // places
     block_rows = rows_dev * tiles_dev + places + share
-    sent = lax.all_to_all(observed.astype(jnp.float16), "row", split_axis=0, concat_axis=0, tiled=True)
-    image = sent.astype(jnp.float32).reshape(height, width)
+    place = lax.axis_index("row")
+    pieces = swapped(observed.astype(jnp.float16), "row")
+    pieces = [piece.astype(jnp.float32) for piece in pieces]
     blocks = pl.pallas_call(
         functools.partial(restore_kernel, devices=(n_frame, n_row), rows_dev=rows_dev, tiles_dev=tiles_dev),
         out_shape=jax.ShapeDtypeStruct((places, block_rows, TILE), jnp.bfloat16),
-        in_specs=[pl.BlockSpec(memory_space=pltpu.SMEM)] * 2 + [pl.BlockSpec(memory_space=pltpu.VMEM)] * 2,
+        in_specs=[pl.BlockSpec(memory_space=pltpu.SMEM)] * 3 + [pl.BlockSpec(memory_space=pltpu.VMEM)] * (n_row + 1),
         out_specs=pl.BlockSpec(memory_space=pltpu.VMEM),
-        scratch_shapes=[pltpu.VMEM((TAPS, height, TILE), jnp.float32), pltpu.VMEM((places, TILE), jnp.float32)],
+        scratch_shapes=[
+            pltpu.VMEM((height, width), jnp.float32),
+            pltpu.VMEM((TAPS, height, TILE), jnp.float32),
+            pltpu.VMEM((places, TILE), jnp.float32),
+        ],
         compiler_params=pltpu.CompilerParams(vmem_limit_bytes=16 << 20),
         name="restore",
-    )(band_kernel, kernels, image, masks.transpose(1, 2, 0))
+    )(place.reshape(1), band_kernel, kernels, *pieces, masks.transpose(1, 2, 0))
     series = lax.all_to_all(blocks, ("frame", "row"), split_axis=0, concat_axis=0, tiled=True)
     spikes, traces = pl.pallas_call(
         functools.partial(temporal_kernel, rows_dev=rows_dev, tiles_dev=tiles_dev, share=share),
@@ -279,7 +297,7 @@
     tiles_dev = masks.shape[2] // mesh.shape["frame"]
     places = mesh.shape["frame"] * mesh.shape["row"]
     return (
-        frames_dev == mesh.shape["row"]
+        frames_dev == mesh.shape["row"] == 4
         and 2 * rows_dev * tiles_dev == TILE
         and rows_dev == 16
         and places == 16

time: 38.7 us -> 35.7 us (0.922)
  blocking collectives: 31.4 us -> 17.7 us
  starting transfers between devices: 0 us -> 5.76 us
  waiting for transfers between devices: 0 us -> 4.95 us
    all_to_all x1 -> x0, blocking collectives: 15 us -> none  [by_frame(): lax.all_to_all(observed.astype(jnp.float16), 'row', split_axis=0, concat_...]
    ppermute x0 -> x3, starting transfers between devices: none -> 5.76 us  [swapped(): lax.ppermute(part, axis, [(i, i ^ step) for i in range(count)])]
    ppermute x0 -> x3, waiting for transfers between devices: none -> 4.95 us  [swapped(): lax.ppermute(part, axis, [(i, i ^ step) for i in range(count)])]
    all_to_all x1, blocking collectives: 16.4 us -> 17.7 us  [by_frame(): lax.all_to_all(blocks, ('frame', 'row'), split_axis=0, concat_axis=0, til...]
    convert_element_type x1 -> x4, other arithmetic: 1.07 us -> 1.1 us  [the longest x1 1.07 us: by_frame(): pieces = swapped(observed.astype(jnp.float16), 'row')]
  transfers between devices with their start and end apart: 0 -> 3, of which waited for: 0 -> 2; matrix products, arithmetic and copies ran while one was open for 0% -> 0% of each run, Pallas kernels for 0% -> 0%
where the time goes in v2:
time: 35.7 us; the launch traced here: 35.5 us
  blocking collectives  17.7 us (50%)
  starting transfers between devices  5.76 us (16%)
  waiting for transfers between devices  4.95 us (14%)
  Pallas kernels  4.43 us (12%)
  other arithmetic  1.16 us (3%)
  local copies, waits for them, and re-layouts  0.79 us (2%)
  between operations  0.7 us (2%)
    all_to_all x1, blocking collectives, by_frame(): lax.all_to_all(blocks, ('frame', 'row'), split_axis=0, concat_axis=0, til...  17.7 us
    ppermute x3, starting transfers between devices, swapped(): lax.ppermute(part, axis, [(i, i ^ step) for i in range(count)])  5.76 us
    ppermute x3, waiting for transfers between devices, swapped(): lax.ppermute(part, axis, [(i, i ^ step) for i in range(count)])  4.95 us
    pallas_call x1, Pallas kernels, by_frame(): pl.pallas_call(functools.partial(restore_kernel, devices=(n_frame, n_row)...  3.27 us
    pallas_call x1, Pallas kernels, by_frame(): pl.pallas_call(functools.partial(temporal_kernel, rows_dev=rows_dev, tile...  1.15 us
    convert_element_type x1, other arithmetic, by_frame(): pieces = swapped(observed.astype(jnp.float16), 'row')  1.07 us
    unnamed x6, local copies, waits for them, and re-layouts  0.79 us
  transfers between devices with their start and end apart: 3, of which 2 were waited for; matrix products, arithmetic and copies ran while one was open for 0% of the time, Pallas kernels for 0%

profile of v2, /device:TPU:0, one launch (start us, length us, event | category | flops | bytes accessed | tf_op | source)
XLA Modules:
  0.0 35.5 jit_solution(18318439285822414876)
XLA Ops:
  0.6 1.1 %convert_element_type.17 = f16[4,16,2048]{2,1,0:T(8,128)(2,1)S(1)} convert(f32[4,16,2048]{2,1,0:T(8,128)} %param.4) | non-fusion elementwise | flops 131072 | bytes 786432 | tf_op jit(solution)/shard_map/convert_element_type | solution.py:263
  1.7 0.1 dynamic-slice_bitcast_fusion
  1.8 5.1 %collective-permute-start.2 = (f16[16,2048]{1,0:T(8,128)(2,1)S(1)}, f16[16,2048]{1,0:T(8,128)(2,1)S(1)}, u32[]{:S(2)}, u32[]{:S(2)}) collective-permute-start(f16[16,2048]{1,0:T(8,128)(2,1)S(1)} %get-tuple-element.2), channel_id=1, source_target_pairs={{0,3},{1,2},{2,1},{3,0},{4,7},{5,6},{6,5},{7,4},{8,11},{9,10},{10,... | collective-permute-start | bytes 196616 | tf_op jit(solution)/shard_map/ppermute | solution.py:251
  6.9 0.0 collective-permute-start.1
  6.9 0.6 %collective-permute-start = (f16[16,2048]{1,0:T(8,128)(2,1)S(1)}, f16[16,2048]{1,0:T(8,128)(2,1)S(1)}, u32[]{:S(2)}, u32[]{:S(2)}) collective-permute-start(f16[16,2048]{1,0:T(8,128)(2,1)S(1)} %get-tuple-element.4), channel_id=1, source_target_pairs={{0,1},{1,0},{2,3},{3,2},{4,5},{5,4},{6,7},{7,6},{8,9},{9,8},{10,11... | collective-permute-start | bytes 196616 | tf_op jit(solution)/shard_map/ppermute | solution.py:251
  7.5 1.9 %collective-permute-done.2 = f16[16,2048]{1,0:T(8,128)(2,1)S(1)} collective-permute-done((f16[16,2048]{1,0:T(8,128)(2,1)S(1)}, f16[16,2048]{1,0:T(8,128)(2,1)S(1)}, u32[]{:S(2)}, u32[]{:S(2)}) %collective-permute-start.2) | collective-permute-done | bytes 65568 | tf_op jit(solution)/shard_map/ppermute | solution.py:251
  9.5 3.0 %collective-permute-done.1 = f16[16,2048]{1,0:T(8,128)(2,1)S(1)} collective-permute-done((f16[16,2048]{1,0:T(8,128)(2,1)S(1)}, f16[16,2048]{1,0:T(8,128)(2,1)S(1)}, u32[]{:S(2)}, u32[]{:S(2)}) %collective-permute-start.1) | collective-permute-done | bytes 65568 | tf_op jit(solution)/shard_map/ppermute | solution.py:251
  12.5 0.0 copy-start
  12.5 0.0 collective-permute-done
  12.5 0.0 copy-start.1
  12.6 0.0 copy-start.2
  12.6 0.8 %copy-done = s32[256,16,4]{0,2,1:T(4,128)S(1)} copy-done((s32[256,16,4]{0,2,1:T(4,128)S(1)}, s32[256,16,4]{0,2,1:T(4,128)}, u32[]{:S(2)}) %copy-start) | copy-done | bytes 65560
  13.3 0.0 copy-done.1
  13.3 0.0 copy-done.2
  13.3 3.3 %restore.1 = bf16[16,96,128]{2,1,0:T(8,128)(2,1)S(1)} custom-call(s32[1]{0:T(128)} %bitcast.place_ref, s32[8]{0:T(128)S(1)} %copy-done.2, f32[8,5]{1,0:T(8,128)S(1)} %copy-done.1, f32[16,2048]{1,0:T(8,128)S(1)} %get-tuple-element.5.refs_0_, f32[16,2048]{1,0:T(8,128)S(1)} %convert_element_type.20.refs_1_, f32[16,2048]{1,0:T(8,128)S(1)} %convert_element_type.21.refs_2_, ...), custom_call_target="tpu_custom_call" | custom-call | tf_op jit(solution)/shard_map/restore/pallas_call | solution.py:265
  16.6 17.7 %all_to_all.5.in_ref = bf16[16,96,128]{2,1,0:T(8,128)(2,1)S(1)} all-to-all(bf16[16,96,128]{2,1,0:T(8,128)(2,1)S(1)} %restore.1), channel_id=1, replica_groups=mesh['groups'=2,'frame'=4,'row'=4] {'frame','row'}, dimensions={0} | all-to-all | bytes 786432 | tf_op jit(solution)/shard_map/all_to_all | solution.py:278
  34.3 1.2 %temporal.1 = (bf16[16,16,512]{2,1,0:T(8,128)(2,1)}, f32[16,16]{1,0:T(8,128)}) custom-call(bf16[16,96,128]{2,1,0:T(8,128)(2,1)S(1)} %all_to_all.5.in_ref), custom_call_target="tpu_custom_call" | custom-call | tf_op jit(solution)/shard_map/temporal/pallas_call | solution.py:279
  (3 shorter events, 0.0 us)
Async XLA Ops:
  1.8 7.7 %collective-permute-start.2 = (f16[16,2048]{1,0:T(8,128)(2,1)S(1)}, f16[16,2048]{1,0:T(8,128)(2,1)S(1)}, u32[]{:S(2)}, u32[]{:S(2)}) collective-permute-start(f16[16,2048]{1,0:T(8,128)(2,1)S(1)} %get-tuple-element.2), channel_id=1, source_target_pairs={{0,3},{1,2},{2,1},{3,0},{4,7},{5,6},{6,5},{7,4},{8,11},{9,10},{10,... | collective-permute-start | bytes 196616 | tf_op jit(solution)/shard_map/ppermute | solution.py:251
  6.9 5.6 %collective-permute-start.1 = (f16[16,2048]{1,0:T(8,128)(2,1)S(1)}, f16[16,2048]{1,0:T(8,128)(2,1)S(1)}, u32[]{:S(2)}, u32[]{:S(2)}) collective-permute-start(f16[16,2048]{1,0:T(8,128)(2,1)S(1)} %get-tuple-element.3), channel_id=1, source_target_pairs={{0,2},{1,3},{2,0},{3,1},{4,6},{5,7},{6,4},{7,5},{8,10},{9,11},{10,... | collective-permute-start | bytes 196616 | tf_op jit(solution)/shard_map/ppermute | solution.py:251
  6.9 5.6 %collective-permute-start = (f16[16,2048]{1,0:T(8,128)(2,1)S(1)}, f16[16,2048]{1,0:T(8,128)(2,1)S(1)}, u32[]{:S(2)}, u32[]{:S(2)}) collective-permute-start(f16[16,2048]{1,0:T(8,128)(2,1)S(1)} %get-tuple-element.4), channel_id=1, source_target_pairs={{0,1},{1,0},{2,3},{3,2},{4,5},{5,4},{6,7},{7,6},{8,9},{9,8},{10,11... | collective-permute-start | bytes 196616 | tf_op jit(solution)/shard_map/ppermute | solution.py:251
  12.5 0.8 %copy-start = (s32[256,16,4]{0,2,1:T(4,128)S(1)}, s32[256,16,4]{0,2,1:T(4,128)}, u32[]{:S(2)}) copy-start(s32[256,16,4]{0,2,1:T(4,128)} %param.7) | copy-start | bytes 196612
  12.5 0.8 %copy-start.1 = (f32[8,5]{1,0:T(8,128)S(1)}, f32[8,5]{1,0:T(8,128)}, u32[]{:S(2)}) copy-start(f32[8,5]{1,0:T(8,128)} %kernels_ref.1) | copy-start | bytes 484
  12.6 0.8 %copy-start.2 = (s32[8]{0:T(128)S(1)}, s32[8]{0:T(128)}, u32[]{:S(2)}) copy-start(s32[8]{0:T(128)} %band_ref.1) | copy-start | bytes 100

commit v3 on v2

--- a/solution.py
+++ b/solution.py
@@ -131,7 +131,7 @@
     n_frame, n_row = devices
     pieces, (masks_ref, out_ref, observed_ref, tap_ref, sums_ref) = refs[:n_row], refs[n_row:]
     for step, piece in enumerate(pieces):
-        start = pl.multiple_of((place_ref[0] ^ step) * rows_dev, rows_dev)
+        start = pl.multiple_of((place_ref[1] ^ step) * rows_dev, rows_dev)
         observed_ref[pl.ds(start, rows_dev), :] = piece[...]
     height, _ = observed_ref.shape
     positions = rows_dev * tiles_dev
@@ -148,11 +148,18 @@
             weight = jnp.where((target >= 0) & (target < height), weight, 0.0)
             tap_ref[tap, band * BAND : (band + 1) * BAND, :] = weight
     flat = jnp.concatenate([masks_ref[row].astype(jnp.float32) for row in range(rows_dev)], axis=0)
-    both = jnp.concatenate([flat, flat], axis=0).T.astype(jnp.bfloat16)
+    both = jnp.concatenate([flat, flat], axis=0).T
     share = both.shape[0] // (n_frame * n_row)
-    est_rows = rows_dev * tiles_dev
-    for place in range(n_frame * n_row):
-        out_ref[place, est_rows + rows_dev : est_rows + rows_dev + share, :] = both[place * share : (place + 1) * share]
+    left = lax.broadcasted_iota(jnp.int32, (share, TILE), 1) < positions
+    sums_row = n_frame * positions
+    masks_row = sums_row + n_frame * n_row
+    for row in range(n_row):
+        for pair in range(n_frame // 2):
+            first = (2 * pair * n_row + row) * share
+            second = first + n_row * share
+            halves = jnp.where(left, both[first : first + share], both[second : second + share])
+            start = masks_row + pair * share
+            out_ref[row, start : start + share, :] = halves.astype(jnp.bfloat16)
     lanes = lax.broadcasted_iota(jnp.int32, (rows_dev, TILE), 1)
     own_rows = lax.broadcasted_iota(jnp.int32, (rows_dev, TILE), 0)
     ones = jnp.ones((TILE, TILE), jnp.bfloat16)
@@ -174,9 +181,8 @@
                 current = current * back
             estimate = current.astype(jnp.bfloat16)
             for row in range(n_row):
-                out_ref[block * n_row + row, tile * rows_dev : (tile + 1) * rows_dev, :] = estimate[
-                    row * rows_dev : (row + 1) * rows_dev
-                ]
+                start = pl.multiple_of(block * positions + tile * rows_dev, rows_dev)
+                out_ref[row, pl.ds(start, rows_dev), :] = estimate[row * rows_dev : (row + 1) * rows_dev]
             tile_sums = jnp.dot(estimate, ones, preferred_element_type=jnp.float32)
             here = lanes % positions == own_rows * tiles_dev + tile
             for row in range(n_row):
@@ -191,8 +197,21 @@
     high = sums.astype(jnp.bfloat16).astype(jnp.float32)
     split = jnp.where(lax.broadcasted_iota(jnp.int32, sums.shape, 1) < positions, high, sums - high)
     split = split.astype(jnp.bfloat16)
-    for place in range(n_frame * n_row):
-        out_ref[place, est_rows : est_rows + rows_dev, :] = split
+    for row in range(n_row):
+        out_ref[row, sums_row:masks_row, :] = split
+
+
+def regroup_kernel(*refs, positions, places, share):
+    pieces, out_ref = refs[:-1], refs[-1]
+    n_frame = out_ref.shape[0]
+    sums_row = n_frame * positions
+    masks_row = sums_row + places
+    for block in range(n_frame):
+        for step, piece in enumerate(pieces):
+            out_ref[block, step, :positions, :] = piece[block * positions : (block + 1) * positions, :]
+            out_ref[block, step, positions : positions + places, :] = piece[sums_row:masks_row, :]
+            start = masks_row + block // 2 * share
+            out_ref[block, step, positions + places :, :] = piece[start : start + share, :]
 
 
 def deconvolved(series, factors):
@@ -222,7 +241,12 @@
     return factors
 
 
-def temporal_kernel(in_ref, spikes_ref, traces_ref, sums_ref, *, rows_dev, tiles_dev, share):
+def temporal_kernel(place_ref, *refs, devices, rows_dev, tiles_dev, share):
+    n_frame, n_row = devices
+    pieces, (spikes_ref, traces_ref, in_ref, sums_ref) = refs[:n_frame], refs[n_frame:]
+    for step, piece in enumerate(pieces):
+        for inner in range(n_row):
+            in_ref[(place_ref[0] ^ step) * n_row + (place_ref[1] ^ inner)] = piece[inner]
     frames = in_ref.shape[0]
     factors = solve_factors(frames)
     for tile in range(tiles_dev):
@@ -232,14 +256,16 @@
     first = rows_dev * tiles_dev
     series = [in_ref[t, first : first + frames, :].astype(jnp.float32) for t in range(frames)]
     for t, sums in enumerate(deconvolved(series, factors)):
-        sums_ref[t * frames : (t + 1) * frames, :] = sums
+        sums_ref[t * frames : (t + 1) * frames, :] = sums + pltpu.roll(sums, TILE // 2, 1)
     first += frames
     weights = jnp.concatenate([in_ref[j, first : first + share, :].astype(jnp.float32) for j in range(frames)], axis=1)
+    halves = lax.broadcasted_iota(jnp.int32, weights.shape, 1) // (TILE // 2)
+    weights = jnp.where(halves % 2 == place_ref[0] % 2, weights, 0.0)
     sums = jnp.concatenate([sums_ref[pl.ds(j, frames, stride=frames), :] for j in range(frames)], axis=1)
     trace_sums = lax.dot_general(
         weights, sums, (((1,), (1,)), ((), ())), precision=lax.Precision.HIGHEST, preferred_element_type=jnp.float32
     )
-    counts = 0.5 * jnp.sum(weights, axis=1, keepdims=True)
+    counts = jnp.sum(weights, axis=1, keepdims=True)
     traces_ref[...] = trace_sums / (TILE * counts)
 
 
@@ -253,41 +279,53 @@
 
 
 def by_frame(observed, kernels, band_kernel, masks):
-    n_frame, n_row = lax.axis_size("frame"), lax.axis_size("row")
+    devices = n_frame, n_row = lax.axis_size("frame"), lax.axis_size("row")
     places = n_frame * n_row
     components, rows_dev, tiles_dev = masks.shape
     height, width = rows_dev * n_row, observed.shape[2]
     share = components // places
-    block_rows = rows_dev * tiles_dev + places + share
-    place = lax.axis_index("row")
-    pieces = swapped(observed.astype(jnp.float16), "row")
-    pieces = [piece.astype(jnp.float32) for piece in pieces]
+    positions = rows_dev * tiles_dev
+    place = jnp.stack([lax.axis_index("frame"), lax.axis_index("row")])
+    smem, vmem = pl.BlockSpec(memory_space=pltpu.SMEM), pl.BlockSpec(memory_space=pltpu.VMEM)
+    params = pltpu.CompilerParams(vmem_limit_bytes=16 << 20)
+    pieces = [piece.astype(jnp.float32) for piece in swapped(observed.astype(jnp.float16), "row")]
+    block_rows = n_frame * positions + places + n_frame // 2 * share
     blocks = pl.pallas_call(
-        functools.partial(restore_kernel, devices=(n_frame, n_row), rows_dev=rows_dev, tiles_dev=tiles_dev),
-        out_shape=jax.ShapeDtypeStruct((places, block_rows, TILE), jnp.bfloat16),
-        in_specs=[pl.BlockSpec(memory_space=pltpu.SMEM)] * 3 + [pl.BlockSpec(memory_space=pltpu.VMEM)] * (n_row + 1),
-        out_specs=pl.BlockSpec(memory_space=pltpu.VMEM),
+        functools.partial(restore_kernel, devices=devices, rows_dev=rows_dev, tiles_dev=tiles_dev),
+        out_shape=jax.ShapeDtypeStruct((n_row, block_rows, TILE), jnp.bfloat16),
+        in_specs=[smem] * 3 + [vmem] * (n_row + 1),
+        out_specs=vmem,
         scratch_shapes=[
             pltpu.VMEM((height, width), jnp.float32),
             pltpu.VMEM((TAPS, height, TILE), jnp.float32),
             pltpu.VMEM((places, TILE), jnp.float32),
         ],
-        compiler_params=pltpu.CompilerParams(vmem_limit_bytes=16 << 20),
+        compiler_params=params,
         name="restore",
-    )(place.reshape(1), band_kernel, kernels, *pieces, masks.transpose(1, 2, 0))
-    series = lax.all_to_all(blocks, ("frame", "row"), split_axis=0, concat_axis=0, tiled=True)
+    )(place, band_kernel, kernels, *pieces, masks.transpose(1, 2, 0))
+    blocks = pl.pallas_call(
+        functools.partial(regroup_kernel, positions=positions, places=places, share=share),
+        out_shape=jax.ShapeDtypeStruct((n_frame, n_row, positions + places + share, TILE), jnp.bfloat16),
+        in_specs=[vmem] * n_row,
+        out_specs=vmem,
+        compiler_params=params,
+        name="regroup",
+    )(*swapped(blocks, "row"))
     spikes, traces = pl.pallas_call(
-        functools.partial(temporal_kernel, rows_dev=rows_dev, tiles_dev=tiles_dev, share=share),
+        functools.partial(temporal_kernel, devices=devices, rows_dev=rows_dev, tiles_dev=tiles_dev, share=share),
         out_shape=(
             jax.ShapeDtypeStruct((places, rows_dev, tiles_dev * TILE), jnp.bfloat16),
             jax.ShapeDtypeStruct((share, places), jnp.float32),
         ),
-        in_specs=[pl.BlockSpec(memory_space=pltpu.VMEM)],
-        out_specs=(pl.BlockSpec(memory_space=pltpu.VMEM),) * 2,
-        scratch_shapes=[pltpu.VMEM((places * places, TILE), jnp.float32)],
-        compiler_params=pltpu.CompilerParams(vmem_limit_bytes=16 << 20),
+        in_specs=[smem] + [vmem] * n_frame,
+        out_specs=(vmem, vmem),
+        scratch_shapes=[
+            pltpu.VMEM((places, positions + places + share, TILE), jnp.bfloat16),
+            pltpu.VMEM((places * places, TILE), jnp.float32),
+        ],
+        compiler_params=params,
         name="temporal",
-    )(series)
+    )(place, *swapped(blocks, "frame"))
     return (spikes, traces)
 
 
@@ -298,6 +336,7 @@
     places = mesh.shape["frame"] * mesh.shape["row"]
     return (
         frames_dev == mesh.shape["row"] == 4
+        and mesh.shape["frame"] == 4
         and 2 * rows_dev * tiles_dev == TILE
         and rows_dev == 16
         and places == 16

time: 35.7 us -> 35.5 us (level)
  blocking collectives: 17.7 us -> 0 us
  waiting for transfers between devices: 4.95 us -> 15.4 us
  starting transfers between devices: 5.76 us -> 12.1 us
  Pallas kernels: 4.43 us -> 5.16 us
    all_to_all x1 -> x0, blocking collectives: 17.7 us -> none  [by_frame(): lax.all_to_all(blocks, ('frame', 'row'), split_axis=0, concat_axis=0, til...]
    ppermute x3 -> x9, waiting for transfers between devices: 4.95 us -> 15.4 us  [swapped(): lax.ppermute(part, axis, [(i, i ^ step) for i in range(count)])]
    ppermute x3 -> x9, starting transfers between devices: 5.76 us -> 12.1 us  [swapped(): lax.ppermute(part, axis, [(i, i ^ step) for i in range(count)])]
    pallas_call x2 -> x3, Pallas kernels: 4.43 us -> 5.16 us  [the longest x1 3.3 us: by_frame(): pl.pallas_call(functools.partial(restore_kernel, devices=devices, rows_de...]
  transfers between devices with their start and end apart: 3 -> 9, of which waited for: 2 -> 6; matrix products, arithmetic and copies ran while one was open for 0% -> 0% of each run, Pallas kernels for 0% -> 0%
where the time goes in v3:
time: 35.5 us; the launch traced here: 35.3 us
  waiting for transfers between devices  15.4 us (43%)
  starting transfers between devices  12.1 us (34%)
  Pallas kernels  5.16 us (15%)
  other arithmetic  1.23 us (3%)
  local copies, waits for them, and re-layouts  0.74 us (2%)
  between operations  0.73 us (2%)
    ppermute x9, waiting for transfers between devices, swapped(): lax.ppermute(part, axis, [(i, i ^ step) for i in range(count)])  15.4 us
    ppermute x9, starting transfers between devices, swapped(): lax.ppermute(part, axis, [(i, i ^ step) for i in range(count)])  12.1 us
    pallas_call x1, Pallas kernels, by_frame(): pl.pallas_call(functools.partial(restore_kernel, devices=devices, rows_de...  3.3 us
    pallas_call x1, Pallas kernels, by_frame(): pl.pallas_call(functools.partial(temporal_kernel, devices=devices, rows_d...  1.82 us
    convert_element_type x1, other arithmetic, by_frame(): observed.astype(jnp.float16)  1.07 us
  transfers between devices with their start and end apart: 9, of which 6 were waited for; matrix products, arithmetic and copies ran while one was open for 0% of the time, Pallas kernels for 0%

profile of v3, /device:TPU:0, one launch (start us, length us, event | category | flops | bytes accessed | tf_op | source)
XLA Modules:
  0.0 35.3 jit_solution(10974119828382659620)
XLA Ops:
  0.6 1.1 %convert_element_type.17 = f16[4,16,2048]{2,1,0:T(8,128)(2,1)S(1)} convert(f32[4,16,2048]{2,1,0:T(8,128)} %param.4) | non-fusion elementwise | flops 131072 | bytes 786432 | tf_op jit(solution)/shard_map/convert_element_type | solution.py:291
  1.7 0.1 dynamic-slice_bitcast_fusion.8
  1.8 3.1 %collective-permute-start = (f16[16,2048]{1,0:T(8,128)(2,1)S(1)}, f16[16,2048]{1,0:T(8,128)(2,1)S(1)}, u32[]{:S(2)}, u32[]{:S(2)}) collective-permute-start(f16[16,2048]{1,0:T(8,128)(2,1)S(1)} %get-tuple-element.12), channel_id=1, source_target_pairs={{0,1},{1,0},{2,3},{3,2},{4,5},{5,4},{6,7},{7,6},{8,9},{9,8},{10,11... | collective-permute-start | bytes 196616 | tf_op jit(solution)/shard_map/ppermute | solution.py:277
  4.9 2.6 %collective-permute-start.1 = (f16[16,2048]{1,0:T(8,128)(2,1)S(1)}, f16[16,2048]{1,0:T(8,128)(2,1)S(1)}, u32[]{:S(2)}, u32[]{:S(2)}) collective-permute-start(f16[16,2048]{1,0:T(8,128)(2,1)S(1)} %get-tuple-element.11), channel_id=1, source_target_pairs={{0,2},{1,3},{2,0},{3,1},{4,6},{5,7},{6,4},{7,5},{8,10},{9,11},{10,... | collective-permute-start | bytes 196616 | tf_op jit(solution)/shard_map/ppermute | solution.py:277
  7.4 0.0 collective-permute-start.2
  7.5 0.1 pad_add_fusion.place_ref
  7.5 0.0 collective-permute-done
  7.5 4.6 %collective-permute-done.1 = f16[16,2048]{1,0:T(8,128)(2,1)S(1)} collective-permute-done((f16[16,2048]{1,0:T(8,128)(2,1)S(1)}, f16[16,2048]{1,0:T(8,128)(2,1)S(1)}, u32[]{:S(2)}, u32[]{:S(2)}) %collective-permute-start.1) | collective-permute-done | bytes 65568 | tf_op jit(solution)/shard_map/ppermute | solution.py:277
  12.1 0.0 copy-start
  12.1 1.4 %collective-permute-done.2 = f16[16,2048]{1,0:T(8,128)(2,1)S(1)} collective-permute-done((f16[16,2048]{1,0:T(8,128)(2,1)S(1)}, f16[16,2048]{1,0:T(8,128)(2,1)S(1)}, u32[]{:S(2)}, u32[]{:S(2)}) %collective-permute-start.2) | collective-permute-done | bytes 65568 | tf_op jit(solution)/shard_map/ppermute | solution.py:277
  13.5 0.0 copy-start.1
  13.5 0.0 copy-start.2
  13.6 0.0 copy-done
  13.6 0.6 %copy-done.1 = f32[8,5]{1,0:T(8,128)S(1)} copy-done((f32[8,5]{1,0:T(8,128)S(1)}, f32[8,5]{1,0:T(8,128)}, u32[]{:S(2)}) %copy-start.1) | copy-done | bytes 184
  14.2 0.0 copy-done.2
  14.2 3.3 %restore.1 = bf16[4,304,128]{2,1,0:T(8,128)(2,1)S(1)} custom-call(s32[2]{0:T(128)S(1)} %pad_add_fusion.place_ref, s32[8]{0:T(128)S(1)} %copy-done.2, f32[8,5]{1,0:T(8,128)S(1)} %copy-done.1, f32[16,2048]{1,0:T(8,128)S(1)} %get-tuple-element.13.refs_0_, f32[16,2048]{1,0:T(8,128)S(1)} %convert_element_type.20.refs_1_, ...), custom_call_target="tpu_custom_call" | custom-call | tf_op jit(solution)/shard_map/restore/pallas_call | solution.py:293
  17.6 0.1 collective-permute-start.3
  17.6 2.5 %collective-permute-start.4 = (bf16[304,128]{1,0:T(8,128)(2,1)S(1)}, bf16[304,128]{1,0:T(8,128)(2,1)S(1)}, u32[]{:S(2)}, u32[]{:S(2)}) collective-permute-start(bf16[304,128]{1,0:T(8,128)(2,1)S(1)} %get-tuple-element.7), channel_id=1, source_target_pairs={{0,2},{1,3},{2,0},{3,1},{4,6},{5,7},{6,4},{7,5},{8,10},{9,11},{10,... | collective-permute-start | bytes 233480 | tf_op jit(solution)/shard_map/ppermute | solution.py:277
  20.1 1.9 %collective-permute-start.5 = (bf16[304,128]{1,0:T(8,128)(2,1)S(1)}, bf16[304,128]{1,0:T(8,128)(2,1)S(1)}, u32[]{:S(2)}, u32[]{:S(2)}) collective-permute-start(bf16[304,128]{1,0:T(8,128)(2,1)S(1)} %get-tuple-element.6), channel_id=1, source_target_pairs={{0,3},{1,2},{2,1},{3,0},{4,7},{5,6},{6,5},{7,4},{8,11},{9,10},{10,... | collective-permute-start | bytes 233480 | tf_op jit(solution)/shard_map/ppermute | solution.py:277
  22.0 0.0 collective-permute-done.3.refs_1_
  22.0 2.9 %collective-permute-done.4.refs_2_ = bf16[304,128]{1,0:T(8,128)(2,1)S(1)} collective-permute-done((bf16[304,128]{1,0:T(8,128)(2,1)S(1)}, bf16[304,128]{1,0:T(8,128)(2,1)S(1)}, u32[]{:S(2)}, u32[]{:S(2)}) %collective-permute-start.4) | collective-permute-done | bytes 77856 | tf_op jit(solution)/shard_map/ppermute | solution.py:277
  24.9 1.6 %collective-permute-done.5.refs_3_ = bf16[304,128]{1,0:T(8,128)(2,1)S(1)} collective-permute-done((bf16[304,128]{1,0:T(8,128)(2,1)S(1)}, bf16[304,128]{1,0:T(8,128)(2,1)S(1)}, u32[]{:S(2)}, u32[]{:S(2)}) %collective-permute-start.5) | collective-permute-done | bytes 77856 | tf_op jit(solution)/shard_map/ppermute | solution.py:277
  26.5 0.1 collective-permute-start.6
  26.6 1.6 %collective-permute-start.7 = (bf16[4,96,128]{2,1,0:T(8,128)(2,1)S(1)}, bf16[4,96,128]{2,1,0:T(8,128)(2,1)S(1)}, u32[]{:S(2)}, u32[]{:S(2)}) collective-permute-start(bf16[4,96,128]{2,1,0:T(8,128)(2,1)S(1)} %get-tuple-element.3), channel_id=1, source_target_pairs={{0,8},{4,12},{8,0},{12,4},{1,9},{5,13},{9,1},{13,5},{2,10},{6,14},... | collective-permute-start | bytes 294920 | tf_op jit(solution)/shard_map/ppermute | solution.py:277
  28.2 0.3 collective-permute-start.8
  28.5 0.0 collective-permute-done.6.refs_1_
  28.5 3.8 %collective-permute-done.7.refs_2_ = bf16[4,96,128]{2,1,0:T(8,128)(2,1)S(1)} collective-permute-done((bf16[4,96,128]{2,1,0:T(8,128)(2,1)S(1)}, bf16[4,96,128]{2,1,0:T(8,128)(2,1)S(1)}, u32[]{:S(2)}, u32[]{:S(2)}) %collective-permute-start.7) | collective-permute-done | bytes 98336 | tf_op jit(solution)/shard_map/ppermute | solution.py:277
  32.3 1.2 %collective-permute-done.8.refs_3_ = bf16[4,96,128]{2,1,0:T(8,128)(2,1)S(1)} collective-permute-done((bf16[4,96,128]{2,1,0:T(8,128)(2,1)S(1)}, bf16[4,96,128]{2,1,0:T(8,128)(2,1)S(1)}, u32[]{:S(2)}, u32[]{:S(2)}) %collective-permute-start.8) | collective-permute-done | bytes 98336 | tf_op jit(solution)/shard_map/ppermute | solution.py:277
  33.5 1.8 %temporal.1 = (bf16[16,16,512]{2,1,0:T(8,128)(2,1)}, f32[16,16]{1,0:T(8,128)}) custom-call(s32[2]{0:T(128)S(1)} %pad_add_fusion.place_ref, bf16[4,96,128]{2,1,0:T(8,128)(2,1)S(1)} %get-tuple-element.5.refs_0_, bf16[4,96,128]{2,1,0:T(8,128)(2,1)S(1)} %collective-permute-done.6.refs_1_, bf16[4,96,128]{2,1,0:T(8,128)(2,1)S(1)} %collective-permute-done.7.refs_2_, ...), custom_call_target="tpu_custom_call" | custom-call | tf_op jit(solution)/shard_map/temporal/pallas_call | solution.py:314
  (6 shorter events, 0.1 us)
Async XLA Ops:
  1.8 5.8 %collective-permute-start = (f16[16,2048]{1,0:T(8,128)(2,1)S(1)}, f16[16,2048]{1,0:T(8,128)(2,1)S(1)}, u32[]{:S(2)}, u32[]{:S(2)}) collective-permute-start(f16[16,2048]{1,0:T(8,128)(2,1)S(1)} %get-tuple-element.12), channel_id=1, source_target_pairs={{0,1},{1,0},{2,3},{3,2},{4,5},{5,4},{6,7},{7,6},{8,9},{9,8},{10,11... | collective-permute-start | bytes 196616 | tf_op jit(solution)/shard_map/ppermute | solution.py:277
  4.9 7.3 %collective-permute-start.1 = (f16[16,2048]{1,0:T(8,128)(2,1)S(1)}, f16[16,2048]{1,0:T(8,128)(2,1)S(1)}, u32[]{:S(2)}, u32[]{:S(2)}) collective-permute-start(f16[16,2048]{1,0:T(8,128)(2,1)S(1)} %get-tuple-element.11), channel_id=1, source_target_pairs={{0,2},{1,3},{2,0},{3,1},{4,6},{5,7},{6,4},{7,5},{8,10},{9,11},{10,... | collective-permute-start | bytes 196616 | tf_op jit(solution)/shard_map/ppermute | solution.py:277
  7.4 6.1 %collective-permute-start.2 = (f16[16,2048]{1,0:T(8,128)(2,1)S(1)}, f16[16,2048]{1,0:T(8,128)(2,1)S(1)}, u32[]{:S(2)}, u32[]{:S(2)}) collective-permute-start(f16[16,2048]{1,0:T(8,128)(2,1)S(1)} %get-tuple-element.10), channel_id=1, source_target_pairs={{0,3},{1,2},{2,1},{3,0},{4,7},{5,6},{6,5},{7,4},{8,11},{9,10},{10,... | collective-permute-start | bytes 196616 | tf_op jit(solution)/shard_map/ppermute | solution.py:277
  12.1 1.4 %copy-start = (s32[256,16,4]{0,2,1:T(4,128)S(1)}, s32[256,16,4]{0,2,1:T(4,128)}, u32[]{:S(2)}) copy-start(s32[256,16,4]{0,2,1:T(4,128)} %param.7) | copy-start | bytes 196612
  13.5 0.7 %copy-start.1 = (f32[8,5]{1,0:T(8,128)S(1)}, f32[8,5]{1,0:T(8,128)}, u32[]{:S(2)}) copy-start(f32[8,5]{1,0:T(8,128)} %kernels_ref.1) | copy-start | bytes 484
  13.5 0.7 %copy-start.2 = (s32[8]{0:T(128)S(1)}, s32[8]{0:T(128)}, u32[]{:S(2)}) copy-start(s32[8]{0:T(128)} %band_ref.1) | copy-start | bytes 100
  17.6 4.5 %collective-permute-start.3 = (bf16[304,128]{1,0:T(8,128)(2,1)S(1)}, bf16[304,128]{1,0:T(8,128)(2,1)S(1)}, u32[]{:S(2)}, u32[]{:S(2)}) collective-permute-start(bf16[304,128]{1,0:T(8,128)(2,1)S(1)} %get-tuple-element.8), channel_id=1, source_target_pairs={{0,1},{1,0},{2,3},{3,2},{4,5},{5,4},{6,7},{7,6},{8,9},{9,8},{10,11... | collective-permute-start | bytes 233480 | tf_op jit(solution)/shard_map/ppermute | solution.py:277
  17.6 7.2 %collective-permute-start.4 = (bf16[304,128]{1,0:T(8,128)(2,1)S(1)}, bf16[304,128]{1,0:T(8,128)(2,1)S(1)}, u32[]{:S(2)}, u32[]{:S(2)}) collective-permute-start(bf16[304,128]{1,0:T(8,128)(2,1)S(1)} %get-tuple-element.7), channel_id=1, source_target_pairs={{0,2},{1,3},{2,0},{3,1},{4,6},{5,7},{6,4},{7,5},{8,10},{9,11},{10,... | collective-permute-start | bytes 233480 | tf_op jit(solution)/shard_map/ppermute | solution.py:277
  20.1 6.3 %collective-permute-start.5 = (bf16[304,128]{1,0:T(8,128)(2,1)S(1)}, bf16[304,128]{1,0:T(8,128)(2,1)S(1)}, u32[]{:S(2)}, u32[]{:S(2)}) collective-permute-start(bf16[304,128]{1,0:T(8,128)(2,1)S(1)} %get-tuple-element.6), channel_id=1, source_target_pairs={{0,3},{1,2},{2,1},{3,0},{4,7},{5,6},{6,5},{7,4},{8,11},{9,10},{10,... | collective-permute-start | bytes 233480 | tf_op jit(solution)/shard_map/ppermute | solution.py:277
  26.5 1.9 %collective-permute-start.6 = (bf16[4,96,128]{2,1,0:T(8,128)(2,1)S(1)}, bf16[4,96,128]{2,1,0:T(8,128)(2,1)S(1)}, u32[]{:S(2)}, u32[]{:S(2)}) collective-permute-start(bf16[4,96,128]{2,1,0:T(8,128)(2,1)S(1)} %get-tuple-element.4), channel_id=1, source_target_pairs={{0,4},{4,0},{8,12},{12,8},{1,5},{5,1},{9,13},{13,9},{2,6},{6,2},{1... | collective-permute-start | bytes 294920 | tf_op jit(solution)/shard_map/ppermute | solution.py:277
  26.6 5.7 %collective-permute-start.7 = (bf16[4,96,128]{2,1,0:T(8,128)(2,1)S(1)}, bf16[4,96,128]{2,1,0:T(8,128)(2,1)S(1)}, u32[]{:S(2)}, u32[]{:S(2)}) collective-permute-start(bf16[4,96,128]{2,1,0:T(8,128)(2,1)S(1)} %get-tuple-element.3), channel_id=1, source_target_pairs={{0,8},{4,12},{8,0},{12,4},{1,9},{5,13},{9,1},{13,5},{2,10},{6,14},... | collective-permute-start | bytes 294920 | tf_op jit(solution)/shard_map/ppermute | solution.py:277
  28.2 5.3 %collective-permute-start.8 = (bf16[4,96,128]{2,1,0:T(8,128)(2,1)S(1)}, bf16[4,96,128]{2,1,0:T(8,128)(2,1)S(1)}, u32[]{:S(2)}, u32[]{:S(2)}) collective-permute-start(bf16[4,96,128]{2,1,0:T(8,128)(2,1)S(1)} %get-tuple-element.2), channel_id=1, source_target_pairs={{0,12},{4,8},{8,4},{12,0},{1,13},{5,9},{9,5},{13,1},{2,14},{6,10},... | collective-permute-start | bytes 294920 | tf_op jit(solution)/shard_map/ppermute | solution.py:277

commit v4 on v0

--- a/solution.py
+++ b/solution.py
@@ -1,11 +1,19 @@
+import functools
+
 import jax
 import jax.numpy as jnp
 from jax import lax
+from jax.experimental import pallas as pl
+from jax.experimental.pallas import tpu as pltpu
 from jax.sharding import PartitionSpec as P
 
 TILE = 128
 BAND = 8
 ITERS = 3
+TAPS = 5
+NEAR, FAR = 8, 4
+MARGIN = 2 * BAND
+STEPS = (((0, 48), (8, 40)), ((8, 40), (8, 40)), ((8, 40), (16, 32)))
 
 
 SMOOTHING = 1024.0
@@ -115,6 +123,317 @@
     return (spikes, traces)
 
 
+def to_half(cells):
+    return cells.astype(jnp.float16)
+
+
+def halo_kernel(observed_ref, first_ref, second_ref, own_ref):
+    even = lax.axis_index("row") % 2 == 0
+    frames = observed_ref.shape[0]
+    own_ref[...] = observed_ref[...]
+    for frame in range(frames):
+        image = observed_ref[frame]
+        near, far = slice(frame * NEAR, (frame + 1) * NEAR), slice(frames * NEAR + frame * FAR, frames * NEAR + (frame + 1) * FAR)
+        low, high = image[-NEAR:], image[:NEAR]
+        first_ref[near, :] = jnp.where(even, low, high)
+        second_ref[near, :] = jnp.where(even, high, low)
+        low, high = image[-NEAR - FAR : -NEAR], image[NEAR : NEAR + FAR]
+        first_ref[far, :] = jnp.where(even, low, high)
+        second_ref[far, :] = jnp.where(even, high, low)
+
+
+def tables_kernel(band_ref, kernels_ref, masks_ref, taps_ref, back_ref, guard_ref, feet_ref, pad_ref, *, height):
+    rows_dev = masks_ref.shape[0]
+    span = rows_dev + 2 * MARGIN
+    first_row = lax.axis_index("row") * rows_dev - MARGIN
+    row_ids = lax.broadcasted_iota(jnp.int32, (BAND, TILE), 0)
+    pad_ref[...] = jnp.zeros_like(pad_ref)
+    for band in range(span // BAND):
+        row = first_row + band * BAND
+        inside = (row >= 0) & (row < height)
+        kernel = band_ref[jnp.clip(row, 0, height - 1) // BAND]
+        raw = [kernels_ref[kernel, tap] for tap in range(TAPS)]
+        total = raw[0]
+        for tap in range(1, TAPS):
+            total = total + raw[tap]
+        total = jnp.full((BAND, TILE), total, jnp.float32)
+        start = band * BAND
+        guard_ref[start : start + BAND, :] = jnp.where(inside, 0.0, jnp.ones((BAND, TILE), jnp.float32))
+        for tap in range(TAPS):
+            weight = jnp.full((BAND, TILE), raw[tap], jnp.float32) / total
+            target = row_ids + (row + tap - TAPS // 2)
+            weight = jnp.where(inside & (target >= 0) & (target < height), weight, 0.0)
+            taps_ref[tap, start : start + BAND, :] = weight
+            pad_ref[tap, BAND + start : 2 * BAND + start, :] = weight
+    for tap in range(TAPS):
+        start = BAND + TAPS // 2 - tap
+        back_ref[tap] = pad_ref[tap, start : start + span, :]
+    flat = jnp.concatenate([masks_ref[row].astype(jnp.float32) for row in range(rows_dev)], axis=0)
+    positions = flat.shape[0]
+    both = jnp.concatenate([flat, flat], axis=0).T
+    half = feet_ref.shape[1]
+    left = lax.broadcasted_iota(jnp.int32, (half, TILE), 1) < positions
+    for block in range(feet_ref.shape[0]):
+        start = 2 * block * half
+        halves = jnp.where(left, both[start : start + half], both[start + half : start + 2 * half])
+        feet_ref[block] = halves.astype(jnp.bfloat16)
+
+
+def restore_kernel(taps_ref, back_ref, guard_ref, feet_ref, own_ref, first_ref, second_ref, out_ref):
+    n_frame = out_ref.shape[0]
+    frames, rows_dev, width = own_ref.shape
+    tiles_dev = width // (n_frame * TILE)
+    positions = rows_dev * tiles_dev
+    span = rows_dev + 2 * MARGIN
+    even = lax.axis_index("row") % 2 == 0
+
+    def between(cells, middle, start, stop):
+        pieces = [cells[:start]] if start else []
+        pieces.append(middle)
+        return jnp.concatenate(pieces + ([cells[stop:]] if stop < span else []), axis=0)
+
+    def blur(cells, start, stop):
+        total = guard_ref[start:stop, :] + taps_ref[2, start:stop, :] * cells[start:stop]
+        for tap in (0, 1, 3, 4):
+            total = total + taps_ref[tap, start:stop, :] * pltpu.roll(cells, (2 - tap) % span, 0)[start:stop]
+        return total
+
+    def spread(cells, start, stop):
+        total = back_ref[2, start:stop, :] * cells[start:stop]
+        for tap in (0, 1, 3, 4):
+            total = total + back_ref[tap, start:stop, :] * pltpu.roll(cells, (tap - 2) % span, 0)[start:stop]
+        return total
+
+    def column_block(block, carry):
+        for tile in range(tiles_dev):
+            columns = pl.ds(pl.multiple_of((block * tiles_dev + tile) * TILE, TILE), TILE)
+            for frame in range(frames):
+                near, far = frame * NEAR, frames * NEAR + frame * FAR
+                nears = first_ref[near : near + NEAR, columns], second_ref[near : near + NEAR, columns]
+                fars = first_ref[far : far + FAR, columns], second_ref[far : far + FAR, columns]
+                blank = jnp.zeros((MARGIN - NEAR - FAR, TILE), jnp.float32)
+                image = jnp.concatenate(
+                    [
+                        blank,
+                        jnp.where(even, fars[1], fars[0]),
+                        jnp.where(even, nears[1], nears[0]),
+                        own_ref[frame, :, columns],
+                        jnp.where(even, nears[0], nears[1]),
+                        jnp.where(even, fars[0], fars[1]),
+                        blank,
+                    ],
+                    axis=0,
+                )
+                current = image
+                for (low, high), (back_low, back_high) in STEPS:
+                    quotient = image[low:high] / blur(current, low, high)
+                    quotient = between(image, quotient, low, high)
+                    updated = current[back_low:back_high] * spread(quotient, back_low, back_high)
+                    current = between(image, updated, back_low, back_high)
+                estimate = current[MARGIN : MARGIN + rows_dev].astype(jnp.bfloat16)
+                start = frame * positions + tile * rows_dev
+                out_ref[block, start : start + rows_dev, :] = estimate
+        return carry
+
+    lax.fori_loop(0, n_frame, column_block, 0)
+    ones_row = lax.broadcasted_iota(jnp.int32, (TILE, TILE), 1) % tiles_dev
+    gathered = jnp.zeros((frames * n_frame * rows_dev, TILE), jnp.float32)
+    for tile in range(tiles_dev):
+        pieces = []
+        for frame in range(frames):
+            start = frame * positions + tile * rows_dev
+            pieces += [out_ref[block, start : start + rows_dev, :] for block in range(n_frame)]
+        picked = jnp.where(ones_row == tile, 1.0, 0.0).astype(jnp.bfloat16)
+        gathered = gathered + jnp.dot(jnp.concatenate(pieces, axis=0), picked, preferred_element_type=jnp.float32)
+    lanes = lax.broadcasted_iota(jnp.int32, (rows_dev, TILE), 1)
+    here = lanes % positions // tiles_dev == lax.broadcasted_iota(jnp.int32, (rows_dev, TILE), 0)
+    sums = []
+    for place in range(frames * n_frame):
+        part = jnp.where(here, gathered[place * rows_dev : (place + 1) * rows_dev], 0.0)
+        sums.append(jnp.sum(part, axis=0, keepdims=True))
+    sums = jnp.concatenate(sums, axis=0)
+    high = sums.astype(jnp.bfloat16).astype(jnp.float32)
+    split = jnp.where(lax.broadcasted_iota(jnp.int32, sums.shape, 1) < positions, high, sums - high).astype(jnp.bfloat16)
+    start = frames * positions
+    for block in range(n_frame):
+        out_ref[block, start : start + frames * n_frame, :] = split
+        out_ref[block, start + frames * n_frame :, :] = feet_ref[block]
+
+
+def deconvolved(series):
+    total = len(series)
+    factors = []
+    for step in range(total):
+        middle = 1.0 + SMOOTHING * (1.0 if step in (0, total - 1) else 2.0)
+        if step:
+            middle -= SMOOTHING * SMOOTHING * factors[-1]
+        factors.append(1.0 / middle)
+    forward = [series[0] * factors[0]]
+    for step in range(1, total):
+        forward.append((series[step] + SMOOTHING * forward[step - 1]) * factors[step])
+    baseline = [None] * total
+    baseline[total - 1] = forward[total - 1]
+    for step in range(total - 2, -1, -1):
+        baseline[step] = forward[step] + (SMOOTHING * factors[step]) * baseline[step + 1]
+    result, earlier = [], None
+    for step in range(total):
+        detrended = series[step] - baseline[step]
+        result.append(detrended if earlier is None else detrended - DECAY_RATE * earlier)
+        earlier = detrended
+    return result
+
+
+def partial_kernel(*refs, frames, positions):
+    pieces, (out_ref, sums_ref, feet_ref) = refs[:-3], refs[-3:]
+    n_frame = len(pieces)
+    place = lax.axis_index("frame")
+    start = frames * positions
+    rows = frames * n_frame
+    half = feet_ref.shape[1]
+    for step, piece in enumerate(pieces):
+        sums_ref[pl.ds(pl.multiple_of((place ^ step) * rows, rows), rows), :] = piece[start : start + rows, :].astype(jnp.float32)
+        feet_ref[place ^ step] = piece[start + rows :, :].astype(jnp.float32)
+    series = [sums_ref[t * n_frame : (t + 1) * n_frame, :] for t in range(rows)]
+    for t, sums in enumerate(deconvolved(series)):
+        sums_ref[t * n_frame : (t + 1) * n_frame, :] = sums + pltpu.roll(sums, TILE // 2, 1)
+    left = lax.broadcasted_iota(jnp.int32, (half, TILE), 1) < positions
+    weights, sums = [], []
+    extra = jnp.where(lax.broadcasted_iota(jnp.int32, (8, TILE), 0) == 0, 1.0, 0.0)
+    for block in range(n_frame):
+        feet = feet_ref[block]
+        weights.append(jnp.concatenate([jnp.where(left, feet, 0.0), jnp.where(left, 0.0, feet)], axis=0))
+        sums.append(jnp.concatenate([sums_ref[pl.ds(block, rows, stride=n_frame), :], extra], axis=0))
+    totals = lax.dot_general(
+        jnp.concatenate(weights, axis=1),
+        jnp.concatenate(sums, axis=1),
+        (((1,), (1,)), ((), ())),
+        precision=lax.Precision.HIGHEST,
+        preferred_element_type=jnp.float32,
+    )
+    share = out_ref.shape[1]
+    out_ref[...] = jnp.zeros_like(out_ref)
+    for row in range(out_ref.shape[0]):
+        out_ref[row, :, : rows + 8] = totals[row * share : (row + 1) * share]
+
+
+def temporal_kernel(*refs, frames):
+    pieces, (spikes_ref, in_ref) = refs[:-2], refs[-2:]
+    place = lax.axis_index("frame")
+    for step, piece in enumerate(pieces):
+        in_ref[place ^ step] = piece[: in_ref.shape[1], :]
+    total, rows_dev, columns = spikes_ref.shape
+    positions = in_ref.shape[1] // frames
+    for tile in range(columns // TILE):
+        series = []
+        for t in range(total):
+            start = t % frames * positions + tile * rows_dev
+            series.append(in_ref[t // frames, start : start + rows_dev, :].astype(jnp.float32))
+        for t, spikes in enumerate(deconvolved(series)):
+            spikes_ref[t, :, tile * TILE : (tile + 1) * TILE] = spikes.astype(spikes_ref.dtype)
+
+
+def means_kernel(*refs):
+    pieces, traces_ref = refs[:-1], refs[-1]
+    frames = traces_ref.shape[1]
+    total = pieces[0][...]
+    for piece in pieces[1:]:
+        total = total + piece[...]
+    traces_ref[...] = total[:, :frames] / (TILE * total[:, frames : frames + 1])
+
+
+def swapped(parts, axis):
+    count, place = lax.axis_size(axis), lax.axis_index(axis)
+    arrived = [lax.dynamic_index_in_dim(parts, place, 0, keepdims=False, allow_negative_indices=False)]
+    for step in range(1, count):
+        part = lax.dynamic_index_in_dim(parts, place ^ step, 0, keepdims=False, allow_negative_indices=False)
+        arrived.append(lax.ppermute(part, axis, [(i, i ^ step) for i in range(count)]))
+    return arrived
+
+
+def by_halo(observed, kernels, band_kernel, masks):
+    n_frame, n_row = lax.axis_size("frame"), lax.axis_size("row")
+    frames, rows_dev, width = observed.shape
+    components, _, tiles_dev = masks.shape
+    positions = rows_dev * tiles_dev
+    share = components // (n_frame * n_row)
+    span = rows_dev + 2 * MARGIN
+    smem, vmem = pl.BlockSpec(memory_space=pltpu.SMEM), pl.BlockSpec(memory_space=pltpu.VMEM)
+
+    def call(kernel, name, in_specs, out_shape, scratch=(), cost=1000000):
+        many = isinstance(out_shape, tuple)
+        return pl.pallas_call(
+            kernel,
+            name=name,
+            out_shape=out_shape,
+            in_specs=in_specs,
+            out_specs=(vmem,) * len(out_shape) if many else vmem,
+            scratch_shapes=scratch,
+            compiler_params=pltpu.CompilerParams(vmem_limit_bytes=16 << 20),
+            cost_estimate=pl.CostEstimate(flops=cost, bytes_accessed=cost, transcendentals=0),
+        )
+
+    def array(*shape, dtype=jnp.float32):
+        return jax.ShapeDtypeStruct(shape, dtype)
+
+    packed = array(frames * (NEAR + FAR), width)
+    first, second, own = call(halo_kernel, "halo", [vmem], (packed, packed, array(*observed.shape)))(observed)
+    pairs = [(i, i + 1) for i in range(0, n_row - 1, 2)], [(i, i + 1) for i in range(1, n_row - 1, 2)]
+    first, second = (
+        lax.ppermute(to_half(sent), "row", pair + [(j, i) for i, j in pair]).astype(jnp.float32)
+        for sent, pair in zip((first, second), pairs)
+    )
+    taps, back, guard, feet = call(
+        functools.partial(tables_kernel, height=rows_dev * n_row),
+        "tables",
+        [smem, smem, vmem],
+        (
+            array(TAPS, span, TILE),
+            array(TAPS, span, TILE),
+            array(span, TILE),
+            array(n_frame, n_row * share // 2, TILE, dtype=jnp.bfloat16),
+        ),
+        [pltpu.VMEM((TAPS, span + 2 * BAND, TILE), jnp.float32)],
+    )(band_kernel, kernels, masks.transpose(1, 2, 0))
+    block_rows = frames * positions + frames * n_frame + n_row * share // 2
+    blocks = call(restore_kernel, "restore", [vmem] * 7, array(n_frame, block_rows, TILE, dtype=jnp.bfloat16))(
+        taps, back, guard, feet, own, first, second
+    )
+    pieces = swapped(blocks, "frame")
+    partial = call(
+        functools.partial(partial_kernel, frames=frames, positions=positions),
+        "partial",
+        [vmem] * n_frame,
+        array(n_row, share, TILE),
+        [
+            pltpu.VMEM((n_frame * frames * n_frame, TILE), jnp.float32),
+            pltpu.VMEM((n_frame, n_row * share // 2, TILE), jnp.float32),
+        ],
+    )(*pieces)
+    shares = swapped(partial, "row")
+    spikes = call(
+        functools.partial(temporal_kernel, frames=frames),
+        "temporal",
+        [vmem] * n_frame,
+        array(n_frame * frames, rows_dev, tiles_dev * TILE, dtype=jnp.bfloat16),
+        [pltpu.VMEM((n_frame, frames * positions, TILE), jnp.bfloat16)],
+    )(*pieces)
+    traces = call(means_kernel, "means", [vmem] * n_row, array(share, n_frame * frames))(*shares)
+    return (spikes, traces)
+
+
+def fits(mesh, observed, masks):
+    frames_dev = observed.shape[0] // mesh.shape["frame"]
+    rows_dev = masks.shape[1] // (mesh.shape["groups"] * mesh.shape["row"])
+    tiles_dev = masks.shape[2] // mesh.shape["frame"]
+    places = mesh.shape["frame"] * mesh.shape["row"]
+    return (
+        frames_dev == mesh.shape["frame"] == mesh.shape["row"] == 4
+        and 2 * rows_dev * tiles_dev == TILE
+        and rows_dev == 16
+        and masks.shape[0] // places == 16
+    )
+
+
 def solution(mesh):
     in_specs = (
         P("frame", ("groups", "row"), None),
@@ -123,4 +442,10 @@
         P(None, ("groups", "row"), "frame"),
     )
     out_specs = (P(None, ("groups", "row"), "frame"), P(("groups", "frame", "row"), None))
-    return jax.shard_map(local, mesh=mesh, in_specs=in_specs, out_specs=out_specs, check_vma=False)
+
+    def whole(observed, kernels, band_kernel, masks):
+        body = by_halo if fits(mesh, observed, masks) else local
+        mapped = jax.shard_map(body, mesh=mesh, in_specs=in_specs, out_specs=out_specs, check_vma=False)
+        return mapped(observed, kernels, band_kernel, masks)
+
+    return whole

time: 223 us -> 33.8 us (0.15)
  waiting for transfers between devices: 64.8 us -> 10.2 us
  between operations: 44.1 us -> 0.75 us
  blocking collectives: 35.6 us -> 0 us
  starting transfers between devices: 38.9 us -> 13.2 us
  other arithmetic: 20.2 us -> 0.1 us
  local copies, waits for them, and re-layouts: 18 us -> 1.77 us
  Pallas kernels: 0 us -> 7.54 us
    unnamed x2 -> x0, waiting for transfers between devices: 51.6 us -> none
    unnamed x1 -> x0, blocking collectives: 35.6 us -> none
    ppermute x12 -> x8, starting transfers between devices: 35.5 us -> 13.2 us  [the longest x6 9.42 us: swapped(): lax.ppermute(part, axis, [(i, i ^ step) for i in range(count)])]
    div x6 -> x0, other arithmetic: 12.6 us -> none  [the longest x1 9.26 us: temporal(): lax.linalg.tridiagonal_solve(sub_diag, middle, super_diag, values)]
    pallas_call x0 -> x6, Pallas kernels: none -> 7.54 us  [the longest x1 4.71 us: by_halo(): call(restore_kernel, 'restore', [vmem] * 7, array(n_frame, block_rows, TI...]
    unnamed x34 -> x8, local copies, waits for them, and re-layouts: 8.98 us -> 1.72 us
    all_to_all x1 -> x0, starting transfers between devices: 3.41 us -> none  [local(): lax.all_to_all(estimate, 'frame', split_axis=2, concat_axis=0, tiled=True)]
    slice x9 -> x0, local copies, waits for them, and re-layouts: 3.32 us -> none  [the longest x3 2.13 us: temporal(): lax.linalg.tridiagonal_solve(sub_diag, middle, super_diag, values)]
  transfers between devices with their start and end apart: 14 -> 8, of which waited for: 9 -> 5; matrix products, arithmetic and copies ran while one was open for 4% -> 0% of each run, Pallas kernels for 0% -> 5%
where the time goes in v4:
time: 33.8 us; the launch traced here: 33.5 us
  starting transfers between devices  13.2 us (39%)
  waiting for transfers between devices  10.2 us (30%)
  Pallas kernels  7.54 us (22%)
  local copies, waits for them, and re-layouts  1.77 us (5%)
  between operations  0.75 us (2%)
    ppermute x6, starting transfers between devices, swapped(): lax.ppermute(part, axis, [(i, i ^ step) for i in range(count)])  9.42 us
    ppermute x6, waiting for transfers between devices, swapped(): lax.ppermute(part, axis, [(i, i ^ step) for i in range(count)])  7.43 us
    pallas_call x1, Pallas kernels, by_halo(): call(restore_kernel, 'restore', [vmem] * 7, array(n_frame, block_rows, TI...  4.71 us
    ppermute x2, starting transfers between devices, by_halo(): lax.ppermute(to_half(sent), 'row', pair + [(j, i) for i, j in pair])  3.76 us
    ppermute x2, waiting for transfers between devices, by_halo(): lax.ppermute(to_half(sent), 'row', pair + [(j, i) for i, j in pair])  2.76 us
    unnamed x8, local copies, waits for them, and re-layouts  1.72 us
    pallas_call x1, Pallas kernels, by_halo(): call(functools.partial(temporal_kernel, frames=frames), 'temporal', [vmem...  0.92 us
    pallas_call x1, Pallas kernels, by_halo(): call(functools.partial(tables_kernel, height=rows_dev * n_row), 'tables',...  0.72 us
  transfers between devices with their start and end apart: 8, of which 5 were waited for; matrix products, arithmetic and copies ran while one was open for 0% of the time, Pallas kernels for 5%

profile of v4, /device:TPU:0, one launch (start us, length us, event | category | flops | bytes accessed | tf_op | source)
XLA Modules:
  0.0 33.5 jit_solution(16904490377249873678)
XLA Ops:
  0.6 0.0 copy-start
  0.6 1.0 %copy-done = f32[4,16,2048]{2,1,0:T(8,128)S(1)} copy-done((f32[4,16,2048]{2,1,0:T(8,128)S(1)}, f32[4,16,2048]{2,1,0:T(8,128)}, u32[]{:S(2)}) %copy-start) | copy-done | bytes 524312
  1.7 0.1 halo.1
  1.8 3.1 %collective-permute-start = (f16[48,2048]{1,0:T(8,128)(2,1)S(1)}, f16[48,2048]{1,0:T(8,128)(2,1)S(1)}, u32[]{:S(2)}, u32[]{:S(2)}) collective-permute-start(f16[48,2048]{1,0:T(8,128)(2,1)S(1)} %convert_element_type.12), channel_id=1, source_target_pairs={{0,1},{2,3},{1,0},{3,2},{4,5},{6,7},{5,4},{7,6},{8,9},{10,11},{9,8... | collective-permute-start | bytes 589832 | tf_op jit(solution)/shard_map/ppermute | solution.py:382
  4.9 0.0 copy-start.1
  4.9 0.7 %collective-permute-start.1 = (f16[48,2048]{1,0:T(8,128)(2,1)S(1)}, f16[48,2048]{1,0:T(8,128)(2,1)S(1)}, u32[]{:S(2)}, u32[]{:S(2)}) collective-permute-start(f16[48,2048]{1,0:T(8,128)(2,1)S(1)} %convert_element_type.14), channel_id=1, source_target_pairs={{1,2},{2,1},{5,6},{6,5},{9,10},{10,9},{13,14},{14,13},{17,18},{18,... | collective-permute-start | bytes 589832 | tf_op jit(solution)/shard_map/ppermute | solution.py:382
  5.6 0.0 copy-start.2
  5.6 0.0 copy-start.3
  5.6 0.1 copy-done.1
  5.7 0.6 %copy-done.2 = f32[8,5]{1,0:T(8,128)S(1)} copy-done((f32[8,5]{1,0:T(8,128)S(1)}, f32[8,5]{1,0:T(8,128)}, u32[]{:S(2)}) %copy-start.2) | copy-done | bytes 184
  6.3 0.0 copy-done.3
  6.3 0.7 %tables.1 = (f32[5,48,128]{2,1,0:T(8,128)S(1)}, f32[5,48,128]{2,1,0:T(8,128)S(1)}, f32[48,128]{1,0:T(8,128)S(1)}, bf16[4,32,128]{2,1,0:T(8,128)(2,1)S(1)}) custom-call(s32[8]{0:T(128)S(1)} %copy-done.3, f32[8,5]{1,0:T(8,128)S(1)} %copy-done.2, s32[16,4,256]{2,1,0:T(4,128)S(1)} %bitcast.17), custom_call_target="tpu_custom_call" | custom-call | flops 1000000 | bytes 1000000 | tf_op jit(solution)/shard_map/tables/pallas_call | solution.py:385
  7.0 2.8 %collective-permute-done = f16[48,2048]{1,0:T(8,128)(2,1)S(1)} collective-permute-done((f16[48,2048]{1,0:T(8,128)(2,1)S(1)}, f16[48,2048]{1,0:T(8,128)(2,1)S(1)}, u32[]{:S(2)}, u32[]{:S(2)}) %collective-permute-start) | collective-permute-done | bytes 196640 | tf_op jit(solution)/shard_map/ppermute | solution.py:382
  9.8 0.0 collective-permute-done.1
  9.9 4.7 %restore.1 = bf16[4,304,128]{2,1,0:T(8,128)(2,1)S(1)} custom-call(f32[5,48,128]{2,1,0:T(8,128)S(1)} %get-tuple-element.9.taps_ref, f32[5,48,128]{2,1,0:T(8,128)S(1)} %get-tuple-element.10.back_ref, f32[48,128]{1,0:T(8,128)S(1)} %get-tuple-element.11.guard_ref, bf16[4,32,128]{2,1,0:T(8,128)(2,1)S(1)} %get-tuple-element.12.feet_ref, ...), custom_call_target="tpu_custom_call" | custom-call | flops 1000000 | bytes 1000000 | tf_op jit(solution)/shard_map/restore/pallas_call | solution.py:398
  14.6 0.1 collective-permute-start.2
  14.7 1.7 %collective-permute-start.3 = (bf16[304,128]{1,0:T(8,128)(2,1)S(1)}, bf16[304,128]{1,0:T(8,128)(2,1)S(1)}, u32[]{:S(2)}, u32[]{:S(2)}) collective-permute-start(bf16[304,128]{1,0:T(8,128)(2,1)S(1)} %get-tuple-element.17), channel_id=1, source_target_pairs={{0,8},{4,12},{8,0},{12,4},{1,9},{5,13},{9,1},{13,5},{2,10},{6,14},... | collective-permute-start | bytes 233480 | tf_op jit(solution)/shard_map/ppermute | solution.py:349
  16.4 0.1 collective-permute-start.4
  16.6 0.0 collective-permute-done.2.refs_1_
  16.6 3.0 %collective-permute-done.3.refs_2_ = bf16[304,128]{1,0:T(8,128)(2,1)S(1)} collective-permute-done((bf16[304,128]{1,0:T(8,128)(2,1)S(1)}, bf16[304,128]{1,0:T(8,128)(2,1)S(1)}, u32[]{:S(2)}, u32[]{:S(2)}) %collective-permute-start.3) | collective-permute-done | bytes 77856 | tf_op jit(solution)/shard_map/ppermute | solution.py:349
  19.5 1.3 %collective-permute-done.4.refs_3_ = bf16[304,128]{1,0:T(8,128)(2,1)S(1)} collective-permute-done((bf16[304,128]{1,0:T(8,128)(2,1)S(1)}, bf16[304,128]{1,0:T(8,128)(2,1)S(1)}, u32[]{:S(2)}, u32[]{:S(2)}) %collective-permute-start.4) | collective-permute-done | bytes 77856 | tf_op jit(solution)/shard_map/ppermute | solution.py:349
  20.9 0.4 %partial.1 = f32[4,16,128]{2,1,0:T(8,128)S(1)} custom-call(bf16[304,128]{1,0:T(8,128)(2,1)S(1)} %get-tuple-element.19.refs_0_, bf16[304,128]{1,0:T(8,128)(2,1)S(1)} %collective-permute-done.2.refs_1_, bf16[304,128]{1,0:T(8,128)(2,1)S(1)} %collective-permute-done.3.refs_2_, bf16[304,128]{1,0:T(8,128)(2,1)S(1)} %collective-permute-done.4.refs_3_), custom_call_target="tpu_custom_call" | custom-call | flops 1000000 | bytes 1000000 | tf_op jit(solution)/shard_map/partial/pallas_call | solution.py:402
  21.3 4.9 %collective-permute-start.5 = (f32[16,128]{1,0:T(8,128)S(1)}, f32[16,128]{1,0:T(8,128)S(1)}, u32[]{:S(2)}, u32[]{:S(2)}) collective-permute-start(f32[16,128]{1,0:T(8,128)S(1)} %get-tuple-element.22), channel_id=1, source_target_pairs={{0,1},{1,0},{2,3},{3,2},{4,5},{5,4},{6,7},{7,6},{8,9},{9,8},{10,11... | collective-permute-start | bytes 24584 | tf_op jit(solution)/shard_map/ppermute | solution.py:349
  26.2 1.2 %collective-permute-start.6 = (f32[16,128]{1,0:T(8,128)S(1)}, f32[16,128]{1,0:T(8,128)S(1)}, u32[]{:S(2)}, u32[]{:S(2)}) collective-permute-start(f32[16,128]{1,0:T(8,128)S(1)} %get-tuple-element.21), channel_id=1, source_target_pairs={{0,2},{1,3},{2,0},{3,1},{4,6},{5,7},{6,4},{7,5},{8,10},{9,11},{10,... | collective-permute-start | bytes 24584 | tf_op jit(solution)/shard_map/ppermute | solution.py:349
  27.4 1.4 %collective-permute-start.7 = (f32[16,128]{1,0:T(8,128)S(1)}, f32[16,128]{1,0:T(8,128)S(1)}, u32[]{:S(2)}, u32[]{:S(2)}) collective-permute-start(f32[16,128]{1,0:T(8,128)S(1)} %get-tuple-element.20), channel_id=1, source_target_pairs={{0,3},{1,2},{2,1},{3,0},{4,7},{5,6},{6,5},{7,4},{8,11},{9,10},{10,... | collective-permute-start | bytes 24584 | tf_op jit(solution)/shard_map/ppermute | solution.py:349
  28.8 0.9 %temporal.1 = bf16[16,16,512]{2,1,0:T(8,128)(2,1)} custom-call(bf16[304,128]{1,0:T(8,128)(2,1)S(1)} %get-tuple-element.19.refs_0_, bf16[304,128]{1,0:T(8,128)(2,1)S(1)} %collective-permute-done.2.refs_1_, bf16[304,128]{1,0:T(8,128)(2,1)S(1)} %collective-permute-done.3.refs_2_, bf16[304,128]{1,0:T(8,128)(2,1)S(1)} %collective-permute-done.4.refs_3_), custom_call_target="tpu_custom_call" | custom-call | flops 1000000 | bytes 1000000 | tf_op jit(solution)/shard_map/temporal/pallas_call | solution.py:413
  29.7 0.0 collective-permute-done.5.refs_1_
  29.7 1.0 %collective-permute-done.6.refs_2_ = f32[16,128]{1,0:T(8,128)S(1)} collective-permute-done((f32[16,128]{1,0:T(8,128)S(1)}, f32[16,128]{1,0:T(8,128)S(1)}, u32[]{:S(2)}, u32[]{:S(2)}) %collective-permute-start.6) | collective-permute-done | bytes 8224 | tf_op jit(solution)/shard_map/ppermute | solution.py:349
  30.7 2.1 %collective-permute-done.7.refs_3_ = f32[16,128]{1,0:T(8,128)S(1)} collective-permute-done((f32[16,128]{1,0:T(8,128)S(1)}, f32[16,128]{1,0:T(8,128)S(1)}, u32[]{:S(2)}, u32[]{:S(2)}) %collective-permute-start.7) | collective-permute-done | bytes 8224 | tf_op jit(solution)/shard_map/ppermute | solution.py:349
  32.9 0.7 %means.1 = f32[16,16]{1,0:T(8,128)} custom-call(f32[16,128]{1,0:T(8,128)S(1)} %get-tuple-element.23.refs_0_, f32[16,128]{1,0:T(8,128)S(1)} %collective-permute-done.5.refs_1_, f32[16,128]{1,0:T(8,128)S(1)} %collective-permute-done.6.refs_2_, f32[16,128]{1,0:T(8,128)S(1)} %collective-permute-done.7.refs_3_), custom_call_target="tpu_custom_call" | custom-call | flops 1000000 | bytes 1000000 | tf_op jit(solution)/shard_map/means/pallas_call | solution.py:420
  (6 shorter events, 0.2 us)
Async XLA Ops:
  0.6 1.0 %copy-start = (f32[4,16,2048]{2,1,0:T(8,128)S(1)}, f32[4,16,2048]{2,1,0:T(8,128)}, u32[]{:S(2)}) copy-start(f32[4,16,2048]{2,1,0:T(8,128)} %observed_ref.1) | copy-start | bytes 1572868
  1.8 8.0 %collective-permute-start = (f16[48,2048]{1,0:T(8,128)(2,1)S(1)}, f16[48,2048]{1,0:T(8,128)(2,1)S(1)}, u32[]{:S(2)}, u32[]{:S(2)}) collective-permute-start(f16[48,2048]{1,0:T(8,128)(2,1)S(1)} %convert_element_type.12), channel_id=1, source_target_pairs={{0,1},{2,3},{1,0},{3,2},{4,5},{6,7},{5,4},{7,6},{8,9},{10,11},{9,8... | collective-permute-start | bytes 589832 | tf_op jit(solution)/shard_map/ppermute | solution.py:382
  4.9 0.8 %copy-start.1 = (s32[256,16,4]{0,2,1:T(4,128)S(1)}, s32[256,16,4]{0,2,1:T(4,128)}, u32[]{:S(2)}) copy-start(s32[256,16,4]{0,2,1:T(4,128)} %param.7) | copy-start | bytes 196612
  4.9 4.9 %collective-permute-start.1 = (f16[48,2048]{1,0:T(8,128)(2,1)S(1)}, f16[48,2048]{1,0:T(8,128)(2,1)S(1)}, u32[]{:S(2)}, u32[]{:S(2)}) collective-permute-start(f16[48,2048]{1,0:T(8,128)(2,1)S(1)} %convert_element_type.14), channel_id=1, source_target_pairs={{1,2},{2,1},{5,6},{6,5},{9,10},{10,9},{13,14},{14,13},{17,18},{18,... | collective-permute-start | bytes 589832 | tf_op jit(solution)/shard_map/ppermute | solution.py:382
  5.6 0.7 %copy-start.2 = (f32[8,5]{1,0:T(8,128)S(1)}, f32[8,5]{1,0:T(8,128)}, u32[]{:S(2)}) copy-start(f32[8,5]{1,0:T(8,128)} %kernels_ref.1) | copy-start | bytes 484
  5.6 0.7 %copy-start.3 = (s32[8]{0:T(128)S(1)}, s32[8]{0:T(128)}, u32[]{:S(2)}) copy-start(s32[8]{0:T(128)} %band_ref.1) | copy-start | bytes 100
  14.6 1.9 %collective-permute-start.2 = (bf16[304,128]{1,0:T(8,128)(2,1)S(1)}, bf16[304,128]{1,0:T(8,128)(2,1)S(1)}, u32[]{:S(2)}, u32[]{:S(2)}) collective-permute-start(bf16[304,128]{1,0:T(8,128)(2,1)S(1)} %get-tuple-element.18), channel_id=1, source_target_pairs={{0,4},{4,0},{8,12},{12,8},{1,5},{5,1},{9,13},{13,9},{2,6},{6,2},{1... | collective-permute-start | bytes 233480 | tf_op jit(solution)/shard_map/ppermute | solution.py:349
  14.7 4.8 %collective-permute-start.3 = (bf16[304,128]{1,0:T(8,128)(2,1)S(1)}, bf16[304,128]{1,0:T(8,128)(2,1)S(1)}, u32[]{:S(2)}, u32[]{:S(2)}) collective-permute-start(bf16[304,128]{1,0:T(8,128)(2,1)S(1)} %get-tuple-element.17), channel_id=1, source_target_pairs={{0,8},{4,12},{8,0},{12,4},{1,9},{5,13},{9,1},{13,5},{2,10},{6,14},... | collective-permute-start | bytes 233480 | tf_op jit(solution)/shard_map/ppermute | solution.py:349
  16.4 4.4 %collective-permute-start.4 = (bf16[304,128]{1,0:T(8,128)(2,1)S(1)}, bf16[304,128]{1,0:T(8,128)(2,1)S(1)}, u32[]{:S(2)}, u32[]{:S(2)}) collective-permute-start(bf16[304,128]{1,0:T(8,128)(2,1)S(1)} %get-tuple-element.16), channel_id=1, source_target_pairs={{0,12},{4,8},{8,4},{12,0},{1,13},{5,9},{9,5},{13,1},{2,14},{6,10},... | collective-permute-start | bytes 233480 | tf_op jit(solution)/shard_map/ppermute | solution.py:349
  21.3 8.4 %collective-permute-start.5 = (f32[16,128]{1,0:T(8,128)S(1)}, f32[16,128]{1,0:T(8,128)S(1)}, u32[]{:S(2)}, u32[]{:S(2)}) collective-permute-start(f32[16,128]{1,0:T(8,128)S(1)} %get-tuple-element.22), channel_id=1, source_target_pairs={{0,1},{1,0},{2,3},{3,2},{4,5},{5,4},{6,7},{7,6},{8,9},{9,8},{10,11... | collective-permute-start | bytes 24584 | tf_op jit(solution)/shard_map/ppermute | solution.py:349
  26.2 4.5 %collective-permute-start.6 = (f32[16,128]{1,0:T(8,128)S(1)}, f32[16,128]{1,0:T(8,128)S(1)}, u32[]{:S(2)}, u32[]{:S(2)}) collective-permute-start(f32[16,128]{1,0:T(8,128)S(1)} %get-tuple-element.21), channel_id=1, source_target_pairs={{0,2},{1,3},{2,0},{3,1},{4,6},{5,7},{6,4},{7,5},{8,10},{9,11},{10,... | collective-permute-start | bytes 24584 | tf_op jit(solution)/shard_map/ppermute | solution.py:349
  27.4 5.4 %collective-permute-start.7 = (f32[16,128]{1,0:T(8,128)S(1)}, f32[16,128]{1,0:T(8,128)S(1)}, u32[]{:S(2)}, u32[]{:S(2)}) collective-permute-start(f32[16,128]{1,0:T(8,128)S(1)} %get-tuple-element.20), channel_id=1, source_target_pairs={{0,3},{1,2},{2,1},{3,0},{4,7},{5,6},{6,5},{7,4},{8,11},{9,10},{10,... | collective-permute-start | bytes 24584 | tf_op jit(solution)/shard_map/ppermute | solution.py:349

commit v5 on v4

--- a/solution.py
+++ b/solution.py
@@ -13,7 +13,11 @@
 TAPS = 5
 NEAR, FAR = 8, 4
 MARGIN = 2 * BAND
-STEPS = (((0, 48), (8, 40)), ((8, 40), (8, 40)), ((8, 40), (16, 32)))
+PAD = BAND
+STEPS = (((6, 46), (8, 40)), ((10, 42), (12, 36)), ((14, 38), (16, 32)))
+SIDES = (0, 1, 3, 4)
+HALVES = 2
+TOGETHER = 2
 
 
 SMOOTHING = 1024.0
@@ -123,26 +127,30 @@
     return (spikes, traces)
 
 
-def to_half(cells):
-    return cells.astype(jnp.float16)
-
-
-def halo_kernel(observed_ref, first_ref, second_ref, own_ref):
+def halo_kernel(observed_ref, *refs):
+    sent, (own_ref, arrived) = refs[:-2], refs[-2:]
     even = lax.axis_index("row") % 2 == 0
-    frames = observed_ref.shape[0]
-    own_ref[...] = observed_ref[...]
-    for frame in range(frames):
-        image = observed_ref[frame]
-        near, far = slice(frame * NEAR, (frame + 1) * NEAR), slice(frames * NEAR + frame * FAR, frames * NEAR + (frame + 1) * FAR)
-        low, high = image[-NEAR:], image[:NEAR]
-        first_ref[near, :] = jnp.where(even, low, high)
-        second_ref[near, :] = jnp.where(even, high, low)
-        low, high = image[-NEAR - FAR : -NEAR], image[NEAR : NEAR + FAR]
-        first_ref[far, :] = jnp.where(even, low, high)
-        second_ref[far, :] = jnp.where(even, high, low)
-
-
-def tables_kernel(band_ref, kernels_ref, masks_ref, taps_ref, back_ref, guard_ref, feet_ref, pad_ref, *, height):
+    copies = [
+        pltpu.make_async_copy(observed_ref.at[frame], own_ref.at[frame], arrived.at[frame])
+        for frame in range(own_ref.shape[0])
+    ]
+    for copy in copies:
+        copy.start()
+    frames = len(copies) // HALVES
+    for frame, copy in enumerate(copies):
+        first_ref, second_ref = sent[2 * (frame // frames) : 2 * (frame // frames) + 2]
+        copy.wait()
+        near = frame % frames * NEAR
+        far = frames * NEAR + frame % frames * FAR
+        low, high = own_ref[frame, -NEAR:, :], own_ref[frame, :NEAR, :]
+        first_ref[near : near + NEAR, :] = jnp.where(even, low, high)
+        second_ref[near : near + NEAR, :] = jnp.where(even, high, low)
+        low, high = own_ref[frame, -NEAR - FAR : -NEAR, :], own_ref[frame, NEAR : NEAR + FAR, :]
+        first_ref[far : far + FAR, :] = jnp.where(even, low, high)
+        second_ref[far : far + FAR, :] = jnp.where(even, high, low)
+
+
+def tables_kernel(band_ref, kernels_ref, masks_ref, taps_ref, back_ref, feet_ref, pad_ref, *, height):
     rows_dev = masks_ref.shape[0]
     span = rows_dev + 2 * MARGIN
     first_row = lax.axis_index("row") * rows_dev - MARGIN
@@ -152,22 +160,17 @@
         row = first_row + band * BAND
         inside = (row >= 0) & (row < height)
         kernel = band_ref[jnp.clip(row, 0, height - 1) // BAND]
-        raw = [kernels_ref[kernel, tap] for tap in range(TAPS)]
-        total = raw[0]
-        for tap in range(1, TAPS):
-            total = total + raw[tap]
-        total = jnp.full((BAND, TILE), total, jnp.float32)
+        centre = jnp.full((BAND, TILE), kernels_ref[kernel, TAPS // 2], jnp.float32)
         start = band * BAND
-        guard_ref[start : start + BAND, :] = jnp.where(inside, 0.0, jnp.ones((BAND, TILE), jnp.float32))
-        for tap in range(TAPS):
-            weight = jnp.full((BAND, TILE), raw[tap], jnp.float32) / total
+        for slot, tap in enumerate(SIDES):
+            weight = jnp.full((BAND, TILE), kernels_ref[kernel, tap], jnp.float32) / centre
             target = row_ids + (row + tap - TAPS // 2)
             weight = jnp.where(inside & (target >= 0) & (target < height), weight, 0.0)
-            taps_ref[tap, start : start + BAND, :] = weight
-            pad_ref[tap, BAND + start : 2 * BAND + start, :] = weight
-    for tap in range(TAPS):
+            taps_ref[slot, start : start + BAND, :] = weight
+            pad_ref[slot, BAND + start : 2 * BAND + start, :] = weight
+    for slot, tap in enumerate(SIDES):
         start = BAND + TAPS // 2 - tap
-        back_ref[tap] = pad_ref[tap, start : start + span, :]
+        back_ref[slot] = pad_ref[slot, start : start + span, :]
     flat = jnp.concatenate([masks_ref[row].astype(jnp.float32) for row in range(rows_dev)], axis=0)
     positions = flat.shape[0]
     both = jnp.concatenate([flat, flat], axis=0).T
@@ -179,71 +182,69 @@
         feet_ref[block] = halves.astype(jnp.bfloat16)
 
 
-def restore_kernel(taps_ref, back_ref, guard_ref, feet_ref, own_ref, first_ref, second_ref, out_ref):
+def restore_half(taps_ref, back_ref, own_ref, inner_ref, outer_ref, out_ref, image_ref, current_ref, quotient_ref, half):
     n_frame = out_ref.shape[0]
-    frames, rows_dev, width = own_ref.shape
+    _, rows_dev, width = own_ref.shape
+    frames = own_ref.shape[0] // HALVES
     tiles_dev = width // (n_frame * TILE)
     positions = rows_dev * tiles_dev
-    span = rows_dev + 2 * MARGIN
-    even = lax.axis_index("row") % 2 == 0
-
-    def between(cells, middle, start, stop):
-        pieces = [cells[:start]] if start else []
-        pieces.append(middle)
-        return jnp.concatenate(pieces + ([cells[stop:]] if stop < span else []), axis=0)
-
-    def blur(cells, start, stop):
-        total = guard_ref[start:stop, :] + taps_ref[2, start:stop, :] * cells[start:stop]
-        for tap in (0, 1, 3, 4):
-            total = total + taps_ref[tap, start:stop, :] * pltpu.roll(cells, (2 - tap) % span, 0)[start:stop]
-        return total
-
-    def spread(cells, start, stop):
-        total = back_ref[2, start:stop, :] * cells[start:stop]
-        for tap in (0, 1, 3, 4):
-            total = total + back_ref[tap, start:stop, :] * pltpu.roll(cells, (tap - 2) % span, 0)[start:stop]
-        return total
-
-    def column_block(block, carry):
-        for tile in range(tiles_dev):
-            columns = pl.ds(pl.multiple_of((block * tiles_dev + tile) * TILE, TILE), TILE)
-            for frame in range(frames):
-                near, far = frame * NEAR, frames * NEAR + frame * FAR
-                nears = first_ref[near : near + NEAR, columns], second_ref[near : near + NEAR, columns]
-                fars = first_ref[far : far + FAR, columns], second_ref[far : far + FAR, columns]
-                blank = jnp.zeros((MARGIN - NEAR - FAR, TILE), jnp.float32)
-                image = jnp.concatenate(
-                    [
-                        blank,
-                        jnp.where(even, fars[1], fars[0]),
-                        jnp.where(even, nears[1], nears[0]),
-                        own_ref[frame, :, columns],
-                        jnp.where(even, nears[0], nears[1]),
-                        jnp.where(even, fars[0], fars[1]),
-                        blank,
-                    ],
-                    axis=0,
-                )
-                current = image
-                for (low, high), (back_low, back_high) in STEPS:
-                    quotient = image[low:high] / blur(current, low, high)
-                    quotient = between(image, quotient, low, high)
-                    updated = current[back_low:back_high] * spread(quotient, back_low, back_high)
-                    current = between(image, updated, back_low, back_high)
-                estimate = current[MARGIN : MARGIN + rows_dev].astype(jnp.bfloat16)
-                start = frame * positions + tile * rows_dev
-                out_ref[block, start : start + rows_dev, :] = estimate
+    units = [(frame, tile) for frame in range(frames) for tile in range(TOGETHER)]
+    for ref in (image_ref, current_ref, quotient_ref):
+        ref[...] = jnp.ones_like(ref)
+    row = lax.axis_index("row")
+    even = row % 2 == 0
+    fill = jnp.where((row == 0) | (row == lax.axis_size("row") - 1), 1.0, 0.0)
+
+    def columns_step(step, carry):
+        for unit, (frame, tile) in enumerate(units):
+            columns = pl.ds(pl.multiple_of((step * TOGETHER + tile) * TILE, TILE), TILE)
+            near, far = frame * NEAR, frames * NEAR + frame * FAR
+            start, stop = PAD + MARGIN, PAD + MARGIN + rows_dev
+            inner, outer = inner_ref[near : near + NEAR, columns], outer_ref[near : near + NEAR, columns] + fill
+            image_ref[unit, start - NEAR : start, :] = jnp.where(even, outer, inner)
+            image_ref[unit, stop : stop + NEAR, :] = jnp.where(even, inner, outer)
+            inner, outer = inner_ref[far : far + FAR, columns], outer_ref[far : far + FAR, columns] + fill
+            image_ref[unit, start - NEAR - FAR : start - NEAR, :] = jnp.where(even, outer, inner)
+            image_ref[unit, stop + NEAR : stop + NEAR + FAR, :] = jnp.where(even, inner, outer)
+            image_ref[unit, start:stop, :] = own_ref[half * frames + frame, :, columns]
+        source_ref = image_ref
+        for (low, high), (back_low, back_high) in STEPS:
+            for row in range(low, high, BAND):
+                weights = [taps_ref[slot, row : row + BAND, :] for slot in range(len(SIDES))]
+                for unit in range(len(units)):
+                    rows = slice(PAD + row, PAD + row + BAND)
+                    blurred = source_ref[unit, rows, :]
+                    for weight, tap in zip(weights, SIDES):
+                        start = PAD + row + tap - TAPS // 2
+                        blurred = blurred + weight * source_ref[unit, start : start + BAND, :]
+                    quotient_ref[unit, rows, :] = image_ref[unit, rows, :] / blurred
+            for row in range(back_low, back_high, BAND):
+                weights = [back_ref[slot, row : row + BAND, :] for slot in range(len(SIDES))]
+                for unit in range(len(units)):
+                    rows = slice(PAD + row, PAD + row + BAND)
+                    spread = quotient_ref[unit, rows, :]
+                    for weight, tap in zip(weights, SIDES):
+                        start = PAD + row - tap + TAPS // 2
+                        spread = spread + weight * quotient_ref[unit, start : start + BAND, :]
+                    current_ref[unit, rows, :] = source_ref[unit, rows, :] * spread
+            source_ref = current_ref
+        steps = tiles_dev // TOGETHER
+        first = pl.multiple_of(lax.rem(step, steps) * (TOGETHER * rows_dev), TOGETHER * rows_dev)
+        for unit, (frame, tile) in enumerate(units):
+            estimate = current_ref[unit, PAD + MARGIN : PAD + MARGIN + rows_dev, :].astype(jnp.bfloat16)
+            start = first + ((half * frames + frame) * positions + tile * rows_dev)
+            out_ref[step // steps, pl.ds(pl.multiple_of(start, rows_dev), rows_dev), :] = estimate
         return carry
 
-    lax.fori_loop(0, n_frame, column_block, 0)
-    ones_row = lax.broadcasted_iota(jnp.int32, (TILE, TILE), 1) % tiles_dev
+    lax.fori_loop(0, n_frame * tiles_dev // TOGETHER, columns_step, 0)
+    lane_tiles = lax.broadcasted_iota(jnp.int32, (TILE, TILE), 1) % tiles_dev
     gathered = jnp.zeros((frames * n_frame * rows_dev, TILE), jnp.float32)
     for tile in range(tiles_dev):
         pieces = []
         for frame in range(frames):
-            start = frame * positions + tile * rows_dev
+            start = (half * frames + frame) * positions + tile * rows_dev
             pieces += [out_ref[block, start : start + rows_dev, :] for block in range(n_frame)]
-        picked = jnp.where(ones_row == tile, 1.0, 0.0).astype(jnp.bfloat16)
+        picked = jnp.where(lane_tiles == tile, 1.0, 0.0).astype(jnp.bfloat16)
         gathered = gathered + jnp.dot(jnp.concatenate(pieces, axis=0), picked, preferred_element_type=jnp.float32)
     lanes = lax.broadcasted_iota(jnp.int32, (rows_dev, TILE), 1)
     here = lanes % positions // tiles_dev == lax.broadcasted_iota(jnp.int32, (rows_dev, TILE), 0)
@@ -251,13 +252,27 @@
     for place in range(frames * n_frame):
         part = jnp.where(here, gathered[place * rows_dev : (place + 1) * rows_dev], 0.0)
         sums.append(jnp.sum(part, axis=0, keepdims=True))
-    sums = jnp.concatenate(sums, axis=0)
+    return jnp.concatenate(sums, axis=0)
+
+
+def first_kernel(taps_ref, back_ref, own_ref, inner_ref, outer_ref, out_ref, sums_ref, *scratch):
+    sums_ref[...] = restore_half(taps_ref, back_ref, own_ref, inner_ref, outer_ref, out_ref, *scratch, 0)
+
+
+def second_kernel(
+    taps_ref, back_ref, own_ref, inner_ref, outer_ref, feet_ref, estimate_ref, sums_ref, out_ref, *scratch
+):
+    sums = restore_half(taps_ref, back_ref, own_ref, inner_ref, outer_ref, out_ref, *scratch, 1)
+    sums = jnp.concatenate([sums_ref[...], sums], axis=0)
+    n_frame, done, _ = estimate_ref.shape
+    positions = done * HALVES // own_ref.shape[0]
     high = sums.astype(jnp.bfloat16).astype(jnp.float32)
     split = jnp.where(lax.broadcasted_iota(jnp.int32, sums.shape, 1) < positions, high, sums - high).astype(jnp.bfloat16)
-    start = frames * positions
+    start = HALVES * done
     for block in range(n_frame):
-        out_ref[block, start : start + frames * n_frame, :] = split
-        out_ref[block, start + frames * n_frame :, :] = feet_ref[block]
+        out_ref[block, :done, :] = estimate_ref[block]
+        out_ref[block, start : start + split.shape[0], :] = split
+        out_ref[block, start + split.shape[0] :, :] = feet_ref[block]
 
 
 def deconvolved(series):
@@ -375,29 +390,43 @@
     def array(*shape, dtype=jnp.float32):
         return jax.ShapeDtypeStruct(shape, dtype)
 
-    packed = array(frames * (NEAR + FAR), width)
-    first, second, own = call(halo_kernel, "halo", [vmem], (packed, packed, array(*observed.shape)))(observed)
+    half = frames // HALVES
+    packed = array(half * (NEAR + FAR), width)
+    *sent, own = call(
+        halo_kernel,
+        "halo",
+        [pl.BlockSpec(memory_space=pltpu.HBM)],
+        (packed,) * (2 * HALVES) + (array(*observed.shape),),
+        [pltpu.SemaphoreType.DMA((frames,))],
+    )(observed)
     pairs = [(i, i + 1) for i in range(0, n_row - 1, 2)], [(i, i + 1) for i in range(1, n_row - 1, 2)]
-    first, second = (
-        lax.ppermute(to_half(sent), "row", pair + [(j, i) for i, j in pair]).astype(jnp.float32)
-        for sent, pair in zip((first, second), pairs)
-    )
-    taps, back, guard, feet = call(
+    pairs = [pair + [(j, i) for i, j in pair] for pair in pairs]
+    arrived = [lax.ppermute(rows.astype(jnp.float16), "row", pairs[i % 2]) for i, rows in enumerate(sent)]
+    taps, back, feet = call(
         functools.partial(tables_kernel, height=rows_dev * n_row),
         "tables",
         [smem, smem, vmem],
         (
-            array(TAPS, span, TILE),
-            array(TAPS, span, TILE),
-            array(span, TILE),
+            array(len(SIDES), span, TILE),
+            array(len(SIDES), span, TILE),
             array(n_frame, n_row * share // 2, TILE, dtype=jnp.bfloat16),
         ),
-        [pltpu.VMEM((TAPS, span + 2 * BAND, TILE), jnp.float32)],
+        [pltpu.VMEM((len(SIDES), span + 2 * BAND, TILE), jnp.float32)],
     )(band_kernel, kernels, masks.transpose(1, 2, 0))
+    arrived = [rows.astype(jnp.float32) for rows in arrived]
+    buffers = [pltpu.VMEM((half * TOGETHER, span + 2 * PAD, TILE), jnp.float32)] * 3
+    estimate, sums = call(
+        first_kernel,
+        "restore1",
+        [vmem] * 5,
+        (array(n_frame, half * positions, TILE, dtype=jnp.bfloat16), array(half * n_frame, TILE)),
+        buffers,
+        cost=6000000,
+    )(taps, back, own, *arrived[:2])
     block_rows = frames * positions + frames * n_frame + n_row * share // 2
-    blocks = call(restore_kernel, "restore", [vmem] * 7, array(n_frame, block_rows, TILE, dtype=jnp.bfloat16))(
-        taps, back, guard, feet, own, first, second
-    )
+    blocks = call(
+        second_kernel, "restore2", [vmem] * 8, array(n_frame, block_rows, TILE, dtype=jnp.bfloat16), buffers, cost=6000000
+    )(taps, back, own, *arrived[2:], feet, estimate, sums)
     pieces = swapped(blocks, "frame")
     partial = call(
         functools.partial(partial_kernel, frames=frames, positions=positions),

time: 33.8 us -> 32.1 us (0.950)
  waiting for transfers between devices: 10.2 us -> 6.82 us
  starting transfers between devices: 13.2 us -> 15.4 us
  Pallas kernels: 7.54 us -> 6.97 us
    ppermute x2 -> x4, starting transfers between devices: 3.76 us -> 9.02 us  [by_halo(): lax.ppermute(rows.astype(jnp.float16), 'row', pairs[i % 2])]
    ppermute x6, starting transfers between devices: 9.42 us -> 6.38 us  [swapped(): lax.ppermute(part, axis, [(i, i ^ step) for i in range(count)])]
    ppermute x2 -> x4, waiting for transfers between devices: 2.76 us -> 0.01 us  [by_halo(): lax.ppermute(rows.astype(jnp.float16), 'row', pairs[i % 2])]
    ppermute x6, waiting for transfers between devices: 7.43 us -> 6.81 us  [swapped(): lax.ppermute(part, axis, [(i, i ^ step) for i in range(count)])]
    pallas_call x2 -> x3, Pallas kernels: 4.82 us -> 4.24 us  [the longest x1 1.73 us: by_halo(): call(second_kernel, 'restore2', [vmem] * 8, array(n_frame, block_rows, TI...]
  transfers between devices with their start and end apart: 8 -> 10, of which waited for: 5 -> 5; matrix products, arithmetic and copies ran while one was open for 0% -> 0% of each run, Pallas kernels for 5% -> 11%
where the time goes in v5:
time: 32.1 us; the launch traced here: 31.9 us
  starting transfers between devices  15.4 us (48%)
  Pallas kernels  6.97 us (22%)
  waiting for transfers between devices  6.82 us (21%)
  local copies, waits for them, and re-layouts  1.78 us (6%)
  between operations  0.81 us (3%)
    ppermute x4, starting transfers between devices, by_halo(): lax.ppermute(rows.astype(jnp.float16), 'row', pairs[i % 2])  9.02 us
    ppermute x6, waiting for transfers between devices, swapped(): lax.ppermute(part, axis, [(i, i ^ step) for i in range(count)])  6.81 us
    ppermute x6, starting transfers between devices, swapped(): lax.ppermute(part, axis, [(i, i ^ step) for i in range(count)])  6.38 us
    pallas_call x1, Pallas kernels, by_halo(): call(second_kernel, 'restore2', [vmem] * 8, array(n_frame, block_rows, TI...  1.73 us
    pallas_call x1, Pallas kernels, by_halo(): call(first_kernel, 'restore1', [vmem] * 5, (array(n_frame, half * positio...  1.73 us
    unnamed x8, local copies, waits for them, and re-layouts  1.73 us
    pallas_call x1, Pallas kernels, by_halo(): call(functools.partial(temporal_kernel, frames=frames), 'temporal', [vmem...  0.92 us
    pallas_call x1, Pallas kernels, by_halo(): call(halo_kernel, 'halo', [pl.BlockSpec(memory_space=pltpu.HBM)], (packed...  0.78 us
  transfers between devices with their start and end apart: 10, of which 5 were waited for; matrix products, arithmetic and copies ran while one was open for 0% of the time, Pallas kernels for 11%

profile of v5, /device:TPU:0, one launch (start us, length us, event | category | flops | bytes accessed | tf_op | source)
XLA Modules:
  0.0 31.9 jit_solution(6668528970542328098)
XLA Ops:
  0.6 1.0 %copy-done = f32[4,16,2048]{2,1,0:T(8,128)S(1)} copy-done((f32[4,16,2048]{2,1,0:T(8,128)S(1)}, f32[4,16,2048]{2,1,0:T(8,128)}, u32[]{:S(2)}) %copy-start) | copy-done | bytes 524312
  1.7 0.8 %halo.1 = (f32[24,2048]{1,0:T(8,128)S(1)}, f32[24,2048]{1,0:T(8,128)S(1)}, f32[24,2048]{1,0:T(8,128)S(1)}, f32[24,2048]{1,0:T(8,128)S(1)}, f32[4,16,2048]{2,1,0:T(8,128)S(1)}) custom-call(f32[4,16,2048]{2,1,0:T(8,128)S(1)} %copy-done), custom_call_target="tpu_custom_call" | custom-call | flops 1000000 | bytes 1000000 | tf_op jit(solution)/shard_map/halo/pallas_call | solution.py:395
  2.5 0.7 %collective-permute-start.3 = (f16[24,2048]{1,0:T(8,128)(2,1)S(1)}, f16[24,2048]{1,0:T(8,128)(2,1)S(1)}, u32[]{:S(2)}, u32[]{:S(2)}) collective-permute-start(f16[24,2048]{1,0:T(8,128)(2,1)S(1)} %convert_element_type.30), channel_id=1, source_target_pairs={{1,2},{2,1},{5,6},{6,5},{9,10},{10,9},{13,14},{14,13},{17,18},{18,... | collective-permute-start | bytes 294920 | tf_op jit(solution)/shard_map/ppermute | solution.py:404
  3.2 5.9 %collective-permute-start.2 = (f16[24,2048]{1,0:T(8,128)(2,1)S(1)}, f16[24,2048]{1,0:T(8,128)(2,1)S(1)}, u32[]{:S(2)}, u32[]{:S(2)}) collective-permute-start(f16[24,2048]{1,0:T(8,128)(2,1)S(1)} %convert_element_type.28), channel_id=1, source_target_pairs={{0,1},{2,3},{1,0},{3,2},{4,5},{6,7},{5,4},{7,6},{8,9},{10,11},{9,8... | collective-permute-start | bytes 294920 | tf_op jit(solution)/shard_map/ppermute | solution.py:404
  9.1 0.7 %collective-permute-start.1 = (f16[24,2048]{1,0:T(8,128)(2,1)S(1)}, f16[24,2048]{1,0:T(8,128)(2,1)S(1)}, u32[]{:S(2)}, u32[]{:S(2)}) collective-permute-start(f16[24,2048]{1,0:T(8,128)(2,1)S(1)} %convert_element_type.26), channel_id=1, source_target_pairs={{1,2},{2,1},{5,6},{6,5},{9,10},{10,9},{13,14},{14,13},{17,18},{18,... | collective-permute-start | bytes 294920 | tf_op jit(solution)/shard_map/ppermute | solution.py:404
  9.8 0.0 copy-start.1
  9.8 1.8 %collective-permute-start = (f16[24,2048]{1,0:T(8,128)(2,1)S(1)}, f16[24,2048]{1,0:T(8,128)(2,1)S(1)}, u32[]{:S(2)}, u32[]{:S(2)}) collective-permute-start(f16[24,2048]{1,0:T(8,128)(2,1)S(1)} %convert_element_type.24), channel_id=1, source_target_pairs={{0,1},{2,3},{1,0},{3,2},{4,5},{6,7},{5,4},{7,6},{8,9},{10,11},{9,8... | collective-permute-start | bytes 294920 | tf_op jit(solution)/shard_map/ppermute | solution.py:404
  11.6 0.0 copy-done.1
  11.6 0.7 %copy-done.2 = f32[8,5]{1,0:T(8,128)S(1)} copy-done((f32[8,5]{1,0:T(8,128)S(1)}, f32[8,5]{1,0:T(8,128)}, u32[]{:S(2)}) %copy-start.2) | copy-done | bytes 184
  12.3 0.0 copy-done.3
  12.3 0.7 %tables.1 = (f32[4,48,128]{2,1,0:T(8,128)S(1)}, f32[4,48,128]{2,1,0:T(8,128)S(1)}, bf16[4,32,128]{2,1,0:T(8,128)(2,1)S(1)}) custom-call(s32[8]{0:T(128)S(1)} %copy-done.3, f32[8,5]{1,0:T(8,128)S(1)} %copy-done.2, s32[16,4,256]{2,1,0:T(4,128)S(1)} %bitcast.17), custom_call_target="tpu_custom_call" | custom-call | flops 1000000 | bytes 1000000 | tf_op jit(solution)/shard_map/tables/pallas_call | solution.py:405
  13.0 0.0 collective-permute-done.3
  13.0 0.0 collective-permute-done.2
  13.1 0.0 collective-permute-done.1
  13.1 1.7 %restore1.1 = (bf16[4,128,128]{2,1,0:T(8,128)(2,1)S(1)}, f32[8,128]{1,0:T(8,128)S(1)}) custom-call(f32[4,48,128]{2,1,0:T(8,128)S(1)} %get-tuple-element.12.taps_ref, f32[4,48,128]{2,1,0:T(8,128)S(1)} %get-tuple-element.13.back_ref, f32[4,16,2048]{2,1,0:T(8,128)S(1)} %get-tuple-element.14.own_ref, f32[24,2048]{1,0:T(8,128)S(1)} %convert_element_type.29.inner_ref, ...), custom_call_target="tpu_custom_call" | custom-call | flops 6000000 | bytes 6000000 | tf_op jit(solution)/shard_map/restore1/pallas_call | solution.py:418
  14.8 0.0 collective-permute-done
  14.9 1.7 %restore2.1 = bf16[4,304,128]{2,1,0:T(8,128)(2,1)S(1)} custom-call(f32[4,48,128]{2,1,0:T(8,128)S(1)} %get-tuple-element.12.taps_ref, f32[4,48,128]{2,1,0:T(8,128)S(1)} %get-tuple-element.13.back_ref, f32[4,16,2048]{2,1,0:T(8,128)S(1)} %get-tuple-element.14.own_ref, f32[24,2048]{1,0:T(8,128)S(1)} %convert_element_type.25.inner_ref, ...), custom_call_target="tpu_custom_call" | custom-call | flops 6000000 | bytes 6000000 | tf_op jit(solution)/shard_map/restore2/pallas_call | solution.py:427
  16.7 0.2 collective-permute-start.6
  16.8 1.5 %collective-permute-start.5 = (bf16[304,128]{1,0:T(8,128)(2,1)S(1)}, bf16[304,128]{1,0:T(8,128)(2,1)S(1)}, u32[]{:S(2)}, u32[]{:S(2)}) collective-permute-start(bf16[304,128]{1,0:T(8,128)(2,1)S(1)} %get-tuple-element.23), channel_id=1, source_target_pairs={{0,8},{4,12},{8,0},{12,4},{1,9},{5,13},{9,1},{13,5},{2,10},{6,14},... | collective-permute-start | bytes 233480 | tf_op jit(solution)/shard_map/ppermute | solution.py:364
  18.3 0.3 collective-permute-start.4
  18.6 2.7 %collective-permute-done.6.refs_3_ = bf16[304,128]{1,0:T(8,128)(2,1)S(1)} collective-permute-done((bf16[304,128]{1,0:T(8,128)(2,1)S(1)}, bf16[304,128]{1,0:T(8,128)(2,1)S(1)}, u32[]{:S(2)}, u32[]{:S(2)}) %collective-permute-start.6) | collective-permute-done | bytes 77856 | tf_op jit(solution)/shard_map/ppermute | solution.py:364
  21.3 1.7 %collective-permute-done.5.refs_2_ = bf16[304,128]{1,0:T(8,128)(2,1)S(1)} collective-permute-done((bf16[304,128]{1,0:T(8,128)(2,1)S(1)}, bf16[304,128]{1,0:T(8,128)(2,1)S(1)}, u32[]{:S(2)}, u32[]{:S(2)}) %collective-permute-start.5) | collective-permute-done | bytes 77856 | tf_op jit(solution)/shard_map/ppermute | solution.py:364
  23.0 0.0 collective-permute-done.4.refs_1_
  23.0 0.4 %partial.1 = f32[4,16,128]{2,1,0:T(8,128)S(1)} custom-call(bf16[304,128]{1,0:T(8,128)(2,1)S(1)} %get-tuple-element.25.refs_0_, bf16[304,128]{1,0:T(8,128)(2,1)S(1)} %collective-permute-done.4.refs_1_, bf16[304,128]{1,0:T(8,128)(2,1)S(1)} %collective-permute-done.5.refs_2_, bf16[304,128]{1,0:T(8,128)(2,1)S(1)} %collective-permute-done.6.refs_3_), custom_call_target="tpu_custom_call" | custom-call | flops 1000000 | bytes 1000000 | tf_op jit(solution)/shard_map/partial/pallas_call | solution.py:431
  23.5 2.5 %collective-permute-start.9 = (f32[16,128]{1,0:T(8,128)S(1)}, f32[16,128]{1,0:T(8,128)S(1)}, u32[]{:S(2)}, u32[]{:S(2)}) collective-permute-start(f32[16,128]{1,0:T(8,128)S(1)} %get-tuple-element.26), channel_id=1, source_target_pairs={{0,3},{1,2},{2,1},{3,0},{4,7},{5,6},{6,5},{7,4},{8,11},{9,10},{10,... | collective-permute-start | bytes 24584 | tf_op jit(solution)/shard_map/ppermute | solution.py:364
  26.0 1.5 %collective-permute-start.8 = (f32[16,128]{1,0:T(8,128)S(1)}, f32[16,128]{1,0:T(8,128)S(1)}, u32[]{:S(2)}, u32[]{:S(2)}) collective-permute-start(f32[16,128]{1,0:T(8,128)S(1)} %get-tuple-element.27), channel_id=1, source_target_pairs={{0,2},{1,3},{2,0},{3,1},{4,6},{5,7},{6,4},{7,5},{8,10},{9,11},{10,... | collective-permute-start | bytes 24584 | tf_op jit(solution)/shard_map/ppermute | solution.py:364
  27.6 0.4 %collective-permute-start.7 = (f32[16,128]{1,0:T(8,128)S(1)}, f32[16,128]{1,0:T(8,128)S(1)}, u32[]{:S(2)}, u32[]{:S(2)}) collective-permute-start(f32[16,128]{1,0:T(8,128)S(1)} %get-tuple-element.28), channel_id=1, source_target_pairs={{0,1},{1,0},{2,3},{3,2},{4,5},{5,4},{6,7},{7,6},{8,9},{9,8},{10,11... | collective-permute-start | bytes 24584 | tf_op jit(solution)/shard_map/ppermute | solution.py:364
  27.9 0.9 %temporal.1 = bf16[16,16,512]{2,1,0:T(8,128)(2,1)} custom-call(bf16[304,128]{1,0:T(8,128)(2,1)S(1)} %get-tuple-element.25.refs_0_, bf16[304,128]{1,0:T(8,128)(2,1)S(1)} %collective-permute-done.4.refs_1_, bf16[304,128]{1,0:T(8,128)(2,1)S(1)} %collective-permute-done.5.refs_2_, bf16[304,128]{1,0:T(8,128)(2,1)S(1)} %collective-permute-done.6.refs_3_), custom_call_target="tpu_custom_call" | custom-call | flops 1000000 | bytes 1000000 | tf_op jit(solution)/shard_map/temporal/pallas_call | solution.py:442
  28.9 0.1 collective-permute-done.9.refs_3_
  29.0 1.6 %collective-permute-done.8.refs_2_ = f32[16,128]{1,0:T(8,128)S(1)} collective-permute-done((f32[16,128]{1,0:T(8,128)S(1)}, f32[16,128]{1,0:T(8,128)S(1)}, u32[]{:S(2)}, u32[]{:S(2)}) %collective-permute-start.8) | collective-permute-done | bytes 8224 | tf_op jit(solution)/shard_map/ppermute | solution.py:364
  30.6 0.6 %collective-permute-done.7.refs_1_ = f32[16,128]{1,0:T(8,128)S(1)} collective-permute-done((f32[16,128]{1,0:T(8,128)S(1)}, f32[16,128]{1,0:T(8,128)S(1)}, u32[]{:S(2)}, u32[]{:S(2)}) %collective-permute-start.7) | collective-permute-done | bytes 8224 | tf_op jit(solution)/shard_map/ppermute | solution.py:364
  31.2 0.7 %means.1 = f32[16,16]{1,0:T(8,128)} custom-call(f32[16,128]{1,0:T(8,128)S(1)} %get-tuple-element.29.refs_0_, f32[16,128]{1,0:T(8,128)S(1)} %collective-permute-done.7.refs_1_, f32[16,128]{1,0:T(8,128)S(1)} %collective-permute-done.8.refs_2_, f32[16,128]{1,0:T(8,128)S(1)} %collective-permute-done.9.refs_3_), custom_call_target="tpu_custom_call" | custom-call | flops 1000000 | bytes 1000000 | tf_op jit(solution)/shard_map/means/pallas_call | solution.py:449
  (13 shorter events, 0.2 us)
Async XLA Ops:
  0.6 1.0 %copy-start = (f32[4,16,2048]{2,1,0:T(8,128)S(1)}, f32[4,16,2048]{2,1,0:T(8,128)}, u32[]{:S(2)}) copy-start(f32[4,16,2048]{2,1,0:T(8,128)} %observed_ref.1) | copy-start | bytes 1572868
  2.5 10.5 %collective-permute-start.3 = (f16[24,2048]{1,0:T(8,128)(2,1)S(1)}, f16[24,2048]{1,0:T(8,128)(2,1)S(1)}, u32[]{:S(2)}, u32[]{:S(2)}) collective-permute-start(f16[24,2048]{1,0:T(8,128)(2,1)S(1)} %convert_element_type.30), channel_id=1, source_target_pairs={{1,2},{2,1},{5,6},{6,5},{9,10},{10,9},{13,14},{14,13},{17,18},{18,... | collective-permute-start | bytes 294920 | tf_op jit(solution)/shard_map/ppermute | solution.py:404
  3.2 9.9 %collective-permute-start.2 = (f16[24,2048]{1,0:T(8,128)(2,1)S(1)}, f16[24,2048]{1,0:T(8,128)(2,1)S(1)}, u32[]{:S(2)}, u32[]{:S(2)}) collective-permute-start(f16[24,2048]{1,0:T(8,128)(2,1)S(1)} %convert_element_type.28), channel_id=1, source_target_pairs={{0,1},{2,3},{1,0},{3,2},{4,5},{6,7},{5,4},{7,6},{8,9},{10,11},{9,8... | collective-permute-start | bytes 294920 | tf_op jit(solution)/shard_map/ppermute | solution.py:404
  9.1 4.0 %collective-permute-start.1 = (f16[24,2048]{1,0:T(8,128)(2,1)S(1)}, f16[24,2048]{1,0:T(8,128)(2,1)S(1)}, u32[]{:S(2)}, u32[]{:S(2)}) collective-permute-start(f16[24,2048]{1,0:T(8,128)(2,1)S(1)} %convert_element_type.26), channel_id=1, source_target_pairs={{1,2},{2,1},{5,6},{6,5},{9,10},{10,9},{13,14},{14,13},{17,18},{18,... | collective-permute-start | bytes 294920 | tf_op jit(solution)/shard_map/ppermute | solution.py:404
  9.8 1.8 %copy-start.1 = (s32[256,16,4]{0,2,1:T(4,128)S(1)}, s32[256,16,4]{0,2,1:T(4,128)}, u32[]{:S(2)}) copy-start(s32[256,16,4]{0,2,1:T(4,128)} %param.7) | copy-start | bytes 196612
  9.8 5.0 %collective-permute-start = (f16[24,2048]{1,0:T(8,128)(2,1)S(1)}, f16[24,2048]{1,0:T(8,128)(2,1)S(1)}, u32[]{:S(2)}, u32[]{:S(2)}) collective-permute-start(f16[24,2048]{1,0:T(8,128)(2,1)S(1)} %convert_element_type.24), channel_id=1, source_target_pairs={{0,1},{2,3},{1,0},{3,2},{4,5},{6,7},{5,4},{7,6},{8,9},{10,11},{9,8... | collective-permute-start | bytes 294920 | tf_op jit(solution)/shard_map/ppermute | solution.py:404
  11.6 0.7 %copy-start.2 = (f32[8,5]{1,0:T(8,128)S(1)}, f32[8,5]{1,0:T(8,128)}, u32[]{:S(2)}) copy-start(f32[8,5]{1,0:T(8,128)} %kernels_ref.1) | copy-start | bytes 484
  11.6 0.7 %copy-start.3 = (s32[8]{0:T(128)S(1)}, s32[8]{0:T(128)}, u32[]{:S(2)}) copy-start(s32[8]{0:T(128)} %band_ref.1) | copy-start | bytes 100
  16.7 4.7 %collective-permute-start.6 = (bf16[304,128]{1,0:T(8,128)(2,1)S(1)}, bf16[304,128]{1,0:T(8,128)(2,1)S(1)}, u32[]{:S(2)}, u32[]{:S(2)}) collective-permute-start(bf16[304,128]{1,0:T(8,128)(2,1)S(1)} %get-tuple-element.22), channel_id=1, source_target_pairs={{0,12},{4,8},{8,4},{12,0},{1,13},{5,9},{9,5},{13,1},{2,14},{6,10},... | collective-permute-start | bytes 233480 | tf_op jit(solution)/shard_map/ppermute | solution.py:364
  16.8 6.2 %collective-permute-start.5 = (bf16[304,128]{1,0:T(8,128)(2,1)S(1)}, bf16[304,128]{1,0:T(8,128)(2,1)S(1)}, u32[]{:S(2)}, u32[]{:S(2)}) collective-permute-start(bf16[304,128]{1,0:T(8,128)(2,1)S(1)} %get-tuple-element.23), channel_id=1, source_target_pairs={{0,8},{4,12},{8,0},{12,4},{1,9},{5,13},{9,1},{13,5},{2,10},{6,14},... | collective-permute-start | bytes 233480 | tf_op jit(solution)/shard_map/ppermute | solution.py:364
  18.3 4.8 %collective-permute-start.4 = (bf16[304,128]{1,0:T(8,128)(2,1)S(1)}, bf16[304,128]{1,0:T(8,128)(2,1)S(1)}, u32[]{:S(2)}, u32[]{:S(2)}) collective-permute-start(bf16[304,128]{1,0:T(8,128)(2,1)S(1)} %get-tuple-element.24), channel_id=1, source_target_pairs={{0,4},{4,0},{8,12},{12,8},{1,5},{5,1},{9,13},{13,9},{2,6},{6,2},{1... | collective-permute-start | bytes 233480 | tf_op jit(solution)/shard_map/ppermute | solution.py:364
  23.5 5.5 %collective-permute-start.9 = (f32[16,128]{1,0:T(8,128)S(1)}, f32[16,128]{1,0:T(8,128)S(1)}, u32[]{:S(2)}, u32[]{:S(2)}) collective-permute-start(f32[16,128]{1,0:T(8,128)S(1)} %get-tuple-element.26), channel_id=1, source_target_pairs={{0,3},{1,2},{2,1},{3,0},{4,7},{5,6},{6,5},{7,4},{8,11},{9,10},{10,... | collective-permute-start | bytes 24584 | tf_op jit(solution)/shard_map/ppermute | solution.py:364
  26.0 4.6 %collective-permute-start.8 = (f32[16,128]{1,0:T(8,128)S(1)}, f32[16,128]{1,0:T(8,128)S(1)}, u32[]{:S(2)}, u32[]{:S(2)}) collective-permute-start(f32[16,128]{1,0:T(8,128)S(1)} %get-tuple-element.27), channel_id=1, source_target_pairs={{0,2},{1,3},{2,0},{3,1},{4,6},{5,7},{6,4},{7,5},{8,10},{9,11},{10,... | collective-permute-start | bytes 24584 | tf_op jit(solution)/shard_map/ppermute | solution.py:364
  27.6 3.7 %collective-permute-start.7 = (f32[16,128]{1,0:T(8,128)S(1)}, f32[16,128]{1,0:T(8,128)S(1)}, u32[]{:S(2)}, u32[]{:S(2)}) collective-permute-start(f32[16,128]{1,0:T(8,128)S(1)} %get-tuple-element.28), channel_id=1, source_target_pairs={{0,1},{1,0},{2,3},{3,2},{4,5},{5,4},{6,7},{7,6},{8,9},{9,8},{10,11... | collective-permute-start | bytes 24584 | tf_op jit(solution)/shard_map/ppermute | solution.py:364

commit v6 on v5

--- a/solution.py
+++ b/solution.py
@@ -16,8 +16,6 @@
 PAD = BAND
 STEPS = (((6, 46), (8, 40)), ((10, 42), (12, 36)), ((14, 38), (16, 32)))
 SIDES = (0, 1, 3, 4)
-HALVES = 2
-TOGETHER = 2
 
 
 SMOOTHING = 1024.0
@@ -127,27 +125,23 @@
     return (spikes, traces)
 
 
-def halo_kernel(observed_ref, *refs):
-    sent, (own_ref, arrived) = refs[:-2], refs[-2:]
-    even = lax.axis_index("row") % 2 == 0
-    copies = [
-        pltpu.make_async_copy(observed_ref.at[frame], own_ref.at[frame], arrived.at[frame])
-        for frame in range(own_ref.shape[0])
-    ]
-    for copy in copies:
-        copy.start()
-    frames = len(copies) // HALVES
-    for frame, copy in enumerate(copies):
-        first_ref, second_ref = sent[2 * (frame // frames) : 2 * (frame // frames) + 2]
-        copy.wait()
-        near = frame % frames * NEAR
-        far = frames * NEAR + frame % frames * FAR
-        low, high = own_ref[frame, -NEAR:, :], own_ref[frame, :NEAR, :]
-        first_ref[near : near + NEAR, :] = jnp.where(even, low, high)
-        second_ref[near : near + NEAR, :] = jnp.where(even, high, low)
-        low, high = own_ref[frame, -NEAR - FAR : -NEAR, :], own_ref[frame, NEAR : NEAR + FAR, :]
-        first_ref[far : far + FAR, :] = jnp.where(even, low, high)
-        second_ref[far : far + FAR, :] = jnp.where(even, high, low)
+def low_first():
+    return (lax.axis_index("row") + lax.axis_index("frame")) % 2 == 0
+
+
+def halo_kernel(observed_ref, first_ref, second_ref, own_ref):
+    low = low_first()
+    frames = observed_ref.shape[0]
+    own_ref[...] = observed_ref[...]
+    for frame in range(frames):
+        near = frame * NEAR
+        far = frames * NEAR + frame * FAR
+        bottom, top = observed_ref[frame, -NEAR:, :], observed_ref[frame, :NEAR, :]
+        first_ref[near : near + NEAR, :] = jnp.where(low, bottom, top)
+        second_ref[near : near + NEAR, :] = jnp.where(low, top, bottom)
+        bottom, top = observed_ref[frame, -NEAR - FAR : -NEAR, :], observed_ref[frame, NEAR : NEAR + FAR, :]
+        first_ref[far : far + FAR, :] = jnp.where(low, bottom, top)
+        second_ref[far : far + FAR, :] = jnp.where(low, top, bottom)
 
 
 def tables_kernel(band_ref, kernels_ref, masks_ref, taps_ref, back_ref, feet_ref, pad_ref, *, height):
@@ -182,67 +176,67 @@
         feet_ref[block] = halves.astype(jnp.bfloat16)
 
 
-def restore_half(taps_ref, back_ref, own_ref, inner_ref, outer_ref, out_ref, image_ref, current_ref, quotient_ref, half):
+def restore_kernel(
+    taps_ref, back_ref, feet_ref, own_ref, first_ref, second_ref, out_ref, side_ref, image_ref, current_ref, quotient_ref
+):
     n_frame = out_ref.shape[0]
-    _, rows_dev, width = own_ref.shape
-    frames = own_ref.shape[0] // HALVES
+    frames, rows_dev, width = own_ref.shape
     tiles_dev = width // (n_frame * TILE)
     positions = rows_dev * tiles_dev
-    units = [(frame, tile) for frame in range(frames) for tile in range(TOGETHER)]
     for ref in (image_ref, current_ref, quotient_ref):
         ref[...] = jnp.ones_like(ref)
+    low = low_first()
     row = lax.axis_index("row")
-    even = row % 2 == 0
-    fill = jnp.where((row == 0) | (row == lax.axis_size("row") - 1), 1.0, 0.0)
+    above = jnp.where(row == 0, 1.0, 0.0)
+    below = jnp.where(row == lax.axis_size("row") - 1, 1.0, 0.0)
 
     def columns_step(step, carry):
-        for unit, (frame, tile) in enumerate(units):
-            columns = pl.ds(pl.multiple_of((step * TOGETHER + tile) * TILE, TILE), TILE)
+        columns = pl.ds(pl.multiple_of(step * TILE, TILE), TILE)
+        for frame in range(frames):
             near, far = frame * NEAR, frames * NEAR + frame * FAR
             start, stop = PAD + MARGIN, PAD + MARGIN + rows_dev
-            inner, outer = inner_ref[near : near + NEAR, columns], outer_ref[near : near + NEAR, columns] + fill
-            image_ref[unit, start - NEAR : start, :] = jnp.where(even, outer, inner)
-            image_ref[unit, stop : stop + NEAR, :] = jnp.where(even, inner, outer)
-            inner, outer = inner_ref[far : far + FAR, columns], outer_ref[far : far + FAR, columns] + fill
-            image_ref[unit, start - NEAR - FAR : start - NEAR, :] = jnp.where(even, outer, inner)
-            image_ref[unit, stop + NEAR : stop + NEAR + FAR, :] = jnp.where(even, inner, outer)
-            image_ref[unit, start:stop, :] = own_ref[half * frames + frame, :, columns]
+            first, second = first_ref[near : near + NEAR, columns], second_ref[near : near + NEAR, columns]
+            image_ref[frame, start - NEAR : start, :] = jnp.where(low, second, first) + above
+            image_ref[frame, stop : stop + NEAR, :] = jnp.where(low, first, second) + below
+            first, second = first_ref[far : far + FAR, columns], second_ref[far : far + FAR, columns]
+            image_ref[frame, start - NEAR - FAR : start - NEAR, :] = jnp.where(low, second, first) + above
+            image_ref[frame, stop + NEAR : stop + NEAR + FAR, :] = jnp.where(low, first, second) + below
+            image_ref[frame, start:stop, :] = own_ref[frame, :, columns]
         source_ref = image_ref
-        for (low, high), (back_low, back_high) in STEPS:
-            for row in range(low, high, BAND):
+        for (first, last), (back_first, back_last) in STEPS:
+            for row in range(first, last, BAND):
                 weights = [taps_ref[slot, row : row + BAND, :] for slot in range(len(SIDES))]
-                for unit in range(len(units)):
+                for frame in range(frames):
                     rows = slice(PAD + row, PAD + row + BAND)
-                    blurred = source_ref[unit, rows, :]
+                    blurred = source_ref[frame, rows, :]
                     for weight, tap in zip(weights, SIDES):
                         start = PAD + row + tap - TAPS // 2
-                        blurred = blurred + weight * source_ref[unit, start : start + BAND, :]
-                    quotient_ref[unit, rows, :] = image_ref[unit, rows, :] / blurred
-            for row in range(back_low, back_high, BAND):
+                        blurred = blurred + weight * source_ref[frame, start : start + BAND, :]
+                    quotient_ref[frame, rows, :] = image_ref[frame, rows, :] / blurred
+            for row in range(back_first, back_last, BAND):
                 weights = [back_ref[slot, row : row + BAND, :] for slot in range(len(SIDES))]
-                for unit in range(len(units)):
+                for frame in range(frames):
                     rows = slice(PAD + row, PAD + row + BAND)
-                    spread = quotient_ref[unit, rows, :]
+                    spread = quotient_ref[frame, rows, :]
                     for weight, tap in zip(weights, SIDES):
                         start = PAD + row - tap + TAPS // 2
-                        spread = spread + weight * quotient_ref[unit, start : start + BAND, :]
-                    current_ref[unit, rows, :] = source_ref[unit, rows, :] * spread
+                        spread = spread + weight * quotient_ref[frame, start : start + BAND, :]
+                    current_ref[frame, rows, :] = source_ref[frame, rows, :] * spread
             source_ref = current_ref
-        steps = tiles_dev // TOGETHER
-        first = pl.multiple_of(lax.rem(step, steps) * (TOGETHER * rows_dev), TOGETHER * rows_dev)
-        for unit, (frame, tile) in enumerate(units):
-            estimate = current_ref[unit, PAD + MARGIN : PAD + MARGIN + rows_dev, :].astype(jnp.bfloat16)
-            start = first + ((half * frames + frame) * positions + tile * rows_dev)
-            out_ref[step // steps, pl.ds(pl.multiple_of(start, rows_dev), rows_dev), :] = estimate
+        first = pl.multiple_of(lax.rem(step, tiles_dev) * rows_dev, rows_dev)
+        for frame in range(frames):
+            estimate = current_ref[frame, PAD + MARGIN : PAD + MARGIN + rows_dev, :].astype(jnp.bfloat16)
+            start = pl.multiple_of(first + frame * positions, rows_dev)
+            out_ref[step // tiles_dev, pl.ds(start, rows_dev), :] = estimate
         return carry
 
-    lax.fori_loop(0, n_frame * tiles_dev // TOGETHER, columns_step, 0)
+    lax.fori_loop(0, n_frame * tiles_dev, columns_step, 0)
     lane_tiles = lax.broadcasted_iota(jnp.int32, (TILE, TILE), 1) % tiles_dev
     gathered = jnp.zeros((frames * n_frame * rows_dev, TILE), jnp.float32)
     for tile in range(tiles_dev):
         pieces = []
         for frame in range(frames):
-            start = (half * frames + frame) * positions + tile * rows_dev
+            start = frame * positions + tile * rows_dev
             pieces += [out_ref[block, start : start + rows_dev, :] for block in range(n_frame)]
         picked = jnp.where(lane_tiles == tile, 1.0, 0.0).astype(jnp.bfloat16)
         gathered = gathered + jnp.dot(jnp.concatenate(pieces, axis=0), picked, preferred_element_type=jnp.float32)
@@ -252,27 +246,12 @@
     for place in range(frames * n_frame):
         part = jnp.where(here, gathered[place * rows_dev : (place + 1) * rows_dev], 0.0)
         sums.append(jnp.sum(part, axis=0, keepdims=True))
-    return jnp.concatenate(sums, axis=0)
-
-
-def first_kernel(taps_ref, back_ref, own_ref, inner_ref, outer_ref, out_ref, sums_ref, *scratch):
-    sums_ref[...] = restore_half(taps_ref, back_ref, own_ref, inner_ref, outer_ref, out_ref, *scratch, 0)
-
-
-def second_kernel(
-    taps_ref, back_ref, own_ref, inner_ref, outer_ref, feet_ref, estimate_ref, sums_ref, out_ref, *scratch
-):
-    sums = restore_half(taps_ref, back_ref, own_ref, inner_ref, outer_ref, out_ref, *scratch, 1)
-    sums = jnp.concatenate([sums_ref[...], sums], axis=0)
-    n_frame, done, _ = estimate_ref.shape
-    positions = done * HALVES // own_ref.shape[0]
+    sums = jnp.concatenate(sums, axis=0)
     high = sums.astype(jnp.bfloat16).astype(jnp.float32)
     split = jnp.where(lax.broadcasted_iota(jnp.int32, sums.shape, 1) < positions, high, sums - high).astype(jnp.bfloat16)
-    start = HALVES * done
     for block in range(n_frame):
-        out_ref[block, :done, :] = estimate_ref[block]
-        out_ref[block, start : start + split.shape[0], :] = split
-        out_ref[block, start + split.shape[0] :, :] = feet_ref[block]
+        side_ref[block, : split.shape[0], :] = split
+        side_ref[block, split.shape[0] :, :] = feet_ref[block]
 
 
 def deconvolved(series):
@@ -298,16 +277,15 @@
     return result
 
 
-def partial_kernel(*refs, frames, positions):
+def partial_kernel(*refs, positions):
     pieces, (out_ref, sums_ref, feet_ref) = refs[:-3], refs[-3:]
     n_frame = len(pieces)
     place = lax.axis_index("frame")
-    start = frames * positions
-    rows = frames * n_frame
+    rows = sums_ref.shape[0] // n_frame
     half = feet_ref.shape[1]
     for step, piece in enumerate(pieces):
-        sums_ref[pl.ds(pl.multiple_of((place ^ step) * rows, rows), rows), :] = piece[start : start + rows, :].astype(jnp.float32)
-        feet_ref[place ^ step] = piece[start + rows :, :].astype(jnp.float32)
+        sums_ref[pl.ds(pl.multiple_of((place ^ step) * rows, rows), rows), :] = piece[:rows, :].astype(jnp.float32)
+        feet_ref[place ^ step] = piece[rows:, :].astype(jnp.float32)
     series = [sums_ref[t * n_frame : (t + 1) * n_frame, :] for t in range(rows)]
     for t, sums in enumerate(deconvolved(series)):
         sums_ref[t * n_frame : (t + 1) * n_frame, :] = sums + pltpu.roll(sums, TILE // 2, 1)
@@ -335,7 +313,7 @@
     pieces, (spikes_ref, in_ref) = refs[:-2], refs[-2:]
     place = lax.axis_index("frame")
     for step, piece in enumerate(pieces):
-        in_ref[place ^ step] = piece[: in_ref.shape[1], :]
+        in_ref[place ^ step] = piece[...]
     total, rows_dev, columns = spikes_ref.shape
     positions = in_ref.shape[1] // frames
     for tile in range(columns // TILE):
@@ -390,18 +368,17 @@
     def array(*shape, dtype=jnp.float32):
         return jax.ShapeDtypeStruct(shape, dtype)
 
-    half = frames // HALVES
-    packed = array(half * (NEAR + FAR), width)
-    *sent, own = call(
-        halo_kernel,
-        "halo",
-        [pl.BlockSpec(memory_space=pltpu.HBM)],
-        (packed,) * (2 * HALVES) + (array(*observed.shape),),
-        [pltpu.SemaphoreType.DMA((frames,))],
-    )(observed)
-    pairs = [(i, i + 1) for i in range(0, n_row - 1, 2)], [(i, i + 1) for i in range(1, n_row - 1, 2)]
-    pairs = [pair + [(j, i) for i, j in pair] for pair in pairs]
-    arrived = [lax.ppermute(rows.astype(jnp.float16), "row", pairs[i % 2]) for i, rows in enumerate(sent)]
+    packed = array(frames * (NEAR + FAR), width)
+    *sent, own = call(halo_kernel, "halo", [vmem], (packed, packed, array(*observed.shape)))(observed)
+    pairs = [[(i, i + 1) for i in range(first, n_row - 1, 2)] for first in (0, 1)]
+    swaps = [
+        [(f * n_row + i, f * n_row + j) for f in range(n_frame) for pair in pairs[(f + turn) % 2] for i, j in (pair, pair[::-1])]
+        for turn in range(2)
+    ]
+    arrived = [
+        lax.ppermute(rows.astype(jnp.float16), ("frame", "row"), swap).astype(jnp.float32)
+        for rows, swap in zip(sent, swaps)
+    ]
     taps, back, feet = call(
         functools.partial(tables_kernel, height=rows_dev * n_row),
         "tables",
@@ -411,25 +388,23 @@
             array(len(SIDES), span, TILE),
             array(n_frame, n_row * share // 2, TILE, dtype=jnp.bfloat16),
         ),
-        [pltpu.VMEM((len(SIDES), span + 2 * BAND, TILE), jnp.float32)],
+        [pltpu.VMEM((len(SIDES), span + 2 * PAD, TILE), jnp.float32)],
     )(band_kernel, kernels, masks.transpose(1, 2, 0))
-    arrived = [rows.astype(jnp.float32) for rows in arrived]
-    buffers = [pltpu.VMEM((half * TOGETHER, span + 2 * PAD, TILE), jnp.float32)] * 3
-    estimate, sums = call(
-        first_kernel,
-        "restore1",
-        [vmem] * 5,
-        (array(n_frame, half * positions, TILE, dtype=jnp.bfloat16), array(half * n_frame, TILE)),
-        buffers,
-        cost=6000000,
-    )(taps, back, own, *arrived[:2])
-    block_rows = frames * positions + frames * n_frame + n_row * share // 2
-    blocks = call(
-        second_kernel, "restore2", [vmem] * 8, array(n_frame, block_rows, TILE, dtype=jnp.bfloat16), buffers, cost=6000000
-    )(taps, back, own, *arrived[2:], feet, estimate, sums)
+    side_rows = frames * n_frame + n_row * share // 2
+    blocks, sides = call(
+        restore_kernel,
+        "restore",
+        [vmem] * 6,
+        (
+            array(n_frame, frames * positions, TILE, dtype=jnp.bfloat16),
+            array(n_frame, side_rows, TILE, dtype=jnp.bfloat16),
+        ),
+        [pltpu.VMEM((frames, span + 2 * PAD, TILE), jnp.float32)] * 3,
+    )(taps, back, feet, own, *arrived)
+    sides = swapped(sides, "frame")
     pieces = swapped(blocks, "frame")
     partial = call(
-        functools.partial(partial_kernel, frames=frames, positions=positions),
+        functools.partial(partial_kernel, positions=positions),
         "partial",
         [vmem] * n_frame,
         array(n_row, share, TILE),
@@ -437,7 +412,7 @@
             pltpu.VMEM((n_frame * frames * n_frame, TILE), jnp.float32),
             pltpu.VMEM((n_frame, n_row * share // 2, TILE), jnp.float32),
         ],
-    )(*pieces)
+    )(*sides)
     shares = swapped(partial, "row")
     spikes = call(
         functools.partial(temporal_kernel, frames=frames),
@@ -446,6 +421,7 @@
         array(n_frame * frames, rows_dev, tiles_dev * TILE, dtype=jnp.bfloat16),
         [pltpu.VMEM((n_frame, frames * positions, TILE), jnp.bfloat16)],
     )(*pieces)
+    spikes, *shares = lax.optimization_barrier((spikes, *shares))
     traces = call(means_kernel, "means", [vmem] * n_row, array(share, n_frame * frames))(*shares)
     return (spikes, traces)
 

time: 32.1 us -> 31.7 us (0.988)
  starting transfers between devices: 15.4 us -> 16.5 us
  Pallas kernels: 6.97 us -> 6.16 us
  waiting for transfers between devices: 6.82 us -> 6.09 us
    ppermute x6 -> x9, starting transfers between devices: 6.38 us -> 10.9 us  [swapped(): lax.ppermute(part, axis, [(i, i ^ step) for i in range(count)])]
    ppermute x4 -> x2, starting transfers between devices: 9.02 us -> 5.61 us  [by_halo(): lax.ppermute(rows.astype(jnp.float16), ('frame', 'row'), swap)]
    ppermute x6 -> x9, waiting for transfers between devices: 6.81 us -> 4.61 us  [swapped(): lax.ppermute(part, axis, [(i, i ^ step) for i in range(count)])]
    ppermute x4 -> x2, waiting for transfers between devices: 0.01 us -> 1.48 us  [by_halo(): lax.ppermute(rows.astype(jnp.float16), ('frame', 'row'), swap)]
    pallas_call x4 -> x3, Pallas kernels: 4.65 us -> 3.84 us  [the longest x1 3.33 us: by_halo(): call(restore_kernel, 'restore', [vmem] * 6, (array(n_frame, frames * posi...]
  transfers between devices with their start and end apart: 10 -> 11, of which waited for: 5 -> 4; matrix products, arithmetic and copies ran while one was open for 0% -> 0% of each run, Pallas kernels for 11% -> 6%
where the time goes in v6:
time: 31.7 us; the launch traced here: 31.4 us
  starting transfers between devices  16.5 us (52%)
  Pallas kernels  6.16 us (19%)
  waiting for transfers between devices  6.09 us (19%)
  local copies, waits for them, and re-layouts  1.78 us (6%)
  between operations  0.78 us (2%)
    ppermute x9, starting transfers between devices, swapped(): lax.ppermute(part, axis, [(i, i ^ step) for i in range(count)])  10.9 us
    ppermute x2, starting transfers between devices, by_halo(): lax.ppermute(rows.astype(jnp.float16), ('frame', 'row'), swap)  5.61 us
    ppermute x9, waiting for transfers between devices, swapped(): lax.ppermute(part, axis, [(i, i ^ step) for i in range(count)])  4.61 us
    pallas_call x1, Pallas kernels, by_halo(): call(restore_kernel, 'restore', [vmem] * 6, (array(n_frame, frames * posi...  3.33 us
    unnamed x8, local copies, waits for them, and re-layouts  1.72 us
    ppermute x2, waiting for transfers between devices, by_halo(): lax.ppermute(rows.astype(jnp.float16), ('frame', 'row'), swap)  1.48 us
    pallas_call x1, Pallas kernels, by_halo(): call(functools.partial(temporal_kernel, frames=frames), 'temporal', [vmem...  0.92 us
    pallas_call x1, Pallas kernels, by_halo(): call(functools.partial(tables_kernel, height=rows_dev * n_row), 'tables',...  0.72 us
  transfers between devices with their start and end apart: 11, of which 4 were waited for; matrix products, arithmetic and copies ran while one was open for 0% of the time, Pallas kernels for 6%

profile of v6, /device:TPU:0, one launch (start us, length us, event | category | flops | bytes accessed | tf_op | source)
XLA Modules:
  0.0 31.4 jit_solution(16973731260339400952)
XLA Ops:
  0.6 1.0 %copy-done = f32[4,16,2048]{2,1,0:T(8,128)S(1)} copy-done((f32[4,16,2048]{2,1,0:T(8,128)S(1)}, f32[4,16,2048]{2,1,0:T(8,128)}, u32[]{:S(2)}) %copy-start) | copy-done | bytes 524312
  1.7 0.1 halo.1
  1.8 4.9 %collective-permute-start = (f16[48,2048]{1,0:T(8,128)(2,1)S(1)}, f16[48,2048]{1,0:T(8,128)(2,1)S(1)}, u32[]{:S(2)}, u32[]{:S(2)}) collective-permute-start(f16[48,2048]{1,0:T(8,128)(2,1)S(1)} %convert_element_type.12), channel_id=1, source_target_pairs={{0,1},{1,0},{2,3},{3,2},{5,6},{6,5},{8,9},{9,8},{10,11},{11,10},{1... | collective-permute-start | bytes 589832 | tf_op jit(solution)/shard_map/ppermute | solution.py:379
  6.8 0.0 copy-start.1
  6.8 0.7 %collective-permute-start.1 = (f16[48,2048]{1,0:T(8,128)(2,1)S(1)}, f16[48,2048]{1,0:T(8,128)(2,1)S(1)}, u32[]{:S(2)}, u32[]{:S(2)}) collective-permute-start(f16[48,2048]{1,0:T(8,128)(2,1)S(1)} %convert_element_type.14), channel_id=1, source_target_pairs={{1,2},{2,1},{4,5},{5,4},{6,7},{7,6},{9,10},{10,9},{12,13},{13,12},... | collective-permute-start | bytes 589832 | tf_op jit(solution)/shard_map/ppermute | solution.py:379
  7.5 0.0 copy-start.2
  7.5 0.0 copy-start.3
  7.5 0.1 copy-done.1
  7.6 0.6 %copy-done.2 = f32[8,5]{1,0:T(8,128)S(1)} copy-done((f32[8,5]{1,0:T(8,128)S(1)}, f32[8,5]{1,0:T(8,128)}, u32[]{:S(2)}) %copy-start.2) | copy-done | bytes 184
  8.2 0.7 %tables.1 = (f32[4,48,128]{2,1,0:T(8,128)S(1)}, f32[4,48,128]{2,1,0:T(8,128)S(1)}, bf16[4,32,128]{2,1,0:T(8,128)(2,1)S(1)}) custom-call(s32[8]{0:T(128)S(1)} %copy-done.3, f32[8,5]{1,0:T(8,128)S(1)} %copy-done.2, s32[16,4,256]{2,1,0:T(4,128)S(1)} %bitcast.25), custom_call_target="tpu_custom_call" | custom-call | flops 1000000 | bytes 1000000 | tf_op jit(solution)/shard_map/tables/pallas_call | solution.py:382
  8.9 1.5 %collective-permute-done = f16[48,2048]{1,0:T(8,128)(2,1)S(1)} collective-permute-done((f16[48,2048]{1,0:T(8,128)(2,1)S(1)}, f16[48,2048]{1,0:T(8,128)(2,1)S(1)}, u32[]{:S(2)}, u32[]{:S(2)}) %collective-permute-start) | collective-permute-done | bytes 196640 | tf_op jit(solution)/shard_map/ppermute | solution.py:379
  10.4 0.0 collective-permute-done.1
  10.5 3.3 %restore.1 = (bf16[4,256,128]{2,1,0:T(8,128)(2,1)S(1)}, bf16[4,48,128]{2,1,0:T(8,128)(2,1)S(1)}) custom-call(f32[4,48,128]{2,1,0:T(8,128)S(1)} %get-tuple-element.15.taps_ref, f32[4,48,128]{2,1,0:T(8,128)S(1)} %get-tuple-element.16.back_ref, bf16[4,32,128]{2,1,0:T(8,128)(2,1)S(1)} %get-tuple-element.17.feet_ref, ...), custom_call_target="tpu_custom_call" | custom-call | flops 1000000 | bytes 1000000 | tf_op jit(solution)/shard_map/restore/pallas_call | solution.py:394
  13.8 2.2 %collective-permute-start.5 = (bf16[48,128]{1,0:T(8,128)(2,1)S(1)}, bf16[48,128]{1,0:T(8,128)(2,1)S(1)}, u32[]{:S(2)}, u32[]{:S(2)}) collective-permute-start(bf16[48,128]{1,0:T(8,128)(2,1)S(1)} %get-tuple-element.34), channel_id=1, source_target_pairs={{0,4},{4,0},{8,12},{12,8},{1,5},{5,1},{9,13},{13,9},{2,6},{6,2},{1... | collective-permute-start | bytes 36872 | tf_op jit(solution)/shard_map/ppermute | solution.py:342
  16.1 1.6 %collective-permute-start.6 = (bf16[48,128]{1,0:T(8,128)(2,1)S(1)}, bf16[48,128]{1,0:T(8,128)(2,1)S(1)}, u32[]{:S(2)}, u32[]{:S(2)}) collective-permute-start(bf16[48,128]{1,0:T(8,128)(2,1)S(1)} %get-tuple-element.33), channel_id=1, source_target_pairs={{0,8},{4,12},{8,0},{12,4},{1,9},{5,13},{9,1},{13,5},{2,10},{6,14},... | collective-permute-start | bytes 36872 | tf_op jit(solution)/shard_map/ppermute | solution.py:342
  17.7 0.0 collective-permute-start.7
  17.7 0.6 %collective-permute-start.2 = (bf16[256,128]{1,0:T(8,128)(2,1)S(1)}, bf16[256,128]{1,0:T(8,128)(2,1)S(1)}, u32[]{:S(2)}, u32[]{:S(2)}) collective-permute-start(bf16[256,128]{1,0:T(8,128)(2,1)S(1)} %get-tuple-element.30), channel_id=1, source_target_pairs={{0,4},{4,0},{8,12},{12,8},{1,5},{5,1},{9,13},{13,9},{2,6},{6,2},{1... | collective-permute-start | bytes 196616 | tf_op jit(solution)/shard_map/ppermute | solution.py:342
  18.3 1.6 %collective-permute-start.3 = (bf16[256,128]{1,0:T(8,128)(2,1)S(1)}, bf16[256,128]{1,0:T(8,128)(2,1)S(1)}, u32[]{:S(2)}, u32[]{:S(2)}) collective-permute-start(bf16[256,128]{1,0:T(8,128)(2,1)S(1)} %get-tuple-element.29), channel_id=1, source_target_pairs={{0,8},{4,12},{8,0},{12,4},{1,9},{5,13},{9,1},{13,5},{2,10},{6,14},... | collective-permute-start | bytes 196616 | tf_op jit(solution)/shard_map/ppermute | solution.py:342
  19.9 0.0 collective-permute-done.5.refs_1_
  19.9 0.0 collective-permute-start.4
  20.0 1.0 %collective-permute-done.7.refs_3_ = bf16[48,128]{1,0:T(8,128)(2,1)S(1)} collective-permute-done((bf16[48,128]{1,0:T(8,128)(2,1)S(1)}, bf16[48,128]{1,0:T(8,128)(2,1)S(1)}, u32[]{:S(2)}, u32[]{:S(2)}) %collective-permute-start.7) | collective-permute-done | bytes 12320 | tf_op jit(solution)/shard_map/ppermute | solution.py:342
  20.9 0.4 %partial.1 = f32[4,16,128]{2,1,0:T(8,128)S(1)} custom-call(bf16[48,128]{1,0:T(8,128)(2,1)S(1)} %get-tuple-element.35.refs_0_, bf16[48,128]{1,0:T(8,128)(2,1)S(1)} %collective-permute-done.5.refs_1_, bf16[48,128]{1,0:T(8,128)(2,1)S(1)} %collective-permute-done.6.refs_2_, bf16[48,128]{1,0:T(8,128)(2,1)S(1)} %collective-permute-done.7.refs_3_), custom_call_target="tpu_custom_call" | custom-call | flops 1000000 | bytes 1000000 | tf_op jit(solution)/shard_map/partial/pallas_call | solution.py:406
  21.4 3.6 %collective-permute-start.10 = (f32[16,128]{1,0:T(8,128)S(1)}, f32[16,128]{1,0:T(8,128)S(1)}, u32[]{:S(2)}, u32[]{:S(2)}) collective-permute-start(f32[16,128]{1,0:T(8,128)S(1)} %get-tuple-element.36), channel_id=1, source_target_pairs={{0,3},{1,2},{2,1},{3,0},{4,7},{5,6},{6,5},{7,4},{8,11},{9,10},{10,... | collective-permute-start | bytes 24584 | tf_op jit(solution)/shard_map/ppermute | solution.py:342
  25.0 1.2 %collective-permute-start.8 = (f32[16,128]{1,0:T(8,128)S(1)}, f32[16,128]{1,0:T(8,128)S(1)}, u32[]{:S(2)}, u32[]{:S(2)}) collective-permute-start(f32[16,128]{1,0:T(8,128)S(1)} %get-tuple-element.38), channel_id=1, source_target_pairs={{0,1},{1,0},{2,3},{3,2},{4,5},{5,4},{6,7},{7,6},{8,9},{9,8},{10,11... | collective-permute-start | bytes 24584 | tf_op jit(solution)/shard_map/ppermute | solution.py:342
  26.2 0.0 collective-permute-done.2.refs_1_
  26.2 0.0 collective-permute-start.9
  26.2 0.0 collective-permute-done.3.refs_2_
  26.2 0.9 %temporal.1 = bf16[16,16,512]{2,1,0:T(8,128)(2,1)} custom-call(bf16[256,128]{1,0:T(8,128)(2,1)S(1)} %get-tuple-element.31.refs_0_, bf16[256,128]{1,0:T(8,128)(2,1)S(1)} %collective-permute-done.2.refs_1_, bf16[256,128]{1,0:T(8,128)(2,1)S(1)} %collective-permute-done.3.refs_2_, bf16[256,128]{1,0:T(8,128)(2,1)S(1)} %collective-permute-done.4.refs_3_), custom_call_target="tpu_custom_call" | custom-call | flops 1000000 | bytes 1000000 | tf_op jit(solution)/shard_map/temporal/pallas_call | solution.py:417
  27.1 0.0 collective-permute-done.10.refs_3_
  27.1 1.5 %collective-permute-done.8.refs_1_ = f32[16,128]{1,0:T(8,128)S(1)} collective-permute-done((f32[16,128]{1,0:T(8,128)S(1)}, f32[16,128]{1,0:T(8,128)S(1)}, u32[]{:S(2)}, u32[]{:S(2)}) %collective-permute-start.8) | collective-permute-done | bytes 8224 | tf_op jit(solution)/shard_map/ppermute | solution.py:342
  28.6 2.1 %collective-permute-done.9.refs_2_ = f32[16,128]{1,0:T(8,128)S(1)} collective-permute-done((f32[16,128]{1,0:T(8,128)S(1)}, f32[16,128]{1,0:T(8,128)S(1)}, u32[]{:S(2)}, u32[]{:S(2)}) %collective-permute-start.9) | collective-permute-done | bytes 8224 | tf_op jit(solution)/shard_map/ppermute | solution.py:342
  30.7 0.7 %means.1 = f32[16,16]{1,0:T(8,128)} custom-call(f32[16,128]{1,0:T(8,128)S(1)} %get-tuple-element.24.refs_0_, f32[16,128]{1,0:T(8,128)S(1)} %collective-permute-done.8.refs_1_, f32[16,128]{1,0:T(8,128)S(1)} %collective-permute-done.9.refs_2_, f32[16,128]{1,0:T(8,128)S(1)} %collective-permute-done.10.refs_3_), custom_call_target="tpu_custom_call" | custom-call | flops 1000000 | bytes 1000000 | tf_op jit(solution)/shard_map/means/pallas_call | solution.py:425
  (11 shorter events, 0.2 us)
Async XLA Ops:
  0.6 1.0 %copy-start = (f32[4,16,2048]{2,1,0:T(8,128)S(1)}, f32[4,16,2048]{2,1,0:T(8,128)}, u32[]{:S(2)}) copy-start(f32[4,16,2048]{2,1,0:T(8,128)} %observed_ref.1) | copy-start | bytes 1572868
  1.8 8.6 %collective-permute-start = (f16[48,2048]{1,0:T(8,128)(2,1)S(1)}, f16[48,2048]{1,0:T(8,128)(2,1)S(1)}, u32[]{:S(2)}, u32[]{:S(2)}) collective-permute-start(f16[48,2048]{1,0:T(8,128)(2,1)S(1)} %convert_element_type.12), channel_id=1, source_target_pairs={{0,1},{1,0},{2,3},{3,2},{5,6},{6,5},{8,9},{9,8},{10,11},{11,10},{1... | collective-permute-start | bytes 589832 | tf_op jit(solution)/shard_map/ppermute | solution.py:379
  6.8 0.8 %copy-start.1 = (s32[256,16,4]{0,2,1:T(4,128)S(1)}, s32[256,16,4]{0,2,1:T(4,128)}, u32[]{:S(2)}) copy-start(s32[256,16,4]{0,2,1:T(4,128)} %param.7) | copy-start | bytes 196612
  6.8 3.6 %collective-permute-start.1 = (f16[48,2048]{1,0:T(8,128)(2,1)S(1)}, f16[48,2048]{1,0:T(8,128)(2,1)S(1)}, u32[]{:S(2)}, u32[]{:S(2)}) collective-permute-start(f16[48,2048]{1,0:T(8,128)(2,1)S(1)} %convert_element_type.14), channel_id=1, source_target_pairs={{1,2},{2,1},{4,5},{5,4},{6,7},{7,6},{9,10},{10,9},{12,13},{13,12},... | collective-permute-start | bytes 589832 | tf_op jit(solution)/shard_map/ppermute | solution.py:379
  7.5 0.7 %copy-start.2 = (f32[8,5]{1,0:T(8,128)S(1)}, f32[8,5]{1,0:T(8,128)}, u32[]{:S(2)}) copy-start(f32[8,5]{1,0:T(8,128)} %kernels_ref.1) | copy-start | bytes 484
  7.5 0.7 %copy-start.3 = (s32[8]{0:T(128)S(1)}, s32[8]{0:T(128)}, u32[]{:S(2)}) copy-start(s32[8]{0:T(128)} %band_ref.1) | copy-start | bytes 100
  13.8 6.1 %collective-permute-start.5 = (bf16[48,128]{1,0:T(8,128)(2,1)S(1)}, bf16[48,128]{1,0:T(8,128)(2,1)S(1)}, u32[]{:S(2)}, u32[]{:S(2)}) collective-permute-start(bf16[48,128]{1,0:T(8,128)(2,1)S(1)} %get-tuple-element.34), channel_id=1, source_target_pairs={{0,4},{4,0},{8,12},{12,8},{1,5},{5,1},{9,13},{13,9},{2,6},{6,2},{1... | collective-permute-start | bytes 36872 | tf_op jit(solution)/shard_map/ppermute | solution.py:342
  16.1 3.9 %collective-permute-start.6 = (bf16[48,128]{1,0:T(8,128)(2,1)S(1)}, bf16[48,128]{1,0:T(8,128)(2,1)S(1)}, u32[]{:S(2)}, u32[]{:S(2)}) collective-permute-start(bf16[48,128]{1,0:T(8,128)(2,1)S(1)} %get-tuple-element.33), channel_id=1, source_target_pairs={{0,8},{4,12},{8,0},{12,4},{1,9},{5,13},{9,1},{13,5},{2,10},{6,14},... | collective-permute-start | bytes 36872 | tf_op jit(solution)/shard_map/ppermute | solution.py:342
  17.7 3.2 %collective-permute-start.7 = (bf16[48,128]{1,0:T(8,128)(2,1)S(1)}, bf16[48,128]{1,0:T(8,128)(2,1)S(1)}, u32[]{:S(2)}, u32[]{:S(2)}) collective-permute-start(bf16[48,128]{1,0:T(8,128)(2,1)S(1)} %get-tuple-element.32), channel_id=1, source_target_pairs={{0,12},{4,8},{8,4},{12,0},{1,13},{5,9},{9,5},{13,1},{2,14},{6,10},... | collective-permute-start | bytes 36872 | tf_op jit(solution)/shard_map/ppermute | solution.py:342
  17.7 8.4 %collective-permute-start.2 = (bf16[256,128]{1,0:T(8,128)(2,1)S(1)}, bf16[256,128]{1,0:T(8,128)(2,1)S(1)}, u32[]{:S(2)}, u32[]{:S(2)}) collective-permute-start(bf16[256,128]{1,0:T(8,128)(2,1)S(1)} %get-tuple-element.30), channel_id=1, source_target_pairs={{0,4},{4,0},{8,12},{12,8},{1,5},{5,1},{9,13},{13,9},{2,6},{6,2},{1... | collective-permute-start | bytes 196616 | tf_op jit(solution)/shard_map/ppermute | solution.py:342
  18.3 7.9 %collective-permute-start.3 = (bf16[256,128]{1,0:T(8,128)(2,1)S(1)}, bf16[256,128]{1,0:T(8,128)(2,1)S(1)}, u32[]{:S(2)}, u32[]{:S(2)}) collective-permute-start(bf16[256,128]{1,0:T(8,128)(2,1)S(1)} %get-tuple-element.29), channel_id=1, source_target_pairs={{0,8},{4,12},{8,0},{12,4},{1,9},{5,13},{9,1},{13,5},{2,10},{6,14},... | collective-permute-start | bytes 196616 | tf_op jit(solution)/shard_map/ppermute | solution.py:342
  19.9 6.2 %collective-permute-start.4 = (bf16[256,128]{1,0:T(8,128)(2,1)S(1)}, bf16[256,128]{1,0:T(8,128)(2,1)S(1)}, u32[]{:S(2)}, u32[]{:S(2)}) collective-permute-start(bf16[256,128]{1,0:T(8,128)(2,1)S(1)} %get-tuple-element.28), channel_id=1, source_target_pairs={{0,12},{4,8},{8,4},{12,0},{1,13},{5,9},{9,5},{13,1},{2,14},{6,10},... | collective-permute-start | bytes 196616 | tf_op jit(solution)/shard_map/ppermute | solution.py:342
  21.4 5.7 %collective-permute-start.10 = (f32[16,128]{1,0:T(8,128)S(1)}, f32[16,128]{1,0:T(8,128)S(1)}, u32[]{:S(2)}, u32[]{:S(2)}) collective-permute-start(f32[16,128]{1,0:T(8,128)S(1)} %get-tuple-element.36), channel_id=1, source_target_pairs={{0,3},{1,2},{2,1},{3,0},{4,7},{5,6},{6,5},{7,4},{8,11},{9,10},{10,... | collective-permute-start | bytes 24584 | tf_op jit(solution)/shard_map/ppermute | solution.py:342
  25.0 3.7 %collective-permute-start.8 = (f32[16,128]{1,0:T(8,128)S(1)}, f32[16,128]{1,0:T(8,128)S(1)}, u32[]{:S(2)}, u32[]{:S(2)}) collective-permute-start(f32[16,128]{1,0:T(8,128)S(1)} %get-tuple-element.38), channel_id=1, source_target_pairs={{0,1},{1,0},{2,3},{3,2},{4,5},{5,4},{6,7},{7,6},{8,9},{9,8},{10,11... | collective-permute-start | bytes 24584 | tf_op jit(solution)/shard_map/ppermute | solution.py:342
  26.2 4.6 %collective-permute-start.9 = (f32[16,128]{1,0:T(8,128)S(1)}, f32[16,128]{1,0:T(8,128)S(1)}, u32[]{:S(2)}, u32[]{:S(2)}) collective-permute-start(f32[16,128]{1,0:T(8,128)S(1)} %get-tuple-element.37), channel_id=1, source_target_pairs={{0,2},{1,3},{2,0},{3,1},{4,6},{5,7},{6,4},{7,5},{8,10},{9,11},{10,... | collective-permute-start | bytes 24584 | tf_op jit(solution)/shard_map/ppermute | solution.py:342

commit v7 on v5

--- a/solution.py
+++ b/solution.py
@@ -128,26 +128,20 @@
 
 
 def halo_kernel(observed_ref, *refs):
-    sent, (own_ref, arrived) = refs[:-2], refs[-2:]
+    sent, own_ref = refs[:-1], refs[-1]
     even = lax.axis_index("row") % 2 == 0
-    copies = [
-        pltpu.make_async_copy(observed_ref.at[frame], own_ref.at[frame], arrived.at[frame])
-        for frame in range(own_ref.shape[0])
-    ]
-    for copy in copies:
-        copy.start()
-    frames = len(copies) // HALVES
-    for frame, copy in enumerate(copies):
-        first_ref, second_ref = sent[2 * (frame // frames) : 2 * (frame // frames) + 2]
-        copy.wait()
+    frames = observed_ref.shape[0] // HALVES
+    own_ref[...] = observed_ref[...]
+    for frame in range(observed_ref.shape[0]):
+        inner_ref, outer_ref = sent[2 * (frame // frames) : 2 * (frame // frames) + 2]
         near = frame % frames * NEAR
         far = frames * NEAR + frame % frames * FAR
-        low, high = own_ref[frame, -NEAR:, :], own_ref[frame, :NEAR, :]
-        first_ref[near : near + NEAR, :] = jnp.where(even, low, high)
-        second_ref[near : near + NEAR, :] = jnp.where(even, high, low)
-        low, high = own_ref[frame, -NEAR - FAR : -NEAR, :], own_ref[frame, NEAR : NEAR + FAR, :]
-        first_ref[far : far + FAR, :] = jnp.where(even, low, high)
-        second_ref[far : far + FAR, :] = jnp.where(even, high, low)
+        bottom, top = observed_ref[frame, -NEAR:, :], observed_ref[frame, :NEAR, :]
+        inner_ref[near : near + NEAR, :] = jnp.where(even, bottom, top)
+        outer_ref[near : near + NEAR, :] = jnp.where(even, top, bottom)
+        bottom, top = observed_ref[frame, -NEAR - FAR : -NEAR, :], observed_ref[frame, NEAR : NEAR + FAR, :]
+        inner_ref[far : far + FAR, :] = jnp.where(even, bottom, top)
+        outer_ref[far : far + FAR, :] = jnp.where(even, top, bottom)
 
 
 def tables_kernel(band_ref, kernels_ref, masks_ref, taps_ref, back_ref, feet_ref, pad_ref, *, height):
@@ -260,7 +254,7 @@
 
 
 def second_kernel(
-    taps_ref, back_ref, own_ref, inner_ref, outer_ref, feet_ref, estimate_ref, sums_ref, out_ref, *scratch
+    taps_ref, back_ref, own_ref, inner_ref, outer_ref, feet_ref, estimate_ref, sums_ref, out_ref, side_ref, *scratch
 ):
     sums = restore_half(taps_ref, back_ref, own_ref, inner_ref, outer_ref, out_ref, *scratch, 1)
     sums = jnp.concatenate([sums_ref[...], sums], axis=0)
@@ -268,11 +262,10 @@
     positions = done * HALVES // own_ref.shape[0]
     high = sums.astype(jnp.bfloat16).astype(jnp.float32)
     split = jnp.where(lax.broadcasted_iota(jnp.int32, sums.shape, 1) < positions, high, sums - high).astype(jnp.bfloat16)
-    start = HALVES * done
     for block in range(n_frame):
         out_ref[block, :done, :] = estimate_ref[block]
-        out_ref[block, start : start + split.shape[0], :] = split
-        out_ref[block, start + split.shape[0] :, :] = feet_ref[block]
+        side_ref[block, : split.shape[0], :] = split
+        side_ref[block, split.shape[0] :, :] = feet_ref[block]
 
 
 def deconvolved(series):
@@ -298,16 +291,15 @@
     return result
 
 
-def partial_kernel(*refs, frames, positions):
+def partial_kernel(*refs, positions):
     pieces, (out_ref, sums_ref, feet_ref) = refs[:-3], refs[-3:]
     n_frame = len(pieces)
     place = lax.axis_index("frame")
-    start = frames * positions
-    rows = frames * n_frame
+    rows = sums_ref.shape[0] // n_frame
     half = feet_ref.shape[1]
     for step, piece in enumerate(pieces):
-        sums_ref[pl.ds(pl.multiple_of((place ^ step) * rows, rows), rows), :] = piece[start : start + rows, :].astype(jnp.float32)
-        feet_ref[place ^ step] = piece[start + rows :, :].astype(jnp.float32)
+        sums_ref[pl.ds(pl.multiple_of((place ^ step) * rows, rows), rows), :] = piece[:rows, :].astype(jnp.float32)
+        feet_ref[place ^ step] = piece[rows:, :].astype(jnp.float32)
     series = [sums_ref[t * n_frame : (t + 1) * n_frame, :] for t in range(rows)]
     for t, sums in enumerate(deconvolved(series)):
         sums_ref[t * n_frame : (t + 1) * n_frame, :] = sums + pltpu.roll(sums, TILE // 2, 1)
@@ -335,7 +327,7 @@
     pieces, (spikes_ref, in_ref) = refs[:-2], refs[-2:]
     place = lax.axis_index("frame")
     for step, piece in enumerate(pieces):
-        in_ref[place ^ step] = piece[: in_ref.shape[1], :]
+        in_ref[place ^ step] = piece[...]
     total, rows_dev, columns = spikes_ref.shape
     positions = in_ref.shape[1] // frames
     for tile in range(columns // TILE):
@@ -365,6 +357,13 @@
     return arrived
 
 
+def in_turn(*arrays):
+    done = []
+    for array in arrays:
+        done = list(lax.optimization_barrier((*done, array)))
+    return done
+
+
 def by_halo(observed, kernels, band_kernel, masks):
     n_frame, n_row = lax.axis_size("frame"), lax.axis_size("row")
     frames, rows_dev, width = observed.shape
@@ -374,7 +373,7 @@
     span = rows_dev + 2 * MARGIN
     smem, vmem = pl.BlockSpec(memory_space=pltpu.SMEM), pl.BlockSpec(memory_space=pltpu.VMEM)
 
-    def call(kernel, name, in_specs, out_shape, scratch=(), cost=1000000):
+    def call(kernel, name, in_specs, out_shape, scratch=(), cost=1000):
         many = isinstance(out_shape, tuple)
         return pl.pallas_call(
             kernel,
@@ -392,16 +391,18 @@
 
     half = frames // HALVES
     packed = array(half * (NEAR + FAR), width)
-    *sent, own = call(
-        halo_kernel,
-        "halo",
-        [pl.BlockSpec(memory_space=pltpu.HBM)],
-        (packed,) * (2 * HALVES) + (array(*observed.shape),),
-        [pltpu.SemaphoreType.DMA((frames,))],
-    )(observed)
-    pairs = [(i, i + 1) for i in range(0, n_row - 1, 2)], [(i, i + 1) for i in range(1, n_row - 1, 2)]
-    pairs = [pair + [(j, i) for i, j in pair] for pair in pairs]
-    arrived = [lax.ppermute(rows.astype(jnp.float16), "row", pairs[i % 2]) for i, rows in enumerate(sent)]
+    *sent, own = call(halo_kernel, "halo", [vmem], (packed,) * (2 * HALVES) + (array(*observed.shape),))(observed)
+    swaps = [
+        [pair for i in range(first, n_row - 1, 2) for pair in ((i, i + 1), (i + 1, i))] for first in (0, 1)
+    ]
+
+    def swap(inner, outer):
+        inner, outer = inner.astype(jnp.float16), outer.astype(jnp.float16)
+        return inner, lax.ppermute(outer, "row", swaps[1]), lax.ppermute(inner, "row", swaps[0])
+
+    last, *arrived1 = swap(*sent[:2])
+    outer1, inner1 = in_turn(*arrived1)
+    band_kernel, last = lax.optimization_barrier((band_kernel, last))
     taps, back, feet = call(
         functools.partial(tables_kernel, height=rows_dev * n_row),
         "tables",
@@ -411,9 +412,10 @@
             array(len(SIDES), span, TILE),
             array(n_frame, n_row * share // 2, TILE, dtype=jnp.bfloat16),
         ),
-        [pltpu.VMEM((len(SIDES), span + 2 * BAND, TILE), jnp.float32)],
+        [pltpu.VMEM((len(SIDES), span + 2 * PAD, TILE), jnp.float32)],
     )(band_kernel, kernels, masks.transpose(1, 2, 0))
-    arrived = [rows.astype(jnp.float32) for rows in arrived]
+    *sent, taps = lax.optimization_barrier((*sent[2:], taps))
+    _, *arrived2 = swap(*sent)
     buffers = [pltpu.VMEM((half * TOGETHER, span + 2 * PAD, TILE), jnp.float32)] * 3
     estimate, sums = call(
         first_kernel,
@@ -421,15 +423,23 @@
         [vmem] * 5,
         (array(n_frame, half * positions, TILE, dtype=jnp.bfloat16), array(half * n_frame, TILE)),
         buffers,
-        cost=6000000,
-    )(taps, back, own, *arrived[:2])
-    block_rows = frames * positions + frames * n_frame + n_row * share // 2
-    blocks = call(
-        second_kernel, "restore2", [vmem] * 8, array(n_frame, block_rows, TILE, dtype=jnp.bfloat16), buffers, cost=6000000
-    )(taps, back, own, *arrived[2:], feet, estimate, sums)
+    )(taps, back, own, inner1.astype(jnp.float32), outer1.astype(jnp.float32))
+    estimate, outer2, inner2 = in_turn(estimate, *arrived2)
+    side_rows = frames * n_frame + n_row * share // 2
+    blocks, sides = call(
+        second_kernel,
+        "restore2",
+        [vmem] * 8,
+        (
+            array(n_frame, frames * positions, TILE, dtype=jnp.bfloat16),
+            array(n_frame, side_rows, TILE, dtype=jnp.bfloat16),
+        ),
+        buffers,
+    )(taps, back, own, inner2.astype(jnp.float32), outer2.astype(jnp.float32), feet, estimate, sums)
+    sides = swapped(sides, "frame")
     pieces = swapped(blocks, "frame")
     partial = call(
-        functools.partial(partial_kernel, frames=frames, positions=positions),
+        functools.partial(partial_kernel, positions=positions),
         "partial",
         [vmem] * n_frame,
         array(n_row, share, TILE),
@@ -437,7 +447,7 @@
             pltpu.VMEM((n_frame * frames * n_frame, TILE), jnp.float32),
             pltpu.VMEM((n_frame, n_row * share // 2, TILE), jnp.float32),
         ],
-    )(*pieces)
+    )(*sides)
     shares = swapped(partial, "row")
     spikes = call(
         functools.partial(temporal_kernel, frames=frames),
@@ -446,6 +456,7 @@
         array(n_frame * frames, rows_dev, tiles_dev * TILE, dtype=jnp.bfloat16),
         [pltpu.VMEM((n_frame, frames * positions, TILE), jnp.bfloat16)],
     )(*pieces)
+    spikes, *shares = in_turn(spikes, *shares[::-1])
     traces = call(means_kernel, "means", [vmem] * n_row, array(share, n_frame * frames))(*shares)
     return (spikes, traces)
 

time: 32.1 us -> 30.8 us (0.960)
  starting transfers between devices: 15.4 us -> 18.6 us
  waiting for transfers between devices: 6.82 us -> 3.93 us
  Pallas kernels: 6.97 us -> 6.07 us
  local copies, waits for them, and re-layouts: 1.78 us -> 1.1 us
    ppermute x6 -> x9, waiting for transfers between devices: 6.81 us -> 3.01 us  [swapped(): lax.ppermute(part, axis, [(i, i ^ step) for i in range(count)])]
    ppermute x6 -> x9, starting transfers between devices: 6.38 us -> 8.33 us  [swapped(): lax.ppermute(part, axis, [(i, i ^ step) for i in range(count)])]
    ppermute x4, starting transfers between devices: 9.02 us -> 10.3 us  [the longest x2 8.8 us: swap(): lax.ppermute(inner, 'row', swaps[0])]
    ppermute x4, waiting for transfers between devices: 0.01 us -> 0.92 us  [the longest x2 0.92 us: swap(): lax.ppermute(inner, 'row', swaps[0])]
    pallas_call x3, Pallas kernels: 2.92 us -> 2.14 us  [the longest x1 1.62 us: by_halo(): call(second_kernel, 'restore2', [vmem] * 8, (array(n_frame, frames * posi...]
    unnamed x8, local copies, waits for them, and re-layouts: 1.73 us -> 1.05 us
  transfers between devices with their start and end apart: 10 -> 13, of which waited for: 5 -> 4; matrix products, arithmetic and copies ran while one was open for 0% -> 0% of each run, Pallas kernels for 11% -> 12%
where the time goes in v7:
time: 30.8 us; the launch traced here: 30.6 us
  starting transfers between devices  18.6 us (60%)
  Pallas kernels  6.07 us (20%)
  waiting for transfers between devices  3.93 us (13%)
  local copies, waits for them, and re-layouts  1.1 us (4%)
  between operations  0.81 us (3%)
    ppermute x2, starting transfers between devices, swap(): lax.ppermute(inner, 'row', swaps[0])  8.8 us
    ppermute x9, starting transfers between devices, swapped(): lax.ppermute(part, axis, [(i, i ^ step) for i in range(count)])  8.33 us
    ppermute x9, waiting for transfers between devices, swapped(): lax.ppermute(part, axis, [(i, i ^ step) for i in range(count)])  3.01 us
    pallas_call x1, Pallas kernels, by_halo(): call(second_kernel, 'restore2', [vmem] * 8, (array(n_frame, frames * posi...  1.62 us
    pallas_call x1, Pallas kernels, by_halo(): call(first_kernel, 'restore1', [vmem] * 5, (array(n_frame, half * positio...  1.61 us
    ppermute x2, starting transfers between devices, swap(): lax.ppermute(outer, 'row', swaps[1])  1.47 us
    unnamed x8, local copies, waits for them, and re-layouts  1.05 us
    pallas_call x1, Pallas kernels, by_halo(): call(functools.partial(temporal_kernel, frames=frames), 'temporal', [vmem...  0.92 us
  transfers between devices with their start and end apart: 13, of which 4 were waited for; matrix products, arithmetic and copies ran while one was open for 0% of the time, Pallas kernels for 12%

profile of v7, /device:TPU:0, one launch (start us, length us, event | category | flops | bytes accessed | tf_op | source)
XLA Modules:
  0.0 30.6 jit_solution(18380008534811054225)
XLA Ops:
  0.6 1.0 %copy-done = f32[4,16,2048]{2,1,0:T(8,128)S(1)} copy-done((f32[4,16,2048]{2,1,0:T(8,128)S(1)}, f32[4,16,2048]{2,1,0:T(8,128)}, u32[]{:S(2)}) %copy-start) | copy-done | bytes 524312
  1.7 0.1 halo.1
  1.8 3.1 %collective-permute-start.1 = (f16[24,2048]{1,0:T(8,128)(2,1)S(1)}, f16[24,2048]{1,0:T(8,128)(2,1)S(1)}, u32[]{:S(2)}, u32[]{:S(2)}) collective-permute-start(f16[24,2048]{1,0:T(8,128)(2,1)S(1)} %convert_element_type.24), channel_id=1, source_target_pairs={{0,1},{1,0},{2,3},{3,2},{4,5},{5,4},{6,7},{7,6},{8,9},{9,8},{10,11... | collective-permute-start | bytes 294920 | tf_op jit(solution)/shard_map/ppermute | solution.py:401
  4.9 0.0 copy-start.3
  4.9 0.8 %collective-permute-start = (f16[24,2048]{1,0:T(8,128)(2,1)S(1)}, f16[24,2048]{1,0:T(8,128)(2,1)S(1)}, u32[]{:S(2)}, u32[]{:S(2)}) collective-permute-start(f16[24,2048]{1,0:T(8,128)(2,1)S(1)} %convert_element_type.25), channel_id=1, source_target_pairs={{1,2},{2,1},{5,6},{6,5},{9,10},{10,9},{13,14},{14,13},{17,18},{18,... | collective-permute-start | bytes 294920 | tf_op jit(solution)/shard_map/ppermute | solution.py:401
  5.8 0.7 %tables.1 = (f32[4,48,128]{2,1,0:T(8,128)S(1)}, f32[4,48,128]{2,1,0:T(8,128)S(1)}, bf16[4,32,128]{2,1,0:T(8,128)(2,1)S(1)}) custom-call(s32[8]{0:T(128)S(1)} %copy-done.3, f32[8,5]{1,0:T(8,128)S(1)} %copy-done.2, s32[16,4,256]{2,1,0:T(4,128)S(1)} %bitcast.25), custom_call_target="tpu_custom_call" | custom-call | flops 1000 | bytes 1000 | tf_op jit(solution)/shard_map/tables/pallas_call | solution.py:406
  6.5 0.7 %collective-permute-start.2 = (f16[24,2048]{1,0:T(8,128)(2,1)S(1)}, f16[24,2048]{1,0:T(8,128)(2,1)S(1)}, u32[]{:S(2)}, u32[]{:S(2)}) collective-permute-start(f16[24,2048]{1,0:T(8,128)(2,1)S(1)} %convert_element_type.28), channel_id=1, source_target_pairs={{1,2},{2,1},{5,6},{6,5},{9,10},{10,9},{13,14},{14,13},{17,18},{18,... | collective-permute-start | bytes 294920 | tf_op jit(solution)/shard_map/ppermute | solution.py:401
  7.2 5.7 %collective-permute-start.3 = (f16[24,2048]{1,0:T(8,128)(2,1)S(1)}, f16[24,2048]{1,0:T(8,128)(2,1)S(1)}, u32[]{:S(2)}, u32[]{:S(2)}) collective-permute-start(f16[24,2048]{1,0:T(8,128)(2,1)S(1)} %convert_element_type.29), channel_id=1, source_target_pairs={{0,1},{1,0},{2,3},{3,2},{4,5},{5,4},{6,7},{7,6},{8,9},{9,8},{10,11... | collective-permute-start | bytes 294920 | tf_op jit(solution)/shard_map/ppermute | solution.py:401
  12.9 0.0 collective-permute-done
  12.9 0.0 collective-permute-done.1
  13.0 1.6 %restore1.1 = (bf16[4,128,128]{2,1,0:T(8,128)(2,1)S(1)}, f32[8,128]{1,0:T(8,128)S(1)}) custom-call(f32[4,48,128]{2,1,0:T(8,128)S(1)} %get-tuple-element.44.taps_ref, f32[4,48,128]{2,1,0:T(8,128)S(1)} %get-tuple-element.45.back_ref, f32[4,16,2048]{2,1,0:T(8,128)S(1)} %get-tuple-element.46.own_ref, f32[24,2048]{1,0:T(8,128)S(1)} %convert_element_type.26.inner_ref, ...), custom_call_target="tpu_custom_call" | custom-call | flops 1000 | bytes 1000 | tf_op jit(solution)/shard_map/restore1/pallas_call | solution.py:420
  14.6 0.9 %collective-permute-done.3 = f16[24,2048]{1,0:T(8,128)(2,1)S(1)} collective-permute-done((f16[24,2048]{1,0:T(8,128)(2,1)S(1)}, f16[24,2048]{1,0:T(8,128)(2,1)S(1)}, u32[]{:S(2)}, u32[]{:S(2)}) %collective-permute-start.3) | collective-permute-done | bytes 98336 | tf_op jit(solution)/shard_map/ppermute | solution.py:401
  15.6 1.6 %restore2.1 = (bf16[4,256,128]{2,1,0:T(8,128)(2,1)S(1)}, bf16[4,48,128]{2,1,0:T(8,128)(2,1)S(1)}) custom-call(f32[4,48,128]{2,1,0:T(8,128)S(1)} %get-tuple-element.44.taps_ref, f32[4,48,128]{2,1,0:T(8,128)S(1)} %get-tuple-element.45.back_ref, f32[4,16,2048]{2,1,0:T(8,128)S(1)} %get-tuple-element.46.own_ref, f32[24,2048]{1,0:T(8,128)S(1)} %convert_element_type.30.inner_ref, ...), custom_call_target="tpu_custom_call" | custom-call | flops 1000 | bytes 1000 | tf_op jit(solution)/shard_map/restore2/pallas_call | solution.py:429
  17.2 0.1 collective-permute-start.7
  17.3 1.6 %collective-permute-start.8 = (bf16[48,128]{1,0:T(8,128)(2,1)S(1)}, bf16[48,128]{1,0:T(8,128)(2,1)S(1)}, u32[]{:S(2)}, u32[]{:S(2)}) collective-permute-start(bf16[48,128]{1,0:T(8,128)(2,1)S(1)} %get-tuple-element.81), channel_id=1, source_target_pairs={{0,8},{4,12},{8,0},{12,4},{1,9},{5,13},{9,1},{13,5},{2,10},{6,14},... | collective-permute-start | bytes 36872 | tf_op jit(solution)/shard_map/ppermute | solution.py:356
  18.9 0.3 collective-permute-start.9
  19.2 0.4 %collective-permute-start.4 = (bf16[256,128]{1,0:T(8,128)(2,1)S(1)}, bf16[256,128]{1,0:T(8,128)(2,1)S(1)}, u32[]{:S(2)}, u32[]{:S(2)}) collective-permute-start(bf16[256,128]{1,0:T(8,128)(2,1)S(1)} %get-tuple-element.78), channel_id=1, source_target_pairs={{0,4},{4,0},{8,12},{12,8},{1,5},{5,1},{9,13},{13,9},{2,6},{6,2},{1... | collective-permute-start | bytes 196616 | tf_op jit(solution)/shard_map/ppermute | solution.py:356
  19.6 1.5 %collective-permute-start.5 = (bf16[256,128]{1,0:T(8,128)(2,1)S(1)}, bf16[256,128]{1,0:T(8,128)(2,1)S(1)}, u32[]{:S(2)}, u32[]{:S(2)}) collective-permute-start(bf16[256,128]{1,0:T(8,128)(2,1)S(1)} %get-tuple-element.77), channel_id=1, source_target_pairs={{0,8},{4,12},{8,0},{12,4},{1,9},{5,13},{9,1},{13,5},{2,10},{6,14},... | collective-permute-start | bytes 196616 | tf_op jit(solution)/shard_map/ppermute | solution.py:356
  21.1 0.0 collective-permute-done.7.refs_1_
  21.1 0.0 collective-permute-start.6
  21.1 0.8 %collective-permute-done.9.refs_3_ = bf16[48,128]{1,0:T(8,128)(2,1)S(1)} collective-permute-done((bf16[48,128]{1,0:T(8,128)(2,1)S(1)}, bf16[48,128]{1,0:T(8,128)(2,1)S(1)}, u32[]{:S(2)}, u32[]{:S(2)}) %collective-permute-start.9) | collective-permute-done | bytes 12320 | tf_op jit(solution)/shard_map/ppermute | solution.py:356
  22.0 0.4 %partial.1 = f32[4,16,128]{2,1,0:T(8,128)S(1)} custom-call(bf16[48,128]{1,0:T(8,128)(2,1)S(1)} %get-tuple-element.83.refs_0_, bf16[48,128]{1,0:T(8,128)(2,1)S(1)} %collective-permute-done.7.refs_1_, bf16[48,128]{1,0:T(8,128)(2,1)S(1)} %collective-permute-done.8.refs_2_, bf16[48,128]{1,0:T(8,128)(2,1)S(1)} %collective-permute-done.9.refs_3_), custom_call_target="tpu_custom_call" | custom-call | flops 1000 | bytes 1000 | tf_op jit(solution)/shard_map/partial/pallas_call | solution.py:441
  22.4 3.0 %collective-permute-start.10 = (f32[16,128]{1,0:T(8,128)S(1)}, f32[16,128]{1,0:T(8,128)S(1)}, u32[]{:S(2)}, u32[]{:S(2)}) collective-permute-start(f32[16,128]{1,0:T(8,128)S(1)} %get-tuple-element.87), channel_id=1, source_target_pairs={{0,3},{1,2},{2,1},{3,0},{4,7},{5,6},{6,5},{7,4},{8,11},{9,10},{10,... | collective-permute-start | bytes 24584 | tf_op jit(solution)/shard_map/ppermute | solution.py:356
  25.4 0.6 %collective-permute-start.11 = (f32[16,128]{1,0:T(8,128)S(1)}, f32[16,128]{1,0:T(8,128)S(1)}, u32[]{:S(2)}, u32[]{:S(2)}) collective-permute-start(f32[16,128]{1,0:T(8,128)S(1)} %get-tuple-element.86), channel_id=1, source_target_pairs={{0,2},{1,3},{2,0},{3,1},{4,6},{5,7},{6,4},{7,5},{8,10},{9,11},{10,... | collective-permute-start | bytes 24584 | tf_op jit(solution)/shard_map/ppermute | solution.py:356
  26.0 0.8 %collective-permute-start.12 = (f32[16,128]{1,0:T(8,128)S(1)}, f32[16,128]{1,0:T(8,128)S(1)}, u32[]{:S(2)}, u32[]{:S(2)}) collective-permute-start(f32[16,128]{1,0:T(8,128)S(1)} %get-tuple-element.85), channel_id=1, source_target_pairs={{0,1},{1,0},{2,3},{3,2},{4,5},{5,4},{6,7},{7,6},{8,9},{9,8},{10,11... | collective-permute-start | bytes 24584 | tf_op jit(solution)/shard_map/ppermute | solution.py:356
  26.9 0.0 collective-permute-done.5.refs_2_
  26.9 0.0 collective-permute-done.6.refs_3_
  26.9 0.9 %temporal.1 = bf16[16,16,512]{2,1,0:T(8,128)(2,1)} custom-call(bf16[256,128]{1,0:T(8,128)(2,1)S(1)} %get-tuple-element.79.refs_0_, bf16[256,128]{1,0:T(8,128)(2,1)S(1)} %collective-permute-done.4.refs_1_, bf16[256,128]{1,0:T(8,128)(2,1)S(1)} %collective-permute-done.5.refs_2_, bf16[256,128]{1,0:T(8,128)(2,1)S(1)} %collective-permute-done.6.refs_3_), custom_call_target="tpu_custom_call" | custom-call | flops 1000 | bytes 1000 | tf_op jit(solution)/shard_map/temporal/pallas_call | solution.py:452
  27.8 0.1 collective-permute-done.10.refs_0_
  27.9 2.0 %collective-permute-done.11.refs_1_ = f32[16,128]{1,0:T(8,128)S(1)} collective-permute-done((f32[16,128]{1,0:T(8,128)S(1)}, f32[16,128]{1,0:T(8,128)S(1)}, u32[]{:S(2)}, u32[]{:S(2)}) %collective-permute-start.11) | collective-permute-done | bytes 8224 | tf_op jit(solution)/shard_map/ppermute | solution.py:356
  29.9 0.0 collective-permute-done.12.refs_2_
  29.9 0.7 %means.1 = f32[16,16]{1,0:T(8,128)} custom-call(f32[16,128]{1,0:T(8,128)S(1)} %collective-permute-done.10.refs_0_, f32[16,128]{1,0:T(8,128)S(1)} %collective-permute-done.11.refs_1_, f32[16,128]{1,0:T(8,128)S(1)} %collective-permute-done.12.refs_2_, f32[16,128]{1,0:T(8,128)S(1)} %get-tuple-element.75.refs_3_), custom_call_target="tpu_custom_call" | custom-call | flops 1000 | bytes 1000 | tf_op jit(solution)/shard_map/means/pallas_call | solution.py:460
  (20 shorter events, 0.2 us)
Async XLA Ops:
  0.6 1.0 %copy-start = (f32[4,16,2048]{2,1,0:T(8,128)S(1)}, f32[4,16,2048]{2,1,0:T(8,128)}, u32[]{:S(2)}) copy-start(f32[4,16,2048]{2,1,0:T(8,128)} %observed_ref.1) | copy-start | bytes 1572868
  1.8 11.1 %collective-permute-start.1 = (f16[24,2048]{1,0:T(8,128)(2,1)S(1)}, f16[24,2048]{1,0:T(8,128)(2,1)S(1)}, u32[]{:S(2)}, u32[]{:S(2)}) collective-permute-start(f16[24,2048]{1,0:T(8,128)(2,1)S(1)} %convert_element_type.24), channel_id=1, source_target_pairs={{0,1},{1,0},{2,3},{3,2},{4,5},{5,4},{6,7},{7,6},{8,9},{9,8},{10,11... | collective-permute-start | bytes 294920 | tf_op jit(solution)/shard_map/ppermute | solution.py:401
  4.9 0.8 %copy-start.1 = (s32[256,16,4]{0,2,1:T(4,128)S(1)}, s32[256,16,4]{0,2,1:T(4,128)}, u32[]{:S(2)}) copy-start(s32[256,16,4]{0,2,1:T(4,128)} %param.7) | copy-start | bytes 196612
  4.9 0.8 %copy-start.2 = (f32[8,5]{1,0:T(8,128)S(1)}, f32[8,5]{1,0:T(8,128)}, u32[]{:S(2)}) copy-start(f32[8,5]{1,0:T(8,128)} %kernels_ref.1) | copy-start | bytes 484
  4.9 0.8 %copy-start.3 = (s32[8]{0:T(128)S(1)}, s32[8]{0:T(128)}, u32[]{:S(2)}) copy-start(s32[8]{0:T(128)} %band_ref) | copy-start | bytes 100
  4.9 8.0 %collective-permute-start = (f16[24,2048]{1,0:T(8,128)(2,1)S(1)}, f16[24,2048]{1,0:T(8,128)(2,1)S(1)}, u32[]{:S(2)}, u32[]{:S(2)}) collective-permute-start(f16[24,2048]{1,0:T(8,128)(2,1)S(1)} %convert_element_type.25), channel_id=1, source_target_pairs={{1,2},{2,1},{5,6},{6,5},{9,10},{10,9},{13,14},{14,13},{17,18},{18,... | collective-permute-start | bytes 294920 | tf_op jit(solution)/shard_map/ppermute | solution.py:401
  6.5 8.1 %collective-permute-start.2 = (f16[24,2048]{1,0:T(8,128)(2,1)S(1)}, f16[24,2048]{1,0:T(8,128)(2,1)S(1)}, u32[]{:S(2)}, u32[]{:S(2)}) collective-permute-start(f16[24,2048]{1,0:T(8,128)(2,1)S(1)} %convert_element_type.28), channel_id=1, source_target_pairs={{1,2},{2,1},{5,6},{6,5},{9,10},{10,9},{13,14},{14,13},{17,18},{18,... | collective-permute-start | bytes 294920 | tf_op jit(solution)/shard_map/ppermute | solution.py:401
  7.2 8.3 %collective-permute-start.3 = (f16[24,2048]{1,0:T(8,128)(2,1)S(1)}, f16[24,2048]{1,0:T(8,128)(2,1)S(1)}, u32[]{:S(2)}, u32[]{:S(2)}) collective-permute-start(f16[24,2048]{1,0:T(8,128)(2,1)S(1)} %convert_element_type.29), channel_id=1, source_target_pairs={{0,1},{1,0},{2,3},{3,2},{4,5},{5,4},{6,7},{7,6},{8,9},{9,8},{10,11... | collective-permute-start | bytes 294920 | tf_op jit(solution)/shard_map/ppermute | solution.py:401
  17.2 3.9 %collective-permute-start.7 = (bf16[48,128]{1,0:T(8,128)(2,1)S(1)}, bf16[48,128]{1,0:T(8,128)(2,1)S(1)}, u32[]{:S(2)}, u32[]{:S(2)}) collective-permute-start(bf16[48,128]{1,0:T(8,128)(2,1)S(1)} %get-tuple-element.82), channel_id=1, source_target_pairs={{0,4},{4,0},{8,12},{12,8},{1,5},{5,1},{9,13},{13,9},{2,6},{6,2},{1... | collective-permute-start | bytes 36872 | tf_op jit(solution)/shard_map/ppermute | solution.py:356
  17.3 3.8 %collective-permute-start.8 = (bf16[48,128]{1,0:T(8,128)(2,1)S(1)}, bf16[48,128]{1,0:T(8,128)(2,1)S(1)}, u32[]{:S(2)}, u32[]{:S(2)}) collective-permute-start(bf16[48,128]{1,0:T(8,128)(2,1)S(1)} %get-tuple-element.81), channel_id=1, source_target_pairs={{0,8},{4,12},{8,0},{12,4},{1,9},{5,13},{9,1},{13,5},{2,10},{6,14},... | collective-permute-start | bytes 36872 | tf_op jit(solution)/shard_map/ppermute | solution.py:356
  18.9 3.1 %collective-permute-start.9 = (bf16[48,128]{1,0:T(8,128)(2,1)S(1)}, bf16[48,128]{1,0:T(8,128)(2,1)S(1)}, u32[]{:S(2)}, u32[]{:S(2)}) collective-permute-start(bf16[48,128]{1,0:T(8,128)(2,1)S(1)} %get-tuple-element.80), channel_id=1, source_target_pairs={{0,12},{4,8},{8,4},{12,0},{1,13},{5,9},{9,5},{13,1},{2,14},{6,10},... | collective-permute-start | bytes 36872 | tf_op jit(solution)/shard_map/ppermute | solution.py:356
  19.2 6.8 %collective-permute-start.4 = (bf16[256,128]{1,0:T(8,128)(2,1)S(1)}, bf16[256,128]{1,0:T(8,128)(2,1)S(1)}, u32[]{:S(2)}, u32[]{:S(2)}) collective-permute-start(bf16[256,128]{1,0:T(8,128)(2,1)S(1)} %get-tuple-element.78), channel_id=1, source_target_pairs={{0,4},{4,0},{8,12},{12,8},{1,5},{5,1},{9,13},{13,9},{2,6},{6,2},{1... | collective-permute-start | bytes 196616 | tf_op jit(solution)/shard_map/ppermute | solution.py:356
  19.6 7.3 %collective-permute-start.5 = (bf16[256,128]{1,0:T(8,128)(2,1)S(1)}, bf16[256,128]{1,0:T(8,128)(2,1)S(1)}, u32[]{:S(2)}, u32[]{:S(2)}) collective-permute-start(bf16[256,128]{1,0:T(8,128)(2,1)S(1)} %get-tuple-element.77), channel_id=1, source_target_pairs={{0,8},{4,12},{8,0},{12,4},{1,9},{5,13},{9,1},{13,5},{2,10},{6,14},... | collective-permute-start | bytes 196616 | tf_op jit(solution)/shard_map/ppermute | solution.py:356
  21.1 5.8 %collective-permute-start.6 = (bf16[256,128]{1,0:T(8,128)(2,1)S(1)}, bf16[256,128]{1,0:T(8,128)(2,1)S(1)}, u32[]{:S(2)}, u32[]{:S(2)}) collective-permute-start(bf16[256,128]{1,0:T(8,128)(2,1)S(1)} %get-tuple-element.76), channel_id=1, source_target_pairs={{0,12},{4,8},{8,4},{12,0},{1,13},{5,9},{9,5},{13,1},{2,14},{6,10},... | collective-permute-start | bytes 196616 | tf_op jit(solution)/shard_map/ppermute | solution.py:356
  22.4 5.5 %collective-permute-start.10 = (f32[16,128]{1,0:T(8,128)S(1)}, f32[16,128]{1,0:T(8,128)S(1)}, u32[]{:S(2)}, u32[]{:S(2)}) collective-permute-start(f32[16,128]{1,0:T(8,128)S(1)} %get-tuple-element.87), channel_id=1, source_target_pairs={{0,3},{1,2},{2,1},{3,0},{4,7},{5,6},{6,5},{7,4},{8,11},{9,10},{10,... | collective-permute-start | bytes 24584 | tf_op jit(solution)/shard_map/ppermute | solution.py:356
  25.4 4.5 %collective-permute-start.11 = (f32[16,128]{1,0:T(8,128)S(1)}, f32[16,128]{1,0:T(8,128)S(1)}, u32[]{:S(2)}, u32[]{:S(2)}) collective-permute-start(f32[16,128]{1,0:T(8,128)S(1)} %get-tuple-element.86), channel_id=1, source_target_pairs={{0,2},{1,3},{2,0},{3,1},{4,6},{5,7},{6,4},{7,5},{8,10},{9,11},{10,... | collective-permute-start | bytes 24584 | tf_op jit(solution)/shard_map/ppermute | solution.py:356
  26.0 3.9 %collective-permute-start.12 = (f32[16,128]{1,0:T(8,128)S(1)}, f32[16,128]{1,0:T(8,128)S(1)}, u32[]{:S(2)}, u32[]{:S(2)}) collective-permute-start(f32[16,128]{1,0:T(8,128)S(1)} %get-tuple-element.85), channel_id=1, source_target_pairs={{0,1},{1,0},{2,3},{3,2},{4,5},{5,4},{6,7},{7,6},{8,9},{9,8},{10,11... | collective-permute-start | bytes 24584 | tf_op jit(solution)/shard_map/ppermute | solution.py:356

commit v8 on v7

--- a/solution.py
+++ b/solution.py
@@ -144,8 +144,7 @@
         outer_ref[far : far + FAR, :] = jnp.where(even, top, bottom)
 
 
-def tables_kernel(band_ref, kernels_ref, masks_ref, taps_ref, back_ref, feet_ref, pad_ref, *, height):
-    rows_dev = masks_ref.shape[0]
+def taps_kernel(band_ref, kernels_ref, taps_ref, back_ref, pad_ref, *, height, rows_dev):
     span = rows_dev + 2 * MARGIN
     first_row = lax.axis_index("row") * rows_dev - MARGIN
     row_ids = lax.broadcasted_iota(jnp.int32, (BAND, TILE), 0)
@@ -165,6 +164,10 @@
     for slot, tap in enumerate(SIDES):
         start = BAND + TAPS // 2 - tap
         back_ref[slot] = pad_ref[slot, start : start + span, :]
+
+
+def feet_kernel(masks_ref, feet_ref):
+    rows_dev = masks_ref.shape[0]
     flat = jnp.concatenate([masks_ref[row].astype(jnp.float32) for row in range(rows_dev)], axis=0)
     positions = flat.shape[0]
     both = jnp.concatenate([flat, flat], axis=0).T
@@ -391,31 +394,20 @@
 
     half = frames // HALVES
     packed = array(half * (NEAR + FAR), width)
+    taps, back = call(
+        functools.partial(taps_kernel, height=rows_dev * n_row, rows_dev=rows_dev),
+        "taps",
+        [smem, smem],
+        (array(len(SIDES), span, TILE),) * 2,
+        [pltpu.VMEM((len(SIDES), span + 2 * PAD, TILE), jnp.float32)],
+    )(band_kernel, kernels)
     *sent, own = call(halo_kernel, "halo", [vmem], (packed,) * (2 * HALVES) + (array(*observed.shape),))(observed)
     swaps = [
         [pair for i in range(first, n_row - 1, 2) for pair in ((i, i + 1), (i + 1, i))] for first in (0, 1)
     ]
-
-    def swap(inner, outer):
-        inner, outer = inner.astype(jnp.float16), outer.astype(jnp.float16)
-        return inner, lax.ppermute(outer, "row", swaps[1]), lax.ppermute(inner, "row", swaps[0])
-
-    last, *arrived1 = swap(*sent[:2])
-    outer1, inner1 = in_turn(*arrived1)
-    band_kernel, last = lax.optimization_barrier((band_kernel, last))
-    taps, back, feet = call(
-        functools.partial(tables_kernel, height=rows_dev * n_row),
-        "tables",
-        [smem, smem, vmem],
-        (
-            array(len(SIDES), span, TILE),
-            array(len(SIDES), span, TILE),
-            array(n_frame, n_row * share // 2, TILE, dtype=jnp.bfloat16),
-        ),
-        [pltpu.VMEM((len(SIDES), span + 2 * PAD, TILE), jnp.float32)],
-    )(band_kernel, kernels, masks.transpose(1, 2, 0))
-    *sent, taps = lax.optimization_barrier((*sent[2:], taps))
-    _, *arrived2 = swap(*sent)
+    taps, *sent = lax.optimization_barrier((taps, *sent))
+    sent = [rows.astype(jnp.float16) for rows in sent]
+    inner1, outer1, inner2, outer2 = (lax.ppermute(rows, "row", swaps[i % 2]) for i, rows in enumerate(sent))
     buffers = [pltpu.VMEM((half * TOGETHER, span + 2 * PAD, TILE), jnp.float32)] * 3
     estimate, sums = call(
         first_kernel,
@@ -424,7 +416,9 @@
         (array(n_frame, half * positions, TILE, dtype=jnp.bfloat16), array(half * n_frame, TILE)),
         buffers,
     )(taps, back, own, inner1.astype(jnp.float32), outer1.astype(jnp.float32))
-    estimate, outer2, inner2 = in_turn(estimate, *arrived2)
+    estimate, masks = in_turn(estimate, masks.transpose(1, 2, 0))
+    feet = call(feet_kernel, "feet", [vmem], array(n_frame, n_row * share // 2, TILE, dtype=jnp.bfloat16))(masks)
+    feet, outer2, inner2 = in_turn(feet, outer2, inner2)
     side_rows = frames * n_frame + n_row * share // 2
     blocks, sides = call(
         second_kernel,

time: 30.8 us -> 28.9 us (0.938)
  starting transfers between devices: 18.6 us -> 17.3 us
  waiting for transfers between devices: 3.93 us -> 2.63 us
  local copies, waits for them, and re-layouts: 1.1 us -> 1.66 us
    ppermute x9, waiting for transfers between devices: 3.01 us -> 1.52 us  [swapped(): lax.ppermute(part, axis, [(i, i ^ step) for i in range(count)])]
    ppermute x4, starting transfers between devices: 10.3 us -> 9.02 us  [by_halo(): lax.ppermute(rows, 'row', swaps[i % 2])]
    unnamed x8, local copies, waits for them, and re-layouts: 1.05 us -> 1.6 us
    pallas_call x1 -> x2, Pallas kernels: 0.72 us -> 0.79 us  [the longest x1 0.69 us: by_halo(): call(functools.partial(taps_kernel, height=rows_dev * n_row, rows_dev=row...]
  transfers between devices with their start and end apart: 13 -> 13, of which waited for: 4 -> 5; matrix products, arithmetic and copies ran while one was open for 0% -> 0% of each run, Pallas kernels for 12% -> 11%
where the time goes in v8:
time: 28.9 us; the launch traced here: 28.7 us
  starting transfers between devices  17.3 us (60%)
  Pallas kernels  6.16 us (21%)
  waiting for transfers between devices  2.63 us (9%)
  local copies, waits for them, and re-layouts  1.66 us (6%)
  between operations  0.8 us (3%)
    ppermute x4, starting transfers between devices, by_halo(): lax.ppermute(rows, 'row', swaps[i % 2])  9.02 us
    ppermute x9, starting transfers between devices, swapped(): lax.ppermute(part, axis, [(i, i ^ step) for i in range(count)])  8.3 us
    pallas_call x1, Pallas kernels, by_halo(): call(second_kernel, 'restore2', [vmem] * 8, (array(n_frame, frames * posi...  1.62 us
    pallas_call x1, Pallas kernels, by_halo(): call(first_kernel, 'restore1', [vmem] * 5, (array(n_frame, half * positio...  1.61 us
    unnamed x8, local copies, waits for them, and re-layouts  1.6 us
    ppermute x9, waiting for transfers between devices, swapped(): lax.ppermute(part, axis, [(i, i ^ step) for i in range(count)])  1.52 us
    ppermute x4, waiting for transfers between devices, by_halo(): lax.ppermute(rows, 'row', swaps[i % 2])  1.11 us
    pallas_call x1, Pallas kernels, by_halo(): call(functools.partial(temporal_kernel, frames=frames), 'temporal', [vmem...  0.92 us
  transfers between devices with their start and end apart: 13, of which 5 were waited for; matrix products, arithmetic and copies ran while one was open for 0% of the time, Pallas kernels for 11%

profile of v8, /device:TPU:0, one launch (start us, length us, event | category | flops | bytes accessed | tf_op | source)
XLA Modules:
  0.0 28.7 jit_solution(5442869767913852573)
XLA Ops:
  0.6 1.0 %copy-done = f32[4,16,2048]{2,1,0:T(8,128)S(1)} copy-done((f32[4,16,2048]{2,1,0:T(8,128)S(1)}, f32[4,16,2048]{2,1,0:T(8,128)}, u32[]{:S(2)}) %copy-start) | copy-done | bytes 524312
  1.7 0.1 halo.1
  1.8 0.6 %copy-done.2 = f32[8,5]{1,0:T(8,128)S(1)} copy-done((f32[8,5]{1,0:T(8,128)S(1)}, f32[8,5]{1,0:T(8,128)}, u32[]{:S(2)}) %copy-start.2) | copy-done | bytes 184
  2.4 0.7 %taps.1 = (f32[4,48,128]{2,1,0:T(8,128)S(1)}, f32[4,48,128]{2,1,0:T(8,128)S(1)}) custom-call(s32[8]{0:T(128)S(1)} %copy-done.3, f32[8,5]{1,0:T(8,128)S(1)} %copy-done.2), custom_call_target="tpu_custom_call" | custom-call | flops 1000 | bytes 1000 | tf_op jit(solution)/shard_map/taps/pallas_call | solution.py:397
  3.1 0.7 %collective-permute-start.1 = (f16[24,2048]{1,0:T(8,128)(2,1)S(1)}, f16[24,2048]{1,0:T(8,128)(2,1)S(1)}, u32[]{:S(2)}, u32[]{:S(2)}) collective-permute-start(f16[24,2048]{1,0:T(8,128)(2,1)S(1)} %convert_element_type.26), channel_id=1, source_target_pairs={{1,2},{2,1},{5,6},{6,5},{9,10},{10,9},{13,14},{14,13},{17,18},{18,... | collective-permute-start | bytes 294920 | tf_op jit(solution)/shard_map/ppermute | solution.py:410
  3.8 5.9 %collective-permute-start = (f16[24,2048]{1,0:T(8,128)(2,1)S(1)}, f16[24,2048]{1,0:T(8,128)(2,1)S(1)}, u32[]{:S(2)}, u32[]{:S(2)}) collective-permute-start(f16[24,2048]{1,0:T(8,128)(2,1)S(1)} %convert_element_type.24), channel_id=1, source_target_pairs={{0,1},{1,0},{2,3},{3,2},{4,5},{5,4},{6,7},{7,6},{8,9},{9,8},{10,11... | collective-permute-start | bytes 294920 | tf_op jit(solution)/shard_map/ppermute | solution.py:410
  9.7 0.7 %collective-permute-start.2 = (f16[24,2048]{1,0:T(8,128)(2,1)S(1)}, f16[24,2048]{1,0:T(8,128)(2,1)S(1)}, u32[]{:S(2)}, u32[]{:S(2)}) collective-permute-start(f16[24,2048]{1,0:T(8,128)(2,1)S(1)} %convert_element_type.28), channel_id=1, source_target_pairs={{1,2},{2,1},{5,6},{6,5},{9,10},{10,9},{13,14},{14,13},{17,18},{18,... | collective-permute-start | bytes 294920 | tf_op jit(solution)/shard_map/ppermute | solution.py:410
  10.4 1.8 %collective-permute-start.3 = (f16[24,2048]{1,0:T(8,128)(2,1)S(1)}, f16[24,2048]{1,0:T(8,128)(2,1)S(1)}, u32[]{:S(2)}, u32[]{:S(2)}) collective-permute-start(f16[24,2048]{1,0:T(8,128)(2,1)S(1)} %convert_element_type.29), channel_id=1, source_target_pairs={{0,1},{1,0},{2,3},{3,2},{4,5},{5,4},{6,7},{7,6},{8,9},{9,8},{10,11... | collective-permute-start | bytes 294920 | tf_op jit(solution)/shard_map/ppermute | solution.py:410
  12.2 0.0 collective-permute-done.1
  12.2 0.1 collective-permute-done
  12.3 0.0 copy-start.1
  12.3 1.6 %restore1.1 = (bf16[4,128,128]{2,1,0:T(8,128)(2,1)S(1)}, f32[8,128]{1,0:T(8,128)S(1)}) custom-call(f32[4,48,128]{2,1,0:T(8,128)S(1)} %get-tuple-element.44.taps_ref, f32[4,48,128]{2,1,0:T(8,128)S(1)} %get-tuple-element.45.back_ref, f32[4,16,2048]{2,1,0:T(8,128)S(1)} %get-tuple-element.46.own_ref, f32[24,2048]{1,0:T(8,128)S(1)} %convert_element_type.25.inner_ref, ...), custom_call_target="tpu_custom_call" | custom-call | flops 1000 | bytes 1000 | tf_op jit(solution)/shard_map/restore1/pallas_call | solution.py:412
  13.9 0.1 feet.1.feet_ref
  14.1 1.0 %collective-permute-done.3 = f16[24,2048]{1,0:T(8,128)(2,1)S(1)} collective-permute-done((f16[24,2048]{1,0:T(8,128)(2,1)S(1)}, f16[24,2048]{1,0:T(8,128)(2,1)S(1)}, u32[]{:S(2)}, u32[]{:S(2)}) %collective-permute-start.3) | collective-permute-done | bytes 98336 | tf_op jit(solution)/shard_map/ppermute | solution.py:410
  15.1 1.6 %restore2.1 = (bf16[4,256,128]{2,1,0:T(8,128)(2,1)S(1)}, bf16[4,48,128]{2,1,0:T(8,128)(2,1)S(1)}) custom-call(f32[4,48,128]{2,1,0:T(8,128)S(1)} %get-tuple-element.44.taps_ref, f32[4,48,128]{2,1,0:T(8,128)S(1)} %get-tuple-element.45.back_ref, f32[4,16,2048]{2,1,0:T(8,128)S(1)} %get-tuple-element.46.own_ref, f32[24,2048]{1,0:T(8,128)S(1)} %convert_element_type.30.inner_ref, ...), custom_call_target="tpu_custom_call" | custom-call | flops 1000 | bytes 1000 | tf_op jit(solution)/shard_map/restore2/pallas_call | solution.py:423
  16.8 0.1 collective-permute-start.9
  16.8 1.6 %collective-permute-start.8 = (bf16[48,128]{1,0:T(8,128)(2,1)S(1)}, bf16[48,128]{1,0:T(8,128)(2,1)S(1)}, u32[]{:S(2)}, u32[]{:S(2)}) collective-permute-start(bf16[48,128]{1,0:T(8,128)(2,1)S(1)} %get-tuple-element.81), channel_id=1, source_target_pairs={{0,8},{4,12},{8,0},{12,4},{1,9},{5,13},{9,1},{13,5},{2,10},{6,14},... | collective-permute-start | bytes 36872 | tf_op jit(solution)/shard_map/ppermute | solution.py:359
  18.4 0.3 %collective-permute-start.7 = (bf16[48,128]{1,0:T(8,128)(2,1)S(1)}, bf16[48,128]{1,0:T(8,128)(2,1)S(1)}, u32[]{:S(2)}, u32[]{:S(2)}) collective-permute-start(bf16[48,128]{1,0:T(8,128)(2,1)S(1)} %get-tuple-element.82), channel_id=1, source_target_pairs={{0,4},{4,0},{8,12},{12,8},{1,5},{5,1},{9,13},{13,9},{2,6},{6,2},{1... | collective-permute-start | bytes 36872 | tf_op jit(solution)/shard_map/ppermute | solution.py:359
  18.7 1.2 %collective-permute-start.6 = (bf16[256,128]{1,0:T(8,128)(2,1)S(1)}, bf16[256,128]{1,0:T(8,128)(2,1)S(1)}, u32[]{:S(2)}, u32[]{:S(2)}) collective-permute-start(bf16[256,128]{1,0:T(8,128)(2,1)S(1)} %get-tuple-element.76), channel_id=1, source_target_pairs={{0,12},{4,8},{8,4},{12,0},{1,13},{5,9},{9,5},{13,1},{2,14},{6,10},... | collective-permute-start | bytes 196616 | tf_op jit(solution)/shard_map/ppermute | solution.py:359
  19.9 0.8 %collective-permute-start.5 = (bf16[256,128]{1,0:T(8,128)(2,1)S(1)}, bf16[256,128]{1,0:T(8,128)(2,1)S(1)}, u32[]{:S(2)}, u32[]{:S(2)}) collective-permute-start(bf16[256,128]{1,0:T(8,128)(2,1)S(1)} %get-tuple-element.77), channel_id=1, source_target_pairs={{0,8},{4,12},{8,0},{12,4},{1,9},{5,13},{9,1},{13,5},{2,10},{6,14},... | collective-permute-start | bytes 196616 | tf_op jit(solution)/shard_map/ppermute | solution.py:359
  20.6 0.0 collective-permute-done.9.refs_3_
  20.6 0.0 collective-permute-start.4
  20.6 0.0 collective-permute-done.8.refs_2_
  20.7 0.4 %partial.1 = f32[4,16,128]{2,1,0:T(8,128)S(1)} custom-call(bf16[48,128]{1,0:T(8,128)(2,1)S(1)} %get-tuple-element.83.refs_0_, bf16[48,128]{1,0:T(8,128)(2,1)S(1)} %collective-permute-done.7.refs_1_, bf16[48,128]{1,0:T(8,128)(2,1)S(1)} %collective-permute-done.8.refs_2_, bf16[48,128]{1,0:T(8,128)(2,1)S(1)} %collective-permute-done.9.refs_3_), custom_call_target="tpu_custom_call" | custom-call | flops 1000 | bytes 1000 | tf_op jit(solution)/shard_map/partial/pallas_call | solution.py:435
  21.1 2.2 %collective-permute-start.10 = (f32[16,128]{1,0:T(8,128)S(1)}, f32[16,128]{1,0:T(8,128)S(1)}, u32[]{:S(2)}, u32[]{:S(2)}) collective-permute-start(f32[16,128]{1,0:T(8,128)S(1)} %get-tuple-element.87), channel_id=1, source_target_pairs={{0,3},{1,2},{2,1},{3,0},{4,7},{5,6},{6,5},{7,4},{8,11},{9,10},{10,... | collective-permute-start | bytes 24584 | tf_op jit(solution)/shard_map/ppermute | solution.py:359
  23.3 1.0 %collective-permute-start.11 = (f32[16,128]{1,0:T(8,128)S(1)}, f32[16,128]{1,0:T(8,128)S(1)}, u32[]{:S(2)}, u32[]{:S(2)}) collective-permute-start(f32[16,128]{1,0:T(8,128)S(1)} %get-tuple-element.86), channel_id=1, source_target_pairs={{0,2},{1,3},{2,0},{3,1},{4,6},{5,7},{6,4},{7,5},{8,10},{9,11},{10,... | collective-permute-start | bytes 24584 | tf_op jit(solution)/shard_map/ppermute | solution.py:359
  24.3 1.2 %collective-permute-start.12 = (f32[16,128]{1,0:T(8,128)S(1)}, f32[16,128]{1,0:T(8,128)S(1)}, u32[]{:S(2)}, u32[]{:S(2)}) collective-permute-start(f32[16,128]{1,0:T(8,128)S(1)} %get-tuple-element.85), channel_id=1, source_target_pairs={{0,1},{1,0},{2,3},{3,2},{4,5},{5,4},{6,7},{7,6},{8,9},{9,8},{10,11... | collective-permute-start | bytes 24584 | tf_op jit(solution)/shard_map/ppermute | solution.py:359
  25.6 0.9 %temporal.1 = bf16[16,16,512]{2,1,0:T(8,128)(2,1)} custom-call(bf16[256,128]{1,0:T(8,128)(2,1)S(1)} %get-tuple-element.79.refs_0_, bf16[256,128]{1,0:T(8,128)(2,1)S(1)} %collective-permute-done.4.refs_1_, bf16[256,128]{1,0:T(8,128)(2,1)S(1)} %collective-permute-done.5.refs_2_, bf16[256,128]{1,0:T(8,128)(2,1)S(1)} %collective-permute-done.6.refs_3_), custom_call_target="tpu_custom_call" | custom-call | flops 1000 | bytes 1000 | tf_op jit(solution)/shard_map/temporal/pallas_call | solution.py:446
  26.5 0.1 collective-permute-done.10.refs_0_
  26.6 1.3 %collective-permute-done.11.refs_1_ = f32[16,128]{1,0:T(8,128)S(1)} collective-permute-done((f32[16,128]{1,0:T(8,128)S(1)}, f32[16,128]{1,0:T(8,128)S(1)}, u32[]{:S(2)}, u32[]{:S(2)}) %collective-permute-start.11) | collective-permute-done | bytes 8224 | tf_op jit(solution)/shard_map/ppermute | solution.py:359
  27.9 0.1 collective-permute-done.12.refs_2_
  28.0 0.7 %means.1 = f32[16,16]{1,0:T(8,128)} custom-call(f32[16,128]{1,0:T(8,128)S(1)} %collective-permute-done.10.refs_0_, f32[16,128]{1,0:T(8,128)S(1)} %collective-permute-done.11.refs_1_, f32[16,128]{1,0:T(8,128)S(1)} %collective-permute-done.12.refs_2_, f32[16,128]{1,0:T(8,128)S(1)} %get-tuple-element.75.refs_3_), custom_call_target="tpu_custom_call" | custom-call | flops 1000 | bytes 1000 | tf_op jit(solution)/shard_map/means/pallas_call | solution.py:454
  (21 shorter events, 0.2 us)
Async XLA Ops:
  0.6 1.0 %copy-start = (f32[4,16,2048]{2,1,0:T(8,128)S(1)}, f32[4,16,2048]{2,1,0:T(8,128)}, u32[]{:S(2)}) copy-start(f32[4,16,2048]{2,1,0:T(8,128)} %observed_ref.1) | copy-start | bytes 1572868
  1.7 0.7 %copy-start.2 = (f32[8,5]{1,0:T(8,128)S(1)}, f32[8,5]{1,0:T(8,128)}, u32[]{:S(2)}) copy-start(f32[8,5]{1,0:T(8,128)} %kernels_ref.1) | copy-start | bytes 484
  1.7 0.7 %copy-start.3 = (s32[8]{0:T(128)S(1)}, s32[8]{0:T(128)}, u32[]{:S(2)}) copy-start(s32[8]{0:T(128)} %band_ref.1) | copy-start | bytes 100
  3.1 9.1 %collective-permute-start.1 = (f16[24,2048]{1,0:T(8,128)(2,1)S(1)}, f16[24,2048]{1,0:T(8,128)(2,1)S(1)}, u32[]{:S(2)}, u32[]{:S(2)}) collective-permute-start(f16[24,2048]{1,0:T(8,128)(2,1)S(1)} %convert_element_type.26), channel_id=1, source_target_pairs={{1,2},{2,1},{5,6},{6,5},{9,10},{10,9},{13,14},{14,13},{17,18},{18,... | collective-permute-start | bytes 294920 | tf_op jit(solution)/shard_map/ppermute | solution.py:410
  3.8 8.5 %collective-permute-start = (f16[24,2048]{1,0:T(8,128)(2,1)S(1)}, f16[24,2048]{1,0:T(8,128)(2,1)S(1)}, u32[]{:S(2)}, u32[]{:S(2)}) collective-permute-start(f16[24,2048]{1,0:T(8,128)(2,1)S(1)} %convert_element_type.24), channel_id=1, source_target_pairs={{0,1},{1,0},{2,3},{3,2},{4,5},{5,4},{6,7},{7,6},{8,9},{9,8},{10,11... | collective-permute-start | bytes 294920 | tf_op jit(solution)/shard_map/ppermute | solution.py:410
  9.7 4.4 %collective-permute-start.2 = (f16[24,2048]{1,0:T(8,128)(2,1)S(1)}, f16[24,2048]{1,0:T(8,128)(2,1)S(1)}, u32[]{:S(2)}, u32[]{:S(2)}) collective-permute-start(f16[24,2048]{1,0:T(8,128)(2,1)S(1)} %convert_element_type.28), channel_id=1, source_target_pairs={{1,2},{2,1},{5,6},{6,5},{9,10},{10,9},{13,14},{14,13},{17,18},{18,... | collective-permute-start | bytes 294920 | tf_op jit(solution)/shard_map/ppermute | solution.py:410
  10.4 4.7 %collective-permute-start.3 = (f16[24,2048]{1,0:T(8,128)(2,1)S(1)}, f16[24,2048]{1,0:T(8,128)(2,1)S(1)}, u32[]{:S(2)}, u32[]{:S(2)}) collective-permute-start(f16[24,2048]{1,0:T(8,128)(2,1)S(1)} %convert_element_type.29), channel_id=1, source_target_pairs={{0,1},{1,0},{2,3},{3,2},{4,5},{5,4},{6,7},{7,6},{8,9},{9,8},{10,11... | collective-permute-start | bytes 294920 | tf_op jit(solution)/shard_map/ppermute | solution.py:410
  12.3 1.6 %copy-start.1 = (s32[256,16,4]{0,2,1:T(4,128)S(1)}, s32[256,16,4]{0,2,1:T(4,128)}, u32[]{:S(2)}) copy-start(s32[256,16,4]{0,2,1:T(4,128)} %param.7) | copy-start | bytes 196612
  16.8 3.9 %collective-permute-start.9 = (bf16[48,128]{1,0:T(8,128)(2,1)S(1)}, bf16[48,128]{1,0:T(8,128)(2,1)S(1)}, u32[]{:S(2)}, u32[]{:S(2)}) collective-permute-start(bf16[48,128]{1,0:T(8,128)(2,1)S(1)} %get-tuple-element.80), channel_id=1, source_target_pairs={{0,12},{4,8},{8,4},{12,0},{1,13},{5,9},{9,5},{13,1},{2,14},{6,10},... | collective-permute-start | bytes 36872 | tf_op jit(solution)/shard_map/ppermute | solution.py:359
  16.8 3.8 %collective-permute-start.8 = (bf16[48,128]{1,0:T(8,128)(2,1)S(1)}, bf16[48,128]{1,0:T(8,128)(2,1)S(1)}, u32[]{:S(2)}, u32[]{:S(2)}) collective-permute-start(bf16[48,128]{1,0:T(8,128)(2,1)S(1)} %get-tuple-element.81), channel_id=1, source_target_pairs={{0,8},{4,12},{8,0},{12,4},{1,9},{5,13},{9,1},{13,5},{2,10},{6,14},... | collective-permute-start | bytes 36872 | tf_op jit(solution)/shard_map/ppermute | solution.py:359
  18.4 2.3 %collective-permute-start.7 = (bf16[48,128]{1,0:T(8,128)(2,1)S(1)}, bf16[48,128]{1,0:T(8,128)(2,1)S(1)}, u32[]{:S(2)}, u32[]{:S(2)}) collective-permute-start(bf16[48,128]{1,0:T(8,128)(2,1)S(1)} %get-tuple-element.82), channel_id=1, source_target_pairs={{0,4},{4,0},{8,12},{12,8},{1,5},{5,1},{9,13},{13,9},{2,6},{6,2},{1... | collective-permute-start | bytes 36872 | tf_op jit(solution)/shard_map/ppermute | solution.py:359
  18.7 5.6 %collective-permute-start.6 = (bf16[256,128]{1,0:T(8,128)(2,1)S(1)}, bf16[256,128]{1,0:T(8,128)(2,1)S(1)}, u32[]{:S(2)}, u32[]{:S(2)}) collective-permute-start(bf16[256,128]{1,0:T(8,128)(2,1)S(1)} %get-tuple-element.76), channel_id=1, source_target_pairs={{0,12},{4,8},{8,4},{12,0},{1,13},{5,9},{9,5},{13,1},{2,14},{6,10},... | collective-permute-start | bytes 196616 | tf_op jit(solution)/shard_map/ppermute | solution.py:359
  19.9 5.7 %collective-permute-start.5 = (bf16[256,128]{1,0:T(8,128)(2,1)S(1)}, bf16[256,128]{1,0:T(8,128)(2,1)S(1)}, u32[]{:S(2)}, u32[]{:S(2)}) collective-permute-start(bf16[256,128]{1,0:T(8,128)(2,1)S(1)} %get-tuple-element.77), channel_id=1, source_target_pairs={{0,8},{4,12},{8,0},{12,4},{1,9},{5,13},{9,1},{13,5},{2,10},{6,14},... | collective-permute-start | bytes 196616 | tf_op jit(solution)/shard_map/ppermute | solution.py:359
  20.6 4.9 %collective-permute-start.4 = (bf16[256,128]{1,0:T(8,128)(2,1)S(1)}, bf16[256,128]{1,0:T(8,128)(2,1)S(1)}, u32[]{:S(2)}, u32[]{:S(2)}) collective-permute-start(bf16[256,128]{1,0:T(8,128)(2,1)S(1)} %get-tuple-element.78), channel_id=1, source_target_pairs={{0,4},{4,0},{8,12},{12,8},{1,5},{5,1},{9,13},{13,9},{2,6},{6,2},{1... | collective-permute-start | bytes 196616 | tf_op jit(solution)/shard_map/ppermute | solution.py:359
  21.1 5.5 %collective-permute-start.10 = (f32[16,128]{1,0:T(8,128)S(1)}, f32[16,128]{1,0:T(8,128)S(1)}, u32[]{:S(2)}, u32[]{:S(2)}) collective-permute-start(f32[16,128]{1,0:T(8,128)S(1)} %get-tuple-element.87), channel_id=1, source_target_pairs={{0,3},{1,2},{2,1},{3,0},{4,7},{5,6},{6,5},{7,4},{8,11},{9,10},{10,... | collective-permute-start | bytes 24584 | tf_op jit(solution)/shard_map/ppermute | solution.py:359
  23.3 4.5 %collective-permute-start.11 = (f32[16,128]{1,0:T(8,128)S(1)}, f32[16,128]{1,0:T(8,128)S(1)}, u32[]{:S(2)}, u32[]{:S(2)}) collective-permute-start(f32[16,128]{1,0:T(8,128)S(1)} %get-tuple-element.86), channel_id=1, source_target_pairs={{0,2},{1,3},{2,0},{3,1},{4,6},{5,7},{6,4},{7,5},{8,10},{9,11},{10,... | collective-permute-start | bytes 24584 | tf_op jit(solution)/shard_map/ppermute | solution.py:359
  24.3 3.7 %collective-permute-start.12 = (f32[16,128]{1,0:T(8,128)S(1)}, f32[16,128]{1,0:T(8,128)S(1)}, u32[]{:S(2)}, u32[]{:S(2)}) collective-permute-start(f32[16,128]{1,0:T(8,128)S(1)} %get-tuple-element.85), channel_id=1, source_target_pairs={{0,1},{1,0},{2,3},{3,2},{4,5},{5,4},{6,7},{7,6},{8,9},{9,8},{10,11... | collective-permute-start | bytes 24584 | tf_op jit(solution)/shard_map/ppermute | solution.py:359

commit v9 on v6

--- a/solution.py
+++ b/solution.py
@@ -125,27 +125,22 @@
     return (spikes, traces)
 
 
-def low_first():
-    return (lax.axis_index("row") + lax.axis_index("frame")) % 2 == 0
-
-
-def halo_kernel(observed_ref, first_ref, second_ref, own_ref):
-    low = low_first()
+def halo_kernel(observed_ref, inner_ref, outer_ref, own_ref):
+    even = lax.axis_index("row") % 2 == 0
     frames = observed_ref.shape[0]
     own_ref[...] = observed_ref[...]
     for frame in range(frames):
         near = frame * NEAR
         far = frames * NEAR + frame * FAR
         bottom, top = observed_ref[frame, -NEAR:, :], observed_ref[frame, :NEAR, :]
-        first_ref[near : near + NEAR, :] = jnp.where(low, bottom, top)
-        second_ref[near : near + NEAR, :] = jnp.where(low, top, bottom)
+        inner_ref[near : near + NEAR, :] = jnp.where(even, bottom, top)
+        outer_ref[near : near + NEAR, :] = jnp.where(even, top, bottom)
         bottom, top = observed_ref[frame, -NEAR - FAR : -NEAR, :], observed_ref[frame, NEAR : NEAR + FAR, :]
-        first_ref[far : far + FAR, :] = jnp.where(low, bottom, top)
-        second_ref[far : far + FAR, :] = jnp.where(low, top, bottom)
-
-
-def tables_kernel(band_ref, kernels_ref, masks_ref, taps_ref, back_ref, feet_ref, pad_ref, *, height):
-    rows_dev = masks_ref.shape[0]
+        inner_ref[far : far + FAR, :] = jnp.where(even, bottom, top)
+        outer_ref[far : far + FAR, :] = jnp.where(even, top, bottom)
+
+
+def taps_kernel(band_ref, kernels_ref, taps_ref, back_ref, pad_ref, *, height, rows_dev):
     span = rows_dev + 2 * MARGIN
     first_row = lax.axis_index("row") * rows_dev - MARGIN
     row_ids = lax.broadcasted_iota(jnp.int32, (BAND, TILE), 0)
@@ -165,19 +160,36 @@
     for slot, tap in enumerate(SIDES):
         start = BAND + TAPS // 2 - tap
         back_ref[slot] = pad_ref[slot, start : start + span, :]
-    flat = jnp.concatenate([masks_ref[row].astype(jnp.float32) for row in range(rows_dev)], axis=0)
+
+
+def feet_kernel(masks_ref, feet_ref, *, n_frame, n_row):
+    flat = jnp.concatenate([masks_ref[row].astype(jnp.float32) for row in range(masks_ref.shape[0])], axis=0)
     positions = flat.shape[0]
     both = jnp.concatenate([flat, flat], axis=0).T
-    half = feet_ref.shape[1]
-    left = lax.broadcasted_iota(jnp.int32, (half, TILE), 1) < positions
-    for block in range(feet_ref.shape[0]):
-        start = 2 * block * half
-        halves = jnp.where(left, both[start : start + half], both[start + half : start + 2 * half])
-        feet_ref[block] = halves.astype(jnp.bfloat16)
+    share = both.shape[0] // (n_frame * n_row)
+    left = lax.broadcasted_iota(jnp.int32, (share, TILE), 1) < positions
+    half = n_frame * n_row // 2
+    starts = [(block * n_row + row) * share for row in range(n_row) for block in range(n_frame)]
+    for place in range(half):
+        first, second = starts[place], starts[place + half]
+        halves = jnp.where(left, both[first : first + share], both[second : second + share])
+        feet_ref[place * share : (place + 1) * share, :] = halves.astype(jnp.bfloat16)
+
+
+def gather_kernel(*refs):
+    pieces, feet_ref = refs[:-1], refs[-1]
+    place = lax.axis_index("frame")
+    half = feet_ref.shape[0] // 2
+    left = lax.broadcasted_iota(jnp.int32, (half, TILE), 1) < TILE // 2
+    for step, piece in enumerate(pieces):
+        columns = pl.ds(pl.multiple_of((place ^ step) * TILE, TILE), TILE)
+        feet = piece[...].astype(jnp.float32)
+        feet_ref[:half, columns] = jnp.where(left, feet, 0.0).astype(jnp.bfloat16)
+        feet_ref[half:, columns] = jnp.where(left, 0.0, feet).astype(jnp.bfloat16)
 
 
 def restore_kernel(
-    taps_ref, back_ref, feet_ref, own_ref, first_ref, second_ref, out_ref, side_ref, image_ref, current_ref, quotient_ref
+    taps_ref, back_ref, feet_ref, own_ref, inner_ref, outer_ref, out_ref, sums_ref, image_ref, current_ref, quotient_ref
 ):
     n_frame = out_ref.shape[0]
     frames, rows_dev, width = own_ref.shape
@@ -185,8 +197,8 @@
     positions = rows_dev * tiles_dev
     for ref in (image_ref, current_ref, quotient_ref):
         ref[...] = jnp.ones_like(ref)
-    low = low_first()
     row = lax.axis_index("row")
+    even = row % 2 == 0
     above = jnp.where(row == 0, 1.0, 0.0)
     below = jnp.where(row == lax.axis_size("row") - 1, 1.0, 0.0)
 
@@ -195,12 +207,12 @@
         for frame in range(frames):
             near, far = frame * NEAR, frames * NEAR + frame * FAR
             start, stop = PAD + MARGIN, PAD + MARGIN + rows_dev
-            first, second = first_ref[near : near + NEAR, columns], second_ref[near : near + NEAR, columns]
-            image_ref[frame, start - NEAR : start, :] = jnp.where(low, second, first) + above
-            image_ref[frame, stop : stop + NEAR, :] = jnp.where(low, first, second) + below
-            first, second = first_ref[far : far + FAR, columns], second_ref[far : far + FAR, columns]
-            image_ref[frame, start - NEAR - FAR : start - NEAR, :] = jnp.where(low, second, first) + above
-            image_ref[frame, stop + NEAR : stop + NEAR + FAR, :] = jnp.where(low, first, second) + below
+            inner, outer = inner_ref[near : near + NEAR, columns], outer_ref[near : near + NEAR, columns]
+            image_ref[frame, start - NEAR : start, :] = jnp.where(even, outer, inner) + above
+            image_ref[frame, stop : stop + NEAR, :] = jnp.where(even, inner, outer) + below
+            inner, outer = inner_ref[far : far + FAR, columns], outer_ref[far : far + FAR, columns]
+            image_ref[frame, start - NEAR - FAR : start - NEAR, :] = jnp.where(even, outer, inner) + above
+            image_ref[frame, stop + NEAR : stop + NEAR + FAR, :] = jnp.where(even, inner, outer) + below
             image_ref[frame, start:stop, :] = own_ref[frame, :, columns]
         source_ref = image_ref
         for (first, last), (back_first, back_last) in STEPS:
@@ -242,16 +254,32 @@
         gathered = gathered + jnp.dot(jnp.concatenate(pieces, axis=0), picked, preferred_element_type=jnp.float32)
     lanes = lax.broadcasted_iota(jnp.int32, (rows_dev, TILE), 1)
     here = lanes % positions // tiles_dev == lax.broadcasted_iota(jnp.int32, (rows_dev, TILE), 0)
-    sums = []
-    for place in range(frames * n_frame):
-        part = jnp.where(here, gathered[place * rows_dev : (place + 1) * rows_dev], 0.0)
-        sums.append(jnp.sum(part, axis=0, keepdims=True))
-    sums = jnp.concatenate(sums, axis=0)
-    high = sums.astype(jnp.bfloat16).astype(jnp.float32)
-    split = jnp.where(lax.broadcasted_iota(jnp.int32, sums.shape, 1) < positions, high, sums - high).astype(jnp.bfloat16)
-    for block in range(n_frame):
-        side_ref[block, : split.shape[0], :] = split
-        side_ref[block, split.shape[0] :, :] = feet_ref[block]
+    series = []
+    for frame in range(frames):
+        sums = []
+        for block in range(n_frame):
+            start = (frame * n_frame + block) * rows_dev
+            sums.append(jnp.sum(jnp.where(here, gathered[start : start + rows_dev], 0.0), axis=0, keepdims=True))
+        series.append(jnp.concatenate(sums, axis=1))
+    series = jnp.concatenate(series, axis=0)
+    parts = []
+    for _ in range(3):
+        part = series.astype(jnp.bfloat16).astype(jnp.float32)
+        series = series - part
+        parts.append(part)
+    parts.append(jnp.ones((4, n_frame * TILE), jnp.float32))
+    totals = lax.dot_general(
+        jnp.concatenate(parts, axis=0).astype(jnp.bfloat16),
+        feet_ref[...],
+        (((1,), (1,)), ((), ())),
+        preferred_element_type=jnp.float32,
+    )
+    sums = totals[:frames] + totals[frames : 2 * frames] + totals[2 * frames : 3 * frames]
+    sums = jnp.concatenate([sums, totals[3 * frames :]], axis=0)
+    share = sums.shape[1] // sums_ref.shape[0]
+    sums_ref[...] = jnp.zeros_like(sums_ref)
+    for row in range(sums_ref.shape[0]):
+        sums_ref[row, :, :share] = sums[:, row * share : (row + 1) * share]
 
 
 def deconvolved(series):
@@ -277,38 +305,6 @@
     return result
 
 
-def partial_kernel(*refs, positions):
-    pieces, (out_ref, sums_ref, feet_ref) = refs[:-3], refs[-3:]
-    n_frame = len(pieces)
-    place = lax.axis_index("frame")
-    rows = sums_ref.shape[0] // n_frame
-    half = feet_ref.shape[1]
-    for step, piece in enumerate(pieces):
-        sums_ref[pl.ds(pl.multiple_of((place ^ step) * rows, rows), rows), :] = piece[:rows, :].astype(jnp.float32)
-        feet_ref[place ^ step] = piece[rows:, :].astype(jnp.float32)
-    series = [sums_ref[t * n_frame : (t + 1) * n_frame, :] for t in range(rows)]
-    for t, sums in enumerate(deconvolved(series)):
-        sums_ref[t * n_frame : (t + 1) * n_frame, :] = sums + pltpu.roll(sums, TILE // 2, 1)
-    left = lax.broadcasted_iota(jnp.int32, (half, TILE), 1) < positions
-    weights, sums = [], []
-    extra = jnp.where(lax.broadcasted_iota(jnp.int32, (8, TILE), 0) == 0, 1.0, 0.0)
-    for block in range(n_frame):
-        feet = feet_ref[block]
-        weights.append(jnp.concatenate([jnp.where(left, feet, 0.0), jnp.where(left, 0.0, feet)], axis=0))
-        sums.append(jnp.concatenate([sums_ref[pl.ds(block, rows, stride=n_frame), :], extra], axis=0))
-    totals = lax.dot_general(
-        jnp.concatenate(weights, axis=1),
-        jnp.concatenate(sums, axis=1),
-        (((1,), (1,)), ((), ())),
-        precision=lax.Precision.HIGHEST,
-        preferred_element_type=jnp.float32,
-    )
-    share = out_ref.shape[1]
-    out_ref[...] = jnp.zeros_like(out_ref)
-    for row in range(out_ref.shape[0]):
-        out_ref[row, :, : rows + 8] = totals[row * share : (row + 1) * share]
-
-
 def temporal_kernel(*refs, frames):
     pieces, (spikes_ref, in_ref) = refs[:-2], refs[-2:]
     place = lax.axis_index("frame")
@@ -325,13 +321,23 @@
             spikes_ref[t, :, tile * TILE : (tile + 1) * TILE] = spikes.astype(spikes_ref.dtype)
 
 
-def means_kernel(*refs):
-    pieces, traces_ref = refs[:-1], refs[-1]
-    frames = traces_ref.shape[1]
-    total = pieces[0][...]
-    for piece in pieces[1:]:
+def add_kernel(*refs):
+    total = refs[0][...]
+    for piece in refs[1:-1]:
         total = total + piece[...]
-    traces_ref[...] = total[:, :frames] / (TILE * total[:, frames : frames + 1])
+    refs[-1][...] = total
+
+
+def means_kernel(*refs, frames):
+    pieces, (traces_ref, sums_ref) = refs[:-2], refs[-2:]
+    place = lax.axis_index("frame")
+    for step, piece in enumerate(pieces):
+        sums_ref[place ^ step] = piece[...]
+    share, total = traces_ref.shape
+    series = deconvolved([sums_ref[t // frames, t % frames : t % frames + 1, :] for t in range(total)])
+    means = jnp.concatenate(series, axis=0) / (TILE * sums_ref[0, frames : frames + 1, :])
+    means = pltpu.roll(means, lax.rem(TILE - place * share, TILE), 1)
+    traces_ref[...] = means.T[:share]
 
 
 def swapped(parts, axis):
@@ -341,6 +347,18 @@
         part = lax.dynamic_index_in_dim(parts, place ^ step, 0, keepdims=False, allow_negative_indices=False)
         arrived.append(lax.ppermute(part, axis, [(i, i ^ step) for i in range(count)]))
     return arrived
+
+
+def spread_out(part, axis):
+    count = lax.axis_size(axis)
+    return [part] + [lax.ppermute(part, axis, [(i, i ^ step) for i in range(count)]) for step in range(1, count)]
+
+
+def in_turn(*arrays):
+    done = []
+    for array in arrays:
+        done = list(lax.optimization_barrier((*done, array)))
+    return done
 
 
 def by_halo(observed, kernels, band_kernel, masks):
@@ -352,7 +370,7 @@
     span = rows_dev + 2 * MARGIN
     smem, vmem = pl.BlockSpec(memory_space=pltpu.SMEM), pl.BlockSpec(memory_space=pltpu.VMEM)
 
-    def call(kernel, name, in_specs, out_shape, scratch=(), cost=1000000):
+    def call(kernel, name, in_specs, out_shape, scratch=(), cost=1000):
         many = isinstance(out_shape, tuple)
         return pl.pallas_call(
             kernel,
@@ -369,51 +387,41 @@
         return jax.ShapeDtypeStruct(shape, dtype)
 
     packed = array(frames * (NEAR + FAR), width)
-    *sent, own = call(halo_kernel, "halo", [vmem], (packed, packed, array(*observed.shape)))(observed)
-    pairs = [[(i, i + 1) for i in range(first, n_row - 1, 2)] for first in (0, 1)]
+    inner, outer, own = call(halo_kernel, "halo", [vmem], (packed, packed, array(*observed.shape)))(observed)
     swaps = [
-        [(f * n_row + i, f * n_row + j) for f in range(n_frame) for pair in pairs[(f + turn) % 2] for i, j in (pair, pair[::-1])]
-        for turn in range(2)
+        [pair for i in range(first, n_row - 1, 2) for pair in ((i, i + 1), (i + 1, i))] for first in (0, 1)
     ]
-    arrived = [
-        lax.ppermute(rows.astype(jnp.float16), ("frame", "row"), swap).astype(jnp.float32)
-        for rows, swap in zip(sent, swaps)
-    ]
-    taps, back, feet = call(
-        functools.partial(tables_kernel, height=rows_dev * n_row),
-        "tables",
-        [smem, smem, vmem],
-        (
-            array(len(SIDES), span, TILE),
-            array(len(SIDES), span, TILE),
-            array(n_frame, n_row * share // 2, TILE, dtype=jnp.bfloat16),
-        ),
+    inner, outer = (lax.ppermute(rows.astype(jnp.float16), "row", swap) for rows, swap in zip((inner, outer), swaps))
+    outer, inner = in_turn(outer, inner)
+    taps, back = call(
+        functools.partial(taps_kernel, height=rows_dev * n_row, rows_dev=rows_dev),
+        "taps",
+        [smem, smem],
+        (array(len(SIDES), span, TILE),) * 2,
         [pltpu.VMEM((len(SIDES), span + 2 * PAD, TILE), jnp.float32)],
-    )(band_kernel, kernels, masks.transpose(1, 2, 0))
-    side_rows = frames * n_frame + n_row * share // 2
-    blocks, sides = call(
+    )(band_kernel, kernels)
+    feet = call(
+        functools.partial(feet_kernel, n_frame=n_frame, n_row=n_row),
+        "feet",
+        [vmem],
+        array(components // 2, TILE, dtype=jnp.bfloat16),
+    )(masks.transpose(1, 2, 0))
+    feet = call(
+        gather_kernel, "gather", [vmem] * n_frame, array(components, n_frame * TILE, dtype=jnp.bfloat16)
+    )(*spread_out(feet, "frame"))
+    blocks, sums = call(
         restore_kernel,
         "restore",
         [vmem] * 6,
         (
             array(n_frame, frames * positions, TILE, dtype=jnp.bfloat16),
-            array(n_frame, side_rows, TILE, dtype=jnp.bfloat16),
+            array(n_row, 2 * frames, TILE),
         ),
         [pltpu.VMEM((frames, span + 2 * PAD, TILE), jnp.float32)] * 3,
-    )(taps, back, feet, own, *arrived)
-    sides = swapped(sides, "frame")
+    )(taps, back, feet, own, inner.astype(jnp.float32), outer.astype(jnp.float32))
+    shares = swapped(sums, "row")
     pieces = swapped(blocks, "frame")
-    partial = call(
-        functools.partial(partial_kernel, positions=positions),
-        "partial",
-        [vmem] * n_frame,
-        array(n_row, share, TILE),
-        [
-            pltpu.VMEM((n_frame * frames * n_frame, TILE), jnp.float32),
-            pltpu.VMEM((n_frame, n_row * share // 2, TILE), jnp.float32),
-        ],
-    )(*sides)
-    shares = swapped(partial, "row")
+    sums = call(add_kernel, "add", [vmem] * n_row, array(2 * frames, TILE))(*in_turn(*shares[::-1]))
     spikes = call(
         functools.partial(temporal_kernel, frames=frames),
         "temporal",
@@ -421,8 +429,14 @@
         array(n_frame * frames, rows_dev, tiles_dev * TILE, dtype=jnp.bfloat16),
         [pltpu.VMEM((n_frame, frames * positions, TILE), jnp.bfloat16)],
     )(*pieces)
-    spikes, *shares = lax.optimization_barrier((spikes, *shares))
-    traces = call(means_kernel, "means", [vmem] * n_row, array(share, n_frame * frames))(*shares)
+    spikes, *sums = lax.optimization_barrier((spikes, *spread_out(sums, "frame")))
+    traces = call(
+        functools.partial(means_kernel, frames=frames),
+        "means",
+        [vmem] * n_frame,
+        array(share, n_frame * frames),
+        [pltpu.VMEM((n_frame, 2 * frames, TILE), jnp.float32)],
+    )(*sums)
     return (spikes, traces)
 
 

time: 31.7 us -> 33.1 us (1.044)
  waiting for transfers between devices: 6.09 us -> 9.93 us
  starting transfers between devices: 16.5 us -> 15 us
  local copies, waits for them, and re-layouts: 1.78 us -> 1.1 us
    ppermute x9 -> x6, starting transfers between devices: 10.9 us -> 4.59 us  [swapped(): lax.ppermute(part, axis, [(i, i ^ step) for i in range(count)])]
    ppermute x2 -> x8, starting transfers between devices: 5.61 us -> 10.4 us  [the longest x2 6.57 us: by_halo(): lax.ppermute(rows.astype(jnp.float16), 'row', swap)]
    ppermute x2 -> x8, waiting for transfers between devices: 1.48 us -> 3.58 us  [the longest x6 3.57 us: spread_out(): lax.ppermute(part, axis, [(i, i ^ step) for i in range(count)])]
    ppermute x9 -> x6, waiting for transfers between devices: 4.61 us -> 6.35 us  [swapped(): lax.ppermute(part, axis, [(i, i ^ step) for i in range(count)])]
    unnamed x8, local copies, waits for them, and re-layouts: 1.72 us -> 1.05 us
    pallas_call x3 -> x5, Pallas kernels: 1.79 us -> 1.68 us  [the longest x1 0.83 us: by_halo(): call(functools.partial(means_kernel, frames=frames), 'means', [vmem] * n_...]
  transfers between devices with their start and end apart: 11 -> 14, of which waited for: 4 -> 7; matrix products, arithmetic and copies ran while one was open for 0% -> 0% of each run, Pallas kernels for 6% -> 5%
where the time goes in v9:
time: 33.1 us; the launch traced here: 32.9 us
  starting transfers between devices  15 us (45%)
  waiting for transfers between devices  9.93 us (30%)
  Pallas kernels  6.06 us (18%)
  local copies, waits for them, and re-layouts  1.1 us (3%)
  between operations  0.77 us (2%)
    ppermute x2, starting transfers between devices, by_halo(): lax.ppermute(rows.astype(jnp.float16), 'row', swap)  6.57 us
    ppermute x6, waiting for transfers between devices, swapped(): lax.ppermute(part, axis, [(i, i ^ step) for i in range(count)])  6.35 us
    ppermute x6, starting transfers between devices, swapped(): lax.ppermute(part, axis, [(i, i ^ step) for i in range(count)])  4.59 us
    ppermute x6, starting transfers between devices, spread_out(): lax.ppermute(part, axis, [(i, i ^ step) for i in range(count)])  3.79 us
    ppermute x6, waiting for transfers between devices, spread_out(): lax.ppermute(part, axis, [(i, i ^ step) for i in range(count)])  3.57 us
    pallas_call x1, Pallas kernels, by_halo(): call(restore_kernel, 'restore', [vmem] * 6, (array(n_frame, frames * posi...  3.33 us
    unnamed x8, local copies, waits for them, and re-layouts  1.05 us
    pallas_call x1, Pallas kernels, by_halo(): call(functools.partial(temporal_kernel, frames=frames), 'temporal', [vmem...  0.92 us
  transfers between devices with their start and end apart: 14, of which 7 were waited for; matrix products, arithmetic and copies ran while one was open for 0% of the time, Pallas kernels for 5%

profile of v9, /device:TPU:0, one launch (start us, length us, event | category | flops | bytes accessed | tf_op | source)
XLA Modules:
  0.0 32.9 jit_solution(12978781879971476643)
XLA Ops:
  0.6 1.0 %copy-done = f32[4,16,2048]{2,1,0:T(8,128)S(1)} copy-done((f32[4,16,2048]{2,1,0:T(8,128)S(1)}, f32[4,16,2048]{2,1,0:T(8,128)}, u32[]{:S(2)}) %copy-start) | copy-done | bytes 524312
  1.7 0.1 halo.1
  1.8 0.7 %collective-permute-start.3 = (f16[48,2048]{1,0:T(8,128)(2,1)S(1)}, f16[48,2048]{1,0:T(8,128)(2,1)S(1)}, u32[]{:S(2)}, u32[]{:S(2)}) collective-permute-start(f16[48,2048]{1,0:T(8,128)(2,1)S(1)} %convert_element_type.12), channel_id=1, source_target_pairs={{1,2},{2,1},{5,6},{6,5},{9,10},{10,9},{13,14},{14,13},{17,18},{18,... | collective-permute-start | bytes 589832 | tf_op jit(solution)/shard_map/ppermute | solution.py:394
  2.5 0.0 copy-start.1
  2.6 5.9 %collective-permute-start.4 = (f16[48,2048]{1,0:T(8,128)(2,1)S(1)}, f16[48,2048]{1,0:T(8,128)(2,1)S(1)}, u32[]{:S(2)}, u32[]{:S(2)}) collective-permute-start(f16[48,2048]{1,0:T(8,128)(2,1)S(1)} %convert_element_type.13), channel_id=1, source_target_pairs={{0,1},{1,0},{2,3},{3,2},{4,5},{5,4},{6,7},{7,6},{8,9},{9,8},{10,11... | collective-permute-start | bytes 589832 | tf_op jit(solution)/shard_map/ppermute | solution.py:394
  8.5 0.1 feet.1.refs_0_
  8.6 0.1 collective-permute-start
  8.6 1.6 %collective-permute-start.1 = (bf16[128,128]{1,0:T(8,128)(2,1)S(1)}, bf16[128,128]{1,0:T(8,128)(2,1)S(1)}, u32[]{:S(2)}, u32[]{:S(2)}) collective-permute-start(bf16[128,128]{1,0:T(8,128)(2,1)S(1)} %feet.1.refs_0_), channel_id=1, source_target_pairs={{0,8},{4,12},{8,0},{12,4},{1,9},{5,13},{9,1},{13,5},{2,10},{6,14},... | collective-permute-start | bytes 98312 | tf_op jit(solution)/shard_map/ppermute | solution.py:354
  10.2 0.3 collective-permute-start.2
  10.5 0.7 %taps.1 = (f32[4,48,128]{2,1,0:T(8,128)S(1)}, f32[4,48,128]{2,1,0:T(8,128)S(1)}) custom-call(s32[8]{0:T(128)S(1)} %copy-done.3, f32[8,5]{1,0:T(8,128)S(1)} %copy-done.2), custom_call_target="tpu_custom_call" | custom-call | flops 1000 | bytes 1000 | tf_op jit(solution)/shard_map/taps/pallas_call | solution.py:396
  11.2 0.0 collective-permute-done.refs_1_
  11.2 1.4 %collective-permute-done.1.refs_2_ = bf16[128,128]{1,0:T(8,128)(2,1)S(1)} collective-permute-done((bf16[128,128]{1,0:T(8,128)(2,1)S(1)}, bf16[128,128]{1,0:T(8,128)(2,1)S(1)}, u32[]{:S(2)}, u32[]{:S(2)}) %collective-permute-start.1) | collective-permute-done | bytes 32800 | tf_op jit(solution)/shard_map/ppermute | solution.py:354
  12.6 0.9 %collective-permute-done.2.refs_3_ = bf16[128,128]{1,0:T(8,128)(2,1)S(1)} collective-permute-done((bf16[128,128]{1,0:T(8,128)(2,1)S(1)}, bf16[128,128]{1,0:T(8,128)(2,1)S(1)}, u32[]{:S(2)}, u32[]{:S(2)}) %collective-permute-start.2) | collective-permute-done | bytes 32800 | tf_op jit(solution)/shard_map/ppermute | solution.py:354
  13.5 0.1 gather.1.feet_ref
  13.6 0.0 collective-permute-done.3
  13.6 0.0 collective-permute-done.4
  13.7 3.3 %restore.1 = (bf16[4,256,128]{2,1,0:T(8,128)(2,1)S(1)}, f32[4,8,128]{2,1,0:T(8,128)S(1)}) custom-call(f32[4,48,128]{2,1,0:T(8,128)S(1)} %get-tuple-element.25.taps_ref, f32[4,48,128]{2,1,0:T(8,128)S(1)} %get-tuple-element.26.back_ref, bf16[256,512]{1,0:T(8,128)(2,1)S(1)} %gather.1.feet_ref, f32[4,16,2048]{2,1,0:T(8,128)S(1)} %get-tuple-element.27.own_ref, ...), custom_call_target="tpu_custom_call" | custom-call | flops 1000 | bytes 1000 | tf_op jit(solution)/shard_map/restore/pallas_call | solution.py:412
  17.0 0.1 dynamic-slice_bitcast_fusion
  17.1 0.2 collective-permute-start.5
  17.3 1.0 %collective-permute-start.6 = (bf16[256,128]{1,0:T(8,128)(2,1)S(1)}, bf16[256,128]{1,0:T(8,128)(2,1)S(1)}, u32[]{:S(2)}, u32[]{:S(2)}) collective-permute-start(bf16[256,128]{1,0:T(8,128)(2,1)S(1)} %get-tuple-element.49), channel_id=1, source_target_pairs={{0,8},{4,12},{8,0},{12,4},{1,9},{5,13},{9,1},{13,5},{2,10},{6,14},... | collective-permute-start | bytes 196616 | tf_op jit(solution)/shard_map/ppermute | solution.py:348
  18.3 0.7 %collective-permute-start.7 = (bf16[256,128]{1,0:T(8,128)(2,1)S(1)}, bf16[256,128]{1,0:T(8,128)(2,1)S(1)}, u32[]{:S(2)}, u32[]{:S(2)}) collective-permute-start(bf16[256,128]{1,0:T(8,128)(2,1)S(1)} %get-tuple-element.48), channel_id=1, source_target_pairs={{0,12},{4,8},{8,4},{12,0},{1,13},{5,9},{9,5},{13,1},{2,14},{6,10},... | collective-permute-start | bytes 196616 | tf_op jit(solution)/shard_map/ppermute | solution.py:348
  19.0 1.3 %collective-permute-start.8 = (f32[8,128]{1,0:T(8,128)S(1)}, f32[8,128]{1,0:T(8,128)S(1)}, u32[]{:S(2)}, u32[]{:S(2)}) collective-permute-start(f32[8,128]{1,0:T(8,128)S(1)} %get-tuple-element.55), channel_id=1, source_target_pairs={{0,3},{1,2},{2,1},{3,0},{4,7},{5,6},{6,5},{7,4},{8,11},{9,10},{10,... | collective-permute-start | bytes 12296 | tf_op jit(solution)/shard_map/ppermute | solution.py:348
  20.4 1.3 %collective-permute-start.9 = (f32[8,128]{1,0:T(8,128)S(1)}, f32[8,128]{1,0:T(8,128)S(1)}, u32[]{:S(2)}, u32[]{:S(2)}) collective-permute-start(f32[8,128]{1,0:T(8,128)S(1)} %get-tuple-element.54), channel_id=1, source_target_pairs={{0,2},{1,3},{2,0},{3,1},{4,6},{5,7},{6,4},{7,5},{8,10},{9,11},{10,... | collective-permute-start | bytes 12296 | tf_op jit(solution)/shard_map/ppermute | solution.py:348
  21.7 2.7 %collective-permute-done.8.refs_0_ = f32[8,128]{1,0:T(8,128)S(1)} collective-permute-done((f32[8,128]{1,0:T(8,128)S(1)}, f32[8,128]{1,0:T(8,128)S(1)}, u32[]{:S(2)}, u32[]{:S(2)}) %collective-permute-start.8) | collective-permute-done | bytes 4128 | tf_op jit(solution)/shard_map/ppermute | solution.py:348
  24.4 0.4 %collective-permute-done.9.refs_1_ = f32[8,128]{1,0:T(8,128)S(1)} collective-permute-done((f32[8,128]{1,0:T(8,128)S(1)}, f32[8,128]{1,0:T(8,128)S(1)}, u32[]{:S(2)}, u32[]{:S(2)}) %collective-permute-start.9) | collective-permute-done | bytes 4128 | tf_op jit(solution)/shard_map/ppermute | solution.py:348
  24.9 3.2 %collective-permute-done.10.refs_2_ = f32[8,128]{1,0:T(8,128)S(1)} collective-permute-done((f32[8,128]{1,0:T(8,128)S(1)}, f32[8,128]{1,0:T(8,128)S(1)}, u32[]{:S(2)}, u32[]{:S(2)}) %collective-permute-start.10) | collective-permute-done | bytes 4128 | tf_op jit(solution)/shard_map/ppermute | solution.py:348
  28.0 1.0 %collective-permute-start.12 = (f32[8,128]{1,0:T(8,128)S(1)}, f32[8,128]{1,0:T(8,128)S(1)}, u32[]{:S(2)}, u32[]{:S(2)}) collective-permute-start(f32[8,128]{1,0:T(8,128)S(1)} %add.1.refs_0_), channel_id=1, source_target_pairs={{0,8},{4,12},{8,0},{12,4},{1,9},{5,13},{9,1},{13,5},{2,10},{6,14},... | collective-permute-start | bytes 12296 | tf_op jit(solution)/shard_map/ppermute | solution.py:354
  29.1 0.9 %collective-permute-start.13 = (f32[8,128]{1,0:T(8,128)S(1)}, f32[8,128]{1,0:T(8,128)S(1)}, u32[]{:S(2)}, u32[]{:S(2)}) collective-permute-start(f32[8,128]{1,0:T(8,128)S(1)} %add.1.refs_0_), channel_id=1, source_target_pairs={{0,12},{4,8},{8,4},{12,0},{1,13},{5,9},{9,5},{13,1},{2,14},{6,10},... | collective-permute-start | bytes 12296 | tf_op jit(solution)/shard_map/ppermute | solution.py:354
  29.9 0.9 %temporal.1 = bf16[16,16,512]{2,1,0:T(8,128)(2,1)} custom-call(bf16[256,128]{1,0:T(8,128)(2,1)S(1)} %get-tuple-element.51.refs_0_, bf16[256,128]{1,0:T(8,128)(2,1)S(1)} %collective-permute-done.5.refs_1_, bf16[256,128]{1,0:T(8,128)(2,1)S(1)} %collective-permute-done.6.refs_2_, bf16[256,128]{1,0:T(8,128)(2,1)S(1)} %collective-permute-done.7.refs_3_), custom_call_target="tpu_custom_call" | custom-call | flops 1000 | bytes 1000 | tf_op jit(solution)/shard_map/temporal/pallas_call | solution.py:425
  30.8 0.9 %collective-permute-done.12.refs_2_ = f32[8,128]{1,0:T(8,128)S(1)} collective-permute-done((f32[8,128]{1,0:T(8,128)S(1)}, f32[8,128]{1,0:T(8,128)S(1)}, u32[]{:S(2)}, u32[]{:S(2)}) %collective-permute-start.12) | collective-permute-done | bytes 4128 | tf_op jit(solution)/shard_map/ppermute | solution.py:354
  31.7 0.4 %collective-permute-done.13.refs_3_ = f32[8,128]{1,0:T(8,128)S(1)} collective-permute-done((f32[8,128]{1,0:T(8,128)S(1)}, f32[8,128]{1,0:T(8,128)S(1)}, u32[]{:S(2)}, u32[]{:S(2)}) %collective-permute-start.13) | collective-permute-done | bytes 4128 | tf_op jit(solution)/shard_map/ppermute | solution.py:354
  32.1 0.8 %means.1 = f32[16,16]{1,0:T(8,128)} custom-call(f32[8,128]{1,0:T(8,128)S(1)} %add.1.refs_0_, f32[8,128]{1,0:T(8,128)S(1)} %collective-permute-done.11.refs_1_, f32[8,128]{1,0:T(8,128)S(1)} %collective-permute-done.12.refs_2_, f32[8,128]{1,0:T(8,128)S(1)} %collective-permute-done.13.refs_3_), custom_call_target="tpu_custom_call" | custom-call | flops 1000 | bytes 1000 | tf_op jit(solution)/shard_map/means/pallas_call | solution.py:433
  (18 shorter events, 0.1 us)
Async XLA Ops:
  0.6 1.0 %copy-start = (f32[4,16,2048]{2,1,0:T(8,128)S(1)}, f32[4,16,2048]{2,1,0:T(8,128)}, u32[]{:S(2)}) copy-start(f32[4,16,2048]{2,1,0:T(8,128)} %observed_ref.1) | copy-start | bytes 1572868
  1.8 11.8 %collective-permute-start.3 = (f16[48,2048]{1,0:T(8,128)(2,1)S(1)}, f16[48,2048]{1,0:T(8,128)(2,1)S(1)}, u32[]{:S(2)}, u32[]{:S(2)}) collective-permute-start(f16[48,2048]{1,0:T(8,128)(2,1)S(1)} %convert_element_type.12), channel_id=1, source_target_pairs={{1,2},{2,1},{5,6},{6,5},{9,10},{10,9},{13,14},{14,13},{17,18},{18,... | collective-permute-start | bytes 589832 | tf_op jit(solution)/shard_map/ppermute | solution.py:394
  2.5 5.9 %copy-start.1 = (s32[256,16,4]{0,2,1:T(4,128)S(1)}, s32[256,16,4]{0,2,1:T(4,128)}, u32[]{:S(2)}) copy-start(s32[256,16,4]{0,2,1:T(4,128)} %param.7) | copy-start | bytes 196612
  2.6 11.1 %collective-permute-start.4 = (f16[48,2048]{1,0:T(8,128)(2,1)S(1)}, f16[48,2048]{1,0:T(8,128)(2,1)S(1)}, u32[]{:S(2)}, u32[]{:S(2)}) collective-permute-start(f16[48,2048]{1,0:T(8,128)(2,1)S(1)} %convert_element_type.13), channel_id=1, source_target_pairs={{0,1},{1,0},{2,3},{3,2},{4,5},{5,4},{6,7},{7,6},{8,9},{9,8},{10,11... | collective-permute-start | bytes 589832 | tf_op jit(solution)/shard_map/ppermute | solution.py:394
  8.5 2.1 %copy-start.2 = (f32[8,5]{1,0:T(8,128)S(1)}, f32[8,5]{1,0:T(8,128)}, u32[]{:S(2)}) copy-start(f32[8,5]{1,0:T(8,128)} %kernels_ref.1) | copy-start | bytes 484
  8.5 2.1 %copy-start.3 = (s32[8]{0:T(128)S(1)}, s32[8]{0:T(128)}, u32[]{:S(2)}) copy-start(s32[8]{0:T(128)} %band_ref.1) | copy-start | bytes 100
  8.6 2.6 %collective-permute-start = (bf16[128,128]{1,0:T(8,128)(2,1)S(1)}, bf16[128,128]{1,0:T(8,128)(2,1)S(1)}, u32[]{:S(2)}, u32[]{:S(2)}) collective-permute-start(bf16[128,128]{1,0:T(8,128)(2,1)S(1)} %feet.1.refs_0_), channel_id=1, source_target_pairs={{0,4},{4,0},{8,12},{12,8},{1,5},{5,1},{9,13},{13,9},{2,6},{6,2},{1... | collective-permute-start | bytes 98312 | tf_op jit(solution)/shard_map/ppermute | solution.py:354
  8.6 4.0 %collective-permute-start.1 = (bf16[128,128]{1,0:T(8,128)(2,1)S(1)}, bf16[128,128]{1,0:T(8,128)(2,1)S(1)}, u32[]{:S(2)}, u32[]{:S(2)}) collective-permute-start(bf16[128,128]{1,0:T(8,128)(2,1)S(1)} %feet.1.refs_0_), channel_id=1, source_target_pairs={{0,8},{4,12},{8,0},{12,4},{1,9},{5,13},{9,1},{13,5},{2,10},{6,14},... | collective-permute-start | bytes 98312 | tf_op jit(solution)/shard_map/ppermute | solution.py:354
  10.2 3.3 %collective-permute-start.2 = (bf16[128,128]{1,0:T(8,128)(2,1)S(1)}, bf16[128,128]{1,0:T(8,128)(2,1)S(1)}, u32[]{:S(2)}, u32[]{:S(2)}) collective-permute-start(bf16[128,128]{1,0:T(8,128)(2,1)S(1)} %feet.1.refs_0_), channel_id=1, source_target_pairs={{0,12},{4,8},{8,4},{12,0},{1,13},{5,9},{9,5},{13,1},{2,14},{6,10},... | collective-permute-start | bytes 98312 | tf_op jit(solution)/shard_map/ppermute | solution.py:354
  17.1 12.0 %collective-permute-start.5 = (bf16[256,128]{1,0:T(8,128)(2,1)S(1)}, bf16[256,128]{1,0:T(8,128)(2,1)S(1)}, u32[]{:S(2)}, u32[]{:S(2)}) collective-permute-start(bf16[256,128]{1,0:T(8,128)(2,1)S(1)} %get-tuple-element.50), channel_id=1, source_target_pairs={{0,4},{4,0},{8,12},{12,8},{1,5},{5,1},{9,13},{13,9},{2,6},{6,2},{1... | collective-permute-start | bytes 196616 | tf_op jit(solution)/shard_map/ppermute | solution.py:348
  17.3 12.6 %collective-permute-start.6 = (bf16[256,128]{1,0:T(8,128)(2,1)S(1)}, bf16[256,128]{1,0:T(8,128)(2,1)S(1)}, u32[]{:S(2)}, u32[]{:S(2)}) collective-permute-start(bf16[256,128]{1,0:T(8,128)(2,1)S(1)} %get-tuple-element.49), channel_id=1, source_target_pairs={{0,8},{4,12},{8,0},{12,4},{1,9},{5,13},{9,1},{13,5},{2,10},{6,14},... | collective-permute-start | bytes 196616 | tf_op jit(solution)/shard_map/ppermute | solution.py:348
  18.3 11.6 %collective-permute-start.7 = (bf16[256,128]{1,0:T(8,128)(2,1)S(1)}, bf16[256,128]{1,0:T(8,128)(2,1)S(1)}, u32[]{:S(2)}, u32[]{:S(2)}) collective-permute-start(bf16[256,128]{1,0:T(8,128)(2,1)S(1)} %get-tuple-element.48), channel_id=1, source_target_pairs={{0,12},{4,8},{8,4},{12,0},{1,13},{5,9},{9,5},{13,1},{2,14},{6,10},... | collective-permute-start | bytes 196616 | tf_op jit(solution)/shard_map/ppermute | solution.py:348
  19.0 5.4 %collective-permute-start.8 = (f32[8,128]{1,0:T(8,128)S(1)}, f32[8,128]{1,0:T(8,128)S(1)}, u32[]{:S(2)}, u32[]{:S(2)}) collective-permute-start(f32[8,128]{1,0:T(8,128)S(1)} %get-tuple-element.55), channel_id=1, source_target_pairs={{0,3},{1,2},{2,1},{3,0},{4,7},{5,6},{6,5},{7,4},{8,11},{9,10},{10,... | collective-permute-start | bytes 12296 | tf_op jit(solution)/shard_map/ppermute | solution.py:348
  20.4 4.5 %collective-permute-start.9 = (f32[8,128]{1,0:T(8,128)S(1)}, f32[8,128]{1,0:T(8,128)S(1)}, u32[]{:S(2)}, u32[]{:S(2)}) collective-permute-start(f32[8,128]{1,0:T(8,128)S(1)} %get-tuple-element.54), channel_id=1, source_target_pairs={{0,2},{1,3},{2,0},{3,1},{4,6},{5,7},{6,4},{7,5},{8,10},{9,11},{10,... | collective-permute-start | bytes 12296 | tf_op jit(solution)/shard_map/ppermute | solution.py:348
  24.4 3.6 %collective-permute-start.10 = (f32[8,128]{1,0:T(8,128)S(1)}, f32[8,128]{1,0:T(8,128)S(1)}, u32[]{:S(2)}, u32[]{:S(2)}) collective-permute-start(f32[8,128]{1,0:T(8,128)S(1)} %get-tuple-element.53), channel_id=1, source_target_pairs={{0,1},{1,0},{2,3},{3,2},{4,5},{5,4},{6,7},{7,6},{8,9},{9,8},{10,11... | collective-permute-start | bytes 12296 | tf_op jit(solution)/shard_map/ppermute | solution.py:348
  28.0 2.8 %collective-permute-start.11 = (f32[8,128]{1,0:T(8,128)S(1)}, f32[8,128]{1,0:T(8,128)S(1)}, u32[]{:S(2)}, u32[]{:S(2)}) collective-permute-start(f32[8,128]{1,0:T(8,128)S(1)} %add.1.refs_0_), channel_id=1, source_target_pairs={{0,4},{4,0},{8,12},{12,8},{1,5},{5,1},{9,13},{13,9},{2,6},{6,2},{1... | collective-permute-start | bytes 12296 | tf_op jit(solution)/shard_map/ppermute | solution.py:354
  28.0 3.7 %collective-permute-start.12 = (f32[8,128]{1,0:T(8,128)S(1)}, f32[8,128]{1,0:T(8,128)S(1)}, u32[]{:S(2)}, u32[]{:S(2)}) collective-permute-start(f32[8,128]{1,0:T(8,128)S(1)} %add.1.refs_0_), channel_id=1, source_target_pairs={{0,8},{4,12},{8,0},{12,4},{1,9},{5,13},{9,1},{13,5},{2,10},{6,14},... | collective-permute-start | bytes 12296 | tf_op jit(solution)/shard_map/ppermute | solution.py:354
  29.1 3.0 %collective-permute-start.13 = (f32[8,128]{1,0:T(8,128)S(1)}, f32[8,128]{1,0:T(8,128)S(1)}, u32[]{:S(2)}, u32[]{:S(2)}) collective-permute-start(f32[8,128]{1,0:T(8,128)S(1)} %add.1.refs_0_), channel_id=1, source_target_pairs={{0,12},{4,8},{8,4},{12,0},{1,13},{5,9},{9,5},{13,1},{2,14},{6,10},... | collective-permute-start | bytes 12296 | tf_op jit(solution)/shard_map/ppermute | solution.py:354

commit v10 on v6

--- a/solution.py
+++ b/solution.py
@@ -125,27 +125,22 @@
     return (spikes, traces)
 
 
-def low_first():
-    return (lax.axis_index("row") + lax.axis_index("frame")) % 2 == 0
-
-
-def halo_kernel(observed_ref, first_ref, second_ref, own_ref):
-    low = low_first()
+def halo_kernel(observed_ref, inner_ref, outer_ref, own_ref):
+    even = lax.axis_index("row") % 2 == 0
     frames = observed_ref.shape[0]
     own_ref[...] = observed_ref[...]
     for frame in range(frames):
         near = frame * NEAR
         far = frames * NEAR + frame * FAR
         bottom, top = observed_ref[frame, -NEAR:, :], observed_ref[frame, :NEAR, :]
-        first_ref[near : near + NEAR, :] = jnp.where(low, bottom, top)
-        second_ref[near : near + NEAR, :] = jnp.where(low, top, bottom)
+        inner_ref[near : near + NEAR, :] = jnp.where(even, bottom, top)
+        outer_ref[near : near + NEAR, :] = jnp.where(even, top, bottom)
         bottom, top = observed_ref[frame, -NEAR - FAR : -NEAR, :], observed_ref[frame, NEAR : NEAR + FAR, :]
-        first_ref[far : far + FAR, :] = jnp.where(low, bottom, top)
-        second_ref[far : far + FAR, :] = jnp.where(low, top, bottom)
-
-
-def tables_kernel(band_ref, kernels_ref, masks_ref, taps_ref, back_ref, feet_ref, pad_ref, *, height):
-    rows_dev = masks_ref.shape[0]
+        inner_ref[far : far + FAR, :] = jnp.where(even, bottom, top)
+        outer_ref[far : far + FAR, :] = jnp.where(even, top, bottom)
+
+
+def taps_kernel(band_ref, kernels_ref, taps_ref, back_ref, pad_ref, *, height, rows_dev):
     span = rows_dev + 2 * MARGIN
     first_row = lax.axis_index("row") * rows_dev - MARGIN
     row_ids = lax.broadcasted_iota(jnp.int32, (BAND, TILE), 0)
@@ -165,6 +160,10 @@
     for slot, tap in enumerate(SIDES):
         start = BAND + TAPS // 2 - tap
         back_ref[slot] = pad_ref[slot, start : start + span, :]
+
+
+def feet_kernel(masks_ref, feet_ref):
+    rows_dev = masks_ref.shape[0]
     flat = jnp.concatenate([masks_ref[row].astype(jnp.float32) for row in range(rows_dev)], axis=0)
     positions = flat.shape[0]
     both = jnp.concatenate([flat, flat], axis=0).T
@@ -177,7 +176,7 @@
 
 
 def restore_kernel(
-    taps_ref, back_ref, feet_ref, own_ref, first_ref, second_ref, out_ref, side_ref, image_ref, current_ref, quotient_ref
+    taps_ref, back_ref, feet_ref, own_ref, inner_ref, outer_ref, out_ref, side_ref, image_ref, current_ref, quotient_ref
 ):
     n_frame = out_ref.shape[0]
     frames, rows_dev, width = own_ref.shape
@@ -185,8 +184,8 @@
     positions = rows_dev * tiles_dev
     for ref in (image_ref, current_ref, quotient_ref):
         ref[...] = jnp.ones_like(ref)
-    low = low_first()
     row = lax.axis_index("row")
+    even = row % 2 == 0
     above = jnp.where(row == 0, 1.0, 0.0)
     below = jnp.where(row == lax.axis_size("row") - 1, 1.0, 0.0)
 
@@ -195,12 +194,12 @@
         for frame in range(frames):
             near, far = frame * NEAR, frames * NEAR + frame * FAR
             start, stop = PAD + MARGIN, PAD + MARGIN + rows_dev
-            first, second = first_ref[near : near + NEAR, columns], second_ref[near : near + NEAR, columns]
-            image_ref[frame, start - NEAR : start, :] = jnp.where(low, second, first) + above
-            image_ref[frame, stop : stop + NEAR, :] = jnp.where(low, first, second) + below
-            first, second = first_ref[far : far + FAR, columns], second_ref[far : far + FAR, columns]
-            image_ref[frame, start - NEAR - FAR : start - NEAR, :] = jnp.where(low, second, first) + above
-            image_ref[frame, stop + NEAR : stop + NEAR + FAR, :] = jnp.where(low, first, second) + below
+            inner, outer = inner_ref[near : near + NEAR, columns], outer_ref[near : near + NEAR, columns]
+            image_ref[frame, start - NEAR : start, :] = jnp.where(even, outer, inner) + above
+            image_ref[frame, stop : stop + NEAR, :] = jnp.where(even, inner, outer) + below
+            inner, outer = inner_ref[far : far + FAR, columns], outer_ref[far : far + FAR, columns]
+            image_ref[frame, start - NEAR - FAR : start - NEAR, :] = jnp.where(even, outer, inner) + above
+            image_ref[frame, stop + NEAR : stop + NEAR + FAR, :] = jnp.where(even, inner, outer) + below
             image_ref[frame, start:stop, :] = own_ref[frame, :, columns]
         source_ref = image_ref
         for (first, last), (back_first, back_last) in STEPS:
@@ -343,6 +342,13 @@
     return arrived
 
 
+def in_turn(*arrays):
+    done = []
+    for array in arrays:
+        done = list(lax.optimization_barrier((*done, array)))
+    return done
+
+
 def by_halo(observed, kernels, band_kernel, masks):
     n_frame, n_row = lax.axis_size("frame"), lax.axis_size("row")
     frames, rows_dev, width = observed.shape
@@ -352,7 +358,7 @@
     span = rows_dev + 2 * MARGIN
     smem, vmem = pl.BlockSpec(memory_space=pltpu.SMEM), pl.BlockSpec(memory_space=pltpu.VMEM)
 
-    def call(kernel, name, in_specs, out_shape, scratch=(), cost=1000000):
+    def call(kernel, name, in_specs, out_shape, scratch=(), cost=1000):
         many = isinstance(out_shape, tuple)
         return pl.pallas_call(
             kernel,
@@ -369,27 +375,22 @@
         return jax.ShapeDtypeStruct(shape, dtype)
 
     packed = array(frames * (NEAR + FAR), width)
-    *sent, own = call(halo_kernel, "halo", [vmem], (packed, packed, array(*observed.shape)))(observed)
-    pairs = [[(i, i + 1) for i in range(first, n_row - 1, 2)] for first in (0, 1)]
+    inner, outer, own = call(halo_kernel, "halo", [vmem], (packed, packed, array(*observed.shape)))(observed)
     swaps = [
-        [(f * n_row + i, f * n_row + j) for f in range(n_frame) for pair in pairs[(f + turn) % 2] for i, j in (pair, pair[::-1])]
-        for turn in range(2)
+        [pair for i in range(first, n_row - 1, 2) for pair in ((i, i + 1), (i + 1, i))] for first in (0, 1)
     ]
-    arrived = [
-        lax.ppermute(rows.astype(jnp.float16), ("frame", "row"), swap).astype(jnp.float32)
-        for rows, swap in zip(sent, swaps)
-    ]
-    taps, back, feet = call(
-        functools.partial(tables_kernel, height=rows_dev * n_row),
-        "tables",
-        [smem, smem, vmem],
-        (
-            array(len(SIDES), span, TILE),
-            array(len(SIDES), span, TILE),
-            array(n_frame, n_row * share // 2, TILE, dtype=jnp.bfloat16),
-        ),
+    inner, outer = (lax.ppermute(rows.astype(jnp.float16), "row", swap) for rows, swap in zip((inner, outer), swaps))
+    outer, inner = in_turn(outer, inner)
+    taps, back = call(
+        functools.partial(taps_kernel, height=rows_dev * n_row, rows_dev=rows_dev),
+        "taps",
+        [smem, smem],
+        (array(len(SIDES), span, TILE),) * 2,
         [pltpu.VMEM((len(SIDES), span + 2 * PAD, TILE), jnp.float32)],
-    )(band_kernel, kernels, masks.transpose(1, 2, 0))
+    )(band_kernel, kernels)
+    feet = call(feet_kernel, "feet", [vmem], array(n_frame, n_row * share // 2, TILE, dtype=jnp.bfloat16))(
+        masks.transpose(1, 2, 0)
+    )
     side_rows = frames * n_frame + n_row * share // 2
     blocks, sides = call(
         restore_kernel,
@@ -400,7 +401,7 @@
             array(n_frame, side_rows, TILE, dtype=jnp.bfloat16),
         ),
         [pltpu.VMEM((frames, span + 2 * PAD, TILE), jnp.float32)] * 3,
-    )(taps, back, feet, own, *arrived)
+    )(taps, back, feet, own, inner.astype(jnp.float32), outer.astype(jnp.float32))
     sides = swapped(sides, "frame")
     pieces = swapped(blocks, "frame")
     partial = call(
@@ -421,7 +422,7 @@
         array(n_frame * frames, rows_dev, tiles_dev * TILE, dtype=jnp.bfloat16),
         [pltpu.VMEM((n_frame, frames * positions, TILE), jnp.bfloat16)],
     )(*pieces)
-    spikes, *shares = lax.optimization_barrier((spikes, *shares))
+    spikes, *shares = in_turn(spikes, *shares[::-1])
     traces = call(means_kernel, "means", [vmem] * n_row, array(share, n_frame * frames))(*shares)
     return (spikes, traces)
 

time: 31.7 us -> 29.3 us (0.924)
  starting transfers between devices: 16.5 us -> 14.9 us
  waiting for transfers between devices: 6.09 us -> 5.61 us
    ppermute x9, starting transfers between devices: 10.9 us -> 8.33 us  [swapped(): lax.ppermute(part, axis, [(i, i ^ step) for i in range(count)])]
    ppermute x9, waiting for transfers between devices: 4.61 us -> 2.39 us  [swapped(): lax.ppermute(part, axis, [(i, i ^ step) for i in range(count)])]
    ppermute x2, waiting for transfers between devices: 1.48 us -> 3.22 us  [by_halo(): lax.ppermute(rows.astype(jnp.float16), 'row', swap)]
    ppermute x2, starting transfers between devices: 5.61 us -> 6.57 us  [by_halo(): lax.ppermute(rows.astype(jnp.float16), 'row', swap)]
    pallas_call x1 -> x2, Pallas kernels: 0.72 us -> 0.79 us  [the longest x1 0.69 us: by_halo(): call(functools.partial(taps_kernel, height=rows_dev * n_row, rows_dev=row...]
  transfers between devices with their start and end apart: 11 -> 11, of which waited for: 4 -> 5; matrix products, arithmetic and copies ran while one was open for 0% -> 0% of each run, Pallas kernels for 6% -> 7%
where the time goes in v10:
time: 29.3 us; the launch traced here: 29 us
  starting transfers between devices  14.9 us (51%)
  Pallas kernels  5.98 us (20%)
  waiting for transfers between devices  5.61 us (19%)
  local copies, waits for them, and re-layouts  1.68 us (6%)
  between operations  0.76 us (3%)
    ppermute x9, starting transfers between devices, swapped(): lax.ppermute(part, axis, [(i, i ^ step) for i in range(count)])  8.33 us
    ppermute x2, starting transfers between devices, by_halo(): lax.ppermute(rows.astype(jnp.float16), 'row', swap)  6.57 us
    ppermute x2, waiting for transfers between devices, by_halo(): lax.ppermute(rows.astype(jnp.float16), 'row', swap)  3.22 us
    pallas_call x1, Pallas kernels, by_halo(): call(restore_kernel, 'restore', [vmem] * 6, (array(n_frame, frames * posi...  3.06 us
    ppermute x9, waiting for transfers between devices, swapped(): lax.ppermute(part, axis, [(i, i ^ step) for i in range(count)])  2.39 us
    unnamed x8, local copies, waits for them, and re-layouts  1.62 us
    pallas_call x1, Pallas kernels, by_halo(): call(functools.partial(temporal_kernel, frames=frames), 'temporal', [vmem...  0.92 us
    pallas_call x1, Pallas kernels, by_halo(): call(functools.partial(taps_kernel, height=rows_dev * n_row, rows_dev=row...  0.69 us
  transfers between devices with their start and end apart: 11, of which 5 were waited for; matrix products, arithmetic and copies ran while one was open for 0% of the time, Pallas kernels for 7%

profile of v10, /device:TPU:0, one launch (start us, length us, event | category | flops | bytes accessed | tf_op | source)
XLA Modules:
  0.0 29.0 jit_solution(15358698116466292666)
XLA Ops:
  0.6 1.0 %copy-done = f32[4,16,2048]{2,1,0:T(8,128)S(1)} copy-done((f32[4,16,2048]{2,1,0:T(8,128)S(1)}, f32[4,16,2048]{2,1,0:T(8,128)}, u32[]{:S(2)}) %copy-start) | copy-done | bytes 524312
  1.7 0.1 halo.1
  1.8 0.7 %collective-permute-start = (f16[48,2048]{1,0:T(8,128)(2,1)S(1)}, f16[48,2048]{1,0:T(8,128)(2,1)S(1)}, u32[]{:S(2)}, u32[]{:S(2)}) collective-permute-start(f16[48,2048]{1,0:T(8,128)(2,1)S(1)} %convert_element_type.12), channel_id=1, source_target_pairs={{1,2},{2,1},{5,6},{6,5},{9,10},{10,9},{13,14},{14,13},{17,18},{18,... | collective-permute-start | bytes 589832 | tf_op jit(solution)/shard_map/ppermute | solution.py:382
  2.5 0.0 copy-start.1
  2.6 5.9 %collective-permute-start.1 = (f16[48,2048]{1,0:T(8,128)(2,1)S(1)}, f16[48,2048]{1,0:T(8,128)(2,1)S(1)}, u32[]{:S(2)}, u32[]{:S(2)}) collective-permute-start(f16[48,2048]{1,0:T(8,128)(2,1)S(1)} %convert_element_type.13), channel_id=1, source_target_pairs={{0,1},{1,0},{2,3},{3,2},{4,5},{5,4},{6,7},{7,6},{8,9},{9,8},{10,11... | collective-permute-start | bytes 589832 | tf_op jit(solution)/shard_map/ppermute | solution.py:382
  8.5 0.1 feet.1.feet_ref
  8.6 0.6 %copy-done.2 = f32[8,5]{1,0:T(8,128)S(1)} copy-done((f32[8,5]{1,0:T(8,128)S(1)}, f32[8,5]{1,0:T(8,128)}, u32[]{:S(2)}) %copy-start.2) | copy-done | bytes 184
  9.1 0.7 %taps.1 = (f32[4,48,128]{2,1,0:T(8,128)S(1)}, f32[4,48,128]{2,1,0:T(8,128)S(1)}) custom-call(s32[8]{0:T(128)S(1)} %copy-done.3, f32[8,5]{1,0:T(8,128)S(1)} %copy-done.2), custom_call_target="tpu_custom_call" | custom-call | flops 1000 | bytes 1000 | tf_op jit(solution)/shard_map/taps/pallas_call | solution.py:384
  9.8 0.0 collective-permute-done
  9.9 3.2 %collective-permute-done.1 = f16[48,2048]{1,0:T(8,128)(2,1)S(1)} collective-permute-done((f16[48,2048]{1,0:T(8,128)(2,1)S(1)}, f16[48,2048]{1,0:T(8,128)(2,1)S(1)}, u32[]{:S(2)}, u32[]{:S(2)}) %collective-permute-start.1) | collective-permute-done | bytes 196640 | tf_op jit(solution)/shard_map/ppermute | solution.py:382
  13.1 3.1 %restore.1 = (bf16[4,256,128]{2,1,0:T(8,128)(2,1)S(1)}, bf16[4,48,128]{2,1,0:T(8,128)(2,1)S(1)}) custom-call(f32[4,48,128]{2,1,0:T(8,128)S(1)} %get-tuple-element.25.taps_ref, f32[4,48,128]{2,1,0:T(8,128)S(1)} %get-tuple-element.26.back_ref, bf16[4,32,128]{2,1,0:T(8,128)(2,1)S(1)} %feet.1.feet_ref, f32[4,16,2048]{2,1,0:T(8,128)S(1)} %get-tuple-element.27.own_ref, ...), custom_call_target="tpu_custom_call" | custom-call | flops 1000 | bytes 1000 | tf_op jit(solution)/shard_map/restore/pallas_call | solution.py:395
  16.2 0.1 collective-permute-start.5
  16.3 1.6 %collective-permute-start.6 = (bf16[48,128]{1,0:T(8,128)(2,1)S(1)}, bf16[48,128]{1,0:T(8,128)(2,1)S(1)}, u32[]{:S(2)}, u32[]{:S(2)}) collective-permute-start(bf16[48,128]{1,0:T(8,128)(2,1)S(1)} %get-tuple-element.53), channel_id=1, source_target_pairs={{0,8},{4,12},{8,0},{12,4},{1,9},{5,13},{9,1},{13,5},{2,10},{6,14},... | collective-permute-start | bytes 36872 | tf_op jit(solution)/shard_map/ppermute | solution.py:341
  17.9 0.3 %collective-permute-start.7 = (bf16[48,128]{1,0:T(8,128)(2,1)S(1)}, bf16[48,128]{1,0:T(8,128)(2,1)S(1)}, u32[]{:S(2)}, u32[]{:S(2)}) collective-permute-start(bf16[48,128]{1,0:T(8,128)(2,1)S(1)} %get-tuple-element.52), channel_id=1, source_target_pairs={{0,12},{4,8},{8,4},{12,0},{1,13},{5,9},{9,5},{13,1},{2,14},{6,10},... | collective-permute-start | bytes 36872 | tf_op jit(solution)/shard_map/ppermute | solution.py:341
  18.2 0.4 %collective-permute-start.2 = (bf16[256,128]{1,0:T(8,128)(2,1)S(1)}, bf16[256,128]{1,0:T(8,128)(2,1)S(1)}, u32[]{:S(2)}, u32[]{:S(2)}) collective-permute-start(bf16[256,128]{1,0:T(8,128)(2,1)S(1)} %get-tuple-element.50), channel_id=1, source_target_pairs={{0,4},{4,0},{8,12},{12,8},{1,5},{5,1},{9,13},{13,9},{2,6},{6,2},{1... | collective-permute-start | bytes 196616 | tf_op jit(solution)/shard_map/ppermute | solution.py:341
  18.6 1.5 %collective-permute-start.3 = (bf16[256,128]{1,0:T(8,128)(2,1)S(1)}, bf16[256,128]{1,0:T(8,128)(2,1)S(1)}, u32[]{:S(2)}, u32[]{:S(2)}) collective-permute-start(bf16[256,128]{1,0:T(8,128)(2,1)S(1)} %get-tuple-element.49), channel_id=1, source_target_pairs={{0,8},{4,12},{8,0},{12,4},{1,9},{5,13},{9,1},{13,5},{2,10},{6,14},... | collective-permute-start | bytes 196616 | tf_op jit(solution)/shard_map/ppermute | solution.py:341
  20.1 0.0 collective-permute-done.5.refs_1_
  20.1 0.0 collective-permute-start.4
  20.1 0.0 collective-permute-done.6.refs_2_
  20.1 0.8 %collective-permute-done.7.refs_3_ = bf16[48,128]{1,0:T(8,128)(2,1)S(1)} collective-permute-done((bf16[48,128]{1,0:T(8,128)(2,1)S(1)}, bf16[48,128]{1,0:T(8,128)(2,1)S(1)}, u32[]{:S(2)}, u32[]{:S(2)}) %collective-permute-start.7) | collective-permute-done | bytes 12320 | tf_op jit(solution)/shard_map/ppermute | solution.py:341
  21.0 0.4 %partial.1 = f32[4,16,128]{2,1,0:T(8,128)S(1)} custom-call(bf16[48,128]{1,0:T(8,128)(2,1)S(1)} %get-tuple-element.55.refs_0_, bf16[48,128]{1,0:T(8,128)(2,1)S(1)} %collective-permute-done.5.refs_1_, bf16[48,128]{1,0:T(8,128)(2,1)S(1)} %collective-permute-done.6.refs_2_, bf16[48,128]{1,0:T(8,128)(2,1)S(1)} %collective-permute-done.7.refs_3_), custom_call_target="tpu_custom_call" | custom-call | flops 1000 | bytes 1000 | tf_op jit(solution)/shard_map/partial/pallas_call | solution.py:407
  21.4 1.4 %collective-permute-start.8 = (f32[16,128]{1,0:T(8,128)S(1)}, f32[16,128]{1,0:T(8,128)S(1)}, u32[]{:S(2)}, u32[]{:S(2)}) collective-permute-start(f32[16,128]{1,0:T(8,128)S(1)} %get-tuple-element.59), channel_id=1, source_target_pairs={{0,3},{1,2},{2,1},{3,0},{4,7},{5,6},{6,5},{7,4},{8,11},{9,10},{10,... | collective-permute-start | bytes 24584 | tf_op jit(solution)/shard_map/ppermute | solution.py:341
  22.9 1.9 %collective-permute-start.9 = (f32[16,128]{1,0:T(8,128)S(1)}, f32[16,128]{1,0:T(8,128)S(1)}, u32[]{:S(2)}, u32[]{:S(2)}) collective-permute-start(f32[16,128]{1,0:T(8,128)S(1)} %get-tuple-element.58), channel_id=1, source_target_pairs={{0,2},{1,3},{2,0},{3,1},{4,6},{5,7},{6,4},{7,5},{8,10},{9,11},{10,... | collective-permute-start | bytes 24584 | tf_op jit(solution)/shard_map/ppermute | solution.py:341
  24.7 0.0 collective-permute-done.2.refs_1_
  24.7 1.2 %collective-permute-start.10 = (f32[16,128]{1,0:T(8,128)S(1)}, f32[16,128]{1,0:T(8,128)S(1)}, u32[]{:S(2)}, u32[]{:S(2)}) collective-permute-start(f32[16,128]{1,0:T(8,128)S(1)} %get-tuple-element.57), channel_id=1, source_target_pairs={{0,1},{1,0},{2,3},{3,2},{4,5},{5,4},{6,7},{7,6},{8,9},{9,8},{10,11... | collective-permute-start | bytes 24584 | tf_op jit(solution)/shard_map/ppermute | solution.py:341
  25.9 0.0 collective-permute-done.3.refs_2_
  25.9 0.0 collective-permute-done.4.refs_3_
  25.9 0.9 %temporal.1 = bf16[16,16,512]{2,1,0:T(8,128)(2,1)} custom-call(bf16[256,128]{1,0:T(8,128)(2,1)S(1)} %get-tuple-element.51.refs_0_, bf16[256,128]{1,0:T(8,128)(2,1)S(1)} %collective-permute-done.2.refs_1_, bf16[256,128]{1,0:T(8,128)(2,1)S(1)} %collective-permute-done.3.refs_2_, bf16[256,128]{1,0:T(8,128)(2,1)S(1)} %collective-permute-done.4.refs_3_), custom_call_target="tpu_custom_call" | custom-call | flops 1000 | bytes 1000 | tf_op jit(solution)/shard_map/temporal/pallas_call | solution.py:418
  26.8 0.1 collective-permute-done.8.refs_0_
  27.0 0.4 %collective-permute-done.9.refs_1_ = f32[16,128]{1,0:T(8,128)S(1)} collective-permute-done((f32[16,128]{1,0:T(8,128)S(1)}, f32[16,128]{1,0:T(8,128)S(1)}, u32[]{:S(2)}, u32[]{:S(2)}) %collective-permute-start.9) | collective-permute-done | bytes 8224 | tf_op jit(solution)/shard_map/ppermute | solution.py:341
  27.4 1.0 %collective-permute-done.10.refs_2_ = f32[16,128]{1,0:T(8,128)S(1)} collective-permute-done((f32[16,128]{1,0:T(8,128)S(1)}, f32[16,128]{1,0:T(8,128)S(1)}, u32[]{:S(2)}, u32[]{:S(2)}) %collective-permute-start.10) | collective-permute-done | bytes 8224 | tf_op jit(solution)/shard_map/ppermute | solution.py:341
  28.4 0.7 %means.1 = f32[16,16]{1,0:T(8,128)} custom-call(f32[16,128]{1,0:T(8,128)S(1)} %collective-permute-done.8.refs_0_, f32[16,128]{1,0:T(8,128)S(1)} %collective-permute-done.9.refs_1_, f32[16,128]{1,0:T(8,128)S(1)} %collective-permute-done.10.refs_2_, f32[16,128]{1,0:T(8,128)S(1)} %get-tuple-element.47.refs_3_), custom_call_target="tpu_custom_call" | custom-call | flops 1000 | bytes 1000 | tf_op jit(solution)/shard_map/means/pallas_call | solution.py:426
  (12 shorter events, 0.2 us)
Async XLA Ops:
  0.6 1.0 %copy-start = (f32[4,16,2048]{2,1,0:T(8,128)S(1)}, f32[4,16,2048]{2,1,0:T(8,128)}, u32[]{:S(2)}) copy-start(f32[4,16,2048]{2,1,0:T(8,128)} %observed_ref.1) | copy-start | bytes 1572868
  1.8 8.0 %collective-permute-start = (f16[48,2048]{1,0:T(8,128)(2,1)S(1)}, f16[48,2048]{1,0:T(8,128)(2,1)S(1)}, u32[]{:S(2)}, u32[]{:S(2)}) collective-permute-start(f16[48,2048]{1,0:T(8,128)(2,1)S(1)} %convert_element_type.12), channel_id=1, source_target_pairs={{1,2},{2,1},{5,6},{6,5},{9,10},{10,9},{13,14},{14,13},{17,18},{18,... | collective-permute-start | bytes 589832 | tf_op jit(solution)/shard_map/ppermute | solution.py:382
  2.5 5.9 %copy-start.1 = (s32[256,16,4]{0,2,1:T(4,128)S(1)}, s32[256,16,4]{0,2,1:T(4,128)}, u32[]{:S(2)}) copy-start(s32[256,16,4]{0,2,1:T(4,128)} %param.7) | copy-start | bytes 196612
  2.6 10.5 %collective-permute-start.1 = (f16[48,2048]{1,0:T(8,128)(2,1)S(1)}, f16[48,2048]{1,0:T(8,128)(2,1)S(1)}, u32[]{:S(2)}, u32[]{:S(2)}) collective-permute-start(f16[48,2048]{1,0:T(8,128)(2,1)S(1)} %convert_element_type.13), channel_id=1, source_target_pairs={{0,1},{1,0},{2,3},{3,2},{4,5},{5,4},{6,7},{7,6},{8,9},{9,8},{10,11... | collective-permute-start | bytes 589832 | tf_op jit(solution)/shard_map/ppermute | solution.py:382
  8.5 0.7 %copy-start.2 = (f32[8,5]{1,0:T(8,128)S(1)}, f32[8,5]{1,0:T(8,128)}, u32[]{:S(2)}) copy-start(f32[8,5]{1,0:T(8,128)} %kernels_ref.1) | copy-start | bytes 484
  8.5 0.7 %copy-start.3 = (s32[8]{0:T(128)S(1)}, s32[8]{0:T(128)}, u32[]{:S(2)}) copy-start(s32[8]{0:T(128)} %band_ref.1) | copy-start | bytes 100
  16.2 3.9 %collective-permute-start.5 = (bf16[48,128]{1,0:T(8,128)(2,1)S(1)}, bf16[48,128]{1,0:T(8,128)(2,1)S(1)}, u32[]{:S(2)}, u32[]{:S(2)}) collective-permute-start(bf16[48,128]{1,0:T(8,128)(2,1)S(1)} %get-tuple-element.54), channel_id=1, source_target_pairs={{0,4},{4,0},{8,12},{12,8},{1,5},{5,1},{9,13},{13,9},{2,6},{6,2},{1... | collective-permute-start | bytes 36872 | tf_op jit(solution)/shard_map/ppermute | solution.py:341
  16.3 3.8 %collective-permute-start.6 = (bf16[48,128]{1,0:T(8,128)(2,1)S(1)}, bf16[48,128]{1,0:T(8,128)(2,1)S(1)}, u32[]{:S(2)}, u32[]{:S(2)}) collective-permute-start(bf16[48,128]{1,0:T(8,128)(2,1)S(1)} %get-tuple-element.53), channel_id=1, source_target_pairs={{0,8},{4,12},{8,0},{12,4},{1,9},{5,13},{9,1},{13,5},{2,10},{6,14},... | collective-permute-start | bytes 36872 | tf_op jit(solution)/shard_map/ppermute | solution.py:341
  17.9 3.1 %collective-permute-start.7 = (bf16[48,128]{1,0:T(8,128)(2,1)S(1)}, bf16[48,128]{1,0:T(8,128)(2,1)S(1)}, u32[]{:S(2)}, u32[]{:S(2)}) collective-permute-start(bf16[48,128]{1,0:T(8,128)(2,1)S(1)} %get-tuple-element.52), channel_id=1, source_target_pairs={{0,12},{4,8},{8,4},{12,0},{1,13},{5,9},{9,5},{13,1},{2,14},{6,10},... | collective-permute-start | bytes 36872 | tf_op jit(solution)/shard_map/ppermute | solution.py:341
  18.2 6.5 %collective-permute-start.2 = (bf16[256,128]{1,0:T(8,128)(2,1)S(1)}, bf16[256,128]{1,0:T(8,128)(2,1)S(1)}, u32[]{:S(2)}, u32[]{:S(2)}) collective-permute-start(bf16[256,128]{1,0:T(8,128)(2,1)S(1)} %get-tuple-element.50), channel_id=1, source_target_pairs={{0,4},{4,0},{8,12},{12,8},{1,5},{5,1},{9,13},{13,9},{2,6},{6,2},{1... | collective-permute-start | bytes 196616 | tf_op jit(solution)/shard_map/ppermute | solution.py:341
  18.6 7.3 %collective-permute-start.3 = (bf16[256,128]{1,0:T(8,128)(2,1)S(1)}, bf16[256,128]{1,0:T(8,128)(2,1)S(1)}, u32[]{:S(2)}, u32[]{:S(2)}) collective-permute-start(bf16[256,128]{1,0:T(8,128)(2,1)S(1)} %get-tuple-element.49), channel_id=1, source_target_pairs={{0,8},{4,12},{8,0},{12,4},{1,9},{5,13},{9,1},{13,5},{2,10},{6,14},... | collective-permute-start | bytes 196616 | tf_op jit(solution)/shard_map/ppermute | solution.py:341
  20.1 5.8 %collective-permute-start.4 = (bf16[256,128]{1,0:T(8,128)(2,1)S(1)}, bf16[256,128]{1,0:T(8,128)(2,1)S(1)}, u32[]{:S(2)}, u32[]{:S(2)}) collective-permute-start(bf16[256,128]{1,0:T(8,128)(2,1)S(1)} %get-tuple-element.48), channel_id=1, source_target_pairs={{0,12},{4,8},{8,4},{12,0},{1,13},{5,9},{9,5},{13,1},{2,14},{6,10},... | collective-permute-start | bytes 196616 | tf_op jit(solution)/shard_map/ppermute | solution.py:341
  21.4 5.5 %collective-permute-start.8 = (f32[16,128]{1,0:T(8,128)S(1)}, f32[16,128]{1,0:T(8,128)S(1)}, u32[]{:S(2)}, u32[]{:S(2)}) collective-permute-start(f32[16,128]{1,0:T(8,128)S(1)} %get-tuple-element.59), channel_id=1, source_target_pairs={{0,3},{1,2},{2,1},{3,0},{4,7},{5,6},{6,5},{7,4},{8,11},{9,10},{10,... | collective-permute-start | bytes 24584 | tf_op jit(solution)/shard_map/ppermute | solution.py:341
  22.9 4.5 %collective-permute-start.9 = (f32[16,128]{1,0:T(8,128)S(1)}, f32[16,128]{1,0:T(8,128)S(1)}, u32[]{:S(2)}, u32[]{:S(2)}) collective-permute-start(f32[16,128]{1,0:T(8,128)S(1)} %get-tuple-element.58), channel_id=1, source_target_pairs={{0,2},{1,3},{2,0},{3,1},{4,6},{5,7},{6,4},{7,5},{8,10},{9,11},{10,... | collective-permute-start | bytes 24584 | tf_op jit(solution)/shard_map/ppermute | solution.py:341
  24.7 3.7 %collective-permute-start.10 = (f32[16,128]{1,0:T(8,128)S(1)}, f32[16,128]{1,0:T(8,128)S(1)}, u32[]{:S(2)}, u32[]{:S(2)}) collective-permute-start(f32[16,128]{1,0:T(8,128)S(1)} %get-tuple-element.57), channel_id=1, source_target_pairs={{0,1},{1,0},{2,3},{3,2},{4,5},{5,4},{6,7},{7,6},{8,9},{9,8},{10,11... | collective-permute-start | bytes 24584 | tf_op jit(solution)/shard_map/ppermute | solution.py:341

commit v11 on v10

--- a/solution.py
+++ b/solution.py
@@ -176,7 +176,7 @@
 
 
 def restore_kernel(
-    taps_ref, back_ref, feet_ref, own_ref, inner_ref, outer_ref, out_ref, side_ref, image_ref, current_ref, quotient_ref
+    taps_ref, back_ref, feet_ref, own_ref, top_ref, bottom_ref, out_ref, side_ref, image_ref, current_ref, quotient_ref
 ):
     n_frame = out_ref.shape[0]
     frames, rows_dev, width = own_ref.shape
@@ -184,22 +184,16 @@
     positions = rows_dev * tiles_dev
     for ref in (image_ref, current_ref, quotient_ref):
         ref[...] = jnp.ones_like(ref)
-    row = lax.axis_index("row")
-    even = row % 2 == 0
-    above = jnp.where(row == 0, 1.0, 0.0)
-    below = jnp.where(row == lax.axis_size("row") - 1, 1.0, 0.0)
 
     def columns_step(step, carry):
         columns = pl.ds(pl.multiple_of(step * TILE, TILE), TILE)
         for frame in range(frames):
             near, far = frame * NEAR, frames * NEAR + frame * FAR
             start, stop = PAD + MARGIN, PAD + MARGIN + rows_dev
-            inner, outer = inner_ref[near : near + NEAR, columns], outer_ref[near : near + NEAR, columns]
-            image_ref[frame, start - NEAR : start, :] = jnp.where(even, outer, inner) + above
-            image_ref[frame, stop : stop + NEAR, :] = jnp.where(even, inner, outer) + below
-            inner, outer = inner_ref[far : far + FAR, columns], outer_ref[far : far + FAR, columns]
-            image_ref[frame, start - NEAR - FAR : start - NEAR, :] = jnp.where(even, outer, inner) + above
-            image_ref[frame, stop + NEAR : stop + NEAR + FAR, :] = jnp.where(even, inner, outer) + below
+            image_ref[frame, start - NEAR - FAR : start - NEAR, :] = top_ref[far : far + FAR, columns]
+            image_ref[frame, start - NEAR : start, :] = top_ref[near : near + NEAR, columns]
+            image_ref[frame, stop : stop + NEAR, :] = bottom_ref[near : near + NEAR, columns]
+            image_ref[frame, stop + NEAR : stop + NEAR + FAR, :] = bottom_ref[far : far + FAR, columns]
             image_ref[frame, start:stop, :] = own_ref[frame, :, columns]
         source_ref = image_ref
         for (first, last), (back_first, back_last) in STEPS:
@@ -282,7 +276,7 @@
     place = lax.axis_index("frame")
     rows = sums_ref.shape[0] // n_frame
     half = feet_ref.shape[1]
-    for step, piece in enumerate(pieces):
+    for step, piece in enumerate(pieces[::-1]):
         sums_ref[pl.ds(pl.multiple_of((place ^ step) * rows, rows), rows), :] = piece[:rows, :].astype(jnp.float32)
         feet_ref[place ^ step] = piece[rows:, :].astype(jnp.float32)
     series = [sums_ref[t * n_frame : (t + 1) * n_frame, :] for t in range(rows)]
@@ -311,7 +305,7 @@
 def temporal_kernel(*refs, frames):
     pieces, (spikes_ref, in_ref) = refs[:-2], refs[-2:]
     place = lax.axis_index("frame")
-    for step, piece in enumerate(pieces):
+    for step, piece in enumerate(pieces[::-1]):
         in_ref[place ^ step] = piece[...]
     total, rows_dev, columns = spikes_ref.shape
     positions = in_ref.shape[1] // frames
@@ -391,6 +385,11 @@
     feet = call(feet_kernel, "feet", [vmem], array(n_frame, n_row * share // 2, TILE, dtype=jnp.bfloat16))(
         masks.transpose(1, 2, 0)
     )
+    row = lax.axis_index("row")
+    even = row % 2 == 0
+    alone = (row == 0) | (row == n_row - 1)
+    inner, outer = inner.astype(jnp.float32), jnp.where(alone, 1.0, outer.astype(jnp.float32))
+    top, bottom = jnp.where(even, outer, inner), jnp.where(even, inner, outer)
     side_rows = frames * n_frame + n_row * share // 2
     blocks, sides = call(
         restore_kernel,
@@ -401,7 +400,7 @@
             array(n_frame, side_rows, TILE, dtype=jnp.bfloat16),
         ),
         [pltpu.VMEM((frames, span + 2 * PAD, TILE), jnp.float32)] * 3,
-    )(taps, back, feet, own, inner.astype(jnp.float32), outer.astype(jnp.float32))
+    )(taps, back, feet, own, top, bottom)
     sides = swapped(sides, "frame")
     pieces = swapped(blocks, "frame")
     partial = call(
@@ -413,7 +412,7 @@
             pltpu.VMEM((n_frame * frames * n_frame, TILE), jnp.float32),
             pltpu.VMEM((n_frame, n_row * share // 2, TILE), jnp.float32),
         ],
-    )(*sides)
+    )(*sides[::-1])
     shares = swapped(partial, "row")
     spikes = call(
         functools.partial(temporal_kernel, frames=frames),
@@ -421,7 +420,7 @@
         [vmem] * n_frame,
         array(n_frame * frames, rows_dev, tiles_dev * TILE, dtype=jnp.bfloat16),
         [pltpu.VMEM((n_frame, frames * positions, TILE), jnp.bfloat16)],
-    )(*pieces)
+    )(*pieces[::-1])
     spikes, *shares = in_turn(spikes, *shares[::-1])
     traces = call(means_kernel, "means", [vmem] * n_row, array(share, n_frame * frames))(*shares)
     return (spikes, traces)

time: 29.3 us -> 28.4 us (0.969)
  waiting for transfers between devices: 5.61 us -> 4.76 us
    ppermute x9, waiting for transfers between devices: 2.39 us -> 1.55 us  [swapped(): lax.ppermute(part, axis, [(i, i ^ step) for i in range(count)])]
  transfers between devices with their start and end apart: 11 -> 11, of which waited for: 5 -> 4; matrix products, arithmetic and copies ran while one was open for 0% -> 0% of each run, Pallas kernels for 7% -> 8%
where the time goes in v11:
time: 28.4 us; the launch traced here: 28.2 us
  starting transfers between devices  14.9 us (52%)
  Pallas kernels  5.96 us (21%)
  waiting for transfers between devices  4.76 us (17%)
  local copies, waits for them, and re-layouts  1.68 us (6%)
  between operations  0.76 us (3%)
    ppermute x9, starting transfers between devices, swapped(): lax.ppermute(part, axis, [(i, i ^ step) for i in range(count)])  8.31 us
    ppermute x2, starting transfers between devices, by_halo(): lax.ppermute(rows.astype(jnp.float16), 'row', swap)  6.57 us
    ppermute x2, waiting for transfers between devices, by_halo(): lax.ppermute(rows.astype(jnp.float16), 'row', swap)  3.21 us
    pallas_call x1, Pallas kernels, by_halo(): call(restore_kernel, 'restore', [vmem] * 6, (array(n_frame, frames * posi...  3.04 us
    unnamed x8, local copies, waits for them, and re-layouts  1.62 us
    ppermute x9, waiting for transfers between devices, swapped(): lax.ppermute(part, axis, [(i, i ^ step) for i in range(count)])  1.55 us
    pallas_call x1, Pallas kernels, by_halo(): call(functools.partial(temporal_kernel, frames=frames), 'temporal', [vmem...  0.92 us
    pallas_call x1, Pallas kernels, by_halo(): call(functools.partial(taps_kernel, height=rows_dev * n_row, rows_dev=row...  0.69 us
  transfers between devices with their start and end apart: 11, of which 4 were waited for; matrix products, arithmetic and copies ran while one was open for 0% of the time, Pallas kernels for 8%

profile of v11, /device:TPU:0, one launch (start us, length us, event | category | flops | bytes accessed | tf_op | source)
XLA Modules:
  0.0 28.2 jit_solution(7657228834800287546)
XLA Ops:
  0.6 1.0 %copy-done = f32[4,16,2048]{2,1,0:T(8,128)S(1)} copy-done((f32[4,16,2048]{2,1,0:T(8,128)S(1)}, f32[4,16,2048]{2,1,0:T(8,128)}, u32[]{:S(2)}) %copy-start) | copy-done | bytes 524312
  1.7 0.1 halo.1
  1.8 0.7 %collective-permute-start = (f16[48,2048]{1,0:T(8,128)(2,1)S(1)}, f16[48,2048]{1,0:T(8,128)(2,1)S(1)}, u32[]{:S(2)}, u32[]{:S(2)}) collective-permute-start(f16[48,2048]{1,0:T(8,128)(2,1)S(1)} %convert_element_type.12), channel_id=1, source_target_pairs={{1,2},{2,1},{5,6},{6,5},{9,10},{10,9},{13,14},{14,13},{17,18},{18,... | collective-permute-start | bytes 589832 | tf_op jit(solution)/shard_map/ppermute | solution.py:376
  2.5 0.0 copy-start.1
  2.6 5.9 %collective-permute-start.1 = (f16[48,2048]{1,0:T(8,128)(2,1)S(1)}, f16[48,2048]{1,0:T(8,128)(2,1)S(1)}, u32[]{:S(2)}, u32[]{:S(2)}) collective-permute-start(f16[48,2048]{1,0:T(8,128)(2,1)S(1)} %convert_element_type.13), channel_id=1, source_target_pairs={{0,1},{1,0},{2,3},{3,2},{4,5},{5,4},{6,7},{7,6},{8,9},{9,8},{10,11... | collective-permute-start | bytes 589832 | tf_op jit(solution)/shard_map/ppermute | solution.py:376
  8.5 0.1 feet.1.feet_ref
  8.6 0.6 %copy-done.2 = f32[8,5]{1,0:T(8,128)S(1)} copy-done((f32[8,5]{1,0:T(8,128)S(1)}, f32[8,5]{1,0:T(8,128)}, u32[]{:S(2)}) %copy-start.2) | copy-done | bytes 184
  9.1 0.7 %taps.1 = (f32[4,48,128]{2,1,0:T(8,128)S(1)}, f32[4,48,128]{2,1,0:T(8,128)S(1)}) custom-call(s32[8]{0:T(128)S(1)} %copy-done.3, f32[8,5]{1,0:T(8,128)S(1)} %copy-done.2), custom_call_target="tpu_custom_call" | custom-call | flops 1000 | bytes 1000 | tf_op jit(solution)/shard_map/taps/pallas_call | solution.py:378
  9.9 0.0 collective-permute-done
  9.9 3.2 %collective-permute-done.1 = f16[48,2048]{1,0:T(8,128)(2,1)S(1)} collective-permute-done((f16[48,2048]{1,0:T(8,128)(2,1)S(1)}, f16[48,2048]{1,0:T(8,128)(2,1)S(1)}, u32[]{:S(2)}, u32[]{:S(2)}) %collective-permute-start.1) | collective-permute-done | bytes 196640 | tf_op jit(solution)/shard_map/ppermute | solution.py:376
  13.1 0.1 convert_select_fusion
  13.2 3.0 %restore.1 = (bf16[4,256,128]{2,1,0:T(8,128)(2,1)S(1)}, bf16[4,48,128]{2,1,0:T(8,128)(2,1)S(1)}) custom-call(f32[4,48,128]{2,1,0:T(8,128)S(1)} %get-tuple-element.25.taps_ref, f32[4,48,128]{2,1,0:T(8,128)S(1)} %get-tuple-element.26.back_ref, bf16[4,32,128]{2,1,0:T(8,128)(2,1)S(1)} %feet.1.feet_ref, f32[4,16,2048]{2,1,0:T(8,128)S(1)} %get-tuple-element.27.own_ref, ...), custom_call_target="tpu_custom_call" | custom-call | flops 1000 | bytes 1000 | tf_op jit(solution)/shard_map/restore/pallas_call | solution.py:394
  16.2 0.1 collective-permute-start.5
  16.3 1.5 %collective-permute-start.6 = (bf16[48,128]{1,0:T(8,128)(2,1)S(1)}, bf16[48,128]{1,0:T(8,128)(2,1)S(1)}, u32[]{:S(2)}, u32[]{:S(2)}) collective-permute-start(bf16[48,128]{1,0:T(8,128)(2,1)S(1)} %get-tuple-element.56), channel_id=1, source_target_pairs={{0,8},{4,12},{8,0},{12,4},{1,9},{5,13},{9,1},{13,5},{2,10},{6,14},... | collective-permute-start | bytes 36872 | tf_op jit(solution)/shard_map/ppermute | solution.py:335
  17.9 0.3 %collective-permute-start.7 = (bf16[48,128]{1,0:T(8,128)(2,1)S(1)}, bf16[48,128]{1,0:T(8,128)(2,1)S(1)}, u32[]{:S(2)}, u32[]{:S(2)}) collective-permute-start(bf16[48,128]{1,0:T(8,128)(2,1)S(1)} %get-tuple-element.55), channel_id=1, source_target_pairs={{0,4},{4,0},{8,12},{12,8},{1,5},{5,1},{9,13},{13,9},{2,6},{6,2},{1... | collective-permute-start | bytes 36872 | tf_op jit(solution)/shard_map/ppermute | solution.py:335
  18.2 1.2 %collective-permute-start.2 = (bf16[256,128]{1,0:T(8,128)(2,1)S(1)}, bf16[256,128]{1,0:T(8,128)(2,1)S(1)}, u32[]{:S(2)}, u32[]{:S(2)}) collective-permute-start(bf16[256,128]{1,0:T(8,128)(2,1)S(1)} %get-tuple-element.53), channel_id=1, source_target_pairs={{0,12},{4,8},{8,4},{12,0},{1,13},{5,9},{9,5},{13,1},{2,14},{6,10},... | collective-permute-start | bytes 196616 | tf_op jit(solution)/shard_map/ppermute | solution.py:335
  19.3 0.8 %collective-permute-start.3 = (bf16[256,128]{1,0:T(8,128)(2,1)S(1)}, bf16[256,128]{1,0:T(8,128)(2,1)S(1)}, u32[]{:S(2)}, u32[]{:S(2)}) collective-permute-start(bf16[256,128]{1,0:T(8,128)(2,1)S(1)} %get-tuple-element.52), channel_id=1, source_target_pairs={{0,8},{4,12},{8,0},{12,4},{1,9},{5,13},{9,1},{13,5},{2,10},{6,14},... | collective-permute-start | bytes 196616 | tf_op jit(solution)/shard_map/ppermute | solution.py:335
  20.1 0.0 collective-permute-done.5.refs_0_
  20.1 0.0 collective-permute-start.4
  20.1 0.0 collective-permute-done.6.refs_1_
  20.1 0.0 collective-permute-done.7.refs_2_
  20.1 0.4 %partial.1 = f32[4,16,128]{2,1,0:T(8,128)S(1)} custom-call(bf16[48,128]{1,0:T(8,128)(2,1)S(1)} %collective-permute-done.5.refs_0_, bf16[48,128]{1,0:T(8,128)(2,1)S(1)} %collective-permute-done.6.refs_1_, bf16[48,128]{1,0:T(8,128)(2,1)S(1)} %collective-permute-done.7.refs_2_, bf16[48,128]{1,0:T(8,128)(2,1)S(1)} %get-tuple-element.54.refs_3_), custom_call_target="tpu_custom_call" | custom-call | flops 1000 | bytes 1000 | tf_op jit(solution)/shard_map/partial/pallas_call | solution.py:406
  20.6 1.4 %collective-permute-start.8 = (f32[16,128]{1,0:T(8,128)S(1)}, f32[16,128]{1,0:T(8,128)S(1)}, u32[]{:S(2)}, u32[]{:S(2)}) collective-permute-start(f32[16,128]{1,0:T(8,128)S(1)} %get-tuple-element.61), channel_id=1, source_target_pairs={{0,3},{1,2},{2,1},{3,0},{4,7},{5,6},{6,5},{7,4},{8,11},{9,10},{10,... | collective-permute-start | bytes 24584 | tf_op jit(solution)/shard_map/ppermute | solution.py:335
  22.0 1.9 %collective-permute-start.9 = (f32[16,128]{1,0:T(8,128)S(1)}, f32[16,128]{1,0:T(8,128)S(1)}, u32[]{:S(2)}, u32[]{:S(2)}) collective-permute-start(f32[16,128]{1,0:T(8,128)S(1)} %get-tuple-element.60), channel_id=1, source_target_pairs={{0,2},{1,3},{2,0},{3,1},{4,6},{5,7},{6,4},{7,5},{8,10},{9,11},{10,... | collective-permute-start | bytes 24584 | tf_op jit(solution)/shard_map/ppermute | solution.py:335
  23.8 0.0 collective-permute-done.2.refs_0_
  23.8 1.2 %collective-permute-start.10 = (f32[16,128]{1,0:T(8,128)S(1)}, f32[16,128]{1,0:T(8,128)S(1)}, u32[]{:S(2)}, u32[]{:S(2)}) collective-permute-start(f32[16,128]{1,0:T(8,128)S(1)} %get-tuple-element.59), channel_id=1, source_target_pairs={{0,1},{1,0},{2,3},{3,2},{4,5},{5,4},{6,7},{7,6},{8,9},{9,8},{10,11... | collective-permute-start | bytes 24584 | tf_op jit(solution)/shard_map/ppermute | solution.py:335
  25.0 0.0 collective-permute-done.3.refs_1_
  25.0 0.9 %temporal.1 = bf16[16,16,512]{2,1,0:T(8,128)(2,1)} custom-call(bf16[256,128]{1,0:T(8,128)(2,1)S(1)} %collective-permute-done.2.refs_0_, bf16[256,128]{1,0:T(8,128)(2,1)S(1)} %collective-permute-done.3.refs_1_, bf16[256,128]{1,0:T(8,128)(2,1)S(1)} %collective-permute-done.4.refs_2_, bf16[256,128]{1,0:T(8,128)(2,1)S(1)} %get-tuple-element.50.refs_3_), custom_call_target="tpu_custom_call" | custom-call | flops 1000 | bytes 1000 | tf_op jit(solution)/shard_map/temporal/pallas_call | solution.py:417
  25.9 0.2 collective-permute-done.8.refs_0_
  26.1 0.4 %collective-permute-done.9.refs_1_ = f32[16,128]{1,0:T(8,128)S(1)} collective-permute-done((f32[16,128]{1,0:T(8,128)S(1)}, f32[16,128]{1,0:T(8,128)S(1)}, u32[]{:S(2)}, u32[]{:S(2)}) %collective-permute-start.9) | collective-permute-done | bytes 8224 | tf_op jit(solution)/shard_map/ppermute | solution.py:335
  26.5 0.9 %collective-permute-done.10.refs_2_ = f32[16,128]{1,0:T(8,128)S(1)} collective-permute-done((f32[16,128]{1,0:T(8,128)S(1)}, f32[16,128]{1,0:T(8,128)S(1)}, u32[]{:S(2)}, u32[]{:S(2)}) %collective-permute-start.10) | collective-permute-done | bytes 8224 | tf_op jit(solution)/shard_map/ppermute | solution.py:335
  27.5 0.7 %means.1 = f32[16,16]{1,0:T(8,128)} custom-call(f32[16,128]{1,0:T(8,128)S(1)} %collective-permute-done.8.refs_0_, f32[16,128]{1,0:T(8,128)S(1)} %collective-permute-done.9.refs_1_, f32[16,128]{1,0:T(8,128)S(1)} %collective-permute-done.10.refs_2_, f32[16,128]{1,0:T(8,128)S(1)} %get-tuple-element.47.refs_3_), custom_call_target="tpu_custom_call" | custom-call | flops 1000 | bytes 1000 | tf_op jit(solution)/shard_map/means/pallas_call | solution.py:425
  (11 shorter events, 0.1 us)
Async XLA Ops:
  0.6 1.0 %copy-start = (f32[4,16,2048]{2,1,0:T(8,128)S(1)}, f32[4,16,2048]{2,1,0:T(8,128)}, u32[]{:S(2)}) copy-start(f32[4,16,2048]{2,1,0:T(8,128)} %observed_ref.1) | copy-start | bytes 1572868
  1.8 8.0 %collective-permute-start = (f16[48,2048]{1,0:T(8,128)(2,1)S(1)}, f16[48,2048]{1,0:T(8,128)(2,1)S(1)}, u32[]{:S(2)}, u32[]{:S(2)}) collective-permute-start(f16[48,2048]{1,0:T(8,128)(2,1)S(1)} %convert_element_type.12), channel_id=1, source_target_pairs={{1,2},{2,1},{5,6},{6,5},{9,10},{10,9},{13,14},{14,13},{17,18},{18,... | collective-permute-start | bytes 589832 | tf_op jit(solution)/shard_map/ppermute | solution.py:376
  2.5 5.9 %copy-start.1 = (s32[256,16,4]{0,2,1:T(4,128)S(1)}, s32[256,16,4]{0,2,1:T(4,128)}, u32[]{:S(2)}) copy-start(s32[256,16,4]{0,2,1:T(4,128)} %param.7) | copy-start | bytes 196612
  2.6 10.5 %collective-permute-start.1 = (f16[48,2048]{1,0:T(8,128)(2,1)S(1)}, f16[48,2048]{1,0:T(8,128)(2,1)S(1)}, u32[]{:S(2)}, u32[]{:S(2)}) collective-permute-start(f16[48,2048]{1,0:T(8,128)(2,1)S(1)} %convert_element_type.13), channel_id=1, source_target_pairs={{0,1},{1,0},{2,3},{3,2},{4,5},{5,4},{6,7},{7,6},{8,9},{9,8},{10,11... | collective-permute-start | bytes 589832 | tf_op jit(solution)/shard_map/ppermute | solution.py:376
  8.5 0.7 %copy-start.2 = (f32[8,5]{1,0:T(8,128)S(1)}, f32[8,5]{1,0:T(8,128)}, u32[]{:S(2)}) copy-start(f32[8,5]{1,0:T(8,128)} %kernels_ref.1) | copy-start | bytes 484
  8.5 0.7 %copy-start.3 = (s32[8]{0:T(128)S(1)}, s32[8]{0:T(128)}, u32[]{:S(2)}) copy-start(s32[8]{0:T(128)} %band_ref.1) | copy-start | bytes 100
  16.2 3.9 %collective-permute-start.5 = (bf16[48,128]{1,0:T(8,128)(2,1)S(1)}, bf16[48,128]{1,0:T(8,128)(2,1)S(1)}, u32[]{:S(2)}, u32[]{:S(2)}) collective-permute-start(bf16[48,128]{1,0:T(8,128)(2,1)S(1)} %get-tuple-element.57), channel_id=1, source_target_pairs={{0,12},{4,8},{8,4},{12,0},{1,13},{5,9},{9,5},{13,1},{2,14},{6,10},... | collective-permute-start | bytes 36872 | tf_op jit(solution)/shard_map/ppermute | solution.py:335
  16.3 3.8 %collective-permute-start.6 = (bf16[48,128]{1,0:T(8,128)(2,1)S(1)}, bf16[48,128]{1,0:T(8,128)(2,1)S(1)}, u32[]{:S(2)}, u32[]{:S(2)}) collective-permute-start(bf16[48,128]{1,0:T(8,128)(2,1)S(1)} %get-tuple-element.56), channel_id=1, source_target_pairs={{0,8},{4,12},{8,0},{12,4},{1,9},{5,13},{9,1},{13,5},{2,10},{6,14},... | collective-permute-start | bytes 36872 | tf_op jit(solution)/shard_map/ppermute | solution.py:335
  17.9 2.3 %collective-permute-start.7 = (bf16[48,128]{1,0:T(8,128)(2,1)S(1)}, bf16[48,128]{1,0:T(8,128)(2,1)S(1)}, u32[]{:S(2)}, u32[]{:S(2)}) collective-permute-start(bf16[48,128]{1,0:T(8,128)(2,1)S(1)} %get-tuple-element.55), channel_id=1, source_target_pairs={{0,4},{4,0},{8,12},{12,8},{1,5},{5,1},{9,13},{13,9},{2,6},{6,2},{1... | collective-permute-start | bytes 36872 | tf_op jit(solution)/shard_map/ppermute | solution.py:335
  18.2 5.7 %collective-permute-start.2 = (bf16[256,128]{1,0:T(8,128)(2,1)S(1)}, bf16[256,128]{1,0:T(8,128)(2,1)S(1)}, u32[]{:S(2)}, u32[]{:S(2)}) collective-permute-start(bf16[256,128]{1,0:T(8,128)(2,1)S(1)} %get-tuple-element.53), channel_id=1, source_target_pairs={{0,12},{4,8},{8,4},{12,0},{1,13},{5,9},{9,5},{13,1},{2,14},{6,10},... | collective-permute-start | bytes 196616 | tf_op jit(solution)/shard_map/ppermute | solution.py:335
  19.3 5.7 %collective-permute-start.3 = (bf16[256,128]{1,0:T(8,128)(2,1)S(1)}, bf16[256,128]{1,0:T(8,128)(2,1)S(1)}, u32[]{:S(2)}, u32[]{:S(2)}) collective-permute-start(bf16[256,128]{1,0:T(8,128)(2,1)S(1)} %get-tuple-element.52), channel_id=1, source_target_pairs={{0,8},{4,12},{8,0},{12,4},{1,9},{5,13},{9,1},{13,5},{2,10},{6,14},... | collective-permute-start | bytes 196616 | tf_op jit(solution)/shard_map/ppermute | solution.py:335
  20.1 4.9 %collective-permute-start.4 = (bf16[256,128]{1,0:T(8,128)(2,1)S(1)}, bf16[256,128]{1,0:T(8,128)(2,1)S(1)}, u32[]{:S(2)}, u32[]{:S(2)}) collective-permute-start(bf16[256,128]{1,0:T(8,128)(2,1)S(1)} %get-tuple-element.51), channel_id=1, source_target_pairs={{0,4},{4,0},{8,12},{12,8},{1,5},{5,1},{9,13},{13,9},{2,6},{6,2},{1... | collective-permute-start | bytes 196616 | tf_op jit(solution)/shard_map/ppermute | solution.py:335
  20.6 5.6 %collective-permute-start.8 = (f32[16,128]{1,0:T(8,128)S(1)}, f32[16,128]{1,0:T(8,128)S(1)}, u32[]{:S(2)}, u32[]{:S(2)}) collective-permute-start(f32[16,128]{1,0:T(8,128)S(1)} %get-tuple-element.61), channel_id=1, source_target_pairs={{0,3},{1,2},{2,1},{3,0},{4,7},{5,6},{6,5},{7,4},{8,11},{9,10},{10,... | collective-permute-start | bytes 24584 | tf_op jit(solution)/shard_map/ppermute | solution.py:335
  22.0 4.6 %collective-permute-start.9 = (f32[16,128]{1,0:T(8,128)S(1)}, f32[16,128]{1,0:T(8,128)S(1)}, u32[]{:S(2)}, u32[]{:S(2)}) collective-permute-start(f32[16,128]{1,0:T(8,128)S(1)} %get-tuple-element.60), channel_id=1, source_target_pairs={{0,2},{1,3},{2,0},{3,1},{4,6},{5,7},{6,4},{7,5},{8,10},{9,11},{10,... | collective-permute-start | bytes 24584 | tf_op jit(solution)/shard_map/ppermute | solution.py:335
  23.8 3.7 %collective-permute-start.10 = (f32[16,128]{1,0:T(8,128)S(1)}, f32[16,128]{1,0:T(8,128)S(1)}, u32[]{:S(2)}, u32[]{:S(2)}) collective-permute-start(f32[16,128]{1,0:T(8,128)S(1)} %get-tuple-element.59), channel_id=1, source_target_pairs={{0,1},{1,0},{2,3},{3,2},{4,5},{5,4},{6,7},{7,6},{8,9},{9,8},{10,11... | collective-permute-start | bytes 24584 | tf_op jit(solution)/shard_map/ppermute | solution.py:335

commit v12 on v11

--- a/solution.py
+++ b/solution.py
@@ -125,17 +125,22 @@
     return (spikes, traces)
 
 
-def halo_kernel(observed_ref, inner_ref, outer_ref, own_ref):
+def halo_kernel(observed_ref, inner_ref, outer_ref, own_ref, arrived):
     even = lax.axis_index("row") % 2 == 0
-    frames = observed_ref.shape[0]
-    own_ref[...] = observed_ref[...]
-    for frame in range(frames):
+    frames = own_ref.shape[0]
+    copies = [
+        pltpu.make_async_copy(observed_ref.at[frame], own_ref.at[frame], arrived.at[frame]) for frame in range(frames)
+    ]
+    for copy in copies:
+        copy.start()
+    for frame, copy in enumerate(copies):
+        copy.wait()
         near = frame * NEAR
         far = frames * NEAR + frame * FAR
-        bottom, top = observed_ref[frame, -NEAR:, :], observed_ref[frame, :NEAR, :]
+        bottom, top = own_ref[frame, -NEAR:, :], own_ref[frame, :NEAR, :]
         inner_ref[near : near + NEAR, :] = jnp.where(even, bottom, top)
         outer_ref[near : near + NEAR, :] = jnp.where(even, top, bottom)
-        bottom, top = observed_ref[frame, -NEAR - FAR : -NEAR, :], observed_ref[frame, NEAR : NEAR + FAR, :]
+        bottom, top = own_ref[frame, -NEAR - FAR : -NEAR, :], own_ref[frame, NEAR : NEAR + FAR, :]
         inner_ref[far : far + FAR, :] = jnp.where(even, bottom, top)
         outer_ref[far : far + FAR, :] = jnp.where(even, top, bottom)
 
@@ -369,7 +374,13 @@
         return jax.ShapeDtypeStruct(shape, dtype)
 
     packed = array(frames * (NEAR + FAR), width)
-    inner, outer, own = call(halo_kernel, "halo", [vmem], (packed, packed, array(*observed.shape)))(observed)
+    inner, outer, own = call(
+        halo_kernel,
+        "halo",
+        [pl.BlockSpec(memory_space=pltpu.HBM)],
+        (packed, packed, array(*observed.shape)),
+        [pltpu.SemaphoreType.DMA((frames,))],
+    )(pltpu.with_memory_space_constraint(observed, pltpu.HBM))
     swaps = [
         [pair for i in range(first, n_row - 1, 2) for pair in ((i, i + 1), (i + 1, i))] for first in (0, 1)
     ]

time: 28.4 us -> 28.4 us (level)
  Pallas kernels: 5.96 us -> 7 us
  local copies, waits for them, and re-layouts: 1.68 us -> 0.64 us
    unnamed x8 -> x6, local copies, waits for them, and re-layouts: 1.62 us -> 0.59 us
    pallas_call x1, Pallas kernels: 0.12 us -> 1.16 us  [by_halo(): call(halo_kernel, 'halo', [pl.BlockSpec(memory_space=pltpu.HBM)], (packed...]
where the time goes in v12:
time: 28.4 us; the launch traced here: 28.2 us
  starting transfers between devices  14.9 us (52%)
  Pallas kernels  7 us (25%)
  waiting for transfers between devices  4.76 us (17%)
  between operations  0.76 us (3%)
  local copies, waits for them, and re-layouts  0.64 us (2%)
    ppermute x9, starting transfers between devices, swapped(): lax.ppermute(part, axis, [(i, i ^ step) for i in range(count)])  8.31 us
    ppermute x2, starting transfers between devices, by_halo(): lax.ppermute(rows.astype(jnp.float16), 'row', swap)  6.57 us
    ppermute x2, waiting for transfers between devices, by_halo(): lax.ppermute(rows.astype(jnp.float16), 'row', swap)  3.21 us
    pallas_call x1, Pallas kernels, by_halo(): call(restore_kernel, 'restore', [vmem] * 6, (array(n_frame, frames * posi...  3.03 us
    ppermute x9, waiting for transfers between devices, swapped(): lax.ppermute(part, axis, [(i, i ^ step) for i in range(count)])  1.55 us
    pallas_call x1, Pallas kernels, by_halo(): call(halo_kernel, 'halo', [pl.BlockSpec(memory_space=pltpu.HBM)], (packed...  1.16 us
    pallas_call x1, Pallas kernels, by_halo(): call(functools.partial(temporal_kernel, frames=frames), 'temporal', [vmem...  0.92 us
    pallas_call x1, Pallas kernels, by_halo(): call(functools.partial(taps_kernel, height=rows_dev * n_row, rows_dev=row...  0.69 us
  transfers between devices with their start and end apart: 11, of which 4 were waited for; matrix products, arithmetic and copies ran while one was open for 0% of the time, Pallas kernels for 8%

profile of v12, /device:TPU:0, one launch (start us, length us, event | category | flops | bytes accessed | tf_op | source)
XLA Modules:
  0.0 28.2 jit_solution(2435394557324232113)
XLA Ops:
  0.6 1.2 %halo.1 = (f32[48,2048]{1,0:T(8,128)S(1)}, f32[48,2048]{1,0:T(8,128)S(1)}, f32[4,16,2048]{2,1,0:T(8,128)S(1)}) custom-call(f32[4,16,2048]{2,1,0:T(8,128)} %observed_ref.1), custom_call_target="tpu_custom_call" | custom-call | flops 1000 | bytes 1000 | tf_op jit(solution)/shard_map/halo/pallas_call | solution.py:377
  1.8 0.7 %collective-permute-start = (f16[48,2048]{1,0:T(8,128)(2,1)S(1)}, f16[48,2048]{1,0:T(8,128)(2,1)S(1)}, u32[]{:S(2)}, u32[]{:S(2)}) collective-permute-start(f16[48,2048]{1,0:T(8,128)(2,1)S(1)} %convert_element_type.12), channel_id=1, source_target_pairs={{1,2},{2,1},{5,6},{6,5},{9,10},{10,9},{13,14},{14,13},{17,18},{18,... | collective-permute-start | bytes 589832 | tf_op jit(solution)/shard_map/ppermute | solution.py:387
  2.5 0.0 copy-start
  2.5 5.9 %collective-permute-start.1 = (f16[48,2048]{1,0:T(8,128)(2,1)S(1)}, f16[48,2048]{1,0:T(8,128)(2,1)S(1)}, u32[]{:S(2)}, u32[]{:S(2)}) collective-permute-start(f16[48,2048]{1,0:T(8,128)(2,1)S(1)} %convert_element_type.13), channel_id=1, source_target_pairs={{0,1},{1,0},{2,3},{3,2},{4,5},{5,4},{6,7},{7,6},{8,9},{9,8},{10,11... | collective-permute-start | bytes 589832 | tf_op jit(solution)/shard_map/ppermute | solution.py:387
  8.5 0.1 feet.1.feet_ref
  8.6 0.6 %copy-done.1 = f32[8,5]{1,0:T(8,128)S(1)} copy-done((f32[8,5]{1,0:T(8,128)S(1)}, f32[8,5]{1,0:T(8,128)}, u32[]{:S(2)}) %copy-start.1) | copy-done | bytes 184
  9.1 0.7 %taps.1 = (f32[4,48,128]{2,1,0:T(8,128)S(1)}, f32[4,48,128]{2,1,0:T(8,128)S(1)}) custom-call(s32[8]{0:T(128)S(1)} %copy-done.2, f32[8,5]{1,0:T(8,128)S(1)} %copy-done.1), custom_call_target="tpu_custom_call" | custom-call | flops 1000 | bytes 1000 | tf_op jit(solution)/shard_map/taps/pallas_call | solution.py:389
  9.9 0.0 collective-permute-done
  9.9 3.2 %collective-permute-done.1 = f16[48,2048]{1,0:T(8,128)(2,1)S(1)} collective-permute-done((f16[48,2048]{1,0:T(8,128)(2,1)S(1)}, f16[48,2048]{1,0:T(8,128)(2,1)S(1)}, u32[]{:S(2)}, u32[]{:S(2)}) %collective-permute-start.1) | collective-permute-done | bytes 196640 | tf_op jit(solution)/shard_map/ppermute | solution.py:387
  13.1 0.1 convert_select_fusion
  13.2 3.0 %restore.1 = (bf16[4,256,128]{2,1,0:T(8,128)(2,1)S(1)}, bf16[4,48,128]{2,1,0:T(8,128)(2,1)S(1)}) custom-call(f32[4,48,128]{2,1,0:T(8,128)S(1)} %get-tuple-element.25.taps_ref, f32[4,48,128]{2,1,0:T(8,128)S(1)} %get-tuple-element.26.back_ref, bf16[4,32,128]{2,1,0:T(8,128)(2,1)S(1)} %feet.1.feet_ref, f32[4,16,2048]{2,1,0:T(8,128)S(1)} %get-tuple-element.27.own_ref, ...), custom_call_target="tpu_custom_call" | custom-call | flops 1000 | bytes 1000 | tf_op jit(solution)/shard_map/restore/pallas_call | solution.py:405
  16.2 0.1 collective-permute-start.5
  16.3 1.5 %collective-permute-start.6 = (bf16[48,128]{1,0:T(8,128)(2,1)S(1)}, bf16[48,128]{1,0:T(8,128)(2,1)S(1)}, u32[]{:S(2)}, u32[]{:S(2)}) collective-permute-start(bf16[48,128]{1,0:T(8,128)(2,1)S(1)} %get-tuple-element.56), channel_id=1, source_target_pairs={{0,8},{4,12},{8,0},{12,4},{1,9},{5,13},{9,1},{13,5},{2,10},{6,14},... | collective-permute-start | bytes 36872 | tf_op jit(solution)/shard_map/ppermute | solution.py:340
  17.9 0.3 %collective-permute-start.7 = (bf16[48,128]{1,0:T(8,128)(2,1)S(1)}, bf16[48,128]{1,0:T(8,128)(2,1)S(1)}, u32[]{:S(2)}, u32[]{:S(2)}) collective-permute-start(bf16[48,128]{1,0:T(8,128)(2,1)S(1)} %get-tuple-element.55), channel_id=1, source_target_pairs={{0,4},{4,0},{8,12},{12,8},{1,5},{5,1},{9,13},{13,9},{2,6},{6,2},{1... | collective-permute-start | bytes 36872 | tf_op jit(solution)/shard_map/ppermute | solution.py:340
  18.2 1.2 %collective-permute-start.2 = (bf16[256,128]{1,0:T(8,128)(2,1)S(1)}, bf16[256,128]{1,0:T(8,128)(2,1)S(1)}, u32[]{:S(2)}, u32[]{:S(2)}) collective-permute-start(bf16[256,128]{1,0:T(8,128)(2,1)S(1)} %get-tuple-element.53), channel_id=1, source_target_pairs={{0,12},{4,8},{8,4},{12,0},{1,13},{5,9},{9,5},{13,1},{2,14},{6,10},... | collective-permute-start | bytes 196616 | tf_op jit(solution)/shard_map/ppermute | solution.py:340
  19.3 0.8 %collective-permute-start.3 = (bf16[256,128]{1,0:T(8,128)(2,1)S(1)}, bf16[256,128]{1,0:T(8,128)(2,1)S(1)}, u32[]{:S(2)}, u32[]{:S(2)}) collective-permute-start(bf16[256,128]{1,0:T(8,128)(2,1)S(1)} %get-tuple-element.52), channel_id=1, source_target_pairs={{0,8},{4,12},{8,0},{12,4},{1,9},{5,13},{9,1},{13,5},{2,10},{6,14},... | collective-permute-start | bytes 196616 | tf_op jit(solution)/shard_map/ppermute | solution.py:340
  20.1 0.0 collective-permute-done.5.refs_0_
  20.1 0.0 collective-permute-start.4
  20.1 0.0 collective-permute-done.6.refs_1_
  20.1 0.0 collective-permute-done.7.refs_2_
  20.1 0.4 %partial.1 = f32[4,16,128]{2,1,0:T(8,128)S(1)} custom-call(bf16[48,128]{1,0:T(8,128)(2,1)S(1)} %collective-permute-done.5.refs_0_, bf16[48,128]{1,0:T(8,128)(2,1)S(1)} %collective-permute-done.6.refs_1_, bf16[48,128]{1,0:T(8,128)(2,1)S(1)} %collective-permute-done.7.refs_2_, bf16[48,128]{1,0:T(8,128)(2,1)S(1)} %get-tuple-element.54.refs_3_), custom_call_target="tpu_custom_call" | custom-call | flops 1000 | bytes 1000 | tf_op jit(solution)/shard_map/partial/pallas_call | solution.py:417
  20.6 1.4 %collective-permute-start.8 = (f32[16,128]{1,0:T(8,128)S(1)}, f32[16,128]{1,0:T(8,128)S(1)}, u32[]{:S(2)}, u32[]{:S(2)}) collective-permute-start(f32[16,128]{1,0:T(8,128)S(1)} %get-tuple-element.61), channel_id=1, source_target_pairs={{0,3},{1,2},{2,1},{3,0},{4,7},{5,6},{6,5},{7,4},{8,11},{9,10},{10,... | collective-permute-start | bytes 24584 | tf_op jit(solution)/shard_map/ppermute | solution.py:340
  22.0 1.9 %collective-permute-start.9 = (f32[16,128]{1,0:T(8,128)S(1)}, f32[16,128]{1,0:T(8,128)S(1)}, u32[]{:S(2)}, u32[]{:S(2)}) collective-permute-start(f32[16,128]{1,0:T(8,128)S(1)} %get-tuple-element.60), channel_id=1, source_target_pairs={{0,2},{1,3},{2,0},{3,1},{4,6},{5,7},{6,4},{7,5},{8,10},{9,11},{10,... | collective-permute-start | bytes 24584 | tf_op jit(solution)/shard_map/ppermute | solution.py:340
  23.8 0.0 collective-permute-done.2.refs_0_
  23.8 1.2 %collective-permute-start.10 = (f32[16,128]{1,0:T(8,128)S(1)}, f32[16,128]{1,0:T(8,128)S(1)}, u32[]{:S(2)}, u32[]{:S(2)}) collective-permute-start(f32[16,128]{1,0:T(8,128)S(1)} %get-tuple-element.59), channel_id=1, source_target_pairs={{0,1},{1,0},{2,3},{3,2},{4,5},{5,4},{6,7},{7,6},{8,9},{9,8},{10,11... | collective-permute-start | bytes 24584 | tf_op jit(solution)/shard_map/ppermute | solution.py:340
  25.0 0.0 collective-permute-done.3.refs_1_
  25.0 0.0 collective-permute-done.4.refs_2_
  25.0 0.9 %temporal.1 = bf16[16,16,512]{2,1,0:T(8,128)(2,1)} custom-call(bf16[256,128]{1,0:T(8,128)(2,1)S(1)} %collective-permute-done.2.refs_0_, bf16[256,128]{1,0:T(8,128)(2,1)S(1)} %collective-permute-done.3.refs_1_, bf16[256,128]{1,0:T(8,128)(2,1)S(1)} %collective-permute-done.4.refs_2_, bf16[256,128]{1,0:T(8,128)(2,1)S(1)} %get-tuple-element.50.refs_3_), custom_call_target="tpu_custom_call" | custom-call | flops 1000 | bytes 1000 | tf_op jit(solution)/shard_map/temporal/pallas_call | solution.py:428
  25.9 0.2 collective-permute-done.8.refs_0_
  26.1 0.4 %collective-permute-done.9.refs_1_ = f32[16,128]{1,0:T(8,128)S(1)} collective-permute-done((f32[16,128]{1,0:T(8,128)S(1)}, f32[16,128]{1,0:T(8,128)S(1)}, u32[]{:S(2)}, u32[]{:S(2)}) %collective-permute-start.9) | collective-permute-done | bytes 8224 | tf_op jit(solution)/shard_map/ppermute | solution.py:340
  26.5 1.0 %collective-permute-done.10.refs_2_ = f32[16,128]{1,0:T(8,128)S(1)} collective-permute-done((f32[16,128]{1,0:T(8,128)S(1)}, f32[16,128]{1,0:T(8,128)S(1)}, u32[]{:S(2)}, u32[]{:S(2)}) %collective-permute-start.10) | collective-permute-done | bytes 8224 | tf_op jit(solution)/shard_map/ppermute | solution.py:340
  27.5 0.7 %means.1 = f32[16,16]{1,0:T(8,128)} custom-call(f32[16,128]{1,0:T(8,128)S(1)} %collective-permute-done.8.refs_0_, f32[16,128]{1,0:T(8,128)S(1)} %collective-permute-done.9.refs_1_, f32[16,128]{1,0:T(8,128)S(1)} %collective-permute-done.10.refs_2_, f32[16,128]{1,0:T(8,128)S(1)} %get-tuple-element.47.refs_3_), custom_call_target="tpu_custom_call" | custom-call | flops 1000 | bytes 1000 | tf_op jit(solution)/shard_map/means/pallas_call | solution.py:436
  (9 shorter events, 0.1 us)
Async XLA Ops:
  1.8 8.0 %collective-permute-start = (f16[48,2048]{1,0:T(8,128)(2,1)S(1)}, f16[48,2048]{1,0:T(8,128)(2,1)S(1)}, u32[]{:S(2)}, u32[]{:S(2)}) collective-permute-start(f16[48,2048]{1,0:T(8,128)(2,1)S(1)} %convert_element_type.12), channel_id=1, source_target_pairs={{1,2},{2,1},{5,6},{6,5},{9,10},{10,9},{13,14},{14,13},{17,18},{18,... | collective-permute-start | bytes 589832 | tf_op jit(solution)/shard_map/ppermute | solution.py:387
  2.5 5.9 %copy-start = (s32[256,16,4]{0,2,1:T(4,128)S(1)}, s32[256,16,4]{0,2,1:T(4,128)}, u32[]{:S(2)}) copy-start(s32[256,16,4]{0,2,1:T(4,128)} %param.7) | copy-start | bytes 196612
  2.5 10.5 %collective-permute-start.1 = (f16[48,2048]{1,0:T(8,128)(2,1)S(1)}, f16[48,2048]{1,0:T(8,128)(2,1)S(1)}, u32[]{:S(2)}, u32[]{:S(2)}) collective-permute-start(f16[48,2048]{1,0:T(8,128)(2,1)S(1)} %convert_element_type.13), channel_id=1, source_target_pairs={{0,1},{1,0},{2,3},{3,2},{4,5},{5,4},{6,7},{7,6},{8,9},{9,8},{10,11... | collective-permute-start | bytes 589832 | tf_op jit(solution)/shard_map/ppermute | solution.py:387
  8.5 0.7 %copy-start.1 = (f32[8,5]{1,0:T(8,128)S(1)}, f32[8,5]{1,0:T(8,128)}, u32[]{:S(2)}) copy-start(f32[8,5]{1,0:T(8,128)} %kernels_ref.1) | copy-start | bytes 484
  8.5 0.7 %copy-start.2 = (s32[8]{0:T(128)S(1)}, s32[8]{0:T(128)}, u32[]{:S(2)}) copy-start(s32[8]{0:T(128)} %band_ref.1) | copy-start | bytes 100
  16.2 3.9 %collective-permute-start.5 = (bf16[48,128]{1,0:T(8,128)(2,1)S(1)}, bf16[48,128]{1,0:T(8,128)(2,1)S(1)}, u32[]{:S(2)}, u32[]{:S(2)}) collective-permute-start(bf16[48,128]{1,0:T(8,128)(2,1)S(1)} %get-tuple-element.57), channel_id=1, source_target_pairs={{0,12},{4,8},{8,4},{12,0},{1,13},{5,9},{9,5},{13,1},{2,14},{6,10},... | collective-permute-start | bytes 36872 | tf_op jit(solution)/shard_map/ppermute | solution.py:340
  16.3 3.8 %collective-permute-start.6 = (bf16[48,128]{1,0:T(8,128)(2,1)S(1)}, bf16[48,128]{1,0:T(8,128)(2,1)S(1)}, u32[]{:S(2)}, u32[]{:S(2)}) collective-permute-start(bf16[48,128]{1,0:T(8,128)(2,1)S(1)} %get-tuple-element.56), channel_id=1, source_target_pairs={{0,8},{4,12},{8,0},{12,4},{1,9},{5,13},{9,1},{13,5},{2,10},{6,14},... | collective-permute-start | bytes 36872 | tf_op jit(solution)/shard_map/ppermute | solution.py:340
  17.9 2.3 %collective-permute-start.7 = (bf16[48,128]{1,0:T(8,128)(2,1)S(1)}, bf16[48,128]{1,0:T(8,128)(2,1)S(1)}, u32[]{:S(2)}, u32[]{:S(2)}) collective-permute-start(bf16[48,128]{1,0:T(8,128)(2,1)S(1)} %get-tuple-element.55), channel_id=1, source_target_pairs={{0,4},{4,0},{8,12},{12,8},{1,5},{5,1},{9,13},{13,9},{2,6},{6,2},{1... | collective-permute-start | bytes 36872 | tf_op jit(solution)/shard_map/ppermute | solution.py:340
  18.2 5.7 %collective-permute-start.2 = (bf16[256,128]{1,0:T(8,128)(2,1)S(1)}, bf16[256,128]{1,0:T(8,128)(2,1)S(1)}, u32[]{:S(2)}, u32[]{:S(2)}) collective-permute-start(bf16[256,128]{1,0:T(8,128)(2,1)S(1)} %get-tuple-element.53), channel_id=1, source_target_pairs={{0,12},{4,8},{8,4},{12,0},{1,13},{5,9},{9,5},{13,1},{2,14},{6,10},... | collective-permute-start | bytes 196616 | tf_op jit(solution)/shard_map/ppermute | solution.py:340
  19.3 5.7 %collective-permute-start.3 = (bf16[256,128]{1,0:T(8,128)(2,1)S(1)}, bf16[256,128]{1,0:T(8,128)(2,1)S(1)}, u32[]{:S(2)}, u32[]{:S(2)}) collective-permute-start(bf16[256,128]{1,0:T(8,128)(2,1)S(1)} %get-tuple-element.52), channel_id=1, source_target_pairs={{0,8},{4,12},{8,0},{12,4},{1,9},{5,13},{9,1},{13,5},{2,10},{6,14},... | collective-permute-start | bytes 196616 | tf_op jit(solution)/shard_map/ppermute | solution.py:340
  20.1 4.9 %collective-permute-start.4 = (bf16[256,128]{1,0:T(8,128)(2,1)S(1)}, bf16[256,128]{1,0:T(8,128)(2,1)S(1)}, u32[]{:S(2)}, u32[]{:S(2)}) collective-permute-start(bf16[256,128]{1,0:T(8,128)(2,1)S(1)} %get-tuple-element.51), channel_id=1, source_target_pairs={{0,4},{4,0},{8,12},{12,8},{1,5},{5,1},{9,13},{13,9},{2,6},{6,2},{1... | collective-permute-start | bytes 196616 | tf_op jit(solution)/shard_map/ppermute | solution.py:340
  20.6 5.6 %collective-permute-start.8 = (f32[16,128]{1,0:T(8,128)S(1)}, f32[16,128]{1,0:T(8,128)S(1)}, u32[]{:S(2)}, u32[]{:S(2)}) collective-permute-start(f32[16,128]{1,0:T(8,128)S(1)} %get-tuple-element.61), channel_id=1, source_target_pairs={{0,3},{1,2},{2,1},{3,0},{4,7},{5,6},{6,5},{7,4},{8,11},{9,10},{10,... | collective-permute-start | bytes 24584 | tf_op jit(solution)/shard_map/ppermute | solution.py:340
  22.0 4.6 %collective-permute-start.9 = (f32[16,128]{1,0:T(8,128)S(1)}, f32[16,128]{1,0:T(8,128)S(1)}, u32[]{:S(2)}, u32[]{:S(2)}) collective-permute-start(f32[16,128]{1,0:T(8,128)S(1)} %get-tuple-element.60), channel_id=1, source_target_pairs={{0,2},{1,3},{2,0},{3,1},{4,6},{5,7},{6,4},{7,5},{8,10},{9,11},{10,... | collective-permute-start | bytes 24584 | tf_op jit(solution)/shard_map/ppermute | solution.py:340
  23.8 3.7 %collective-permute-start.10 = (f32[16,128]{1,0:T(8,128)S(1)}, f32[16,128]{1,0:T(8,128)S(1)}, u32[]{:S(2)}, u32[]{:S(2)}) collective-permute-start(f32[16,128]{1,0:T(8,128)S(1)} %get-tuple-element.59), channel_id=1, source_target_pairs={{0,1},{1,0},{2,3},{3,2},{4,5},{5,4},{6,7},{7,6},{8,9},{9,8},{10,11... | collective-permute-start | bytes 24584 | tf_op jit(solution)/shard_map/ppermute | solution.py:340

commit v13 on v11

--- a/solution.py
+++ b/solution.py
@@ -201,19 +201,21 @@
                 weights = [taps_ref[slot, row : row + BAND, :] for slot in range(len(SIDES))]
                 for frame in range(frames):
                     rows = slice(PAD + row, PAD + row + BAND)
-                    blurred = source_ref[frame, rows, :]
+                    terms = []
                     for weight, tap in zip(weights, SIDES):
                         start = PAD + row + tap - TAPS // 2
-                        blurred = blurred + weight * source_ref[frame, start : start + BAND, :]
+                        terms.append(weight * source_ref[frame, start : start + BAND, :])
+                    blurred = source_ref[frame, rows, :] + ((terms[0] + terms[1]) + (terms[2] + terms[3]))
                     quotient_ref[frame, rows, :] = image_ref[frame, rows, :] / blurred
             for row in range(back_first, back_last, BAND):
                 weights = [back_ref[slot, row : row + BAND, :] for slot in range(len(SIDES))]
                 for frame in range(frames):
                     rows = slice(PAD + row, PAD + row + BAND)
-                    spread = quotient_ref[frame, rows, :]
+                    terms = []
                     for weight, tap in zip(weights, SIDES):
                         start = PAD + row - tap + TAPS // 2
-                        spread = spread + weight * quotient_ref[frame, start : start + BAND, :]
+                        terms.append(weight * quotient_ref[frame, start : start + BAND, :])
+                    spread = quotient_ref[frame, rows, :] + ((terms[0] + terms[1]) + (terms[2] + terms[3]))
                     current_ref[frame, rows, :] = source_ref[frame, rows, :] * spread
             source_ref = current_ref
         first = pl.multiple_of(lax.rem(step, tiles_dev) * rows_dev, rows_dev)
@@ -223,7 +225,7 @@
             out_ref[step // tiles_dev, pl.ds(start, rows_dev), :] = estimate
         return carry
 
-    lax.fori_loop(0, n_frame * tiles_dev, columns_step, 0)
+    lax.fori_loop(0, n_frame * tiles_dev, columns_step, 0, unroll=2)
     lane_tiles = lax.broadcasted_iota(jnp.int32, (TILE, TILE), 1) % tiles_dev
     gathered = jnp.zeros((frames * n_frame * rows_dev, TILE), jnp.float32)
     for tile in range(tiles_dev):
@@ -370,10 +372,14 @@
 
     packed = array(frames * (NEAR + FAR), width)
     inner, outer, own = call(halo_kernel, "halo", [vmem], (packed, packed, array(*observed.shape)))(observed)
-    swaps = [
-        [pair for i in range(first, n_row - 1, 2) for pair in ((i, i + 1), (i + 1, i))] for first in (0, 1)
-    ]
-    inner, outer = (lax.ppermute(rows.astype(jnp.float16), "row", swap) for rows, swap in zip((inner, outer), swaps))
+    inner_swap = [(i, i ^ 1) for i in range(n_row)]
+    outer_swap = []
+    for f in range(n_frame):
+        for i in range(n_row):
+            there = (f ^ 1, i) if i in (0, n_row - 1) else (f, (i - 1 ^ 1) + 1)
+            outer_swap.append((f * n_row + i, there[0] * n_row + there[1]))
+    outer = lax.ppermute(outer.astype(jnp.float16), ("frame", "row"), outer_swap)
+    inner = lax.ppermute(inner.astype(jnp.float16), "row", inner_swap)
     outer, inner = in_turn(outer, inner)
     taps, back = call(
         functools.partial(taps_kernel, height=rows_dev * n_row, rows_dev=rows_dev),

time: 28.4 us -> 27.8 us (0.979)
  starting transfers between devices: 14.9 us -> 13.1 us
  waiting for transfers between devices: 4.76 us -> 6.2 us
    ppermute x2, starting transfers between devices: 6.57 us -> 4.73 us  [the longest x1 4.21 us: by_halo(): inner = lax.ppermute(inner.astype(jnp.float16), 'row', inner_swap)]
    ppermute x9, waiting for transfers between devices: 1.55 us -> 2.99 us  [swapped(): lax.ppermute(part, axis, [(i, i ^ step) for i in range(count)])]
  transfers between devices with their start and end apart: 11 -> 11, of which waited for: 4 -> 3; matrix products, arithmetic and copies ran while one was open for 0% -> 0% of each run, Pallas kernels for 8% -> 8%
where the time goes in v13:
time: 27.8 us; the launch traced here: 27.6 us
  starting transfers between devices  13.1 us (47%)
  waiting for transfers between devices  6.2 us (22%)
  Pallas kernels  5.77 us (21%)
  local copies, waits for them, and re-layouts  1.67 us (6%)
  between operations  0.75 us (3%)
    ppermute x9, starting transfers between devices, swapped(): lax.ppermute(part, axis, [(i, i ^ step) for i in range(count)])  8.36 us
    ppermute x1, starting transfers between devices, by_halo(): inner = lax.ppermute(inner.astype(jnp.float16), 'row', inner_swap)  4.21 us
    ppermute x1, waiting for transfers between devices, by_halo(): inner = lax.ppermute(inner.astype(jnp.float16), 'row', inner_swap)  3.2 us
    ppermute x9, waiting for transfers between devices, swapped(): lax.ppermute(part, axis, [(i, i ^ step) for i in range(count)])  2.99 us
    pallas_call x1, Pallas kernels, by_halo(): call(restore_kernel, 'restore', [vmem] * 6, (array(n_frame, frames * posi...  2.84 us
    unnamed x8, local copies, waits for them, and re-layouts  1.62 us
    pallas_call x1, Pallas kernels, by_halo(): call(functools.partial(temporal_kernel, frames=frames), 'temporal', [vmem...  0.92 us
    pallas_call x1, Pallas kernels, by_halo(): call(functools.partial(taps_kernel, height=rows_dev * n_row, rows_dev=row...  0.69 us
  transfers between devices with their start and end apart: 11, of which 3 were waited for; matrix products, arithmetic and copies ran while one was open for 0% of the time, Pallas kernels for 8%

profile of v13, /device:TPU:0, one launch (start us, length us, event | category | flops | bytes accessed | tf_op | source)
XLA Modules:
  0.0 27.6 jit_solution(17503572668996945486)
XLA Ops:
  0.6 1.0 %copy-done = f32[4,16,2048]{2,1,0:T(8,128)S(1)} copy-done((f32[4,16,2048]{2,1,0:T(8,128)S(1)}, f32[4,16,2048]{2,1,0:T(8,128)}, u32[]{:S(2)}) %copy-start) | copy-done | bytes 524312
  1.7 0.1 halo.1
  1.8 0.5 %collective-permute-start = (f16[48,2048]{1,0:T(8,128)(2,1)S(1)}, f16[48,2048]{1,0:T(8,128)(2,1)S(1)}, u32[]{:S(2)}, u32[]{:S(2)}) collective-permute-start(f16[48,2048]{1,0:T(8,128)(2,1)S(1)} %convert_element_type.12), channel_id=1, source_target_pairs={{0,4},{1,2},{2,1},{3,7},{4,0},{5,6},{6,5},{7,3},{8,12},{9,10},{10,... | collective-permute-start | bytes 589832 | tf_op jit(solution)/shard_map/ppermute | solution.py:381
  2.4 4.2 %collective-permute-start.1 = (f16[48,2048]{1,0:T(8,128)(2,1)S(1)}, f16[48,2048]{1,0:T(8,128)(2,1)S(1)}, u32[]{:S(2)}, u32[]{:S(2)}) collective-permute-start(f16[48,2048]{1,0:T(8,128)(2,1)S(1)} %convert_element_type.13), channel_id=1, source_target_pairs={{0,1},{1,0},{2,3},{3,2},{4,5},{5,4},{6,7},{7,6},{8,9},{9,8},{10,11... | collective-permute-start | bytes 589832 | tf_op jit(solution)/shard_map/ppermute | solution.py:382
  6.6 0.1 feet.1.feet_ref
  6.7 0.6 %copy-done.2 = f32[8,5]{1,0:T(8,128)S(1)} copy-done((f32[8,5]{1,0:T(8,128)S(1)}, f32[8,5]{1,0:T(8,128)}, u32[]{:S(2)}) %copy-start.2) | copy-done | bytes 184
  7.3 0.7 %taps.1 = (f32[4,48,128]{2,1,0:T(8,128)S(1)}, f32[4,48,128]{2,1,0:T(8,128)S(1)}) custom-call(s32[8]{0:T(128)S(1)} %copy-done.3, f32[8,5]{1,0:T(8,128)S(1)} %copy-done.2), custom_call_target="tpu_custom_call" | custom-call | flops 1000 | bytes 1000 | tf_op jit(solution)/shard_map/taps/pallas_call | solution.py:384
  8.0 0.0 collective-permute-done
  8.0 3.2 %collective-permute-done.1 = f16[48,2048]{1,0:T(8,128)(2,1)S(1)} collective-permute-done((f16[48,2048]{1,0:T(8,128)(2,1)S(1)}, f16[48,2048]{1,0:T(8,128)(2,1)S(1)}, u32[]{:S(2)}, u32[]{:S(2)}) %collective-permute-start.1) | collective-permute-done | bytes 196640 | tf_op jit(solution)/shard_map/ppermute | solution.py:382
  11.2 0.1 convert_select_fusion
  11.3 2.8 %restore.1 = (bf16[4,256,128]{2,1,0:T(8,128)(2,1)S(1)}, bf16[4,48,128]{2,1,0:T(8,128)(2,1)S(1)}) custom-call(f32[4,48,128]{2,1,0:T(8,128)S(1)} %get-tuple-element.25.taps_ref, f32[4,48,128]{2,1,0:T(8,128)S(1)} %get-tuple-element.26.back_ref, bf16[4,32,128]{2,1,0:T(8,128)(2,1)S(1)} %feet.1.feet_ref, f32[4,16,2048]{2,1,0:T(8,128)S(1)} %get-tuple-element.27.own_ref, ...), custom_call_target="tpu_custom_call" | custom-call | flops 1000 | bytes 1000 | tf_op jit(solution)/shard_map/restore/pallas_call | solution.py:400
  14.2 0.1 collective-permute-start.5
  14.3 1.5 %collective-permute-start.6 = (bf16[48,128]{1,0:T(8,128)(2,1)S(1)}, bf16[48,128]{1,0:T(8,128)(2,1)S(1)}, u32[]{:S(2)}, u32[]{:S(2)}) collective-permute-start(bf16[48,128]{1,0:T(8,128)(2,1)S(1)} %get-tuple-element.56), channel_id=1, source_target_pairs={{0,8},{4,12},{8,0},{12,4},{1,9},{5,13},{9,1},{13,5},{2,10},{6,14},... | collective-permute-start | bytes 36872 | tf_op jit(solution)/shard_map/ppermute | solution.py:337
  15.8 0.3 %collective-permute-start.7 = (bf16[48,128]{1,0:T(8,128)(2,1)S(1)}, bf16[48,128]{1,0:T(8,128)(2,1)S(1)}, u32[]{:S(2)}, u32[]{:S(2)}) collective-permute-start(bf16[48,128]{1,0:T(8,128)(2,1)S(1)} %get-tuple-element.55), channel_id=1, source_target_pairs={{0,4},{4,0},{8,12},{12,8},{1,5},{5,1},{9,13},{13,9},{2,6},{6,2},{1... | collective-permute-start | bytes 36872 | tf_op jit(solution)/shard_map/ppermute | solution.py:337
  16.1 1.2 %collective-permute-start.2 = (bf16[256,128]{1,0:T(8,128)(2,1)S(1)}, bf16[256,128]{1,0:T(8,128)(2,1)S(1)}, u32[]{:S(2)}, u32[]{:S(2)}) collective-permute-start(bf16[256,128]{1,0:T(8,128)(2,1)S(1)} %get-tuple-element.53), channel_id=1, source_target_pairs={{0,12},{4,8},{8,4},{12,0},{1,13},{5,9},{9,5},{13,1},{2,14},{6,10},... | collective-permute-start | bytes 196616 | tf_op jit(solution)/shard_map/ppermute | solution.py:337
  17.3 0.8 %collective-permute-start.3 = (bf16[256,128]{1,0:T(8,128)(2,1)S(1)}, bf16[256,128]{1,0:T(8,128)(2,1)S(1)}, u32[]{:S(2)}, u32[]{:S(2)}) collective-permute-start(bf16[256,128]{1,0:T(8,128)(2,1)S(1)} %get-tuple-element.52), channel_id=1, source_target_pairs={{0,8},{4,12},{8,0},{12,4},{1,9},{5,13},{9,1},{13,5},{2,10},{6,14},... | collective-permute-start | bytes 196616 | tf_op jit(solution)/shard_map/ppermute | solution.py:337
  18.0 0.0 collective-permute-done.5.refs_0_
  18.0 0.0 collective-permute-start.4
  18.0 0.0 collective-permute-done.6.refs_1_
  18.0 0.0 collective-permute-done.7.refs_2_
  18.1 0.4 %partial.1 = f32[4,16,128]{2,1,0:T(8,128)S(1)} custom-call(bf16[48,128]{1,0:T(8,128)(2,1)S(1)} %collective-permute-done.5.refs_0_, bf16[48,128]{1,0:T(8,128)(2,1)S(1)} %collective-permute-done.6.refs_1_, bf16[48,128]{1,0:T(8,128)(2,1)S(1)} %collective-permute-done.7.refs_2_, bf16[48,128]{1,0:T(8,128)(2,1)S(1)} %get-tuple-element.54.refs_3_), custom_call_target="tpu_custom_call" | custom-call | flops 1000 | bytes 1000 | tf_op jit(solution)/shard_map/partial/pallas_call | solution.py:412
  18.5 3.9 %collective-permute-start.8 = (f32[16,128]{1,0:T(8,128)S(1)}, f32[16,128]{1,0:T(8,128)S(1)}, u32[]{:S(2)}, u32[]{:S(2)}) collective-permute-start(f32[16,128]{1,0:T(8,128)S(1)} %get-tuple-element.61), channel_id=1, source_target_pairs={{0,3},{1,2},{2,1},{3,0},{4,7},{5,6},{6,5},{7,4},{8,11},{9,10},{10,... | collective-permute-start | bytes 24584 | tf_op jit(solution)/shard_map/ppermute | solution.py:337
  22.4 0.0 collective-permute-start.9
  22.4 0.0 collective-permute-done.2.refs_0_
  22.4 0.6 %collective-permute-start.10 = (f32[16,128]{1,0:T(8,128)S(1)}, f32[16,128]{1,0:T(8,128)S(1)}, u32[]{:S(2)}, u32[]{:S(2)}) collective-permute-start(f32[16,128]{1,0:T(8,128)S(1)} %get-tuple-element.59), channel_id=1, source_target_pairs={{0,1},{1,0},{2,3},{3,2},{4,5},{5,4},{6,7},{7,6},{8,9},{9,8},{10,11... | collective-permute-start | bytes 24584 | tf_op jit(solution)/shard_map/ppermute | solution.py:337
  23.0 0.0 collective-permute-done.3.refs_1_
  23.0 0.0 collective-permute-done.4.refs_2_
  23.0 0.9 %temporal.1 = bf16[16,16,512]{2,1,0:T(8,128)(2,1)} custom-call(bf16[256,128]{1,0:T(8,128)(2,1)S(1)} %collective-permute-done.2.refs_0_, bf16[256,128]{1,0:T(8,128)(2,1)S(1)} %collective-permute-done.3.refs_1_, bf16[256,128]{1,0:T(8,128)(2,1)S(1)} %collective-permute-done.4.refs_2_, bf16[256,128]{1,0:T(8,128)(2,1)S(1)} %get-tuple-element.50.refs_3_), custom_call_target="tpu_custom_call" | custom-call | flops 1000 | bytes 1000 | tf_op jit(solution)/shard_map/temporal/pallas_call | solution.py:423
  23.9 0.1 collective-permute-done.8.refs_0_
  24.0 2.9 %collective-permute-done.9.refs_1_ = f32[16,128]{1,0:T(8,128)S(1)} collective-permute-done((f32[16,128]{1,0:T(8,128)S(1)}, f32[16,128]{1,0:T(8,128)S(1)}, u32[]{:S(2)}, u32[]{:S(2)}) %collective-permute-start.9) | collective-permute-done | bytes 8224 | tf_op jit(solution)/shard_map/ppermute | solution.py:337
  26.9 0.0 collective-permute-done.10.refs_2_
  26.9 0.7 %means.1 = f32[16,16]{1,0:T(8,128)} custom-call(f32[16,128]{1,0:T(8,128)S(1)} %collective-permute-done.8.refs_0_, f32[16,128]{1,0:T(8,128)S(1)} %collective-permute-done.9.refs_1_, f32[16,128]{1,0:T(8,128)S(1)} %collective-permute-done.10.refs_2_, f32[16,128]{1,0:T(8,128)S(1)} %get-tuple-element.47.refs_3_), custom_call_target="tpu_custom_call" | custom-call | flops 1000 | bytes 1000 | tf_op jit(solution)/shard_map/means/pallas_call | solution.py:431
  (11 shorter events, 0.1 us)
Async XLA Ops:
  0.6 1.0 %copy-start = (f32[4,16,2048]{2,1,0:T(8,128)S(1)}, f32[4,16,2048]{2,1,0:T(8,128)}, u32[]{:S(2)}) copy-start(f32[4,16,2048]{2,1,0:T(8,128)} %observed_ref.1) | copy-start | bytes 1572868
  1.8 6.2 %collective-permute-start = (f16[48,2048]{1,0:T(8,128)(2,1)S(1)}, f16[48,2048]{1,0:T(8,128)(2,1)S(1)}, u32[]{:S(2)}, u32[]{:S(2)}) collective-permute-start(f16[48,2048]{1,0:T(8,128)(2,1)S(1)} %convert_element_type.12), channel_id=1, source_target_pairs={{0,4},{1,2},{2,1},{3,7},{4,0},{5,6},{6,5},{7,3},{8,12},{9,10},{10,... | collective-permute-start | bytes 589832 | tf_op jit(solution)/shard_map/ppermute | solution.py:381
  2.3 4.2 %copy-start.1 = (s32[256,16,4]{0,2,1:T(4,128)S(1)}, s32[256,16,4]{0,2,1:T(4,128)}, u32[]{:S(2)}) copy-start(s32[256,16,4]{0,2,1:T(4,128)} %param.7) | copy-start | bytes 196612
  2.4 8.8 %collective-permute-start.1 = (f16[48,2048]{1,0:T(8,128)(2,1)S(1)}, f16[48,2048]{1,0:T(8,128)(2,1)S(1)}, u32[]{:S(2)}, u32[]{:S(2)}) collective-permute-start(f16[48,2048]{1,0:T(8,128)(2,1)S(1)} %convert_element_type.13), channel_id=1, source_target_pairs={{0,1},{1,0},{2,3},{3,2},{4,5},{5,4},{6,7},{7,6},{8,9},{9,8},{10,11... | collective-permute-start | bytes 589832 | tf_op jit(solution)/shard_map/ppermute | solution.py:382
  6.6 0.7 %copy-start.2 = (f32[8,5]{1,0:T(8,128)S(1)}, f32[8,5]{1,0:T(8,128)}, u32[]{:S(2)}) copy-start(f32[8,5]{1,0:T(8,128)} %kernels_ref.1) | copy-start | bytes 484
  6.6 0.7 %copy-start.3 = (s32[8]{0:T(128)S(1)}, s32[8]{0:T(128)}, u32[]{:S(2)}) copy-start(s32[8]{0:T(128)} %band_ref.1) | copy-start | bytes 100
  14.2 3.9 %collective-permute-start.5 = (bf16[48,128]{1,0:T(8,128)(2,1)S(1)}, bf16[48,128]{1,0:T(8,128)(2,1)S(1)}, u32[]{:S(2)}, u32[]{:S(2)}) collective-permute-start(bf16[48,128]{1,0:T(8,128)(2,1)S(1)} %get-tuple-element.57), channel_id=1, source_target_pairs={{0,12},{4,8},{8,4},{12,0},{1,13},{5,9},{9,5},{13,1},{2,14},{6,10},... | collective-permute-start | bytes 36872 | tf_op jit(solution)/shard_map/ppermute | solution.py:337
  14.3 3.8 %collective-permute-start.6 = (bf16[48,128]{1,0:T(8,128)(2,1)S(1)}, bf16[48,128]{1,0:T(8,128)(2,1)S(1)}, u32[]{:S(2)}, u32[]{:S(2)}) collective-permute-start(bf16[48,128]{1,0:T(8,128)(2,1)S(1)} %get-tuple-element.56), channel_id=1, source_target_pairs={{0,8},{4,12},{8,0},{12,4},{1,9},{5,13},{9,1},{13,5},{2,10},{6,14},... | collective-permute-start | bytes 36872 | tf_op jit(solution)/shard_map/ppermute | solution.py:337
  15.8 2.2 %collective-permute-start.7 = (bf16[48,128]{1,0:T(8,128)(2,1)S(1)}, bf16[48,128]{1,0:T(8,128)(2,1)S(1)}, u32[]{:S(2)}, u32[]{:S(2)}) collective-permute-start(bf16[48,128]{1,0:T(8,128)(2,1)S(1)} %get-tuple-element.55), channel_id=1, source_target_pairs={{0,4},{4,0},{8,12},{12,8},{1,5},{5,1},{9,13},{13,9},{2,6},{6,2},{1... | collective-permute-start | bytes 36872 | tf_op jit(solution)/shard_map/ppermute | solution.py:337
  16.1 6.3 %collective-permute-start.2 = (bf16[256,128]{1,0:T(8,128)(2,1)S(1)}, bf16[256,128]{1,0:T(8,128)(2,1)S(1)}, u32[]{:S(2)}, u32[]{:S(2)}) collective-permute-start(bf16[256,128]{1,0:T(8,128)(2,1)S(1)} %get-tuple-element.53), channel_id=1, source_target_pairs={{0,12},{4,8},{8,4},{12,0},{1,13},{5,9},{9,5},{13,1},{2,14},{6,10},... | collective-permute-start | bytes 196616 | tf_op jit(solution)/shard_map/ppermute | solution.py:337
  17.3 5.7 %collective-permute-start.3 = (bf16[256,128]{1,0:T(8,128)(2,1)S(1)}, bf16[256,128]{1,0:T(8,128)(2,1)S(1)}, u32[]{:S(2)}, u32[]{:S(2)}) collective-permute-start(bf16[256,128]{1,0:T(8,128)(2,1)S(1)} %get-tuple-element.52), channel_id=1, source_target_pairs={{0,8},{4,12},{8,0},{12,4},{1,9},{5,13},{9,1},{13,5},{2,10},{6,14},... | collective-permute-start | bytes 196616 | tf_op jit(solution)/shard_map/ppermute | solution.py:337
  18.0 5.0 %collective-permute-start.4 = (bf16[256,128]{1,0:T(8,128)(2,1)S(1)}, bf16[256,128]{1,0:T(8,128)(2,1)S(1)}, u32[]{:S(2)}, u32[]{:S(2)}) collective-permute-start(bf16[256,128]{1,0:T(8,128)(2,1)S(1)} %get-tuple-element.51), channel_id=1, source_target_pairs={{0,4},{4,0},{8,12},{12,8},{1,5},{5,1},{9,13},{13,9},{2,6},{6,2},{1... | collective-permute-start | bytes 196616 | tf_op jit(solution)/shard_map/ppermute | solution.py:337
  18.5 5.5 %collective-permute-start.8 = (f32[16,128]{1,0:T(8,128)S(1)}, f32[16,128]{1,0:T(8,128)S(1)}, u32[]{:S(2)}, u32[]{:S(2)}) collective-permute-start(f32[16,128]{1,0:T(8,128)S(1)} %get-tuple-element.61), channel_id=1, source_target_pairs={{0,3},{1,2},{2,1},{3,0},{4,7},{5,6},{6,5},{7,4},{8,11},{9,10},{10,... | collective-permute-start | bytes 24584 | tf_op jit(solution)/shard_map/ppermute | solution.py:337
  22.4 4.5 %collective-permute-start.9 = (f32[16,128]{1,0:T(8,128)S(1)}, f32[16,128]{1,0:T(8,128)S(1)}, u32[]{:S(2)}, u32[]{:S(2)}) collective-permute-start(f32[16,128]{1,0:T(8,128)S(1)} %get-tuple-element.60), channel_id=1, source_target_pairs={{0,2},{1,3},{2,0},{3,1},{4,6},{5,7},{6,4},{7,5},{8,10},{9,11},{10,... | collective-permute-start | bytes 24584 | tf_op jit(solution)/shard_map/ppermute | solution.py:337
  22.4 4.5 %collective-permute-start.10 = (f32[16,128]{1,0:T(8,128)S(1)}, f32[16,128]{1,0:T(8,128)S(1)}, u32[]{:S(2)}, u32[]{:S(2)}) collective-permute-start(f32[16,128]{1,0:T(8,128)S(1)} %get-tuple-element.59), channel_id=1, source_target_pairs={{0,1},{1,0},{2,3},{3,2},{4,5},{5,4},{6,7},{7,6},{8,9},{9,8},{10,11... | collective-permute-start | bytes 24584 | tf_op jit(solution)/shard_map/ppermute | solution.py:337

commit v14 on v13

--- a/solution.py
+++ b/solution.py
@@ -378,9 +378,9 @@
         for i in range(n_row):
             there = (f ^ 1, i) if i in (0, n_row - 1) else (f, (i - 1 ^ 1) + 1)
             outer_swap.append((f * n_row + i, there[0] * n_row + there[1]))
+    inner = lax.ppermute(inner.astype(jnp.float16), "row", inner_swap)
     outer = lax.ppermute(outer.astype(jnp.float16), ("frame", "row"), outer_swap)
-    inner = lax.ppermute(inner.astype(jnp.float16), "row", inner_swap)
-    outer, inner = in_turn(outer, inner)
+    inner, outer = in_turn(inner, outer)
     taps, back = call(
         functools.partial(taps_kernel, height=rows_dev * n_row, rows_dev=rows_dev),
         "taps",

time: 27.8 us -> 26.4 us (0.950)
  starting transfers between devices: 13.1 us -> 11.8 us
  waiting for transfers between devices: 6.2 us -> 5.35 us
  local copies, waits for them, and re-layouts: 1.67 us -> 2.4 us
    ppermute x1, starting transfers between devices: 4.21 us -> 3.09 us  [by_halo(): inner = lax.ppermute(inner.astype(jnp.float16), 'row', inner_swap)]
    unnamed x8, local copies, waits for them, and re-layouts: 1.62 us -> 2.35 us
    ppermute x1, waiting for transfers between devices: 3.2 us -> 2.66 us  [by_halo(): inner = lax.ppermute(inner.astype(jnp.float16), 'row', inner_swap)]
    ppermute x1, starting transfers between devices: 0.52 us -> 0.07 us  [by_halo(): lax.ppermute(outer.astype(jnp.float16), ('frame', 'row'), outer_swap)]
    ppermute x9, waiting for transfers between devices: 2.99 us -> 2.69 us  [swapped(): lax.ppermute(part, axis, [(i, i ^ step) for i in range(count)])]
  transfers between devices with their start and end apart: 11 -> 11, of which waited for: 3 -> 2; matrix products, arithmetic and copies ran while one was open for 0% -> 0% of each run, Pallas kernels for 8% -> 8%
where the time goes in v14:
time: 26.4 us; the launch traced here: 26.2 us
  starting transfers between devices  11.8 us (45%)
  Pallas kernels  5.77 us (22%)
  waiting for transfers between devices  5.35 us (20%)
  local copies, waits for them, and re-layouts  2.4 us (9%)
  between operations  0.75 us (3%)
    ppermute x9, starting transfers between devices, swapped(): lax.ppermute(part, axis, [(i, i ^ step) for i in range(count)])  8.61 us
    ppermute x1, starting transfers between devices, by_halo(): inner = lax.ppermute(inner.astype(jnp.float16), 'row', inner_swap)  3.09 us
    pallas_call x1, Pallas kernels, by_halo(): call(restore_kernel, 'restore', [vmem] * 6, (array(n_frame, frames * posi...  2.84 us
    ppermute x9, waiting for transfers between devices, swapped(): lax.ppermute(part, axis, [(i, i ^ step) for i in range(count)])  2.69 us
    ppermute x1, waiting for transfers between devices, by_halo(): inner = lax.ppermute(inner.astype(jnp.float16), 'row', inner_swap)  2.66 us
    unnamed x8, local copies, waits for them, and re-layouts  2.35 us
    pallas_call x1, Pallas kernels, by_halo(): call(functools.partial(temporal_kernel, frames=frames), 'temporal', [vmem...  0.92 us
    pallas_call x1, Pallas kernels, by_halo(): call(functools.partial(taps_kernel, height=rows_dev * n_row, rows_dev=row...  0.69 us
  transfers between devices with their start and end apart: 11, of which 2 were waited for; matrix products, arithmetic and copies ran while one was open for 0% of the time, Pallas kernels for 8%

profile of v14, /device:TPU:0, one launch (start us, length us, event | category | flops | bytes accessed | tf_op | source)
XLA Modules:
  0.0 26.2 jit_solution(11974075724826128050)
XLA Ops:
  0.6 1.0 %copy-done = f32[4,16,2048]{2,1,0:T(8,128)S(1)} copy-done((f32[4,16,2048]{2,1,0:T(8,128)S(1)}, f32[4,16,2048]{2,1,0:T(8,128)}, u32[]{:S(2)}) %copy-start) | copy-done | bytes 524312
  1.7 0.1 halo.1
  1.8 3.1 %collective-permute-start = (f16[48,2048]{1,0:T(8,128)(2,1)S(1)}, f16[48,2048]{1,0:T(8,128)(2,1)S(1)}, u32[]{:S(2)}, u32[]{:S(2)}) collective-permute-start(f16[48,2048]{1,0:T(8,128)(2,1)S(1)} %convert_element_type.12), channel_id=1, source_target_pairs={{0,1},{1,0},{2,3},{3,2},{4,5},{5,4},{6,7},{7,6},{8,9},{9,8},{10,11... | collective-permute-start | bytes 589832 | tf_op jit(solution)/shard_map/ppermute | solution.py:381
  4.9 0.1 collective-permute-start.1
  5.0 0.7 %copy-done.1 = s32[256,16,4]{0,2,1:T(4,128)S(1)} copy-done((s32[256,16,4]{0,2,1:T(4,128)S(1)}, s32[256,16,4]{0,2,1:T(4,128)}, u32[]{:S(2)}) %copy-start.1) | copy-done | bytes 65560
  5.8 0.1 feet.1.feet_ref
  5.9 0.6 %copy-done.2 = f32[8,5]{1,0:T(8,128)S(1)} copy-done((f32[8,5]{1,0:T(8,128)S(1)}, f32[8,5]{1,0:T(8,128)}, u32[]{:S(2)}) %copy-start.2) | copy-done | bytes 184
  6.4 0.7 %taps.1 = (f32[4,48,128]{2,1,0:T(8,128)S(1)}, f32[4,48,128]{2,1,0:T(8,128)S(1)}) custom-call(s32[8]{0:T(128)S(1)} %copy-done.3, f32[8,5]{1,0:T(8,128)S(1)} %copy-done.2), custom_call_target="tpu_custom_call" | custom-call | flops 1000 | bytes 1000 | tf_op jit(solution)/shard_map/taps/pallas_call | solution.py:384
  7.2 2.7 %collective-permute-done = f16[48,2048]{1,0:T(8,128)(2,1)S(1)} collective-permute-done((f16[48,2048]{1,0:T(8,128)(2,1)S(1)}, f16[48,2048]{1,0:T(8,128)(2,1)S(1)}, u32[]{:S(2)}, u32[]{:S(2)}) %collective-permute-start) | collective-permute-done | bytes 196640 | tf_op jit(solution)/shard_map/ppermute | solution.py:381
  9.8 0.0 collective-permute-done.1
  9.8 0.1 convert_select_fusion
  9.9 2.8 %restore.1 = (bf16[4,256,128]{2,1,0:T(8,128)(2,1)S(1)}, bf16[4,48,128]{2,1,0:T(8,128)(2,1)S(1)}) custom-call(f32[4,48,128]{2,1,0:T(8,128)S(1)} %get-tuple-element.25.taps_ref, f32[4,48,128]{2,1,0:T(8,128)S(1)} %get-tuple-element.26.back_ref, bf16[4,32,128]{2,1,0:T(8,128)(2,1)S(1)} %feet.1.feet_ref, f32[4,16,2048]{2,1,0:T(8,128)S(1)} %get-tuple-element.27.own_ref, ...), custom_call_target="tpu_custom_call" | custom-call | flops 1000 | bytes 1000 | tf_op jit(solution)/shard_map/restore/pallas_call | solution.py:400
  12.8 0.3 %collective-permute-start.5 = (bf16[48,128]{1,0:T(8,128)(2,1)S(1)}, bf16[48,128]{1,0:T(8,128)(2,1)S(1)}, u32[]{:S(2)}, u32[]{:S(2)}) collective-permute-start(bf16[48,128]{1,0:T(8,128)(2,1)S(1)} %get-tuple-element.57), channel_id=1, source_target_pairs={{0,12},{4,8},{8,4},{12,0},{1,13},{5,9},{9,5},{13,1},{2,14},{6,10},... | collective-permute-start | bytes 36872 | tf_op jit(solution)/shard_map/ppermute | solution.py:337
  13.1 1.5 %collective-permute-start.6 = (bf16[48,128]{1,0:T(8,128)(2,1)S(1)}, bf16[48,128]{1,0:T(8,128)(2,1)S(1)}, u32[]{:S(2)}, u32[]{:S(2)}) collective-permute-start(bf16[48,128]{1,0:T(8,128)(2,1)S(1)} %get-tuple-element.56), channel_id=1, source_target_pairs={{0,8},{4,12},{8,0},{12,4},{1,9},{5,13},{9,1},{13,5},{2,10},{6,14},... | collective-permute-start | bytes 36872 | tf_op jit(solution)/shard_map/ppermute | solution.py:337
  14.6 0.1 collective-permute-start.7
  14.8 1.3 %collective-permute-start.2 = (bf16[256,128]{1,0:T(8,128)(2,1)S(1)}, bf16[256,128]{1,0:T(8,128)(2,1)S(1)}, u32[]{:S(2)}, u32[]{:S(2)}) collective-permute-start(bf16[256,128]{1,0:T(8,128)(2,1)S(1)} %get-tuple-element.53), channel_id=1, source_target_pairs={{0,12},{4,8},{8,4},{12,0},{1,13},{5,9},{9,5},{13,1},{2,14},{6,10},... | collective-permute-start | bytes 196616 | tf_op jit(solution)/shard_map/ppermute | solution.py:337
  16.1 0.8 %collective-permute-start.3 = (bf16[256,128]{1,0:T(8,128)(2,1)S(1)}, bf16[256,128]{1,0:T(8,128)(2,1)S(1)}, u32[]{:S(2)}, u32[]{:S(2)}) collective-permute-start(bf16[256,128]{1,0:T(8,128)(2,1)S(1)} %get-tuple-element.52), channel_id=1, source_target_pairs={{0,8},{4,12},{8,0},{12,4},{1,9},{5,13},{9,1},{13,5},{2,10},{6,14},... | collective-permute-start | bytes 196616 | tf_op jit(solution)/shard_map/ppermute | solution.py:337
  16.8 0.0 collective-permute-done.5.refs_0_
  16.8 0.0 collective-permute-start.4
  16.8 0.0 collective-permute-done.7.refs_2_
  16.8 0.4 %partial.1 = f32[4,16,128]{2,1,0:T(8,128)S(1)} custom-call(bf16[48,128]{1,0:T(8,128)(2,1)S(1)} %collective-permute-done.5.refs_0_, bf16[48,128]{1,0:T(8,128)(2,1)S(1)} %collective-permute-done.6.refs_1_, bf16[48,128]{1,0:T(8,128)(2,1)S(1)} %collective-permute-done.7.refs_2_, bf16[48,128]{1,0:T(8,128)(2,1)S(1)} %get-tuple-element.54.refs_3_), custom_call_target="tpu_custom_call" | custom-call | flops 1000 | bytes 1000 | tf_op jit(solution)/shard_map/partial/pallas_call | solution.py:412
  17.3 3.7 %collective-permute-start.8 = (f32[16,128]{1,0:T(8,128)S(1)}, f32[16,128]{1,0:T(8,128)S(1)}, u32[]{:S(2)}, u32[]{:S(2)}) collective-permute-start(f32[16,128]{1,0:T(8,128)S(1)} %get-tuple-element.61), channel_id=1, source_target_pairs={{0,3},{1,2},{2,1},{3,0},{4,7},{5,6},{6,5},{7,4},{8,11},{9,10},{10,... | collective-permute-start | bytes 24584 | tf_op jit(solution)/shard_map/ppermute | solution.py:337
  20.9 0.7 %collective-permute-start.9 = (f32[16,128]{1,0:T(8,128)S(1)}, f32[16,128]{1,0:T(8,128)S(1)}, u32[]{:S(2)}, u32[]{:S(2)}) collective-permute-start(f32[16,128]{1,0:T(8,128)S(1)} %get-tuple-element.60), channel_id=1, source_target_pairs={{0,2},{1,3},{2,0},{3,1},{4,6},{5,7},{6,4},{7,5},{8,10},{9,11},{10,... | collective-permute-start | bytes 24584 | tf_op jit(solution)/shard_map/ppermute | solution.py:337
  21.6 0.0 collective-permute-done.2.refs_0_
  21.6 0.3 %collective-permute-start.10 = (f32[16,128]{1,0:T(8,128)S(1)}, f32[16,128]{1,0:T(8,128)S(1)}, u32[]{:S(2)}, u32[]{:S(2)}) collective-permute-start(f32[16,128]{1,0:T(8,128)S(1)} %get-tuple-element.59), channel_id=1, source_target_pairs={{0,1},{1,0},{2,3},{3,2},{4,5},{5,4},{6,7},{7,6},{8,9},{9,8},{10,11... | collective-permute-start | bytes 24584 | tf_op jit(solution)/shard_map/ppermute | solution.py:337
  21.9 0.0 collective-permute-done.3.refs_1_
  21.9 0.0 collective-permute-done.4.refs_2_
  21.9 0.9 %temporal.1 = bf16[16,16,512]{2,1,0:T(8,128)(2,1)} custom-call(bf16[256,128]{1,0:T(8,128)(2,1)S(1)} %collective-permute-done.2.refs_0_, bf16[256,128]{1,0:T(8,128)(2,1)S(1)} %collective-permute-done.3.refs_1_, bf16[256,128]{1,0:T(8,128)(2,1)S(1)} %collective-permute-done.4.refs_2_, bf16[256,128]{1,0:T(8,128)(2,1)S(1)} %get-tuple-element.50.refs_3_), custom_call_target="tpu_custom_call" | custom-call | flops 1000 | bytes 1000 | tf_op jit(solution)/shard_map/temporal/pallas_call | solution.py:423
  22.8 0.0 collective-permute-done.8.refs_0_
  22.8 2.7 %collective-permute-done.9.refs_1_ = f32[16,128]{1,0:T(8,128)S(1)} collective-permute-done((f32[16,128]{1,0:T(8,128)S(1)}, f32[16,128]{1,0:T(8,128)S(1)}, u32[]{:S(2)}, u32[]{:S(2)}) %collective-permute-start.9) | collective-permute-done | bytes 8224 | tf_op jit(solution)/shard_map/ppermute | solution.py:337
  25.5 0.0 collective-permute-done.10.refs_2_
  25.5 0.7 %means.1 = f32[16,16]{1,0:T(8,128)} custom-call(f32[16,128]{1,0:T(8,128)S(1)} %collective-permute-done.8.refs_0_, f32[16,128]{1,0:T(8,128)S(1)} %collective-permute-done.9.refs_1_, f32[16,128]{1,0:T(8,128)S(1)} %collective-permute-done.10.refs_2_, f32[16,128]{1,0:T(8,128)S(1)} %get-tuple-element.47.refs_3_), custom_call_target="tpu_custom_call" | custom-call | flops 1000 | bytes 1000 | tf_op jit(solution)/shard_map/means/pallas_call | solution.py:431
  (11 shorter events, 0.1 us)
Async XLA Ops:
  0.6 1.0 %copy-start = (f32[4,16,2048]{2,1,0:T(8,128)S(1)}, f32[4,16,2048]{2,1,0:T(8,128)}, u32[]{:S(2)}) copy-start(f32[4,16,2048]{2,1,0:T(8,128)} %observed_ref.1) | copy-start | bytes 1572868
  1.8 8.0 %collective-permute-start = (f16[48,2048]{1,0:T(8,128)(2,1)S(1)}, f16[48,2048]{1,0:T(8,128)(2,1)S(1)}, u32[]{:S(2)}, u32[]{:S(2)}) collective-permute-start(f16[48,2048]{1,0:T(8,128)(2,1)S(1)} %convert_element_type.12), channel_id=1, source_target_pairs={{0,1},{1,0},{2,3},{3,2},{4,5},{5,4},{6,7},{7,6},{8,9},{9,8},{10,11... | collective-permute-start | bytes 589832 | tf_op jit(solution)/shard_map/ppermute | solution.py:381
  4.9 0.8 %copy-start.1 = (s32[256,16,4]{0,2,1:T(4,128)S(1)}, s32[256,16,4]{0,2,1:T(4,128)}, u32[]{:S(2)}) copy-start(s32[256,16,4]{0,2,1:T(4,128)} %param.7) | copy-start | bytes 196612
  4.9 4.9 %collective-permute-start.1 = (f16[48,2048]{1,0:T(8,128)(2,1)S(1)}, f16[48,2048]{1,0:T(8,128)(2,1)S(1)}, u32[]{:S(2)}, u32[]{:S(2)}) collective-permute-start(f16[48,2048]{1,0:T(8,128)(2,1)S(1)} %convert_element_type.13), channel_id=1, source_target_pairs={{0,4},{1,2},{2,1},{3,7},{4,0},{5,6},{6,5},{7,3},{8,12},{9,10},{10,... | collective-permute-start | bytes 589832 | tf_op jit(solution)/shard_map/ppermute | solution.py:382
  5.8 0.7 %copy-start.2 = (f32[8,5]{1,0:T(8,128)S(1)}, f32[8,5]{1,0:T(8,128)}, u32[]{:S(2)}) copy-start(f32[8,5]{1,0:T(8,128)} %kernels_ref.1) | copy-start | bytes 484
  5.8 0.7 %copy-start.3 = (s32[8]{0:T(128)S(1)}, s32[8]{0:T(128)}, u32[]{:S(2)}) copy-start(s32[8]{0:T(128)} %band_ref.1) | copy-start | bytes 100
  12.8 4.0 %collective-permute-start.5 = (bf16[48,128]{1,0:T(8,128)(2,1)S(1)}, bf16[48,128]{1,0:T(8,128)(2,1)S(1)}, u32[]{:S(2)}, u32[]{:S(2)}) collective-permute-start(bf16[48,128]{1,0:T(8,128)(2,1)S(1)} %get-tuple-element.57), channel_id=1, source_target_pairs={{0,12},{4,8},{8,4},{12,0},{1,13},{5,9},{9,5},{13,1},{2,14},{6,10},... | collective-permute-start | bytes 36872 | tf_op jit(solution)/shard_map/ppermute | solution.py:337
  13.1 3.7 %collective-permute-start.6 = (bf16[48,128]{1,0:T(8,128)(2,1)S(1)}, bf16[48,128]{1,0:T(8,128)(2,1)S(1)}, u32[]{:S(2)}, u32[]{:S(2)}) collective-permute-start(bf16[48,128]{1,0:T(8,128)(2,1)S(1)} %get-tuple-element.56), channel_id=1, source_target_pairs={{0,8},{4,12},{8,0},{12,4},{1,9},{5,13},{9,1},{13,5},{2,10},{6,14},... | collective-permute-start | bytes 36872 | tf_op jit(solution)/shard_map/ppermute | solution.py:337
  14.6 2.2 %collective-permute-start.7 = (bf16[48,128]{1,0:T(8,128)(2,1)S(1)}, bf16[48,128]{1,0:T(8,128)(2,1)S(1)}, u32[]{:S(2)}, u32[]{:S(2)}) collective-permute-start(bf16[48,128]{1,0:T(8,128)(2,1)S(1)} %get-tuple-element.55), channel_id=1, source_target_pairs={{0,4},{4,0},{8,12},{12,8},{1,5},{5,1},{9,13},{13,9},{2,6},{6,2},{1... | collective-permute-start | bytes 36872 | tf_op jit(solution)/shard_map/ppermute | solution.py:337
  14.8 6.9 %collective-permute-start.2 = (bf16[256,128]{1,0:T(8,128)(2,1)S(1)}, bf16[256,128]{1,0:T(8,128)(2,1)S(1)}, u32[]{:S(2)}, u32[]{:S(2)}) collective-permute-start(bf16[256,128]{1,0:T(8,128)(2,1)S(1)} %get-tuple-element.53), channel_id=1, source_target_pairs={{0,12},{4,8},{8,4},{12,0},{1,13},{5,9},{9,5},{13,1},{2,14},{6,10},... | collective-permute-start | bytes 196616 | tf_op jit(solution)/shard_map/ppermute | solution.py:337
  16.1 5.8 %collective-permute-start.3 = (bf16[256,128]{1,0:T(8,128)(2,1)S(1)}, bf16[256,128]{1,0:T(8,128)(2,1)S(1)}, u32[]{:S(2)}, u32[]{:S(2)}) collective-permute-start(bf16[256,128]{1,0:T(8,128)(2,1)S(1)} %get-tuple-element.52), channel_id=1, source_target_pairs={{0,8},{4,12},{8,0},{12,4},{1,9},{5,13},{9,1},{13,5},{2,10},{6,14},... | collective-permute-start | bytes 196616 | tf_op jit(solution)/shard_map/ppermute | solution.py:337
  16.8 5.1 %collective-permute-start.4 = (bf16[256,128]{1,0:T(8,128)(2,1)S(1)}, bf16[256,128]{1,0:T(8,128)(2,1)S(1)}, u32[]{:S(2)}, u32[]{:S(2)}) collective-permute-start(bf16[256,128]{1,0:T(8,128)(2,1)S(1)} %get-tuple-element.51), channel_id=1, source_target_pairs={{0,4},{4,0},{8,12},{12,8},{1,5},{5,1},{9,13},{13,9},{2,6},{6,2},{1... | collective-permute-start | bytes 196616 | tf_op jit(solution)/shard_map/ppermute | solution.py:337
  17.3 5.6 %collective-permute-start.8 = (f32[16,128]{1,0:T(8,128)S(1)}, f32[16,128]{1,0:T(8,128)S(1)}, u32[]{:S(2)}, u32[]{:S(2)}) collective-permute-start(f32[16,128]{1,0:T(8,128)S(1)} %get-tuple-element.61), channel_id=1, source_target_pairs={{0,3},{1,2},{2,1},{3,0},{4,7},{5,6},{6,5},{7,4},{8,11},{9,10},{10,... | collective-permute-start | bytes 24584 | tf_op jit(solution)/shard_map/ppermute | solution.py:337
  20.9 4.5 %collective-permute-start.9 = (f32[16,128]{1,0:T(8,128)S(1)}, f32[16,128]{1,0:T(8,128)S(1)}, u32[]{:S(2)}, u32[]{:S(2)}) collective-permute-start(f32[16,128]{1,0:T(8,128)S(1)} %get-tuple-element.60), channel_id=1, source_target_pairs={{0,2},{1,3},{2,0},{3,1},{4,6},{5,7},{6,4},{7,5},{8,10},{9,11},{10,... | collective-permute-start | bytes 24584 | tf_op jit(solution)/shard_map/ppermute | solution.py:337
  21.6 3.9 %collective-permute-start.10 = (f32[16,128]{1,0:T(8,128)S(1)}, f32[16,128]{1,0:T(8,128)S(1)}, u32[]{:S(2)}, u32[]{:S(2)}) collective-permute-start(f32[16,128]{1,0:T(8,128)S(1)} %get-tuple-element.59), channel_id=1, source_target_pairs={{0,1},{1,0},{2,3},{3,2},{4,5},{5,4},{6,7},{7,6},{8,9},{9,8},{10,11... | collective-permute-start | bytes 24584 | tf_op jit(solution)/shard_map/ppermute | solution.py:337

commit v15 on v14

--- a/solution.py
+++ b/solution.py
@@ -298,10 +298,10 @@
         precision=lax.Precision.HIGHEST,
         preferred_element_type=jnp.float32,
     )
-    share = out_ref.shape[1]
+    share = out_ref.shape[2]
     out_ref[...] = jnp.zeros_like(out_ref)
-    for row in range(out_ref.shape[0]):
-        out_ref[row, :, : rows + 8] = totals[row * share : (row + 1) * share]
+    for row in range(2 * out_ref.shape[1]):
+        out_ref[row % 2, row // 2, :, : rows + 8] = totals[row * share : (row + 1) * share]
 
 
 def temporal_kernel(*refs, frames):
@@ -320,6 +320,10 @@
             spikes_ref[t, :, tile * TILE : (tile + 1) * TILE] = spikes.astype(spikes_ref.dtype)
 
 
+def add_kernel(first_ref, second_ref, out_ref):
+    out_ref[...] = first_ref[...] + second_ref[...]
+
+
 def means_kernel(*refs):
     pieces, traces_ref = refs[:-1], refs[-1]
     frames = traces_ref.shape[1]
@@ -336,6 +340,13 @@
         part = lax.dynamic_index_in_dim(parts, place ^ step, 0, keepdims=False, allow_negative_indices=False)
         arrived.append(lax.ppermute(part, axis, [(i, i ^ step) for i in range(count)]))
     return arrived
+
+
+def swapped_one(parts, axis, mine, step):
+    own, there = (
+        lax.dynamic_index_in_dim(parts, index, 0, keepdims=False, allow_negative_indices=False) for index in (mine, mine ^ 1)
+    )
+    return own, lax.ppermute(there, axis, [(i, i ^ step) for i in range(lax.axis_size(axis))])
 
 
 def in_turn(*arrays):
@@ -413,13 +424,14 @@
         functools.partial(partial_kernel, positions=positions),
         "partial",
         [vmem] * n_frame,
-        array(n_row, share, TILE),
+        array(2, n_row // 2, share, TILE),
         [
             pltpu.VMEM((n_frame * frames * n_frame, TILE), jnp.float32),
             pltpu.VMEM((n_frame, n_row * share // 2, TILE), jnp.float32),
         ],
     )(*sides[::-1])
-    shares = swapped(partial, "row")
+    pairs = call(add_kernel, "add", [vmem] * 2, array(n_row // 2, share, TILE))(*swapped_one(partial, "row", row % 2, 1))
+    shares = swapped_one(pairs, "row", row // 2, 2)
     spikes = call(
         functools.partial(temporal_kernel, frames=frames),
         "temporal",
@@ -427,8 +439,8 @@
         array(n_frame * frames, rows_dev, tiles_dev * TILE, dtype=jnp.bfloat16),
         [pltpu.VMEM((n_frame, frames * positions, TILE), jnp.bfloat16)],
     )(*pieces[::-1])
-    spikes, *shares = in_turn(spikes, *shares[::-1])
-    traces = call(means_kernel, "means", [vmem] * n_row, array(share, n_frame * frames))(*shares)
+    spikes, *shares = in_turn(spikes, *shares)
+    traces = call(means_kernel, "means", [vmem] * 2, array(share, n_frame * frames))(*shares)
     return (spikes, traces)
 
 

time: 26.4 us -> 27.8 us (1.053)
  starting transfers between devices: 11.8 us -> 12.9 us
    ppermute x0 -> x2, starting transfers between devices: none -> 5.9 us  [swapped_one(): lax.ppermute(there, axis, [(i, i ^ step) for i in range(lax.axis_size(axi...]
    ppermute x9 -> x6, starting transfers between devices: 8.61 us -> 3.89 us  [swapped(): lax.ppermute(part, axis, [(i, i ^ step) for i in range(count)])]
    ppermute x9 -> x6, waiting for transfers between devices: 2.69 us -> 2.94 us  [swapped(): lax.ppermute(part, axis, [(i, i ^ step) for i in range(count)])]
    pallas_call x1 -> x2, Pallas kernels: 0.68 us -> 0.68 us  [the longest x1 0.68 us: by_halo(): call(means_kernel, 'means', [vmem] * 2, array(share, n_frame * frames))]
  transfers between devices with their start and end apart: 11 -> 10, of which waited for: 2 -> 4; matrix products, arithmetic and copies ran while one was open for 0% -> 0% of each run, Pallas kernels for 8% -> 6%
where the time goes in v15:
time: 27.8 us; the launch traced here: 27.6 us
  starting transfers between devices  12.9 us (46%)
  Pallas kernels  5.76 us (21%)
  waiting for transfers between devices  5.6 us (20%)
  local copies, waits for them, and re-layouts  2.41 us (9%)
  between operations  0.76 us (3%)
    ppermute x2, starting transfers between devices, swapped_one(): lax.ppermute(there, axis, [(i, i ^ step) for i in range(lax.axis_size(axi...  5.9 us
    ppermute x6, starting transfers between devices, swapped(): lax.ppermute(part, axis, [(i, i ^ step) for i in range(count)])  3.89 us
    ppermute x1, starting transfers between devices, by_halo(): inner = lax.ppermute(inner.astype(jnp.float16), 'row', inner_swap)  3.09 us
    ppermute x6, waiting for transfers between devices, swapped(): lax.ppermute(part, axis, [(i, i ^ step) for i in range(count)])  2.94 us
    pallas_call x1, Pallas kernels, by_halo(): call(restore_kernel, 'restore', [vmem] * 6, (array(n_frame, frames * posi...  2.84 us
    ppermute x1, waiting for transfers between devices, by_halo(): inner = lax.ppermute(inner.astype(jnp.float16), 'row', inner_swap)  2.65 us
    unnamed x8, local copies, waits for them, and re-layouts  2.35 us
    pallas_call x1, Pallas kernels, by_halo(): call(functools.partial(temporal_kernel, frames=frames), 'temporal', [vmem...  0.92 us
  transfers between devices with their start and end apart: 10, of which 4 were waited for; matrix products, arithmetic and copies ran while one was open for 0% of the time, Pallas kernels for 6%

profile of v15, /device:TPU:0, one launch (start us, length us, event | category | flops | bytes accessed | tf_op | source)
XLA Modules:
  0.0 27.6 jit_solution(13934324604694451552)
XLA Ops:
  0.6 0.0 copy-start
  0.6 1.0 %copy-done = f32[4,16,2048]{2,1,0:T(8,128)S(1)} copy-done((f32[4,16,2048]{2,1,0:T(8,128)S(1)}, f32[4,16,2048]{2,1,0:T(8,128)}, u32[]{:S(2)}) %copy-start) | copy-done | bytes 524312
  1.7 0.1 halo.1
  1.8 3.1 %collective-permute-start = (f16[48,2048]{1,0:T(8,128)(2,1)S(1)}, f16[48,2048]{1,0:T(8,128)(2,1)S(1)}, u32[]{:S(2)}, u32[]{:S(2)}) collective-permute-start(f16[48,2048]{1,0:T(8,128)(2,1)S(1)} %convert_element_type.12), channel_id=1, source_target_pairs={{0,1},{1,0},{2,3},{3,2},{4,5},{5,4},{6,7},{7,6},{8,9},{9,8},{10,11... | collective-permute-start | bytes 589832 | tf_op jit(solution)/shard_map/ppermute | solution.py:392
  4.9 0.1 collective-permute-start.1
  5.0 0.7 %copy-done.1 = s32[256,16,4]{0,2,1:T(4,128)S(1)} copy-done((s32[256,16,4]{0,2,1:T(4,128)S(1)}, s32[256,16,4]{0,2,1:T(4,128)}, u32[]{:S(2)}) %copy-start.1) | copy-done | bytes 65560
  5.8 0.1 feet.1.feet_ref
  5.9 0.6 %copy-done.2 = f32[8,5]{1,0:T(8,128)S(1)} copy-done((f32[8,5]{1,0:T(8,128)S(1)}, f32[8,5]{1,0:T(8,128)}, u32[]{:S(2)}) %copy-start.2) | copy-done | bytes 184
  6.4 0.7 %taps.1 = (f32[4,48,128]{2,1,0:T(8,128)S(1)}, f32[4,48,128]{2,1,0:T(8,128)S(1)}) custom-call(s32[8]{0:T(128)S(1)} %copy-done.3, f32[8,5]{1,0:T(8,128)S(1)} %copy-done.2), custom_call_target="tpu_custom_call" | custom-call | flops 1000 | bytes 1000 | tf_op jit(solution)/shard_map/taps/pallas_call | solution.py:395
  7.2 2.7 %collective-permute-done = f16[48,2048]{1,0:T(8,128)(2,1)S(1)} collective-permute-done((f16[48,2048]{1,0:T(8,128)(2,1)S(1)}, f16[48,2048]{1,0:T(8,128)(2,1)S(1)}, u32[]{:S(2)}, u32[]{:S(2)}) %collective-permute-start) | collective-permute-done | bytes 196640 | tf_op jit(solution)/shard_map/ppermute | solution.py:392
  9.8 0.0 collective-permute-done.1
  9.8 0.1 convert_select_fusion
  9.9 2.8 %restore.1 = (bf16[4,256,128]{2,1,0:T(8,128)(2,1)S(1)}, bf16[4,48,128]{2,1,0:T(8,128)(2,1)S(1)}) custom-call(f32[4,48,128]{2,1,0:T(8,128)S(1)} %get-tuple-element.16.taps_ref, f32[4,48,128]{2,1,0:T(8,128)S(1)} %get-tuple-element.17.back_ref, bf16[4,32,128]{2,1,0:T(8,128)(2,1)S(1)} %feet.1.feet_ref, f32[4,16,2048]{2,1,0:T(8,128)S(1)} %get-tuple-element.18.own_ref, ...), custom_call_target="tpu_custom_call" | custom-call | flops 1000 | bytes 1000 | tf_op jit(solution)/shard_map/restore/pallas_call | solution.py:411
  12.8 0.3 %collective-permute-start.5 = (bf16[48,128]{1,0:T(8,128)(2,1)S(1)}, bf16[48,128]{1,0:T(8,128)(2,1)S(1)}, u32[]{:S(2)}, u32[]{:S(2)}) collective-permute-start(bf16[48,128]{1,0:T(8,128)(2,1)S(1)} %get-tuple-element.39), channel_id=1, source_target_pairs={{0,12},{4,8},{8,4},{12,0},{1,13},{5,9},{9,5},{13,1},{2,14},{6,10},... | collective-permute-start | bytes 36872 | tf_op jit(solution)/shard_map/ppermute | solution.py:341
  13.1 1.5 %collective-permute-start.6 = (bf16[48,128]{1,0:T(8,128)(2,1)S(1)}, bf16[48,128]{1,0:T(8,128)(2,1)S(1)}, u32[]{:S(2)}, u32[]{:S(2)}) collective-permute-start(bf16[48,128]{1,0:T(8,128)(2,1)S(1)} %get-tuple-element.38), channel_id=1, source_target_pairs={{0,8},{4,12},{8,0},{12,4},{1,9},{5,13},{9,1},{13,5},{2,10},{6,14},... | collective-permute-start | bytes 36872 | tf_op jit(solution)/shard_map/ppermute | solution.py:341
  14.6 0.1 collective-permute-start.7
  14.7 1.2 %collective-permute-done.5.refs_0_ = bf16[48,128]{1,0:T(8,128)(2,1)S(1)} collective-permute-done((bf16[48,128]{1,0:T(8,128)(2,1)S(1)}, bf16[48,128]{1,0:T(8,128)(2,1)S(1)}, u32[]{:S(2)}, u32[]{:S(2)}) %collective-permute-start.5) | collective-permute-done | bytes 12320 | tf_op jit(solution)/shard_map/ppermute | solution.py:341
  16.0 0.8 %collective-permute-done.6.refs_1_ = bf16[48,128]{1,0:T(8,128)(2,1)S(1)} collective-permute-done((bf16[48,128]{1,0:T(8,128)(2,1)S(1)}, bf16[48,128]{1,0:T(8,128)(2,1)S(1)}, u32[]{:S(2)}, u32[]{:S(2)}) %collective-permute-start.6) | collective-permute-done | bytes 12320 | tf_op jit(solution)/shard_map/ppermute | solution.py:341
  16.8 0.0 collective-permute-done.7.refs_2_
  16.8 0.4 %partial.1 = f32[2,2,16,128]{3,2,1,0:T(8,128)S(1)} custom-call(bf16[48,128]{1,0:T(8,128)(2,1)S(1)} %collective-permute-done.5.refs_0_, bf16[48,128]{1,0:T(8,128)(2,1)S(1)} %collective-permute-done.6.refs_1_, bf16[48,128]{1,0:T(8,128)(2,1)S(1)} %collective-permute-done.7.refs_2_, bf16[48,128]{1,0:T(8,128)(2,1)S(1)} %get-tuple-element.36.refs_3_), custom_call_target="tpu_custom_call" | custom-call | flops 1000 | bytes 1000 | tf_op jit(solution)/shard_map/partial/pallas_call | solution.py:423
  17.2 2.9 %collective-permute-start.8 = (f32[2,16,128]{2,1,0:T(8,128)S(1)}, f32[2,16,128]{2,1,0:T(8,128)S(1)}, u32[]{:S(2)}, u32[]{:S(2)}) collective-permute-start(f32[2,16,128]{2,1,0:T(8,128)S(1)} %get-tuple-element.40), channel_id=1, source_target_pairs={{0,1},{1,0},{2,3},{3,2},{4,5},{5,4},{6,7},{7,6},{8,9},{9,8},{10,11... | collective-permute-start | bytes 49160 | tf_op jit(solution)/shard_map/ppermute | solution.py:349
  20.1 0.3 %collective-permute-start.2 = (bf16[256,128]{1,0:T(8,128)(2,1)S(1)}, bf16[256,128]{1,0:T(8,128)(2,1)S(1)}, u32[]{:S(2)}, u32[]{:S(2)}) collective-permute-start(bf16[256,128]{1,0:T(8,128)(2,1)S(1)} %get-tuple-element.35), channel_id=1, source_target_pairs={{0,12},{4,8},{8,4},{12,0},{1,13},{5,9},{9,5},{13,1},{2,14},{6,10},... | collective-permute-start | bytes 196616 | tf_op jit(solution)/shard_map/ppermute | solution.py:341
  20.5 1.4 %collective-permute-start.3 = (bf16[256,128]{1,0:T(8,128)(2,1)S(1)}, bf16[256,128]{1,0:T(8,128)(2,1)S(1)}, u32[]{:S(2)}, u32[]{:S(2)}) collective-permute-start(bf16[256,128]{1,0:T(8,128)(2,1)S(1)} %get-tuple-element.34), channel_id=1, source_target_pairs={{0,8},{4,12},{8,0},{12,4},{1,9},{5,13},{9,1},{13,5},{2,10},{6,14},... | collective-permute-start | bytes 196616 | tf_op jit(solution)/shard_map/ppermute | solution.py:341
  21.9 0.2 collective-permute-start.4
  22.1 0.0 collective-permute-done.8.second_ref
  22.1 3.0 %collective-permute-start.9 = (f32[16,128]{1,0:T(8,128)S(1)}, f32[16,128]{1,0:T(8,128)S(1)}, u32[]{:S(2)}, u32[]{:S(2)}) collective-permute-start(f32[16,128]{1,0:T(8,128)S(1)} %get-tuple-element.42), channel_id=1, source_target_pairs={{0,2},{1,3},{2,0},{3,1},{4,6},{5,7},{6,4},{7,5},{8,10},{9,11},{10,... | collective-permute-start | bytes 24584 | tf_op jit(solution)/shard_map/ppermute | solution.py:349
  25.1 0.0 collective-permute-done.2.refs_0_
  25.1 0.9 %collective-permute-done.3.refs_1_ = bf16[256,128]{1,0:T(8,128)(2,1)S(1)} collective-permute-done((bf16[256,128]{1,0:T(8,128)(2,1)S(1)}, bf16[256,128]{1,0:T(8,128)(2,1)S(1)}, u32[]{:S(2)}, u32[]{:S(2)}) %collective-permute-start.3) | collective-permute-done | bytes 65568 | tf_op jit(solution)/shard_map/ppermute | solution.py:341
  26.0 0.0 collective-permute-done.4.refs_2_
  26.0 0.9 %temporal.1 = bf16[16,16,512]{2,1,0:T(8,128)(2,1)} custom-call(bf16[256,128]{1,0:T(8,128)(2,1)S(1)} %collective-permute-done.2.refs_0_, bf16[256,128]{1,0:T(8,128)(2,1)S(1)} %collective-permute-done.3.refs_1_, bf16[256,128]{1,0:T(8,128)(2,1)S(1)} %collective-permute-done.4.refs_2_, bf16[256,128]{1,0:T(8,128)(2,1)S(1)} %get-tuple-element.32.refs_3_), custom_call_target="tpu_custom_call" | custom-call | flops 1000 | bytes 1000 | tf_op jit(solution)/shard_map/temporal/pallas_call | solution.py:435
  26.9 0.0 collective-permute-done.9.refs_1_
  26.9 0.7 %means.1 = f32[16,16]{1,0:T(8,128)} custom-call(f32[16,128]{1,0:T(8,128)S(1)} %get-tuple-element.28.refs_0_, f32[16,128]{1,0:T(8,128)S(1)} %collective-permute-done.9.refs_1_), custom_call_target="tpu_custom_call" | custom-call | flops 1000 | bytes 1000 | tf_op jit(solution)/shard_map/means/pallas_call | solution.py:443
  (11 shorter events, 0.1 us)
Async XLA Ops:
  0.6 1.0 %copy-start = (f32[4,16,2048]{2,1,0:T(8,128)S(1)}, f32[4,16,2048]{2,1,0:T(8,128)}, u32[]{:S(2)}) copy-start(f32[4,16,2048]{2,1,0:T(8,128)} %observed_ref.1) | copy-start | bytes 1572868
  1.8 8.0 %collective-permute-start = (f16[48,2048]{1,0:T(8,128)(2,1)S(1)}, f16[48,2048]{1,0:T(8,128)(2,1)S(1)}, u32[]{:S(2)}, u32[]{:S(2)}) collective-permute-start(f16[48,2048]{1,0:T(8,128)(2,1)S(1)} %convert_element_type.12), channel_id=1, source_target_pairs={{0,1},{1,0},{2,3},{3,2},{4,5},{5,4},{6,7},{7,6},{8,9},{9,8},{10,11... | collective-permute-start | bytes 589832 | tf_op jit(solution)/shard_map/ppermute | solution.py:392
  4.9 0.8 %copy-start.1 = (s32[256,16,4]{0,2,1:T(4,128)S(1)}, s32[256,16,4]{0,2,1:T(4,128)}, u32[]{:S(2)}) copy-start(s32[256,16,4]{0,2,1:T(4,128)} %param.7) | copy-start | bytes 196612
  4.9 4.9 %collective-permute-start.1 = (f16[48,2048]{1,0:T(8,128)(2,1)S(1)}, f16[48,2048]{1,0:T(8,128)(2,1)S(1)}, u32[]{:S(2)}, u32[]{:S(2)}) collective-permute-start(f16[48,2048]{1,0:T(8,128)(2,1)S(1)} %convert_element_type.13), channel_id=1, source_target_pairs={{0,4},{1,2},{2,1},{3,7},{4,0},{5,6},{6,5},{7,3},{8,12},{9,10},{10,... | collective-permute-start | bytes 589832 | tf_op jit(solution)/shard_map/ppermute | solution.py:393
  5.8 0.7 %copy-start.2 = (f32[8,5]{1,0:T(8,128)S(1)}, f32[8,5]{1,0:T(8,128)}, u32[]{:S(2)}) copy-start(f32[8,5]{1,0:T(8,128)} %kernels_ref.1) | copy-start | bytes 484
  5.8 0.7 %copy-start.3 = (s32[8]{0:T(128)S(1)}, s32[8]{0:T(128)}, u32[]{:S(2)}) copy-start(s32[8]{0:T(128)} %band_ref.1) | copy-start | bytes 100
  12.8 3.2 %collective-permute-start.5 = (bf16[48,128]{1,0:T(8,128)(2,1)S(1)}, bf16[48,128]{1,0:T(8,128)(2,1)S(1)}, u32[]{:S(2)}, u32[]{:S(2)}) collective-permute-start(bf16[48,128]{1,0:T(8,128)(2,1)S(1)} %get-tuple-element.39), channel_id=1, source_target_pairs={{0,12},{4,8},{8,4},{12,0},{1,13},{5,9},{9,5},{13,1},{2,14},{6,10},... | collective-permute-start | bytes 36872 | tf_op jit(solution)/shard_map/ppermute | solution.py:341
  13.1 3.7 %collective-permute-start.6 = (bf16[48,128]{1,0:T(8,128)(2,1)S(1)}, bf16[48,128]{1,0:T(8,128)(2,1)S(1)}, u32[]{:S(2)}, u32[]{:S(2)}) collective-permute-start(bf16[48,128]{1,0:T(8,128)(2,1)S(1)} %get-tuple-element.38), channel_id=1, source_target_pairs={{0,8},{4,12},{8,0},{12,4},{1,9},{5,13},{9,1},{13,5},{2,10},{6,14},... | collective-permute-start | bytes 36872 | tf_op jit(solution)/shard_map/ppermute | solution.py:341
  14.6 2.2 %collective-permute-start.7 = (bf16[48,128]{1,0:T(8,128)(2,1)S(1)}, bf16[48,128]{1,0:T(8,128)(2,1)S(1)}, u32[]{:S(2)}, u32[]{:S(2)}) collective-permute-start(bf16[48,128]{1,0:T(8,128)(2,1)S(1)} %get-tuple-element.37), channel_id=1, source_target_pairs={{0,4},{4,0},{8,12},{12,8},{1,5},{5,1},{9,13},{13,9},{2,6},{6,2},{1... | collective-permute-start | bytes 36872 | tf_op jit(solution)/shard_map/ppermute | solution.py:341
  17.2 4.9 %collective-permute-start.8 = (f32[2,16,128]{2,1,0:T(8,128)S(1)}, f32[2,16,128]{2,1,0:T(8,128)S(1)}, u32[]{:S(2)}, u32[]{:S(2)}) collective-permute-start(f32[2,16,128]{2,1,0:T(8,128)S(1)} %get-tuple-element.40), channel_id=1, source_target_pairs={{0,1},{1,0},{2,3},{3,2},{4,5},{5,4},{6,7},{7,6},{8,9},{9,8},{10,11... | collective-permute-start | bytes 49160 | tf_op jit(solution)/shard_map/ppermute | solution.py:349
  20.1 5.0 %collective-permute-start.2 = (bf16[256,128]{1,0:T(8,128)(2,1)S(1)}, bf16[256,128]{1,0:T(8,128)(2,1)S(1)}, u32[]{:S(2)}, u32[]{:S(2)}) collective-permute-start(bf16[256,128]{1,0:T(8,128)(2,1)S(1)} %get-tuple-element.35), channel_id=1, source_target_pairs={{0,12},{4,8},{8,4},{12,0},{1,13},{5,9},{9,5},{13,1},{2,14},{6,10},... | collective-permute-start | bytes 196616 | tf_op jit(solution)/shard_map/ppermute | solution.py:341
  20.5 5.5 %collective-permute-start.3 = (bf16[256,128]{1,0:T(8,128)(2,1)S(1)}, bf16[256,128]{1,0:T(8,128)(2,1)S(1)}, u32[]{:S(2)}, u32[]{:S(2)}) collective-permute-start(bf16[256,128]{1,0:T(8,128)(2,1)S(1)} %get-tuple-element.34), channel_id=1, source_target_pairs={{0,8},{4,12},{8,0},{12,4},{1,9},{5,13},{9,1},{13,5},{2,10},{6,14},... | collective-permute-start | bytes 196616 | tf_op jit(solution)/shard_map/ppermute | solution.py:341
  21.9 4.1 %collective-permute-start.4 = (bf16[256,128]{1,0:T(8,128)(2,1)S(1)}, bf16[256,128]{1,0:T(8,128)(2,1)S(1)}, u32[]{:S(2)}, u32[]{:S(2)}) collective-permute-start(bf16[256,128]{1,0:T(8,128)(2,1)S(1)} %get-tuple-element.33), channel_id=1, source_target_pairs={{0,4},{4,0},{8,12},{12,8},{1,5},{5,1},{9,13},{13,9},{2,6},{6,2},{1... | collective-permute-start | bytes 196616 | tf_op jit(solution)/shard_map/ppermute | solution.py:341
  22.1 4.8 %collective-permute-start.9 = (f32[16,128]{1,0:T(8,128)S(1)}, f32[16,128]{1,0:T(8,128)S(1)}, u32[]{:S(2)}, u32[]{:S(2)}) collective-permute-start(f32[16,128]{1,0:T(8,128)S(1)} %get-tuple-element.42), channel_id=1, source_target_pairs={{0,2},{1,3},{2,0},{3,1},{4,6},{5,7},{6,4},{7,5},{8,10},{9,11},{10,... | collective-permute-start | bytes 24584 | tf_op jit(solution)/shard_map/ppermute | solution.py:349

commit v16 on v14

--- a/solution.py
+++ b/solution.py
@@ -257,9 +257,10 @@
         if step:
             middle -= SMOOTHING * SMOOTHING * factors[-1]
         factors.append(1.0 / middle)
-    forward = [series[0] * factors[0]]
+    scaled = [cells * factor for cells, factor in zip(series, factors)]
+    forward = [scaled[0]]
     for step in range(1, total):
-        forward.append((series[step] + SMOOTHING * forward[step - 1]) * factors[step])
+        forward.append(scaled[step] + (SMOOTHING * factors[step]) * forward[step - 1])
     baseline = [None] * total
     baseline[total - 1] = forward[total - 1]
     for step in range(total - 2, -1, -1):
@@ -291,11 +292,15 @@
         feet = feet_ref[block]
         weights.append(jnp.concatenate([jnp.where(left, feet, 0.0), jnp.where(left, 0.0, feet)], axis=0))
         sums.append(jnp.concatenate([sums_ref[pl.ds(block, rows, stride=n_frame), :], extra], axis=0))
+    sums = jnp.concatenate(sums, axis=1)
+    parts = []
+    for _ in range(3):
+        parts.append(sums.astype(jnp.bfloat16))
+        sums = sums - parts[-1].astype(jnp.float32)
     totals = lax.dot_general(
-        jnp.concatenate(weights, axis=1),
-        jnp.concatenate(sums, axis=1),
+        jnp.concatenate(weights * 3, axis=1).astype(jnp.bfloat16),
+        jnp.concatenate(parts, axis=1),
         (((1,), (1,)), ((), ())),
-        precision=lax.Precision.HIGHEST,
         preferred_element_type=jnp.float32,
     )
     share = out_ref.shape[1]

time: 26.4 us -> 26.4 us (level)
  no operation moved by 1% of the time
where the time goes in v16:
time: 26.4 us; the launch traced here: 26.1 us
  starting transfers between devices  11.8 us (45%)
  Pallas kernels  5.69 us (22%)
  waiting for transfers between devices  5.35 us (20%)
  local copies, waits for them, and re-layouts  2.4 us (9%)
  between operations  0.75 us (3%)
    ppermute x9, starting transfers between devices, swapped(): lax.ppermute(part, axis, [(i, i ^ step) for i in range(count)])  8.63 us
    ppermute x1, starting transfers between devices, by_halo(): inner = lax.ppermute(inner.astype(jnp.float16), 'row', inner_swap)  3.09 us
    pallas_call x1, Pallas kernels, by_halo(): call(restore_kernel, 'restore', [vmem] * 6, (array(n_frame, frames * posi...  2.84 us
    ppermute x9, waiting for transfers between devices, swapped(): lax.ppermute(part, axis, [(i, i ^ step) for i in range(count)])  2.69 us
    ppermute x1, waiting for transfers between devices, by_halo(): inner = lax.ppermute(inner.astype(jnp.float16), 'row', inner_swap)  2.66 us
    unnamed x8, local copies, waits for them, and re-layouts  2.35 us
    pallas_call x1, Pallas kernels, by_halo(): call(functools.partial(temporal_kernel, frames=frames), 'temporal', [vmem...  0.91 us
    pallas_call x1, Pallas kernels, by_halo(): call(functools.partial(taps_kernel, height=rows_dev * n_row, rows_dev=row...  0.69 us
  transfers between devices with their start and end apart: 11, of which 2 were waited for; matrix products, arithmetic and copies ran while one was open for 0% of the time, Pallas kernels for 8%

profile of v16, /device:TPU:0, one launch (start us, length us, event | category | flops | bytes accessed | tf_op | source)
XLA Modules:
  0.0 26.1 jit_solution(15239813247047036652)
XLA Ops:
  0.6 1.0 %copy-done = f32[4,16,2048]{2,1,0:T(8,128)S(1)} copy-done((f32[4,16,2048]{2,1,0:T(8,128)S(1)}, f32[4,16,2048]{2,1,0:T(8,128)}, u32[]{:S(2)}) %copy-start) | copy-done | bytes 524312
  1.7 0.1 halo.1
  1.8 3.1 %collective-permute-start = (f16[48,2048]{1,0:T(8,128)(2,1)S(1)}, f16[48,2048]{1,0:T(8,128)(2,1)S(1)}, u32[]{:S(2)}, u32[]{:S(2)}) collective-permute-start(f16[48,2048]{1,0:T(8,128)(2,1)S(1)} %convert_element_type.12), channel_id=1, source_target_pairs={{0,1},{1,0},{2,3},{3,2},{4,5},{5,4},{6,7},{7,6},{8,9},{9,8},{10,11... | collective-permute-start | bytes 589832 | tf_op jit(solution)/shard_map/ppermute | solution.py:386
  4.9 0.1 collective-permute-start.1
  5.0 0.7 %copy-done.1 = s32[256,16,4]{0,2,1:T(4,128)S(1)} copy-done((s32[256,16,4]{0,2,1:T(4,128)S(1)}, s32[256,16,4]{0,2,1:T(4,128)}, u32[]{:S(2)}) %copy-start.1) | copy-done | bytes 65560
  5.8 0.1 feet.1.feet_ref
  5.9 0.6 %copy-done.2 = f32[8,5]{1,0:T(8,128)S(1)} copy-done((f32[8,5]{1,0:T(8,128)S(1)}, f32[8,5]{1,0:T(8,128)}, u32[]{:S(2)}) %copy-start.2) | copy-done | bytes 184
  6.4 0.7 %taps.1 = (f32[4,48,128]{2,1,0:T(8,128)S(1)}, f32[4,48,128]{2,1,0:T(8,128)S(1)}) custom-call(s32[8]{0:T(128)S(1)} %copy-done.3, f32[8,5]{1,0:T(8,128)S(1)} %copy-done.2), custom_call_target="tpu_custom_call" | custom-call | flops 1000 | bytes 1000 | tf_op jit(solution)/shard_map/taps/pallas_call | solution.py:389
  7.2 2.7 %collective-permute-done = f16[48,2048]{1,0:T(8,128)(2,1)S(1)} collective-permute-done((f16[48,2048]{1,0:T(8,128)(2,1)S(1)}, f16[48,2048]{1,0:T(8,128)(2,1)S(1)}, u32[]{:S(2)}, u32[]{:S(2)}) %collective-permute-start) | collective-permute-done | bytes 196640 | tf_op jit(solution)/shard_map/ppermute | solution.py:386
  9.8 0.0 collective-permute-done.1
  9.8 0.1 convert_select_fusion
  9.9 2.8 %restore.1 = (bf16[4,256,128]{2,1,0:T(8,128)(2,1)S(1)}, bf16[4,48,128]{2,1,0:T(8,128)(2,1)S(1)}) custom-call(f32[4,48,128]{2,1,0:T(8,128)S(1)} %get-tuple-element.25.taps_ref, f32[4,48,128]{2,1,0:T(8,128)S(1)} %get-tuple-element.26.back_ref, bf16[4,32,128]{2,1,0:T(8,128)(2,1)S(1)} %feet.1.feet_ref, f32[4,16,2048]{2,1,0:T(8,128)S(1)} %get-tuple-element.27.own_ref, ...), custom_call_target="tpu_custom_call" | custom-call | flops 1000 | bytes 1000 | tf_op jit(solution)/shard_map/restore/pallas_call | solution.py:405
  12.8 0.3 %collective-permute-start.5 = (bf16[48,128]{1,0:T(8,128)(2,1)S(1)}, bf16[48,128]{1,0:T(8,128)(2,1)S(1)}, u32[]{:S(2)}, u32[]{:S(2)}) collective-permute-start(bf16[48,128]{1,0:T(8,128)(2,1)S(1)} %get-tuple-element.57), channel_id=1, source_target_pairs={{0,12},{4,8},{8,4},{12,0},{1,13},{5,9},{9,5},{13,1},{2,14},{6,10},... | collective-permute-start | bytes 36872 | tf_op jit(solution)/shard_map/ppermute | solution.py:342
  13.1 1.5 %collective-permute-start.6 = (bf16[48,128]{1,0:T(8,128)(2,1)S(1)}, bf16[48,128]{1,0:T(8,128)(2,1)S(1)}, u32[]{:S(2)}, u32[]{:S(2)}) collective-permute-start(bf16[48,128]{1,0:T(8,128)(2,1)S(1)} %get-tuple-element.56), channel_id=1, source_target_pairs={{0,8},{4,12},{8,0},{12,4},{1,9},{5,13},{9,1},{13,5},{2,10},{6,14},... | collective-permute-start | bytes 36872 | tf_op jit(solution)/shard_map/ppermute | solution.py:342
  14.6 0.1 collective-permute-start.7
  14.8 1.3 %collective-permute-start.2 = (bf16[256,128]{1,0:T(8,128)(2,1)S(1)}, bf16[256,128]{1,0:T(8,128)(2,1)S(1)}, u32[]{:S(2)}, u32[]{:S(2)}) collective-permute-start(bf16[256,128]{1,0:T(8,128)(2,1)S(1)} %get-tuple-element.53), channel_id=1, source_target_pairs={{0,12},{4,8},{8,4},{12,0},{1,13},{5,9},{9,5},{13,1},{2,14},{6,10},... | collective-permute-start | bytes 196616 | tf_op jit(solution)/shard_map/ppermute | solution.py:342
  16.1 0.8 %collective-permute-start.3 = (bf16[256,128]{1,0:T(8,128)(2,1)S(1)}, bf16[256,128]{1,0:T(8,128)(2,1)S(1)}, u32[]{:S(2)}, u32[]{:S(2)}) collective-permute-start(bf16[256,128]{1,0:T(8,128)(2,1)S(1)} %get-tuple-element.52), channel_id=1, source_target_pairs={{0,8},{4,12},{8,0},{12,4},{1,9},{5,13},{9,1},{13,5},{2,10},{6,14},... | collective-permute-start | bytes 196616 | tf_op jit(solution)/shard_map/ppermute | solution.py:342
  16.8 0.0 collective-permute-done.5.refs_0_
  16.8 0.0 collective-permute-start.4
  16.8 0.0 collective-permute-done.6.refs_1_
  16.8 0.0 collective-permute-done.7.refs_2_
  16.8 0.3 %partial.1 = f32[4,16,128]{2,1,0:T(8,128)S(1)} custom-call(bf16[48,128]{1,0:T(8,128)(2,1)S(1)} %collective-permute-done.5.refs_0_, bf16[48,128]{1,0:T(8,128)(2,1)S(1)} %collective-permute-done.6.refs_1_, bf16[48,128]{1,0:T(8,128)(2,1)S(1)} %collective-permute-done.7.refs_2_, bf16[48,128]{1,0:T(8,128)(2,1)S(1)} %get-tuple-element.54.refs_3_), custom_call_target="tpu_custom_call" | custom-call | flops 1000 | bytes 1000 | tf_op jit(solution)/shard_map/partial/pallas_call | solution.py:417
  17.2 3.7 %collective-permute-start.8 = (f32[16,128]{1,0:T(8,128)S(1)}, f32[16,128]{1,0:T(8,128)S(1)}, u32[]{:S(2)}, u32[]{:S(2)}) collective-permute-start(f32[16,128]{1,0:T(8,128)S(1)} %get-tuple-element.61), channel_id=1, source_target_pairs={{0,3},{1,2},{2,1},{3,0},{4,7},{5,6},{6,5},{7,4},{8,11},{9,10},{10,... | collective-permute-start | bytes 24584 | tf_op jit(solution)/shard_map/ppermute | solution.py:342
  20.9 0.7 %collective-permute-start.9 = (f32[16,128]{1,0:T(8,128)S(1)}, f32[16,128]{1,0:T(8,128)S(1)}, u32[]{:S(2)}, u32[]{:S(2)}) collective-permute-start(f32[16,128]{1,0:T(8,128)S(1)} %get-tuple-element.60), channel_id=1, source_target_pairs={{0,2},{1,3},{2,0},{3,1},{4,6},{5,7},{6,4},{7,5},{8,10},{9,11},{10,... | collective-permute-start | bytes 24584 | tf_op jit(solution)/shard_map/ppermute | solution.py:342
  21.5 0.3 %collective-permute-start.10 = (f32[16,128]{1,0:T(8,128)S(1)}, f32[16,128]{1,0:T(8,128)S(1)}, u32[]{:S(2)}, u32[]{:S(2)}) collective-permute-start(f32[16,128]{1,0:T(8,128)S(1)} %get-tuple-element.59), channel_id=1, source_target_pairs={{0,1},{1,0},{2,3},{3,2},{4,5},{5,4},{6,7},{7,6},{8,9},{9,8},{10,11... | collective-permute-start | bytes 24584 | tf_op jit(solution)/shard_map/ppermute | solution.py:342
  21.8 0.0 collective-permute-done.3.refs_1_
  21.8 0.0 collective-permute-done.4.refs_2_
  21.8 0.9 %temporal.1 = bf16[16,16,512]{2,1,0:T(8,128)(2,1)} custom-call(bf16[256,128]{1,0:T(8,128)(2,1)S(1)} %collective-permute-done.2.refs_0_, bf16[256,128]{1,0:T(8,128)(2,1)S(1)} %collective-permute-done.3.refs_1_, bf16[256,128]{1,0:T(8,128)(2,1)S(1)} %collective-permute-done.4.refs_2_, bf16[256,128]{1,0:T(8,128)(2,1)S(1)} %get-tuple-element.50.refs_3_), custom_call_target="tpu_custom_call" | custom-call | flops 1000 | bytes 1000 | tf_op jit(solution)/shard_map/temporal/pallas_call | solution.py:428
  22.8 0.0 collective-permute-done.8.refs_0_
  22.8 2.7 %collective-permute-done.9.refs_1_ = f32[16,128]{1,0:T(8,128)S(1)} collective-permute-done((f32[16,128]{1,0:T(8,128)S(1)}, f32[16,128]{1,0:T(8,128)S(1)}, u32[]{:S(2)}, u32[]{:S(2)}) %collective-permute-start.9) | collective-permute-done | bytes 8224 | tf_op jit(solution)/shard_map/ppermute | solution.py:342
  25.4 0.0 collective-permute-done.10.refs_2_
  25.4 0.7 %means.1 = f32[16,16]{1,0:T(8,128)} custom-call(f32[16,128]{1,0:T(8,128)S(1)} %collective-permute-done.8.refs_0_, f32[16,128]{1,0:T(8,128)S(1)} %collective-permute-done.9.refs_1_, f32[16,128]{1,0:T(8,128)S(1)} %collective-permute-done.10.refs_2_, f32[16,128]{1,0:T(8,128)S(1)} %get-tuple-element.47.refs_3_), custom_call_target="tpu_custom_call" | custom-call | flops 1000 | bytes 1000 | tf_op jit(solution)/shard_map/means/pallas_call | solution.py:436
  (11 shorter events, 0.1 us)
Async XLA Ops:
  0.6 1.0 %copy-start = (f32[4,16,2048]{2,1,0:T(8,128)S(1)}, f32[4,16,2048]{2,1,0:T(8,128)}, u32[]{:S(2)}) copy-start(f32[4,16,2048]{2,1,0:T(8,128)} %observed_ref.1) | copy-start | bytes 1572868
  1.8 8.0 %collective-permute-start = (f16[48,2048]{1,0:T(8,128)(2,1)S(1)}, f16[48,2048]{1,0:T(8,128)(2,1)S(1)}, u32[]{:S(2)}, u32[]{:S(2)}) collective-permute-start(f16[48,2048]{1,0:T(8,128)(2,1)S(1)} %convert_element_type.12), channel_id=1, source_target_pairs={{0,1},{1,0},{2,3},{3,2},{4,5},{5,4},{6,7},{7,6},{8,9},{9,8},{10,11... | collective-permute-start | bytes 589832 | tf_op jit(solution)/shard_map/ppermute | solution.py:386
  4.9 0.8 %copy-start.1 = (s32[256,16,4]{0,2,1:T(4,128)S(1)}, s32[256,16,4]{0,2,1:T(4,128)}, u32[]{:S(2)}) copy-start(s32[256,16,4]{0,2,1:T(4,128)} %param.7) | copy-start | bytes 196612
  4.9 4.9 %collective-permute-start.1 = (f16[48,2048]{1,0:T(8,128)(2,1)S(1)}, f16[48,2048]{1,0:T(8,128)(2,1)S(1)}, u32[]{:S(2)}, u32[]{:S(2)}) collective-permute-start(f16[48,2048]{1,0:T(8,128)(2,1)S(1)} %convert_element_type.13), channel_id=1, source_target_pairs={{0,4},{1,2},{2,1},{3,7},{4,0},{5,6},{6,5},{7,3},{8,12},{9,10},{10,... | collective-permute-start | bytes 589832 | tf_op jit(solution)/shard_map/ppermute | solution.py:387
  5.8 0.7 %copy-start.2 = (f32[8,5]{1,0:T(8,128)S(1)}, f32[8,5]{1,0:T(8,128)}, u32[]{:S(2)}) copy-start(f32[8,5]{1,0:T(8,128)} %kernels_ref.1) | copy-start | bytes 484
  5.8 0.7 %copy-start.3 = (s32[8]{0:T(128)S(1)}, s32[8]{0:T(128)}, u32[]{:S(2)}) copy-start(s32[8]{0:T(128)} %band_ref.1) | copy-start | bytes 100
  12.8 4.0 %collective-permute-start.5 = (bf16[48,128]{1,0:T(8,128)(2,1)S(1)}, bf16[48,128]{1,0:T(8,128)(2,1)S(1)}, u32[]{:S(2)}, u32[]{:S(2)}) collective-permute-start(bf16[48,128]{1,0:T(8,128)(2,1)S(1)} %get-tuple-element.57), channel_id=1, source_target_pairs={{0,12},{4,8},{8,4},{12,0},{1,13},{5,9},{9,5},{13,1},{2,14},{6,10},... | collective-permute-start | bytes 36872 | tf_op jit(solution)/shard_map/ppermute | solution.py:342
  13.1 3.7 %collective-permute-start.6 = (bf16[48,128]{1,0:T(8,128)(2,1)S(1)}, bf16[48,128]{1,0:T(8,128)(2,1)S(1)}, u32[]{:S(2)}, u32[]{:S(2)}) collective-permute-start(bf16[48,128]{1,0:T(8,128)(2,1)S(1)} %get-tuple-element.56), channel_id=1, source_target_pairs={{0,8},{4,12},{8,0},{12,4},{1,9},{5,13},{9,1},{13,5},{2,10},{6,14},... | collective-permute-start | bytes 36872 | tf_op jit(solution)/shard_map/ppermute | solution.py:342
  14.6 2.2 %collective-permute-start.7 = (bf16[48,128]{1,0:T(8,128)(2,1)S(1)}, bf16[48,128]{1,0:T(8,128)(2,1)S(1)}, u32[]{:S(2)}, u32[]{:S(2)}) collective-permute-start(bf16[48,128]{1,0:T(8,128)(2,1)S(1)} %get-tuple-element.55), channel_id=1, source_target_pairs={{0,4},{4,0},{8,12},{12,8},{1,5},{5,1},{9,13},{13,9},{2,6},{6,2},{1... | collective-permute-start | bytes 36872 | tf_op jit(solution)/shard_map/ppermute | solution.py:342
  14.8 6.8 %collective-permute-start.2 = (bf16[256,128]{1,0:T(8,128)(2,1)S(1)}, bf16[256,128]{1,0:T(8,128)(2,1)S(1)}, u32[]{:S(2)}, u32[]{:S(2)}) collective-permute-start(bf16[256,128]{1,0:T(8,128)(2,1)S(1)} %get-tuple-element.53), channel_id=1, source_target_pairs={{0,12},{4,8},{8,4},{12,0},{1,13},{5,9},{9,5},{13,1},{2,14},{6,10},... | collective-permute-start | bytes 196616 | tf_op jit(solution)/shard_map/ppermute | solution.py:342
  16.1 5.8 %collective-permute-start.3 = (bf16[256,128]{1,0:T(8,128)(2,1)S(1)}, bf16[256,128]{1,0:T(8,128)(2,1)S(1)}, u32[]{:S(2)}, u32[]{:S(2)}) collective-permute-start(bf16[256,128]{1,0:T(8,128)(2,1)S(1)} %get-tuple-element.52), channel_id=1, source_target_pairs={{0,8},{4,12},{8,0},{12,4},{1,9},{5,13},{9,1},{13,5},{2,10},{6,14},... | collective-permute-start | bytes 196616 | tf_op jit(solution)/shard_map/ppermute | solution.py:342
  16.8 5.0 %collective-permute-start.4 = (bf16[256,128]{1,0:T(8,128)(2,1)S(1)}, bf16[256,128]{1,0:T(8,128)(2,1)S(1)}, u32[]{:S(2)}, u32[]{:S(2)}) collective-permute-start(bf16[256,128]{1,0:T(8,128)(2,1)S(1)} %get-tuple-element.51), channel_id=1, source_target_pairs={{0,4},{4,0},{8,12},{12,8},{1,5},{5,1},{9,13},{13,9},{2,6},{6,2},{1... | collective-permute-start | bytes 196616 | tf_op jit(solution)/shard_map/ppermute | solution.py:342
  17.2 5.6 %collective-permute-start.8 = (f32[16,128]{1,0:T(8,128)S(1)}, f32[16,128]{1,0:T(8,128)S(1)}, u32[]{:S(2)}, u32[]{:S(2)}) collective-permute-start(f32[16,128]{1,0:T(8,128)S(1)} %get-tuple-element.61), channel_id=1, source_target_pairs={{0,3},{1,2},{2,1},{3,0},{4,7},{5,6},{6,5},{7,4},{8,11},{9,10},{10,... | collective-permute-start | bytes 24584 | tf_op jit(solution)/shard_map/ppermute | solution.py:342
  20.9 4.5 %collective-permute-start.9 = (f32[16,128]{1,0:T(8,128)S(1)}, f32[16,128]{1,0:T(8,128)S(1)}, u32[]{:S(2)}, u32[]{:S(2)}) collective-permute-start(f32[16,128]{1,0:T(8,128)S(1)} %get-tuple-element.60), channel_id=1, source_target_pairs={{0,2},{1,3},{2,0},{3,1},{4,6},{5,7},{6,4},{7,5},{8,10},{9,11},{10,... | collective-permute-start | bytes 24584 | tf_op jit(solution)/shard_map/ppermute | solution.py:342
  21.5 3.9 %collective-permute-start.10 = (f32[16,128]{1,0:T(8,128)S(1)}, f32[16,128]{1,0:T(8,128)S(1)}, u32[]{:S(2)}, u32[]{:S(2)}) collective-permute-start(f32[16,128]{1,0:T(8,128)S(1)} %get-tuple-element.59), channel_id=1, source_target_pairs={{0,1},{1,0},{2,3},{3,2},{4,5},{5,4},{6,7},{7,6},{8,9},{9,8},{10,11... | collective-permute-start | bytes 24584 | tf_op jit(solution)/shard_map/ppermute | solution.py:342

commit v17 on v15

--- a/solution.py
+++ b/solution.py
@@ -257,9 +257,10 @@
         if step:
             middle -= SMOOTHING * SMOOTHING * factors[-1]
         factors.append(1.0 / middle)
-    forward = [series[0] * factors[0]]
+    scaled = [cells * factor for cells, factor in zip(series, factors)]
+    forward = [scaled[0]]
     for step in range(1, total):
-        forward.append((series[step] + SMOOTHING * forward[step - 1]) * factors[step])
+        forward.append(scaled[step] + (SMOOTHING * factors[step]) * forward[step - 1])
     baseline = [None] * total
     baseline[total - 1] = forward[total - 1]
     for step in range(total - 2, -1, -1):
@@ -291,11 +292,15 @@
         feet = feet_ref[block]
         weights.append(jnp.concatenate([jnp.where(left, feet, 0.0), jnp.where(left, 0.0, feet)], axis=0))
         sums.append(jnp.concatenate([sums_ref[pl.ds(block, rows, stride=n_frame), :], extra], axis=0))
+    sums = jnp.concatenate(sums, axis=1)
+    parts = []
+    for _ in range(3):
+        parts.append(sums.astype(jnp.bfloat16))
+        sums = sums - parts[-1].astype(jnp.float32)
     totals = lax.dot_general(
-        jnp.concatenate(weights, axis=1),
-        jnp.concatenate(sums, axis=1),
+        jnp.concatenate(weights * 3, axis=1).astype(jnp.bfloat16),
+        jnp.concatenate(parts, axis=1),
         (((1,), (1,)), ((), ())),
-        precision=lax.Precision.HIGHEST,
         preferred_element_type=jnp.float32,
     )
     share = out_ref.shape[2]
@@ -430,7 +435,9 @@
             pltpu.VMEM((n_frame, n_row * share // 2, TILE), jnp.float32),
         ],
     )(*sides[::-1])
-    pairs = call(add_kernel, "add", [vmem] * 2, array(n_row // 2, share, TILE))(*swapped_one(partial, "row", row % 2, 1))
+    own, there = swapped_one(partial, "row", row % 2, 1)
+    *pieces, there = lax.optimization_barrier((*pieces[::-1], there))
+    pairs = call(add_kernel, "add", [vmem] * 2, array(n_row // 2, share, TILE))(own, there)
     shares = swapped_one(pairs, "row", row // 2, 2)
     spikes = call(
         functools.partial(temporal_kernel, frames=frames),
@@ -438,7 +445,7 @@
         [vmem] * n_frame,
         array(n_frame * frames, rows_dev, tiles_dev * TILE, dtype=jnp.bfloat16),
         [pltpu.VMEM((n_frame, frames * positions, TILE), jnp.bfloat16)],
-    )(*pieces[::-1])
+    )(*pieces)
     spikes, *shares = in_turn(spikes, *shares)
     traces = call(means_kernel, "means", [vmem] * 2, array(share, n_frame * frames))(*shares)
     return (spikes, traces)

time: 27.8 us -> 27.6 us (level)
  waiting for transfers between devices: 5.6 us -> 5.11 us
  starting transfers between devices: 12.9 us -> 13.3 us
    ppermute x6, waiting for transfers between devices: 2.94 us -> 0.02 us  [swapped(): lax.ppermute(part, axis, [(i, i ^ step) for i in range(count)])]
    ppermute x2, waiting for transfers between devices: 0.01 us -> 2.44 us  [swapped_one(): lax.ppermute(there, axis, [(i, i ^ step) for i in range(lax.axis_size(axi...]
  transfers between devices with their start and end apart: 10 -> 10, of which waited for: 4 -> 3; matrix products, arithmetic and copies ran while one was open for 0% -> 0% of each run, Pallas kernels for 6% -> 7%
where the time goes in v17:
time: 27.6 us; the launch traced here: 27.4 us
  starting transfers between devices  13.3 us (48%)
  Pallas kernels  5.69 us (21%)
  waiting for transfers between devices  5.11 us (19%)
  local copies, waits for them, and re-layouts  2.41 us (9%)
  between operations  0.78 us (3%)
    ppermute x2, starting transfers between devices, swapped_one(): lax.ppermute(there, axis, [(i, i ^ step) for i in range(lax.axis_size(axi...  6.13 us
    ppermute x6, starting transfers between devices, swapped(): lax.ppermute(part, axis, [(i, i ^ step) for i in range(count)])  4.01 us
    ppermute x1, starting transfers between devices, by_halo(): inner = lax.ppermute(inner.astype(jnp.float16), 'row', inner_swap)  3.09 us
    pallas_call x1, Pallas kernels, by_halo(): call(restore_kernel, 'restore', [vmem] * 6, (array(n_frame, frames * posi...  2.84 us
    ppermute x1, waiting for transfers between devices, by_halo(): inner = lax.ppermute(inner.astype(jnp.float16), 'row', inner_swap)  2.65 us
    ppermute x2, waiting for transfers between devices, swapped_one(): lax.ppermute(there, axis, [(i, i ^ step) for i in range(lax.axis_size(axi...  2.44 us
    unnamed x8, local copies, waits for them, and re-layouts  2.35 us
    pallas_call x1, Pallas kernels, by_halo(): call(functools.partial(temporal_kernel, frames=frames), 'temporal', [vmem...  0.91 us
  transfers between devices with their start and end apart: 10, of which 3 were waited for; matrix products, arithmetic and copies ran while one was open for 0% of the time, Pallas kernels for 7%

profile of v17, /device:TPU:0, one launch (start us, length us, event | category | flops | bytes accessed | tf_op | source)
XLA Modules:
  0.0 27.4 jit_solution(10844605483296045755)
XLA Ops:
  0.6 0.0 copy-start
  0.6 1.0 %copy-done = f32[4,16,2048]{2,1,0:T(8,128)S(1)} copy-done((f32[4,16,2048]{2,1,0:T(8,128)S(1)}, f32[4,16,2048]{2,1,0:T(8,128)}, u32[]{:S(2)}) %copy-start) | copy-done | bytes 524312
  1.7 0.1 halo.1
  1.8 3.1 %collective-permute-start = (f16[48,2048]{1,0:T(8,128)(2,1)S(1)}, f16[48,2048]{1,0:T(8,128)(2,1)S(1)}, u32[]{:S(2)}, u32[]{:S(2)}) collective-permute-start(f16[48,2048]{1,0:T(8,128)(2,1)S(1)} %convert_element_type.12), channel_id=1, source_target_pairs={{0,1},{1,0},{2,3},{3,2},{4,5},{5,4},{6,7},{7,6},{8,9},{9,8},{10,11... | collective-permute-start | bytes 589832 | tf_op jit(solution)/shard_map/ppermute | solution.py:397
  4.9 0.1 collective-permute-start.1
  5.0 0.7 %copy-done.1 = s32[256,16,4]{0,2,1:T(4,128)S(1)} copy-done((s32[256,16,4]{0,2,1:T(4,128)S(1)}, s32[256,16,4]{0,2,1:T(4,128)}, u32[]{:S(2)}) %copy-start.1) | copy-done | bytes 65560
  5.8 0.1 feet.1.feet_ref
  5.9 0.6 %copy-done.2 = f32[8,5]{1,0:T(8,128)S(1)} copy-done((f32[8,5]{1,0:T(8,128)S(1)}, f32[8,5]{1,0:T(8,128)}, u32[]{:S(2)}) %copy-start.2) | copy-done | bytes 184
  6.4 0.7 %taps.1 = (f32[4,48,128]{2,1,0:T(8,128)S(1)}, f32[4,48,128]{2,1,0:T(8,128)S(1)}) custom-call(s32[8]{0:T(128)S(1)} %copy-done.3, f32[8,5]{1,0:T(8,128)S(1)} %copy-done.2), custom_call_target="tpu_custom_call" | custom-call | flops 1000 | bytes 1000 | tf_op jit(solution)/shard_map/taps/pallas_call | solution.py:400
  7.2 2.7 %collective-permute-done = f16[48,2048]{1,0:T(8,128)(2,1)S(1)} collective-permute-done((f16[48,2048]{1,0:T(8,128)(2,1)S(1)}, f16[48,2048]{1,0:T(8,128)(2,1)S(1)}, u32[]{:S(2)}, u32[]{:S(2)}) %collective-permute-start) | collective-permute-done | bytes 196640 | tf_op jit(solution)/shard_map/ppermute | solution.py:397
  9.8 0.0 collective-permute-done.1
  9.8 0.1 convert_select_fusion
  9.9 2.8 %restore.1 = (bf16[4,256,128]{2,1,0:T(8,128)(2,1)S(1)}, bf16[4,48,128]{2,1,0:T(8,128)(2,1)S(1)}) custom-call(f32[4,48,128]{2,1,0:T(8,128)S(1)} %get-tuple-element.21.taps_ref, f32[4,48,128]{2,1,0:T(8,128)S(1)} %get-tuple-element.22.back_ref, bf16[4,32,128]{2,1,0:T(8,128)(2,1)S(1)} %feet.1.feet_ref, f32[4,16,2048]{2,1,0:T(8,128)S(1)} %get-tuple-element.23.own_ref, ...), custom_call_target="tpu_custom_call" | custom-call | flops 1000 | bytes 1000 | tf_op jit(solution)/shard_map/restore/pallas_call | solution.py:416
  12.8 0.3 %collective-permute-start.5 = (bf16[48,128]{1,0:T(8,128)(2,1)S(1)}, bf16[48,128]{1,0:T(8,128)(2,1)S(1)}, u32[]{:S(2)}, u32[]{:S(2)}) collective-permute-start(bf16[48,128]{1,0:T(8,128)(2,1)S(1)} %get-tuple-element.49), channel_id=1, source_target_pairs={{0,12},{4,8},{8,4},{12,0},{1,13},{5,9},{9,5},{13,1},{2,14},{6,10},... | collective-permute-start | bytes 36872 | tf_op jit(solution)/shard_map/ppermute | solution.py:346
  13.1 1.5 %collective-permute-start.6 = (bf16[48,128]{1,0:T(8,128)(2,1)S(1)}, bf16[48,128]{1,0:T(8,128)(2,1)S(1)}, u32[]{:S(2)}, u32[]{:S(2)}) collective-permute-start(bf16[48,128]{1,0:T(8,128)(2,1)S(1)} %get-tuple-element.48), channel_id=1, source_target_pairs={{0,8},{4,12},{8,0},{12,4},{1,9},{5,13},{9,1},{13,5},{2,10},{6,14},... | collective-permute-start | bytes 36872 | tf_op jit(solution)/shard_map/ppermute | solution.py:346
  14.6 0.1 collective-permute-start.7
  14.8 1.3 %collective-permute-start.2 = (bf16[256,128]{1,0:T(8,128)(2,1)S(1)}, bf16[256,128]{1,0:T(8,128)(2,1)S(1)}, u32[]{:S(2)}, u32[]{:S(2)}) collective-permute-start(bf16[256,128]{1,0:T(8,128)(2,1)S(1)} %get-tuple-element.45), channel_id=1, source_target_pairs={{0,12},{4,8},{8,4},{12,0},{1,13},{5,9},{9,5},{13,1},{2,14},{6,10},... | collective-permute-start | bytes 196616 | tf_op jit(solution)/shard_map/ppermute | solution.py:346
  16.1 0.8 %collective-permute-start.3 = (bf16[256,128]{1,0:T(8,128)(2,1)S(1)}, bf16[256,128]{1,0:T(8,128)(2,1)S(1)}, u32[]{:S(2)}, u32[]{:S(2)}) collective-permute-start(bf16[256,128]{1,0:T(8,128)(2,1)S(1)} %get-tuple-element.44), channel_id=1, source_target_pairs={{0,8},{4,12},{8,0},{12,4},{1,9},{5,13},{9,1},{13,5},{2,10},{6,14},... | collective-permute-start | bytes 196616 | tf_op jit(solution)/shard_map/ppermute | solution.py:346
  16.8 0.0 collective-permute-done.5.refs_0_
  16.8 0.0 collective-permute-start.4
  16.8 0.0 collective-permute-done.6.refs_1_
  16.8 0.0 collective-permute-done.7.refs_2_
  16.8 0.3 %partial.1 = f32[2,2,16,128]{3,2,1,0:T(8,128)S(1)} custom-call(bf16[48,128]{1,0:T(8,128)(2,1)S(1)} %collective-permute-done.5.refs_0_, bf16[48,128]{1,0:T(8,128)(2,1)S(1)} %collective-permute-done.6.refs_1_, bf16[48,128]{1,0:T(8,128)(2,1)S(1)} %collective-permute-done.7.refs_2_, bf16[48,128]{1,0:T(8,128)(2,1)S(1)} %get-tuple-element.46.refs_3_), custom_call_target="tpu_custom_call" | custom-call | flops 1000 | bytes 1000 | tf_op jit(solution)/shard_map/partial/pallas_call | solution.py:428
  17.2 2.9 %collective-permute-start.8 = (f32[2,16,128]{2,1,0:T(8,128)S(1)}, f32[2,16,128]{2,1,0:T(8,128)S(1)}, u32[]{:S(2)}, u32[]{:S(2)}) collective-permute-start(f32[2,16,128]{2,1,0:T(8,128)S(1)} %get-tuple-element.51), channel_id=1, source_target_pairs={{0,1},{1,0},{2,3},{3,2},{4,5},{5,4},{6,7},{7,6},{8,9},{9,8},{10,11... | collective-permute-start | bytes 49160 | tf_op jit(solution)/shard_map/ppermute | solution.py:354
  20.1 1.7 %collective-permute-done.8.second_ref = f32[2,16,128]{2,1,0:T(8,128)S(1)} collective-permute-done((f32[2,16,128]{2,1,0:T(8,128)S(1)}, f32[2,16,128]{2,1,0:T(8,128)S(1)}, u32[]{:S(2)}, u32[]{:S(2)}) %collective-permute-start.8) | collective-permute-done | bytes 16416 | tf_op jit(solution)/shard_map/ppermute | solution.py:354
  21.8 0.0 collective-permute-done.2.refs_0_
  21.8 0.0 collective-permute-done.3.refs_1_
  21.8 0.0 collective-permute-done.4.refs_2_
  21.8 3.3 %collective-permute-start.9 = (f32[16,128]{1,0:T(8,128)S(1)}, f32[16,128]{1,0:T(8,128)S(1)}, u32[]{:S(2)}, u32[]{:S(2)}) collective-permute-start(f32[16,128]{1,0:T(8,128)S(1)} %get-tuple-element.52), channel_id=1, source_target_pairs={{0,2},{1,3},{2,0},{3,1},{4,6},{5,7},{6,4},{7,5},{8,10},{9,11},{10,... | collective-permute-start | bytes 24584 | tf_op jit(solution)/shard_map/ppermute | solution.py:354
  25.1 0.9 %temporal.1 = bf16[16,16,512]{2,1,0:T(8,128)(2,1)} custom-call(bf16[256,128]{1,0:T(8,128)(2,1)S(1)} %collective-permute-done.2.refs_0_, bf16[256,128]{1,0:T(8,128)(2,1)S(1)} %collective-permute-done.3.refs_1_, bf16[256,128]{1,0:T(8,128)(2,1)S(1)} %collective-permute-done.4.refs_2_, bf16[256,128]{1,0:T(8,128)(2,1)S(1)} %get-tuple-element.33.refs_3_), custom_call_target="tpu_custom_call" | custom-call | flops 1000 | bytes 1000 | tf_op jit(solution)/shard_map/temporal/pallas_call | solution.py:442
  26.0 0.7 %collective-permute-done.9.refs_1_ = f32[16,128]{1,0:T(8,128)S(1)} collective-permute-done((f32[16,128]{1,0:T(8,128)S(1)}, f32[16,128]{1,0:T(8,128)S(1)}, u32[]{:S(2)}, u32[]{:S(2)}) %collective-permute-start.9) | collective-permute-done | bytes 8224 | tf_op jit(solution)/shard_map/ppermute | solution.py:354
  26.7 0.7 %means.1 = f32[16,16]{1,0:T(8,128)} custom-call(f32[16,128]{1,0:T(8,128)S(1)} %get-tuple-element.38.refs_0_, f32[16,128]{1,0:T(8,128)S(1)} %collective-permute-done.9.refs_1_), custom_call_target="tpu_custom_call" | custom-call | flops 1000 | bytes 1000 | tf_op jit(solution)/shard_map/means/pallas_call | solution.py:450
  (11 shorter events, 0.1 us)
Async XLA Ops:
  0.6 1.0 %copy-start = (f32[4,16,2048]{2,1,0:T(8,128)S(1)}, f32[4,16,2048]{2,1,0:T(8,128)}, u32[]{:S(2)}) copy-start(f32[4,16,2048]{2,1,0:T(8,128)} %observed_ref.1) | copy-start | bytes 1572868
  1.8 8.0 %collective-permute-start = (f16[48,2048]{1,0:T(8,128)(2,1)S(1)}, f16[48,2048]{1,0:T(8,128)(2,1)S(1)}, u32[]{:S(2)}, u32[]{:S(2)}) collective-permute-start(f16[48,2048]{1,0:T(8,128)(2,1)S(1)} %convert_element_type.12), channel_id=1, source_target_pairs={{0,1},{1,0},{2,3},{3,2},{4,5},{5,4},{6,7},{7,6},{8,9},{9,8},{10,11... | collective-permute-start | bytes 589832 | tf_op jit(solution)/shard_map/ppermute | solution.py:397
  4.9 0.8 %copy-start.1 = (s32[256,16,4]{0,2,1:T(4,128)S(1)}, s32[256,16,4]{0,2,1:T(4,128)}, u32[]{:S(2)}) copy-start(s32[256,16,4]{0,2,1:T(4,128)} %param.7) | copy-start | bytes 196612
  4.9 4.9 %collective-permute-start.1 = (f16[48,2048]{1,0:T(8,128)(2,1)S(1)}, f16[48,2048]{1,0:T(8,128)(2,1)S(1)}, u32[]{:S(2)}, u32[]{:S(2)}) collective-permute-start(f16[48,2048]{1,0:T(8,128)(2,1)S(1)} %convert_element_type.13), channel_id=1, source_target_pairs={{0,4},{1,2},{2,1},{3,7},{4,0},{5,6},{6,5},{7,3},{8,12},{9,10},{10,... | collective-permute-start | bytes 589832 | tf_op jit(solution)/shard_map/ppermute | solution.py:398
  5.8 0.7 %copy-start.2 = (f32[8,5]{1,0:T(8,128)S(1)}, f32[8,5]{1,0:T(8,128)}, u32[]{:S(2)}) copy-start(f32[8,5]{1,0:T(8,128)} %kernels_ref.1) | copy-start | bytes 484
  5.8 0.7 %copy-start.3 = (s32[8]{0:T(128)S(1)}, s32[8]{0:T(128)}, u32[]{:S(2)}) copy-start(s32[8]{0:T(128)} %band_ref.1) | copy-start | bytes 100
  12.8 4.0 %collective-permute-start.5 = (bf16[48,128]{1,0:T(8,128)(2,1)S(1)}, bf16[48,128]{1,0:T(8,128)(2,1)S(1)}, u32[]{:S(2)}, u32[]{:S(2)}) collective-permute-start(bf16[48,128]{1,0:T(8,128)(2,1)S(1)} %get-tuple-element.49), channel_id=1, source_target_pairs={{0,12},{4,8},{8,4},{12,0},{1,13},{5,9},{9,5},{13,1},{2,14},{6,10},... | collective-permute-start | bytes 36872 | tf_op jit(solution)/shard_map/ppermute | solution.py:346
  13.1 3.7 %collective-permute-start.6 = (bf16[48,128]{1,0:T(8,128)(2,1)S(1)}, bf16[48,128]{1,0:T(8,128)(2,1)S(1)}, u32[]{:S(2)}, u32[]{:S(2)}) collective-permute-start(bf16[48,128]{1,0:T(8,128)(2,1)S(1)} %get-tuple-element.48), channel_id=1, source_target_pairs={{0,8},{4,12},{8,0},{12,4},{1,9},{5,13},{9,1},{13,5},{2,10},{6,14},... | collective-permute-start | bytes 36872 | tf_op jit(solution)/shard_map/ppermute | solution.py:346
  14.6 2.2 %collective-permute-start.7 = (bf16[48,128]{1,0:T(8,128)(2,1)S(1)}, bf16[48,128]{1,0:T(8,128)(2,1)S(1)}, u32[]{:S(2)}, u32[]{:S(2)}) collective-permute-start(bf16[48,128]{1,0:T(8,128)(2,1)S(1)} %get-tuple-element.47), channel_id=1, source_target_pairs={{0,4},{4,0},{8,12},{12,8},{1,5},{5,1},{9,13},{13,9},{2,6},{6,2},{1... | collective-permute-start | bytes 36872 | tf_op jit(solution)/shard_map/ppermute | solution.py:346
  14.8 7.0 %collective-permute-start.2 = (bf16[256,128]{1,0:T(8,128)(2,1)S(1)}, bf16[256,128]{1,0:T(8,128)(2,1)S(1)}, u32[]{:S(2)}, u32[]{:S(2)}) collective-permute-start(bf16[256,128]{1,0:T(8,128)(2,1)S(1)} %get-tuple-element.45), channel_id=1, source_target_pairs={{0,12},{4,8},{8,4},{12,0},{1,13},{5,9},{9,5},{13,1},{2,14},{6,10},... | collective-permute-start | bytes 196616 | tf_op jit(solution)/shard_map/ppermute | solution.py:346
  16.1 5.7 %collective-permute-start.3 = (bf16[256,128]{1,0:T(8,128)(2,1)S(1)}, bf16[256,128]{1,0:T(8,128)(2,1)S(1)}, u32[]{:S(2)}, u32[]{:S(2)}) collective-permute-start(bf16[256,128]{1,0:T(8,128)(2,1)S(1)} %get-tuple-element.44), channel_id=1, source_target_pairs={{0,8},{4,12},{8,0},{12,4},{1,9},{5,13},{9,1},{13,5},{2,10},{6,14},... | collective-permute-start | bytes 196616 | tf_op jit(solution)/shard_map/ppermute | solution.py:346
  16.8 5.0 %collective-permute-start.4 = (bf16[256,128]{1,0:T(8,128)(2,1)S(1)}, bf16[256,128]{1,0:T(8,128)(2,1)S(1)}, u32[]{:S(2)}, u32[]{:S(2)}) collective-permute-start(bf16[256,128]{1,0:T(8,128)(2,1)S(1)} %get-tuple-element.43), channel_id=1, source_target_pairs={{0,4},{4,0},{8,12},{12,8},{1,5},{5,1},{9,13},{13,9},{2,6},{6,2},{1... | collective-permute-start | bytes 196616 | tf_op jit(solution)/shard_map/ppermute | solution.py:346
  17.2 4.6 %collective-permute-start.8 = (f32[2,16,128]{2,1,0:T(8,128)S(1)}, f32[2,16,128]{2,1,0:T(8,128)S(1)}, u32[]{:S(2)}, u32[]{:S(2)}) collective-permute-start(f32[2,16,128]{2,1,0:T(8,128)S(1)} %get-tuple-element.51), channel_id=1, source_target_pairs={{0,1},{1,0},{2,3},{3,2},{4,5},{5,4},{6,7},{7,6},{8,9},{9,8},{10,11... | collective-permute-start | bytes 49160 | tf_op jit(solution)/shard_map/ppermute | solution.py:354
  21.8 4.9 %collective-permute-start.9 = (f32[16,128]{1,0:T(8,128)S(1)}, f32[16,128]{1,0:T(8,128)S(1)}, u32[]{:S(2)}, u32[]{:S(2)}) collective-permute-start(f32[16,128]{1,0:T(8,128)S(1)} %get-tuple-element.52), channel_id=1, source_target_pairs={{0,2},{1,3},{2,0},{3,1},{4,6},{5,7},{6,4},{7,5},{8,10},{9,11},{10,... | collective-permute-start | bytes 24584 | tf_op jit(solution)/shard_map/ppermute | solution.py:354

commit v18 on v16

--- a/solution.py
+++ b/solution.py
@@ -383,9 +383,9 @@
         for i in range(n_row):
             there = (f ^ 1, i) if i in (0, n_row - 1) else (f, (i - 1 ^ 1) + 1)
             outer_swap.append((f * n_row + i, there[0] * n_row + there[1]))
-    inner = lax.ppermute(inner.astype(jnp.float16), "row", inner_swap)
-    outer = lax.ppermute(outer.astype(jnp.float16), ("frame", "row"), outer_swap)
-    inner, outer = in_turn(inner, outer)
+    inner = inner.astype(jnp.float16)
+    inner, band_kernel = lax.optimization_barrier((inner, band_kernel))
+    inner = lax.ppermute(inner, "row", inner_swap)
     taps, back = call(
         functools.partial(taps_kernel, height=rows_dev * n_row, rows_dev=rows_dev),
         "taps",
@@ -393,6 +393,9 @@
         (array(len(SIDES), span, TILE),) * 2,
         [pltpu.VMEM((len(SIDES), span + 2 * PAD, TILE), jnp.float32)],
     )(band_kernel, kernels)
+    outer, taps = lax.optimization_barrier((outer, taps))
+    outer = lax.ppermute(outer.astype(jnp.float16), ("frame", "row"), outer_swap)
+    inner, outer = in_turn(inner, outer)
     feet = call(feet_kernel, "feet", [vmem], array(n_frame, n_row * share // 2, TILE, dtype=jnp.bfloat16))(
         masks.transpose(1, 2, 0)
     )

time: 26.4 us -> 26.8 us (1.015)
  starting transfers between devices: 11.8 us -> 12.5 us
  local copies, waits for them, and re-layouts: 2.4 us -> 1.83 us
  waiting for transfers between devices: 5.35 us -> 5.68 us
    ppermute x9, starting transfers between devices: 8.63 us -> 9.35 us  [swapped(): lax.ppermute(part, axis, [(i, i ^ step) for i in range(count)])]
    unnamed x8, local copies, waits for them, and re-layouts: 2.35 us -> 1.77 us
    ppermute x1, waiting for transfers between devices: 2.66 us -> 3.23 us  [by_halo(): inner = lax.ppermute(inner, 'row', inner_swap)]
  transfers between devices with their start and end apart: 11 -> 11, of which waited for: 2 -> 3; matrix products, arithmetic and copies ran while one was open for 0% -> 0% of each run, Pallas kernels for 8% -> 8%
where the time goes in v18:
time: 26.8 us; the launch traced here: 26.6 us
  starting transfers between devices  12.5 us (47%)
  Pallas kernels  5.69 us (21%)
  waiting for transfers between devices  5.68 us (21%)
  local copies, waits for them, and re-layouts  1.83 us (7%)
  between operations  0.78 us (3%)
    ppermute x9, starting transfers between devices, swapped(): lax.ppermute(part, axis, [(i, i ^ step) for i in range(count)])  9.35 us
    ppermute x1, waiting for transfers between devices, by_halo(): inner = lax.ppermute(inner, 'row', inner_swap)  3.23 us
    ppermute x1, starting transfers between devices, by_halo(): inner = lax.ppermute(inner, 'row', inner_swap)  3.09 us
    pallas_call x1, Pallas kernels, by_halo(): call(restore_kernel, 'restore', [vmem] * 6, (array(n_frame, frames * posi...  2.84 us
    ppermute x9, waiting for transfers between devices, swapped(): lax.ppermute(part, axis, [(i, i ^ step) for i in range(count)])  2.45 us
    unnamed x8, local copies, waits for them, and re-layouts  1.77 us
    pallas_call x1, Pallas kernels, by_halo(): call(functools.partial(temporal_kernel, frames=frames), 'temporal', [vmem...  0.91 us
    pallas_call x1, Pallas kernels, by_halo(): call(functools.partial(taps_kernel, height=rows_dev * n_row, rows_dev=row...  0.69 us
  transfers between devices with their start and end apart: 11, of which 3 were waited for; matrix products, arithmetic and copies ran while one was open for 0% of the time, Pallas kernels for 8%

profile of v18, /device:TPU:0, one launch (start us, length us, event | category | flops | bytes accessed | tf_op | source)
XLA Modules:
  0.0 26.6 jit_solution(11762690008572388203)
XLA Ops:
  0.6 1.0 %copy-done = f32[4,16,2048]{2,1,0:T(8,128)S(1)} copy-done((f32[4,16,2048]{2,1,0:T(8,128)S(1)}, f32[4,16,2048]{2,1,0:T(8,128)}, u32[]{:S(2)}) %copy-start) | copy-done | bytes 524312
  1.7 0.1 halo.1
  1.8 0.0 copy-start.2
  1.8 0.0 copy-start.3
  1.9 3.1 %collective-permute-start = (f16[48,2048]{1,0:T(8,128)(2,1)S(1)}, f16[48,2048]{1,0:T(8,128)(2,1)S(1)}, u32[]{:S(2)}, u32[]{:S(2)}) collective-permute-start(f16[48,2048]{1,0:T(8,128)(2,1)S(1)} %convert_element_type.12), channel_id=1, source_target_pairs={{0,1},{1,0},{2,3},{3,2},{4,5},{5,4},{6,7},{7,6},{8,9},{9,8},{10,11... | collective-permute-start | bytes 589832 | tf_op jit(solution)/shard_map/ppermute | solution.py:388
  4.9 0.7 %taps.1 = (f32[4,48,128]{2,1,0:T(8,128)S(1)}, f32[4,48,128]{2,1,0:T(8,128)S(1)}) custom-call(s32[8]{0:T(128)S(1)} %copy-done.3, f32[8,5]{1,0:T(8,128)S(1)} %copy-done.2), custom_call_target="tpu_custom_call" | custom-call | flops 1000 | bytes 1000 | tf_op jit(solution)/shard_map/taps/pallas_call | solution.py:389
  5.6 0.0 copy-start.1
  5.7 0.1 collective-permute-start.1
  5.8 0.7 %copy-done.1 = s32[256,16,4]{0,2,1:T(4,128)S(1)} copy-done((s32[256,16,4]{0,2,1:T(4,128)S(1)}, s32[256,16,4]{0,2,1:T(4,128)}, u32[]{:S(2)}) %copy-start.1) | copy-done | bytes 65560
  6.5 0.1 feet.1.feet_ref
  6.6 3.2 %collective-permute-done = f16[48,2048]{1,0:T(8,128)(2,1)S(1)} collective-permute-done((f16[48,2048]{1,0:T(8,128)(2,1)S(1)}, f16[48,2048]{1,0:T(8,128)(2,1)S(1)}, u32[]{:S(2)}, u32[]{:S(2)}) %collective-permute-start) | collective-permute-done | bytes 196640 | tf_op jit(solution)/shard_map/ppermute | solution.py:388
  9.8 0.0 collective-permute-done.1
  9.8 0.1 convert_select_fusion
  9.9 2.8 %restore.1 = (bf16[4,256,128]{2,1,0:T(8,128)(2,1)S(1)}, bf16[4,48,128]{2,1,0:T(8,128)(2,1)S(1)}) custom-call(f32[4,48,128]{2,1,0:T(8,128)S(1)} %get-tuple-element.33.taps_ref, f32[4,48,128]{2,1,0:T(8,128)S(1)} %get-tuple-element.34.back_ref, bf16[4,32,128]{2,1,0:T(8,128)(2,1)S(1)} %feet.1.feet_ref, f32[4,16,2048]{2,1,0:T(8,128)S(1)} %get-tuple-element.35.own_ref, ...), custom_call_target="tpu_custom_call" | custom-call | flops 1000 | bytes 1000 | tf_op jit(solution)/shard_map/restore/pallas_call | solution.py:408
  12.8 0.3 %collective-permute-start.5 = (bf16[48,128]{1,0:T(8,128)(2,1)S(1)}, bf16[48,128]{1,0:T(8,128)(2,1)S(1)}, u32[]{:S(2)}, u32[]{:S(2)}) collective-permute-start(bf16[48,128]{1,0:T(8,128)(2,1)S(1)} %get-tuple-element.65), channel_id=1, source_target_pairs={{0,12},{4,8},{8,4},{12,0},{1,13},{5,9},{9,5},{13,1},{2,14},{6,10},... | collective-permute-start | bytes 36872 | tf_op jit(solution)/shard_map/ppermute | solution.py:342
  13.1 1.5 %collective-permute-start.6 = (bf16[48,128]{1,0:T(8,128)(2,1)S(1)}, bf16[48,128]{1,0:T(8,128)(2,1)S(1)}, u32[]{:S(2)}, u32[]{:S(2)}) collective-permute-start(bf16[48,128]{1,0:T(8,128)(2,1)S(1)} %get-tuple-element.64), channel_id=1, source_target_pairs={{0,8},{4,12},{8,0},{12,4},{1,9},{5,13},{9,1},{13,5},{2,10},{6,14},... | collective-permute-start | bytes 36872 | tf_op jit(solution)/shard_map/ppermute | solution.py:342
  14.6 0.1 collective-permute-start.7
  14.8 1.3 %collective-permute-start.2 = (bf16[256,128]{1,0:T(8,128)(2,1)S(1)}, bf16[256,128]{1,0:T(8,128)(2,1)S(1)}, u32[]{:S(2)}, u32[]{:S(2)}) collective-permute-start(bf16[256,128]{1,0:T(8,128)(2,1)S(1)} %get-tuple-element.61), channel_id=1, source_target_pairs={{0,12},{4,8},{8,4},{12,0},{1,13},{5,9},{9,5},{13,1},{2,14},{6,10},... | collective-permute-start | bytes 196616 | tf_op jit(solution)/shard_map/ppermute | solution.py:342
  16.1 0.8 %collective-permute-start.3 = (bf16[256,128]{1,0:T(8,128)(2,1)S(1)}, bf16[256,128]{1,0:T(8,128)(2,1)S(1)}, u32[]{:S(2)}, u32[]{:S(2)}) collective-permute-start(bf16[256,128]{1,0:T(8,128)(2,1)S(1)} %get-tuple-element.60), channel_id=1, source_target_pairs={{0,8},{4,12},{8,0},{12,4},{1,9},{5,13},{9,1},{13,5},{2,10},{6,14},... | collective-permute-start | bytes 196616 | tf_op jit(solution)/shard_map/ppermute | solution.py:342
  16.8 0.0 collective-permute-done.5.refs_0_
  16.8 0.0 collective-permute-start.4
  16.8 0.0 collective-permute-done.6.refs_1_
  16.9 0.3 %partial.1 = f32[4,16,128]{2,1,0:T(8,128)S(1)} custom-call(bf16[48,128]{1,0:T(8,128)(2,1)S(1)} %collective-permute-done.5.refs_0_, bf16[48,128]{1,0:T(8,128)(2,1)S(1)} %collective-permute-done.6.refs_1_, bf16[48,128]{1,0:T(8,128)(2,1)S(1)} %collective-permute-done.7.refs_2_, bf16[48,128]{1,0:T(8,128)(2,1)S(1)} %get-tuple-element.62.refs_3_), custom_call_target="tpu_custom_call" | custom-call | flops 1000 | bytes 1000 | tf_op jit(solution)/shard_map/partial/pallas_call | solution.py:420
  17.2 3.7 %collective-permute-start.8 = (f32[16,128]{1,0:T(8,128)S(1)}, f32[16,128]{1,0:T(8,128)S(1)}, u32[]{:S(2)}, u32[]{:S(2)}) collective-permute-start(f32[16,128]{1,0:T(8,128)S(1)} %get-tuple-element.69), channel_id=1, source_target_pairs={{0,3},{1,2},{2,1},{3,0},{4,7},{5,6},{6,5},{7,4},{8,11},{9,10},{10,... | collective-permute-start | bytes 24584 | tf_op jit(solution)/shard_map/ppermute | solution.py:342
  20.9 1.4 %collective-permute-start.9 = (f32[16,128]{1,0:T(8,128)S(1)}, f32[16,128]{1,0:T(8,128)S(1)}, u32[]{:S(2)}, u32[]{:S(2)}) collective-permute-start(f32[16,128]{1,0:T(8,128)S(1)} %get-tuple-element.68), channel_id=1, source_target_pairs={{0,2},{1,3},{2,0},{3,1},{4,6},{5,7},{6,4},{7,5},{8,10},{9,11},{10,... | collective-permute-start | bytes 24584 | tf_op jit(solution)/shard_map/ppermute | solution.py:342
  22.3 0.0 collective-permute-done.2.refs_0_
  22.3 0.3 %collective-permute-start.10 = (f32[16,128]{1,0:T(8,128)S(1)}, f32[16,128]{1,0:T(8,128)S(1)}, u32[]{:S(2)}, u32[]{:S(2)}) collective-permute-start(f32[16,128]{1,0:T(8,128)S(1)} %get-tuple-element.67), channel_id=1, source_target_pairs={{0,1},{1,0},{2,3},{3,2},{4,5},{5,4},{6,7},{7,6},{8,9},{9,8},{10,11... | collective-permute-start | bytes 24584 | tf_op jit(solution)/shard_map/ppermute | solution.py:342
  22.6 0.0 collective-permute-done.4.refs_2_
  22.6 0.9 %temporal.1 = bf16[16,16,512]{2,1,0:T(8,128)(2,1)} custom-call(bf16[256,128]{1,0:T(8,128)(2,1)S(1)} %collective-permute-done.2.refs_0_, bf16[256,128]{1,0:T(8,128)(2,1)S(1)} %collective-permute-done.3.refs_1_, bf16[256,128]{1,0:T(8,128)(2,1)S(1)} %collective-permute-done.4.refs_2_, bf16[256,128]{1,0:T(8,128)(2,1)S(1)} %get-tuple-element.58.refs_3_), custom_call_target="tpu_custom_call" | custom-call | flops 1000 | bytes 1000 | tf_op jit(solution)/shard_map/temporal/pallas_call | solution.py:431
  23.5 2.0 %collective-permute-done.9.refs_1_ = f32[16,128]{1,0:T(8,128)S(1)} collective-permute-done((f32[16,128]{1,0:T(8,128)S(1)}, f32[16,128]{1,0:T(8,128)S(1)}, u32[]{:S(2)}, u32[]{:S(2)}) %collective-permute-start.9) | collective-permute-done | bytes 8224 | tf_op jit(solution)/shard_map/ppermute | solution.py:342
  25.5 0.5 %collective-permute-done.10.refs_2_ = f32[16,128]{1,0:T(8,128)S(1)} collective-permute-done((f32[16,128]{1,0:T(8,128)S(1)}, f32[16,128]{1,0:T(8,128)S(1)}, u32[]{:S(2)}, u32[]{:S(2)}) %collective-permute-start.10) | collective-permute-done | bytes 8224 | tf_op jit(solution)/shard_map/ppermute | solution.py:342
  25.9 0.7 %means.1 = f32[16,16]{1,0:T(8,128)} custom-call(f32[16,128]{1,0:T(8,128)S(1)} %collective-permute-done.8.refs_0_, f32[16,128]{1,0:T(8,128)S(1)} %collective-permute-done.9.refs_1_, f32[16,128]{1,0:T(8,128)S(1)} %collective-permute-done.10.refs_2_, f32[16,128]{1,0:T(8,128)S(1)} %get-tuple-element.55.refs_3_), custom_call_target="tpu_custom_call" | custom-call | flops 1000 | bytes 1000 | tf_op jit(solution)/shard_map/means/pallas_call | solution.py:439
  (11 shorter events, 0.1 us)
Async XLA Ops:
  0.6 1.0 %copy-start = (f32[4,16,2048]{2,1,0:T(8,128)S(1)}, f32[4,16,2048]{2,1,0:T(8,128)}, u32[]{:S(2)}) copy-start(f32[4,16,2048]{2,1,0:T(8,128)} %observed_ref.1) | copy-start | bytes 1572868
  1.8 3.1 %copy-start.2 = (f32[8,5]{1,0:T(8,128)S(1)}, f32[8,5]{1,0:T(8,128)}, u32[]{:S(2)}) copy-start(f32[8,5]{1,0:T(8,128)} %kernels_ref.1) | copy-start | bytes 484
  1.8 3.1 %copy-start.3 = (s32[8]{0:T(128)S(1)}, s32[8]{0:T(128)}, u32[]{:S(2)}) copy-start(s32[8]{0:T(128)} %band_ref) | copy-start | bytes 100
  1.9 8.0 %collective-permute-start = (f16[48,2048]{1,0:T(8,128)(2,1)S(1)}, f16[48,2048]{1,0:T(8,128)(2,1)S(1)}, u32[]{:S(2)}, u32[]{:S(2)}) collective-permute-start(f16[48,2048]{1,0:T(8,128)(2,1)S(1)} %convert_element_type.12), channel_id=1, source_target_pairs={{0,1},{1,0},{2,3},{3,2},{4,5},{5,4},{6,7},{7,6},{8,9},{9,8},{10,11... | collective-permute-start | bytes 589832 | tf_op jit(solution)/shard_map/ppermute | solution.py:388
  5.6 0.8 %copy-start.1 = (s32[256,16,4]{0,2,1:T(4,128)S(1)}, s32[256,16,4]{0,2,1:T(4,128)}, u32[]{:S(2)}) copy-start(s32[256,16,4]{0,2,1:T(4,128)} %param.7) | copy-start | bytes 196612
  5.7 4.2 %collective-permute-start.1 = (f16[48,2048]{1,0:T(8,128)(2,1)S(1)}, f16[48,2048]{1,0:T(8,128)(2,1)S(1)}, u32[]{:S(2)}, u32[]{:S(2)}) collective-permute-start(f16[48,2048]{1,0:T(8,128)(2,1)S(1)} %convert_element_type.13), channel_id=1, source_target_pairs={{0,4},{1,2},{2,1},{3,7},{4,0},{5,6},{6,5},{7,3},{8,12},{9,10},{10,... | collective-permute-start | bytes 589832 | tf_op jit(solution)/shard_map/ppermute | solution.py:397
  12.8 4.0 %collective-permute-start.5 = (bf16[48,128]{1,0:T(8,128)(2,1)S(1)}, bf16[48,128]{1,0:T(8,128)(2,1)S(1)}, u32[]{:S(2)}, u32[]{:S(2)}) collective-permute-start(bf16[48,128]{1,0:T(8,128)(2,1)S(1)} %get-tuple-element.65), channel_id=1, source_target_pairs={{0,12},{4,8},{8,4},{12,0},{1,13},{5,9},{9,5},{13,1},{2,14},{6,10},... | collective-permute-start | bytes 36872 | tf_op jit(solution)/shard_map/ppermute | solution.py:342
  13.1 3.7 %collective-permute-start.6 = (bf16[48,128]{1,0:T(8,128)(2,1)S(1)}, bf16[48,128]{1,0:T(8,128)(2,1)S(1)}, u32[]{:S(2)}, u32[]{:S(2)}) collective-permute-start(bf16[48,128]{1,0:T(8,128)(2,1)S(1)} %get-tuple-element.64), channel_id=1, source_target_pairs={{0,8},{4,12},{8,0},{12,4},{1,9},{5,13},{9,1},{13,5},{2,10},{6,14},... | collective-permute-start | bytes 36872 | tf_op jit(solution)/shard_map/ppermute | solution.py:342
  14.6 2.2 %collective-permute-start.7 = (bf16[48,128]{1,0:T(8,128)(2,1)S(1)}, bf16[48,128]{1,0:T(8,128)(2,1)S(1)}, u32[]{:S(2)}, u32[]{:S(2)}) collective-permute-start(bf16[48,128]{1,0:T(8,128)(2,1)S(1)} %get-tuple-element.63), channel_id=1, source_target_pairs={{0,4},{4,0},{8,12},{12,8},{1,5},{5,1},{9,13},{13,9},{2,6},{6,2},{1... | collective-permute-start | bytes 36872 | tf_op jit(solution)/shard_map/ppermute | solution.py:342
  14.8 7.5 %collective-permute-start.2 = (bf16[256,128]{1,0:T(8,128)(2,1)S(1)}, bf16[256,128]{1,0:T(8,128)(2,1)S(1)}, u32[]{:S(2)}, u32[]{:S(2)}) collective-permute-start(bf16[256,128]{1,0:T(8,128)(2,1)S(1)} %get-tuple-element.61), channel_id=1, source_target_pairs={{0,12},{4,8},{8,4},{12,0},{1,13},{5,9},{9,5},{13,1},{2,14},{6,10},... | collective-permute-start | bytes 196616 | tf_op jit(solution)/shard_map/ppermute | solution.py:342
  16.1 6.5 %collective-permute-start.3 = (bf16[256,128]{1,0:T(8,128)(2,1)S(1)}, bf16[256,128]{1,0:T(8,128)(2,1)S(1)}, u32[]{:S(2)}, u32[]{:S(2)}) collective-permute-start(bf16[256,128]{1,0:T(8,128)(2,1)S(1)} %get-tuple-element.60), channel_id=1, source_target_pairs={{0,8},{4,12},{8,0},{12,4},{1,9},{5,13},{9,1},{13,5},{2,10},{6,14},... | collective-permute-start | bytes 196616 | tf_op jit(solution)/shard_map/ppermute | solution.py:342
  16.8 5.7 %collective-permute-start.4 = (bf16[256,128]{1,0:T(8,128)(2,1)S(1)}, bf16[256,128]{1,0:T(8,128)(2,1)S(1)}, u32[]{:S(2)}, u32[]{:S(2)}) collective-permute-start(bf16[256,128]{1,0:T(8,128)(2,1)S(1)} %get-tuple-element.59), channel_id=1, source_target_pairs={{0,4},{4,0},{8,12},{12,8},{1,5},{5,1},{9,13},{13,9},{2,6},{6,2},{1... | collective-permute-start | bytes 196616 | tf_op jit(solution)/shard_map/ppermute | solution.py:342
  17.2 6.3 %collective-permute-start.8 = (f32[16,128]{1,0:T(8,128)S(1)}, f32[16,128]{1,0:T(8,128)S(1)}, u32[]{:S(2)}, u32[]{:S(2)}) collective-permute-start(f32[16,128]{1,0:T(8,128)S(1)} %get-tuple-element.69), channel_id=1, source_target_pairs={{0,3},{1,2},{2,1},{3,0},{4,7},{5,6},{6,5},{7,4},{8,11},{9,10},{10,... | collective-permute-start | bytes 24584 | tf_op jit(solution)/shard_map/ppermute | solution.py:342
  20.9 4.5 %collective-permute-start.9 = (f32[16,128]{1,0:T(8,128)S(1)}, f32[16,128]{1,0:T(8,128)S(1)}, u32[]{:S(2)}, u32[]{:S(2)}) collective-permute-start(f32[16,128]{1,0:T(8,128)S(1)} %get-tuple-element.68), channel_id=1, source_target_pairs={{0,2},{1,3},{2,0},{3,1},{4,6},{5,7},{6,4},{7,5},{8,10},{9,11},{10,... | collective-permute-start | bytes 24584 | tf_op jit(solution)/shard_map/ppermute | solution.py:342
  22.3 3.7 %collective-permute-start.10 = (f32[16,128]{1,0:T(8,128)S(1)}, f32[16,128]{1,0:T(8,128)S(1)}, u32[]{:S(2)}, u32[]{:S(2)}) collective-permute-start(f32[16,128]{1,0:T(8,128)S(1)} %get-tuple-element.67), channel_id=1, source_target_pairs={{0,1},{1,0},{2,3},{3,2},{4,5},{5,4},{6,7},{7,6},{8,9},{9,8},{10,11... | collective-permute-start | bytes 24584 | tf_op jit(solution)/shard_map/ppermute | solution.py:342

commit v19 on v16

--- a/solution.py
+++ b/solution.py
@@ -175,8 +175,20 @@
         feet_ref[block] = halves.astype(jnp.bfloat16)
 
 
+def weights_kernel(*refs):
+    pieces, weights_ref = refs[:-1], refs[-1]
+    place = lax.axis_index("frame")
+    half = weights_ref.shape[0] // 2
+    left = lax.broadcasted_iota(jnp.int32, (half, TILE), 1) < TILE // 2
+    for step, piece in enumerate(pieces):
+        columns = pl.ds(pl.multiple_of((place ^ step) * TILE, TILE), TILE)
+        feet = piece[...].astype(jnp.float32)
+        weights_ref[:half, columns] = jnp.where(left, feet, 0.0).astype(jnp.bfloat16)
+        weights_ref[half:, columns] = jnp.where(left, 0.0, feet).astype(jnp.bfloat16)
+
+
 def restore_kernel(
-    taps_ref, back_ref, feet_ref, own_ref, top_ref, bottom_ref, out_ref, side_ref, image_ref, current_ref, quotient_ref
+    taps_ref, back_ref, own_ref, top_ref, bottom_ref, out_ref, side_ref, image_ref, current_ref, quotient_ref
 ):
     n_frame = out_ref.shape[0]
     frames, rows_dev, width = own_ref.shape
@@ -244,9 +256,7 @@
     sums = jnp.concatenate(sums, axis=0)
     high = sums.astype(jnp.bfloat16).astype(jnp.float32)
     split = jnp.where(lax.broadcasted_iota(jnp.int32, sums.shape, 1) < positions, high, sums - high).astype(jnp.bfloat16)
-    for block in range(n_frame):
-        side_ref[block, : split.shape[0], :] = split
-        side_ref[block, split.shape[0] :, :] = feet_ref[block]
+    side_ref[...] = split
 
 
 def deconvolved(series):
@@ -273,32 +283,27 @@
     return result
 
 
-def partial_kernel(*refs, positions):
-    pieces, (out_ref, sums_ref, feet_ref) = refs[:-3], refs[-3:]
+def partial_kernel(weights_ref, *refs):
+    pieces, (out_ref, sums_ref) = refs[:-2], refs[-2:]
     n_frame = len(pieces)
     place = lax.axis_index("frame")
     rows = sums_ref.shape[0] // n_frame
-    half = feet_ref.shape[1]
     for step, piece in enumerate(pieces[::-1]):
-        sums_ref[pl.ds(pl.multiple_of((place ^ step) * rows, rows), rows), :] = piece[:rows, :].astype(jnp.float32)
-        feet_ref[place ^ step] = piece[rows:, :].astype(jnp.float32)
+        sums_ref[pl.ds(pl.multiple_of((place ^ step) * rows, rows), rows), :] = piece[...].astype(jnp.float32)
     series = [sums_ref[t * n_frame : (t + 1) * n_frame, :] for t in range(rows)]
     for t, sums in enumerate(deconvolved(series)):
         sums_ref[t * n_frame : (t + 1) * n_frame, :] = sums + pltpu.roll(sums, TILE // 2, 1)
-    left = lax.broadcasted_iota(jnp.int32, (half, TILE), 1) < positions
-    weights, sums = [], []
     extra = jnp.where(lax.broadcasted_iota(jnp.int32, (8, TILE), 0) == 0, 1.0, 0.0)
-    for block in range(n_frame):
-        feet = feet_ref[block]
-        weights.append(jnp.concatenate([jnp.where(left, feet, 0.0), jnp.where(left, 0.0, feet)], axis=0))
-        sums.append(jnp.concatenate([sums_ref[pl.ds(block, rows, stride=n_frame), :], extra], axis=0))
+    sums = [
+        jnp.concatenate([sums_ref[pl.ds(block, rows, stride=n_frame), :], extra], axis=0) for block in range(n_frame)
+    ]
     sums = jnp.concatenate(sums, axis=1)
     parts = []
     for _ in range(3):
         parts.append(sums.astype(jnp.bfloat16))
         sums = sums - parts[-1].astype(jnp.float32)
     totals = lax.dot_general(
-        jnp.concatenate(weights * 3, axis=1).astype(jnp.bfloat16),
+        jnp.concatenate([weights_ref[...]] * 3, axis=1),
         jnp.concatenate(parts, axis=1),
         (((1,), (1,)), ((), ())),
         preferred_element_type=jnp.float32,
@@ -341,6 +346,11 @@
         part = lax.dynamic_index_in_dim(parts, place ^ step, 0, keepdims=False, allow_negative_indices=False)
         arrived.append(lax.ppermute(part, axis, [(i, i ^ step) for i in range(count)]))
     return arrived
+
+
+def spread_out(part, axis):
+    count = lax.axis_size(axis)
+    return [part] + [lax.ppermute(part, axis, [(i, i ^ step) for i in range(count)]) for step in range(1, count)]
 
 
 def in_turn(*arrays):
@@ -401,29 +411,30 @@
     alone = (row == 0) | (row == n_row - 1)
     inner, outer = inner.astype(jnp.float32), jnp.where(alone, 1.0, outer.astype(jnp.float32))
     top, bottom = jnp.where(even, outer, inner), jnp.where(even, inner, outer)
-    side_rows = frames * n_frame + n_row * share // 2
+    weights = call(weights_kernel, "weights", [vmem] * n_frame, array(n_row * share, n_frame * TILE, dtype=jnp.bfloat16))(
+        *swapped(feet, "frame")
+    )
+    taps, weights = lax.optimization_barrier((taps, weights))
     blocks, sides = call(
         restore_kernel,
         "restore",
-        [vmem] * 6,
+        [vmem] * 5,
         (
             array(n_frame, frames * positions, TILE, dtype=jnp.bfloat16),
-            array(n_frame, side_rows, TILE, dtype=jnp.bfloat16),
+            array(frames * n_frame, TILE, dtype=jnp.bfloat16),
         ),
         [pltpu.VMEM((frames, span + 2 * PAD, TILE), jnp.float32)] * 3,
-    )(taps, back, feet, own, top, bottom)
-    sides = swapped(sides, "frame")
+    )(taps, back, own, top, bottom)
+    own_sums, *sides = spread_out(sides, "frame")
+    sides[1], sides[2], sides[0] = in_turn(sides[1], sides[2], sides[0])
     pieces = swapped(blocks, "frame")
     partial = call(
-        functools.partial(partial_kernel, positions=positions),
+        partial_kernel,
         "partial",
-        [vmem] * n_frame,
+        [vmem] * (n_frame + 1),
         array(n_row, share, TILE),
-        [
-            pltpu.VMEM((n_frame * frames * n_frame, TILE), jnp.float32),
-            pltpu.VMEM((n_frame, n_row * share // 2, TILE), jnp.float32),
-        ],
-    )(*sides[::-1])
+        [pltpu.VMEM((n_frame * frames * n_frame, TILE), jnp.float32)],
+    )(weights, *sides[::-1], own_sums)
     shares = swapped(partial, "row")
     spikes = call(
         functools.partial(temporal_kernel, frames=frames),

time: 26.4 us -> 26.7 us (1.011)
  starting transfers between devices: 11.8 us -> 13.6 us
  waiting for transfers between devices: 5.35 us -> 4.47 us
  local copies, waits for them, and re-layouts: 2.4 us -> 1.83 us
    ppermute x1, waiting for transfers between devices: 2.66 us -> 0.01 us  [by_halo(): inner = lax.ppermute(inner.astype(jnp.float16), 'row', inner_swap)]
    ppermute x0 -> x3, starting transfers between devices: none -> 1.93 us  [spread_out(): lax.ppermute(part, axis, [(i, i ^ step) for i in range(count)])]
    ppermute x9, waiting for transfers between devices: 2.69 us -> 4.31 us  [swapped(): lax.ppermute(part, axis, [(i, i ^ step) for i in range(count)])]
    unnamed x8, local copies, waits for them, and re-layouts: 2.35 us -> 1.78 us
    pallas_call x2 -> x3, Pallas kernels: 3.19 us -> 3.2 us  [the longest x1 2.84 us: by_halo(): call(restore_kernel, 'restore', [vmem] * 5, (array(n_frame, frames * posi...]
  transfers between devices with their start and end apart: 11 -> 14, of which waited for: 2 -> 6; matrix products, arithmetic and copies ran while one was open for 0% -> 0% of each run, Pallas kernels for 8% -> 8%
where the time goes in v19:
time: 26.7 us; the launch traced here: 26.5 us
  starting transfers between devices  13.6 us (51%)
  Pallas kernels  5.7 us (21%)
  waiting for transfers between devices  4.47 us (17%)
  local copies, waits for them, and re-layouts  1.83 us (7%)
  between operations  0.8 us (3%)
    ppermute x9, starting transfers between devices, swapped(): lax.ppermute(part, axis, [(i, i ^ step) for i in range(count)])  8.51 us
    ppermute x9, waiting for transfers between devices, swapped(): lax.ppermute(part, axis, [(i, i ^ step) for i in range(count)])  4.31 us
    ppermute x1, starting transfers between devices, by_halo(): inner = lax.ppermute(inner.astype(jnp.float16), 'row', inner_swap)  3.09 us
    pallas_call x1, Pallas kernels, by_halo(): call(restore_kernel, 'restore', [vmem] * 5, (array(n_frame, frames * posi...  2.84 us
    ppermute x3, starting transfers between devices, spread_out(): lax.ppermute(part, axis, [(i, i ^ step) for i in range(count)])  1.93 us
    unnamed x8, local copies, waits for them, and re-layouts  1.78 us
    pallas_call x1, Pallas kernels, by_halo(): call(functools.partial(temporal_kernel, frames=frames), 'temporal', [vmem...  0.91 us
    pallas_call x1, Pallas kernels, by_halo(): call(functools.partial(taps_kernel, height=rows_dev * n_row, rows_dev=row...  0.69 us
  transfers between devices with their start and end apart: 14, of which 6 were waited for; matrix products, arithmetic and copies ran while one was open for 0% of the time, Pallas kernels for 8%

profile of v19, /device:TPU:0, one launch (start us, length us, event | category | flops | bytes accessed | tf_op | source)
XLA Modules:
  0.0 26.5 jit_solution(3288174306509167729)
XLA Ops:
  0.6 1.0 %copy-done = f32[4,16,2048]{2,1,0:T(8,128)S(1)} copy-done((f32[4,16,2048]{2,1,0:T(8,128)S(1)}, f32[4,16,2048]{2,1,0:T(8,128)}, u32[]{:S(2)}) %copy-start) | copy-done | bytes 524312
  1.7 0.1 halo.1
  1.8 3.1 %collective-permute-start.3 = (f16[48,2048]{1,0:T(8,128)(2,1)S(1)}, f16[48,2048]{1,0:T(8,128)(2,1)S(1)}, u32[]{:S(2)}, u32[]{:S(2)}) collective-permute-start(f16[48,2048]{1,0:T(8,128)(2,1)S(1)} %convert_element_type.12), channel_id=1, source_target_pairs={{0,1},{1,0},{2,3},{3,2},{4,5},{5,4},{6,7},{7,6},{8,9},{9,8},{10,11... | collective-permute-start | bytes 589832 | tf_op jit(solution)/shard_map/ppermute | solution.py:396
  4.9 0.1 collective-permute-start.4
  5.0 0.7 %copy-done.1 = s32[256,16,4]{0,2,1:T(4,128)S(1)} copy-done((s32[256,16,4]{0,2,1:T(4,128)S(1)}, s32[256,16,4]{0,2,1:T(4,128)}, u32[]{:S(2)}) %copy-start.1) | copy-done | bytes 65560
  5.8 0.1 feet.1
  5.9 0.0 copy-start.2
  5.9 0.1 collective-permute-start
  6.0 0.0 copy-start.3
  6.0 1.6 %collective-permute-start.1 = (bf16[32,128]{1,0:T(8,128)(2,1)S(1)}, bf16[32,128]{1,0:T(8,128)(2,1)S(1)}, u32[]{:S(2)}, u32[]{:S(2)}) collective-permute-start(bf16[32,128]{1,0:T(8,128)(2,1)S(1)} %get-tuple-element.73), channel_id=1, source_target_pairs={{0,8},{4,12},{8,0},{12,4},{1,9},{5,13},{9,1},{13,5},{2,10},{6,14},... | collective-permute-start | bytes 24584 | tf_op jit(solution)/shard_map/ppermute | solution.py:347
  7.6 0.3 %collective-permute-start.2 = (bf16[32,128]{1,0:T(8,128)(2,1)S(1)}, bf16[32,128]{1,0:T(8,128)(2,1)S(1)}, u32[]{:S(2)}, u32[]{:S(2)}) collective-permute-start(bf16[32,128]{1,0:T(8,128)(2,1)S(1)} %get-tuple-element.72), channel_id=1, source_target_pairs={{0,12},{4,8},{8,4},{12,0},{1,13},{5,9},{9,5},{13,1},{2,14},{6,10},... | collective-permute-start | bytes 24584 | tf_op jit(solution)/shard_map/ppermute | solution.py:347
  7.9 0.7 %taps.1 = (f32[4,48,128]{2,1,0:T(8,128)S(1)}, f32[4,48,128]{2,1,0:T(8,128)S(1)}) custom-call(s32[8]{0:T(128)S(1)} %copy-done.3, f32[8,5]{1,0:T(8,128)S(1)} %copy-done.2), custom_call_target="tpu_custom_call" | custom-call | flops 1000 | bytes 1000 | tf_op jit(solution)/shard_map/taps/pallas_call | solution.py:399
  8.6 1.1 %collective-permute-done.1.refs_2_ = bf16[32,128]{1,0:T(8,128)(2,1)S(1)} collective-permute-done((bf16[32,128]{1,0:T(8,128)(2,1)S(1)}, bf16[32,128]{1,0:T(8,128)(2,1)S(1)}, u32[]{:S(2)}, u32[]{:S(2)}) %collective-permute-start.1) | collective-permute-done | bytes 8224 | tf_op jit(solution)/shard_map/ppermute | solution.py:347
  9.7 0.9 %collective-permute-done.2.refs_3_ = bf16[32,128]{1,0:T(8,128)(2,1)S(1)} collective-permute-done((bf16[32,128]{1,0:T(8,128)(2,1)S(1)}, bf16[32,128]{1,0:T(8,128)(2,1)S(1)}, u32[]{:S(2)}, u32[]{:S(2)}) %collective-permute-start.2) | collective-permute-done | bytes 8224 | tf_op jit(solution)/shard_map/ppermute | solution.py:347
  10.7 0.0 collective-permute-done.4
  10.7 0.1 convert_select_fusion
  10.8 2.8 %restore.1 = (bf16[4,256,128]{2,1,0:T(8,128)(2,1)S(1)}, bf16[16,128]{1,0:T(8,128)(2,1)S(1)}) custom-call(f32[4,48,128]{2,1,0:T(8,128)S(1)} %get-tuple-element.33.taps_ref, f32[4,48,128]{2,1,0:T(8,128)S(1)} %get-tuple-element.34.back_ref, f32[4,16,2048]{2,1,0:T(8,128)S(1)} %get-tuple-element.35.own_ref, f32[48,2048]{1,0:T(8,128)S(1)} %get-tuple-element.63.top_ref, ...), custom_call_target="tpu_custom_call" | custom-call | flops 1000 | bytes 1000 | tf_op jit(solution)/shard_map/restore/pallas_call | solution.py:418
  13.6 0.6 %collective-permute-start.9 = (bf16[16,128]{1,0:T(8,128)(2,1)S(1)}, bf16[16,128]{1,0:T(8,128)(2,1)S(1)}, u32[]{:S(2)}, u32[]{:S(2)}) collective-permute-start(bf16[16,128]{1,0:T(8,128)(2,1)S(1)} %get-tuple-element.42.refs_3_), channel_id=1, source_target_pairs={{0,12},{4,8},{8,4},{12,0},{1,13},{5,9},{9,5},{13,1},{2,14},{6,10},... | collective-permute-start | bytes 12296 | tf_op jit(solution)/shard_map/ppermute | solution.py:353
  14.2 1.2 %collective-permute-start.8 = (bf16[16,128]{1,0:T(8,128)(2,1)S(1)}, bf16[16,128]{1,0:T(8,128)(2,1)S(1)}, u32[]{:S(2)}, u32[]{:S(2)}) collective-permute-start(bf16[16,128]{1,0:T(8,128)(2,1)S(1)} %get-tuple-element.42.refs_3_), channel_id=1, source_target_pairs={{0,8},{4,12},{8,0},{12,4},{1,9},{5,13},{9,1},{13,5},{2,10},{6,14},... | collective-permute-start | bytes 12296 | tf_op jit(solution)/shard_map/ppermute | solution.py:353
  15.5 0.1 collective-permute-start.10
  15.6 0.9 %collective-permute-start.5 = (bf16[256,128]{1,0:T(8,128)(2,1)S(1)}, bf16[256,128]{1,0:T(8,128)(2,1)S(1)}, u32[]{:S(2)}, u32[]{:S(2)}) collective-permute-start(bf16[256,128]{1,0:T(8,128)(2,1)S(1)} %get-tuple-element.67), channel_id=1, source_target_pairs={{0,12},{4,8},{8,4},{12,0},{1,13},{5,9},{9,5},{13,1},{2,14},{6,10},... | collective-permute-start | bytes 196616 | tf_op jit(solution)/shard_map/ppermute | solution.py:347
  16.5 1.2 %collective-permute-start.6 = (bf16[256,128]{1,0:T(8,128)(2,1)S(1)}, bf16[256,128]{1,0:T(8,128)(2,1)S(1)}, u32[]{:S(2)}, u32[]{:S(2)}) collective-permute-start(bf16[256,128]{1,0:T(8,128)(2,1)S(1)} %get-tuple-element.66), channel_id=1, source_target_pairs={{0,8},{4,12},{8,0},{12,4},{1,9},{5,13},{9,1},{13,5},{2,10},{6,14},... | collective-permute-start | bytes 196616 | tf_op jit(solution)/shard_map/ppermute | solution.py:347
  17.7 0.2 collective-permute-done.8.refs_1_
  17.9 0.3 %partial.1 = f32[4,16,128]{2,1,0:T(8,128)S(1)} custom-call(bf16[64,512]{1,0:T(8,128)(2,1)S(1)} %weights.1.weights_ref, bf16[16,128]{1,0:T(8,128)(2,1)S(1)} %collective-permute-done.9.refs_0_, bf16[16,128]{1,0:T(8,128)(2,1)S(1)} %collective-permute-done.8.refs_1_, bf16[16,128]{1,0:T(8,128)(2,1)S(1)} %collective-permute-done.10.refs_2_, ...), custom_call_target="tpu_custom_call" | custom-call | flops 1000 | bytes 1000 | tf_op jit(solution)/shard_map/partial/pallas_call | solution.py:431
  18.2 2.9 %collective-permute-start.11 = (f32[16,128]{1,0:T(8,128)S(1)}, f32[16,128]{1,0:T(8,128)S(1)}, u32[]{:S(2)}, u32[]{:S(2)}) collective-permute-start(f32[16,128]{1,0:T(8,128)S(1)} %get-tuple-element.71), channel_id=1, source_target_pairs={{0,3},{1,2},{2,1},{3,0},{4,7},{5,6},{6,5},{7,4},{8,11},{9,10},{10,... | collective-permute-start | bytes 24584 | tf_op jit(solution)/shard_map/ppermute | solution.py:347
  21.1 1.1 %collective-permute-start.12 = (f32[16,128]{1,0:T(8,128)S(1)}, f32[16,128]{1,0:T(8,128)S(1)}, u32[]{:S(2)}, u32[]{:S(2)}) collective-permute-start(f32[16,128]{1,0:T(8,128)S(1)} %get-tuple-element.70), channel_id=1, source_target_pairs={{0,2},{1,3},{2,0},{3,1},{4,6},{5,7},{6,4},{7,5},{8,10},{9,11},{10,... | collective-permute-start | bytes 24584 | tf_op jit(solution)/shard_map/ppermute | solution.py:347
  22.2 0.5 %collective-permute-start.13 = (f32[16,128]{1,0:T(8,128)S(1)}, f32[16,128]{1,0:T(8,128)S(1)}, u32[]{:S(2)}, u32[]{:S(2)}) collective-permute-start(f32[16,128]{1,0:T(8,128)S(1)} %get-tuple-element.69), channel_id=1, source_target_pairs={{0,1},{1,0},{2,3},{3,2},{4,5},{5,4},{6,7},{7,6},{8,9},{9,8},{10,11... | collective-permute-start | bytes 24584 | tf_op jit(solution)/shard_map/ppermute | solution.py:347
  22.7 0.9 %temporal.1 = bf16[16,16,512]{2,1,0:T(8,128)(2,1)} custom-call(bf16[256,128]{1,0:T(8,128)(2,1)S(1)} %collective-permute-done.5.refs_0_, bf16[256,128]{1,0:T(8,128)(2,1)S(1)} %collective-permute-done.6.refs_1_, bf16[256,128]{1,0:T(8,128)(2,1)S(1)} %collective-permute-done.7.refs_2_, bf16[256,128]{1,0:T(8,128)(2,1)S(1)} %get-tuple-element.64.refs_3_), custom_call_target="tpu_custom_call" | custom-call | flops 1000 | bytes 1000 | tf_op jit(solution)/shard_map/temporal/pallas_call | solution.py:439
  23.6 0.1 collective-permute-done.11.refs_0_
  23.8 1.9 %collective-permute-done.12.refs_1_ = f32[16,128]{1,0:T(8,128)S(1)} collective-permute-done((f32[16,128]{1,0:T(8,128)S(1)}, f32[16,128]{1,0:T(8,128)S(1)}, u32[]{:S(2)}, u32[]{:S(2)}) %collective-permute-start.12) | collective-permute-done | bytes 8224 | tf_op jit(solution)/shard_map/ppermute | solution.py:347
  25.6 0.2 collective-permute-done.13.refs_2_
  25.9 0.7 %means.1 = f32[16,16]{1,0:T(8,128)} custom-call(f32[16,128]{1,0:T(8,128)S(1)} %collective-permute-done.11.refs_0_, f32[16,128]{1,0:T(8,128)S(1)} %collective-permute-done.12.refs_1_, f32[16,128]{1,0:T(8,128)S(1)} %collective-permute-done.13.refs_2_, f32[16,128]{1,0:T(8,128)S(1)} %get-tuple-element.61.refs_3_), custom_call_target="tpu_custom_call" | custom-call | flops 1000 | bytes 1000 | tf_op jit(solution)/shard_map/means/pallas_call | solution.py:447
  (18 shorter events, 0.1 us)
Async XLA Ops:
  0.6 1.0 %copy-start = (f32[4,16,2048]{2,1,0:T(8,128)S(1)}, f32[4,16,2048]{2,1,0:T(8,128)}, u32[]{:S(2)}) copy-start(f32[4,16,2048]{2,1,0:T(8,128)} %observed_ref.1) | copy-start | bytes 1572868
  1.8 8.8 %collective-permute-start.3 = (f16[48,2048]{1,0:T(8,128)(2,1)S(1)}, f16[48,2048]{1,0:T(8,128)(2,1)S(1)}, u32[]{:S(2)}, u32[]{:S(2)}) collective-permute-start(f16[48,2048]{1,0:T(8,128)(2,1)S(1)} %convert_element_type.12), channel_id=1, source_target_pairs={{0,1},{1,0},{2,3},{3,2},{4,5},{5,4},{6,7},{7,6},{8,9},{9,8},{10,11... | collective-permute-start | bytes 589832 | tf_op jit(solution)/shard_map/ppermute | solution.py:396
  4.9 0.8 %copy-start.1 = (s32[256,16,4]{0,2,1:T(4,128)S(1)}, s32[256,16,4]{0,2,1:T(4,128)}, u32[]{:S(2)}) copy-start(s32[256,16,4]{0,2,1:T(4,128)} %param.7) | copy-start | bytes 196612
  4.9 5.7 %collective-permute-start.4 = (f16[48,2048]{1,0:T(8,128)(2,1)S(1)}, f16[48,2048]{1,0:T(8,128)(2,1)S(1)}, u32[]{:S(2)}, u32[]{:S(2)}) collective-permute-start(f16[48,2048]{1,0:T(8,128)(2,1)S(1)} %convert_element_type.13), channel_id=1, source_target_pairs={{0,4},{1,2},{2,1},{3,7},{4,0},{5,6},{6,5},{7,3},{8,12},{9,10},{10,... | collective-permute-start | bytes 589832 | tf_op jit(solution)/shard_map/ppermute | solution.py:397
  5.9 2.0 %copy-start.2 = (f32[8,5]{1,0:T(8,128)S(1)}, f32[8,5]{1,0:T(8,128)}, u32[]{:S(2)}) copy-start(f32[8,5]{1,0:T(8,128)} %kernels_ref.1) | copy-start | bytes 484
  5.9 2.7 %collective-permute-start = (bf16[32,128]{1,0:T(8,128)(2,1)S(1)}, bf16[32,128]{1,0:T(8,128)(2,1)S(1)}, u32[]{:S(2)}, u32[]{:S(2)}) collective-permute-start(bf16[32,128]{1,0:T(8,128)(2,1)S(1)} %get-tuple-element.74), channel_id=1, source_target_pairs={{0,4},{4,0},{8,12},{12,8},{1,5},{5,1},{9,13},{13,9},{2,6},{6,2},{1... | collective-permute-start | bytes 24584 | tf_op jit(solution)/shard_map/ppermute | solution.py:347
  6.0 1.9 %copy-start.3 = (s32[8]{0:T(128)S(1)}, s32[8]{0:T(128)}, u32[]{:S(2)}) copy-start(s32[8]{0:T(128)} %band_ref.1) | copy-start | bytes 100
  6.0 3.7 %collective-permute-start.1 = (bf16[32,128]{1,0:T(8,128)(2,1)S(1)}, bf16[32,128]{1,0:T(8,128)(2,1)S(1)}, u32[]{:S(2)}, u32[]{:S(2)}) collective-permute-start(bf16[32,128]{1,0:T(8,128)(2,1)S(1)} %get-tuple-element.73), channel_id=1, source_target_pairs={{0,8},{4,12},{8,0},{12,4},{1,9},{5,13},{9,1},{13,5},{2,10},{6,14},... | collective-permute-start | bytes 24584 | tf_op jit(solution)/shard_map/ppermute | solution.py:347
  7.6 3.1 %collective-permute-start.2 = (bf16[32,128]{1,0:T(8,128)(2,1)S(1)}, bf16[32,128]{1,0:T(8,128)(2,1)S(1)}, u32[]{:S(2)}, u32[]{:S(2)}) collective-permute-start(bf16[32,128]{1,0:T(8,128)(2,1)S(1)} %get-tuple-element.72), channel_id=1, source_target_pairs={{0,12},{4,8},{8,4},{12,0},{1,13},{5,9},{9,5},{13,1},{2,14},{6,10},... | collective-permute-start | bytes 24584 | tf_op jit(solution)/shard_map/ppermute | solution.py:347
  13.6 4.2 %collective-permute-start.9 = (bf16[16,128]{1,0:T(8,128)(2,1)S(1)}, bf16[16,128]{1,0:T(8,128)(2,1)S(1)}, u32[]{:S(2)}, u32[]{:S(2)}) collective-permute-start(bf16[16,128]{1,0:T(8,128)(2,1)S(1)} %get-tuple-element.42.refs_3_), channel_id=1, source_target_pairs={{0,12},{4,8},{8,4},{12,0},{1,13},{5,9},{9,5},{13,1},{2,14},{6,10},... | collective-permute-start | bytes 12296 | tf_op jit(solution)/shard_map/ppermute | solution.py:353
  14.2 3.6 %collective-permute-start.8 = (bf16[16,128]{1,0:T(8,128)(2,1)S(1)}, bf16[16,128]{1,0:T(8,128)(2,1)S(1)}, u32[]{:S(2)}, u32[]{:S(2)}) collective-permute-start(bf16[16,128]{1,0:T(8,128)(2,1)S(1)} %get-tuple-element.42.refs_3_), channel_id=1, source_target_pairs={{0,8},{4,12},{8,0},{12,4},{1,9},{5,13},{9,1},{13,5},{2,10},{6,14},... | collective-permute-start | bytes 12296 | tf_op jit(solution)/shard_map/ppermute | solution.py:353
  15.5 2.4 %collective-permute-start.10 = (bf16[16,128]{1,0:T(8,128)(2,1)S(1)}, bf16[16,128]{1,0:T(8,128)(2,1)S(1)}, u32[]{:S(2)}, u32[]{:S(2)}) collective-permute-start(bf16[16,128]{1,0:T(8,128)(2,1)S(1)} %get-tuple-element.42.refs_3_), channel_id=1, source_target_pairs={{0,4},{4,0},{8,12},{12,8},{1,5},{5,1},{9,13},{13,9},{2,6},{6,2},{1... | collective-permute-start | bytes 12296 | tf_op jit(solution)/shard_map/ppermute | solution.py:353
  15.6 6.6 %collective-permute-start.5 = (bf16[256,128]{1,0:T(8,128)(2,1)S(1)}, bf16[256,128]{1,0:T(8,128)(2,1)S(1)}, u32[]{:S(2)}, u32[]{:S(2)}) collective-permute-start(bf16[256,128]{1,0:T(8,128)(2,1)S(1)} %get-tuple-element.67), channel_id=1, source_target_pairs={{0,12},{4,8},{8,4},{12,0},{1,13},{5,9},{9,5},{13,1},{2,14},{6,10},... | collective-permute-start | bytes 196616 | tf_op jit(solution)/shard_map/ppermute | solution.py:347
  16.5 6.2 %collective-permute-start.6 = (bf16[256,128]{1,0:T(8,128)(2,1)S(1)}, bf16[256,128]{1,0:T(8,128)(2,1)S(1)}, u32[]{:S(2)}, u32[]{:S(2)}) collective-permute-start(bf16[256,128]{1,0:T(8,128)(2,1)S(1)} %get-tuple-element.66), channel_id=1, source_target_pairs={{0,8},{4,12},{8,0},{12,4},{1,9},{5,13},{9,1},{13,5},{2,10},{6,14},... | collective-permute-start | bytes 196616 | tf_op jit(solution)/shard_map/ppermute | solution.py:347
  17.8 4.8 %collective-permute-start.7 = (bf16[256,128]{1,0:T(8,128)(2,1)S(1)}, bf16[256,128]{1,0:T(8,128)(2,1)S(1)}, u32[]{:S(2)}, u32[]{:S(2)}) collective-permute-start(bf16[256,128]{1,0:T(8,128)(2,1)S(1)} %get-tuple-element.65), channel_id=1, source_target_pairs={{0,4},{4,0},{8,12},{12,8},{1,5},{5,1},{9,13},{13,9},{2,6},{6,2},{1... | collective-permute-start | bytes 196616 | tf_op jit(solution)/shard_map/ppermute | solution.py:347
  18.2 5.5 %collective-permute-start.11 = (f32[16,128]{1,0:T(8,128)S(1)}, f32[16,128]{1,0:T(8,128)S(1)}, u32[]{:S(2)}, u32[]{:S(2)}) collective-permute-start(f32[16,128]{1,0:T(8,128)S(1)} %get-tuple-element.71), channel_id=1, source_target_pairs={{0,3},{1,2},{2,1},{3,0},{4,7},{5,6},{6,5},{7,4},{8,11},{9,10},{10,... | collective-permute-start | bytes 24584 | tf_op jit(solution)/shard_map/ppermute | solution.py:347
  21.1 4.5 %collective-permute-start.12 = (f32[16,128]{1,0:T(8,128)S(1)}, f32[16,128]{1,0:T(8,128)S(1)}, u32[]{:S(2)}, u32[]{:S(2)}) collective-permute-start(f32[16,128]{1,0:T(8,128)S(1)} %get-tuple-element.70), channel_id=1, source_target_pairs={{0,2},{1,3},{2,0},{3,1},{4,6},{5,7},{6,4},{7,5},{8,10},{9,11},{10,... | collective-permute-start | bytes 24584 | tf_op jit(solution)/shard_map/ppermute | solution.py:347
  22.2 3.7 %collective-permute-start.13 = (f32[16,128]{1,0:T(8,128)S(1)}, f32[16,128]{1,0:T(8,128)S(1)}, u32[]{:S(2)}, u32[]{:S(2)}) collective-permute-start(f32[16,128]{1,0:T(8,128)S(1)} %get-tuple-element.69), channel_id=1, source_target_pairs={{0,1},{1,0},{2,3},{3,2},{4,5},{5,4},{6,7},{7,6},{8,9},{9,8},{10,11... | collective-permute-start | bytes 24584 | tf_op jit(solution)/shard_map/ppermute | solution.py:347

commit v20 on v16

--- a/solution.py
+++ b/solution.py
@@ -125,19 +125,24 @@
     return (spikes, traces)
 
 
-def halo_kernel(observed_ref, inner_ref, outer_ref, own_ref):
-    even = lax.axis_index("row") % 2 == 0
+def pack(observed_ref, out_ref, low):
     frames = observed_ref.shape[0]
-    own_ref[...] = observed_ref[...]
     for frame in range(frames):
         near = frame * NEAR
         far = frames * NEAR + frame * FAR
         bottom, top = observed_ref[frame, -NEAR:, :], observed_ref[frame, :NEAR, :]
-        inner_ref[near : near + NEAR, :] = jnp.where(even, bottom, top)
-        outer_ref[near : near + NEAR, :] = jnp.where(even, top, bottom)
+        out_ref[near : near + NEAR, :] = jnp.where(low, bottom, top)
         bottom, top = observed_ref[frame, -NEAR - FAR : -NEAR, :], observed_ref[frame, NEAR : NEAR + FAR, :]
-        inner_ref[far : far + FAR, :] = jnp.where(even, bottom, top)
-        outer_ref[far : far + FAR, :] = jnp.where(even, top, bottom)
+        out_ref[far : far + FAR, :] = jnp.where(low, bottom, top)
+
+
+def inner_kernel(observed_ref, inner_ref, own_ref):
+    pack(observed_ref, inner_ref, lax.axis_index("row") % 2 == 0)
+    own_ref[...] = observed_ref[...]
+
+
+def outer_kernel(own_ref, outer_ref):
+    pack(own_ref, outer_ref, lax.axis_index("row") % 2 == 1)
 
 
 def taps_kernel(band_ref, kernels_ref, taps_ref, back_ref, pad_ref, *, height, rows_dev):
@@ -294,11 +299,11 @@
         sums.append(jnp.concatenate([sums_ref[pl.ds(block, rows, stride=n_frame), :], extra], axis=0))
     sums = jnp.concatenate(sums, axis=1)
     parts = []
-    for _ in range(3):
+    for _ in range(2):
         parts.append(sums.astype(jnp.bfloat16))
         sums = sums - parts[-1].astype(jnp.float32)
     totals = lax.dot_general(
-        jnp.concatenate(weights * 3, axis=1).astype(jnp.bfloat16),
+        jnp.concatenate(weights * 2, axis=1).astype(jnp.bfloat16),
         jnp.concatenate(parts, axis=1),
         (((1,), (1,)), ((), ())),
         preferred_element_type=jnp.float32,
@@ -376,14 +381,17 @@
         return jax.ShapeDtypeStruct(shape, dtype)
 
     packed = array(frames * (NEAR + FAR), width)
-    inner, outer, own = call(halo_kernel, "halo", [vmem], (packed, packed, array(*observed.shape)))(observed)
+    inner, own = call(inner_kernel, "halo", [vmem], (packed, array(*observed.shape)))(observed)
     inner_swap = [(i, i ^ 1) for i in range(n_row)]
     outer_swap = []
     for f in range(n_frame):
         for i in range(n_row):
             there = (f ^ 1, i) if i in (0, n_row - 1) else (f, (i - 1 ^ 1) + 1)
             outer_swap.append((f * n_row + i, there[0] * n_row + there[1]))
-    inner = lax.ppermute(inner.astype(jnp.float16), "row", inner_swap)
+    inner = inner.astype(jnp.float16)
+    own, inner = lax.optimization_barrier((own, inner))
+    inner = lax.ppermute(inner, "row", inner_swap)
+    outer = call(outer_kernel, "outer", [vmem], packed)(own)
     outer = lax.ppermute(outer.astype(jnp.float16), ("frame", "row"), outer_swap)
     inner, outer = in_turn(inner, outer)
     taps, back = call(

time: 26.4 us -> 26.3 us (level)
  no operation moved by 1% of the time
where the time goes in v20:
time: 26.3 us; the launch traced here: 26.1 us
  starting transfers between devices  11.9 us (45%)
  Pallas kernels  5.7 us (22%)
  waiting for transfers between devices  5.16 us (20%)
  local copies, waits for them, and re-layouts  2.39 us (9%)
  between operations  0.77 us (3%)
    ppermute x9, starting transfers between devices, swapped(): lax.ppermute(part, axis, [(i, i ^ step) for i in range(count)])  8.74 us
    ppermute x1, starting transfers between devices, by_halo(): inner = lax.ppermute(inner, 'row', inner_swap)  3.09 us
    pallas_call x1, Pallas kernels, by_halo(): call(restore_kernel, 'restore', [vmem] * 6, (array(n_frame, frames * posi...  2.84 us
    ppermute x1, waiting for transfers between devices, by_halo(): inner = lax.ppermute(inner, 'row', inner_swap)  2.58 us
    ppermute x9, waiting for transfers between devices, swapped(): lax.ppermute(part, axis, [(i, i ^ step) for i in range(count)])  2.58 us
    unnamed x8, local copies, waits for them, and re-layouts  2.34 us
    pallas_call x1, Pallas kernels, by_halo(): call(functools.partial(temporal_kernel, frames=frames), 'temporal', [vmem...  0.91 us
    pallas_call x1, Pallas kernels, by_halo(): call(functools.partial(taps_kernel, height=rows_dev * n_row, rows_dev=row...  0.69 us
  transfers between devices with their start and end apart: 11, of which 2 were waited for; matrix products, arithmetic and copies ran while one was open for 0% of the time, Pallas kernels for 8%

profile of v20, /device:TPU:0, one launch (start us, length us, event | category | flops | bytes accessed | tf_op | source)
XLA Modules:
  0.0 26.1 jit_solution(369780901181211781)
XLA Ops:
  0.6 1.0 %copy-done = f32[4,16,2048]{2,1,0:T(8,128)S(1)} copy-done((f32[4,16,2048]{2,1,0:T(8,128)S(1)}, f32[4,16,2048]{2,1,0:T(8,128)}, u32[]{:S(2)}) %copy-start) | copy-done | bytes 524312
  1.7 0.1 halo.1
  1.8 3.1 %collective-permute-start = (f16[48,2048]{1,0:T(8,128)(2,1)S(1)}, f16[48,2048]{1,0:T(8,128)(2,1)S(1)}, u32[]{:S(2)}, u32[]{:S(2)}) collective-permute-start(f16[48,2048]{1,0:T(8,128)(2,1)S(1)} %convert_element_type.12), channel_id=1, source_target_pairs={{0,1},{1,0},{2,3},{3,2},{4,5},{5,4},{6,7},{7,6},{8,9},{9,8},{10,11... | collective-permute-start | bytes 589832 | tf_op jit(solution)/shard_map/ppermute | solution.py:393
  4.9 0.1 outer.1
  5.0 0.0 copy-start.1
  5.0 0.1 collective-permute-start.1
  5.1 0.7 %copy-done.1 = s32[256,16,4]{0,2,1:T(4,128)S(1)} copy-done((s32[256,16,4]{0,2,1:T(4,128)S(1)}, s32[256,16,4]{0,2,1:T(4,128)}, u32[]{:S(2)}) %copy-start.1) | copy-done | bytes 65560
  5.8 0.1 feet.1.feet_ref
  5.9 0.6 %copy-done.2 = f32[8,5]{1,0:T(8,128)S(1)} copy-done((f32[8,5]{1,0:T(8,128)S(1)}, f32[8,5]{1,0:T(8,128)}, u32[]{:S(2)}) %copy-start.2) | copy-done | bytes 184
  6.5 0.7 %taps.1 = (f32[4,48,128]{2,1,0:T(8,128)S(1)}, f32[4,48,128]{2,1,0:T(8,128)S(1)}) custom-call(s32[8]{0:T(128)S(1)} %copy-done.3, f32[8,5]{1,0:T(8,128)S(1)} %copy-done.2), custom_call_target="tpu_custom_call" | custom-call | flops 1000 | bytes 1000 | tf_op jit(solution)/shard_map/taps/pallas_call | solution.py:397
  7.2 2.6 %collective-permute-done = f16[48,2048]{1,0:T(8,128)(2,1)S(1)} collective-permute-done((f16[48,2048]{1,0:T(8,128)(2,1)S(1)}, f16[48,2048]{1,0:T(8,128)(2,1)S(1)}, u32[]{:S(2)}, u32[]{:S(2)}) %collective-permute-start) | collective-permute-done | bytes 196640 | tf_op jit(solution)/shard_map/ppermute | solution.py:393
  9.8 0.0 collective-permute-done.1
  9.8 0.1 convert_select_fusion
  9.9 2.8 %restore.1 = (bf16[4,256,128]{2,1,0:T(8,128)(2,1)S(1)}, bf16[4,48,128]{2,1,0:T(8,128)(2,1)S(1)}) custom-call(f32[4,48,128]{2,1,0:T(8,128)S(1)} %get-tuple-element.26.taps_ref, f32[4,48,128]{2,1,0:T(8,128)S(1)} %get-tuple-element.27.back_ref, bf16[4,32,128]{2,1,0:T(8,128)(2,1)S(1)} %feet.1.feet_ref, f32[4,16,2048]{2,1,0:T(8,128)S(1)} %get-tuple-element.30.own_ref, ...), custom_call_target="tpu_custom_call" | custom-call | flops 1000 | bytes 1000 | tf_op jit(solution)/shard_map/restore/pallas_call | solution.py:413
  12.7 0.3 %collective-permute-start.5 = (bf16[48,128]{1,0:T(8,128)(2,1)S(1)}, bf16[48,128]{1,0:T(8,128)(2,1)S(1)}, u32[]{:S(2)}, u32[]{:S(2)}) collective-permute-start(bf16[48,128]{1,0:T(8,128)(2,1)S(1)} %get-tuple-element.59), channel_id=1, source_target_pairs={{0,12},{4,8},{8,4},{12,0},{1,13},{5,9},{9,5},{13,1},{2,14},{6,10},... | collective-permute-start | bytes 36872 | tf_op jit(solution)/shard_map/ppermute | solution.py:347
  13.0 1.5 %collective-permute-start.6 = (bf16[48,128]{1,0:T(8,128)(2,1)S(1)}, bf16[48,128]{1,0:T(8,128)(2,1)S(1)}, u32[]{:S(2)}, u32[]{:S(2)}) collective-permute-start(bf16[48,128]{1,0:T(8,128)(2,1)S(1)} %get-tuple-element.58), channel_id=1, source_target_pairs={{0,8},{4,12},{8,0},{12,4},{1,9},{5,13},{9,1},{13,5},{2,10},{6,14},... | collective-permute-start | bytes 36872 | tf_op jit(solution)/shard_map/ppermute | solution.py:347
  14.5 0.1 collective-permute-start.7
  14.7 1.3 %collective-permute-start.2 = (bf16[256,128]{1,0:T(8,128)(2,1)S(1)}, bf16[256,128]{1,0:T(8,128)(2,1)S(1)}, u32[]{:S(2)}, u32[]{:S(2)}) collective-permute-start(bf16[256,128]{1,0:T(8,128)(2,1)S(1)} %get-tuple-element.55), channel_id=1, source_target_pairs={{0,12},{4,8},{8,4},{12,0},{1,13},{5,9},{9,5},{13,1},{2,14},{6,10},... | collective-permute-start | bytes 196616 | tf_op jit(solution)/shard_map/ppermute | solution.py:347
  16.0 0.8 %collective-permute-start.3 = (bf16[256,128]{1,0:T(8,128)(2,1)S(1)}, bf16[256,128]{1,0:T(8,128)(2,1)S(1)}, u32[]{:S(2)}, u32[]{:S(2)}) collective-permute-start(bf16[256,128]{1,0:T(8,128)(2,1)S(1)} %get-tuple-element.54), channel_id=1, source_target_pairs={{0,8},{4,12},{8,0},{12,4},{1,9},{5,13},{9,1},{13,5},{2,10},{6,14},... | collective-permute-start | bytes 196616 | tf_op jit(solution)/shard_map/ppermute | solution.py:347
  16.8 0.0 collective-permute-done.5.refs_0_
  16.8 0.0 collective-permute-start.4
  16.8 0.0 collective-permute-done.6.refs_1_
  16.8 0.0 collective-permute-done.7.refs_2_
  16.8 0.3 %partial.1 = f32[4,16,128]{2,1,0:T(8,128)S(1)} custom-call(bf16[48,128]{1,0:T(8,128)(2,1)S(1)} %collective-permute-done.5.refs_0_, bf16[48,128]{1,0:T(8,128)(2,1)S(1)} %collective-permute-done.6.refs_1_, bf16[48,128]{1,0:T(8,128)(2,1)S(1)} %collective-permute-done.7.refs_2_, bf16[48,128]{1,0:T(8,128)(2,1)S(1)} %get-tuple-element.56.refs_3_), custom_call_target="tpu_custom_call" | custom-call | flops 1000 | bytes 1000 | tf_op jit(solution)/shard_map/partial/pallas_call | solution.py:425
  17.2 3.7 %collective-permute-start.8 = (f32[16,128]{1,0:T(8,128)S(1)}, f32[16,128]{1,0:T(8,128)S(1)}, u32[]{:S(2)}, u32[]{:S(2)}) collective-permute-start(f32[16,128]{1,0:T(8,128)S(1)} %get-tuple-element.63), channel_id=1, source_target_pairs={{0,3},{1,2},{2,1},{3,0},{4,7},{5,6},{6,5},{7,4},{8,11},{9,10},{10,... | collective-permute-start | bytes 24584 | tf_op jit(solution)/shard_map/ppermute | solution.py:347
  20.8 0.7 %collective-permute-start.9 = (f32[16,128]{1,0:T(8,128)S(1)}, f32[16,128]{1,0:T(8,128)S(1)}, u32[]{:S(2)}, u32[]{:S(2)}) collective-permute-start(f32[16,128]{1,0:T(8,128)S(1)} %get-tuple-element.62), channel_id=1, source_target_pairs={{0,2},{1,3},{2,0},{3,1},{4,6},{5,7},{6,4},{7,5},{8,10},{9,11},{10,... | collective-permute-start | bytes 24584 | tf_op jit(solution)/shard_map/ppermute | solution.py:347
  21.6 0.3 %collective-permute-start.10 = (f32[16,128]{1,0:T(8,128)S(1)}, f32[16,128]{1,0:T(8,128)S(1)}, u32[]{:S(2)}, u32[]{:S(2)}) collective-permute-start(f32[16,128]{1,0:T(8,128)S(1)} %get-tuple-element.61), channel_id=1, source_target_pairs={{0,1},{1,0},{2,3},{3,2},{4,5},{5,4},{6,7},{7,6},{8,9},{9,8},{10,11... | collective-permute-start | bytes 24584 | tf_op jit(solution)/shard_map/ppermute | solution.py:347
  21.9 0.0 collective-permute-done.3.refs_1_
  21.9 0.0 collective-permute-done.4.refs_2_
  21.9 0.9 %temporal.1 = bf16[16,16,512]{2,1,0:T(8,128)(2,1)} custom-call(bf16[256,128]{1,0:T(8,128)(2,1)S(1)} %collective-permute-done.2.refs_0_, bf16[256,128]{1,0:T(8,128)(2,1)S(1)} %collective-permute-done.3.refs_1_, bf16[256,128]{1,0:T(8,128)(2,1)S(1)} %collective-permute-done.4.refs_2_, bf16[256,128]{1,0:T(8,128)(2,1)S(1)} %get-tuple-element.52.refs_3_), custom_call_target="tpu_custom_call" | custom-call | flops 1000 | bytes 1000 | tf_op jit(solution)/shard_map/temporal/pallas_call | solution.py:436
  22.8 2.6 %collective-permute-done.9.refs_1_ = f32[16,128]{1,0:T(8,128)S(1)} collective-permute-done((f32[16,128]{1,0:T(8,128)S(1)}, f32[16,128]{1,0:T(8,128)S(1)}, u32[]{:S(2)}, u32[]{:S(2)}) %collective-permute-start.9) | collective-permute-done | bytes 8224 | tf_op jit(solution)/shard_map/ppermute | solution.py:347
  25.4 0.7 %means.1 = f32[16,16]{1,0:T(8,128)} custom-call(f32[16,128]{1,0:T(8,128)S(1)} %collective-permute-done.8.refs_0_, f32[16,128]{1,0:T(8,128)S(1)} %collective-permute-done.9.refs_1_, f32[16,128]{1,0:T(8,128)S(1)} %collective-permute-done.10.refs_2_, f32[16,128]{1,0:T(8,128)S(1)} %get-tuple-element.49.refs_3_), custom_call_target="tpu_custom_call" | custom-call | flops 1000 | bytes 1000 | tf_op jit(solution)/shard_map/means/pallas_call | solution.py:444
  (12 shorter events, 0.1 us)
Async XLA Ops:
  0.6 1.0 %copy-start = (f32[4,16,2048]{2,1,0:T(8,128)S(1)}, f32[4,16,2048]{2,1,0:T(8,128)}, u32[]{:S(2)}) copy-start(f32[4,16,2048]{2,1,0:T(8,128)} %observed_ref.1) | copy-start | bytes 1572868
  1.8 8.0 %collective-permute-start = (f16[48,2048]{1,0:T(8,128)(2,1)S(1)}, f16[48,2048]{1,0:T(8,128)(2,1)S(1)}, u32[]{:S(2)}, u32[]{:S(2)}) collective-permute-start(f16[48,2048]{1,0:T(8,128)(2,1)S(1)} %convert_element_type.12), channel_id=1, source_target_pairs={{0,1},{1,0},{2,3},{3,2},{4,5},{5,4},{6,7},{7,6},{8,9},{9,8},{10,11... | collective-permute-start | bytes 589832 | tf_op jit(solution)/shard_map/ppermute | solution.py:393
  5.0 0.8 %copy-start.1 = (s32[256,16,4]{0,2,1:T(4,128)S(1)}, s32[256,16,4]{0,2,1:T(4,128)}, u32[]{:S(2)}) copy-start(s32[256,16,4]{0,2,1:T(4,128)} %param.7) | copy-start | bytes 196612
  5.0 4.8 %collective-permute-start.1 = (f16[48,2048]{1,0:T(8,128)(2,1)S(1)}, f16[48,2048]{1,0:T(8,128)(2,1)S(1)}, u32[]{:S(2)}, u32[]{:S(2)}) collective-permute-start(f16[48,2048]{1,0:T(8,128)(2,1)S(1)} %convert_element_type.13), channel_id=1, source_target_pairs={{0,4},{1,2},{2,1},{3,7},{4,0},{5,6},{6,5},{7,3},{8,12},{9,10},{10,... | collective-permute-start | bytes 589832 | tf_op jit(solution)/shard_map/ppermute | solution.py:395
  5.8 0.7 %copy-start.2 = (f32[8,5]{1,0:T(8,128)S(1)}, f32[8,5]{1,0:T(8,128)}, u32[]{:S(2)}) copy-start(f32[8,5]{1,0:T(8,128)} %kernels_ref.1) | copy-start | bytes 484
  5.8 0.7 %copy-start.3 = (s32[8]{0:T(128)S(1)}, s32[8]{0:T(128)}, u32[]{:S(2)}) copy-start(s32[8]{0:T(128)} %band_ref.1) | copy-start | bytes 100
  12.7 4.0 %collective-permute-start.5 = (bf16[48,128]{1,0:T(8,128)(2,1)S(1)}, bf16[48,128]{1,0:T(8,128)(2,1)S(1)}, u32[]{:S(2)}, u32[]{:S(2)}) collective-permute-start(bf16[48,128]{1,0:T(8,128)(2,1)S(1)} %get-tuple-element.59), channel_id=1, source_target_pairs={{0,12},{4,8},{8,4},{12,0},{1,13},{5,9},{9,5},{13,1},{2,14},{6,10},... | collective-permute-start | bytes 36872 | tf_op jit(solution)/shard_map/ppermute | solution.py:347
  13.0 3.7 %collective-permute-start.6 = (bf16[48,128]{1,0:T(8,128)(2,1)S(1)}, bf16[48,128]{1,0:T(8,128)(2,1)S(1)}, u32[]{:S(2)}, u32[]{:S(2)}) collective-permute-start(bf16[48,128]{1,0:T(8,128)(2,1)S(1)} %get-tuple-element.58), channel_id=1, source_target_pairs={{0,8},{4,12},{8,0},{12,4},{1,9},{5,13},{9,1},{13,5},{2,10},{6,14},... | collective-permute-start | bytes 36872 | tf_op jit(solution)/shard_map/ppermute | solution.py:347
  14.5 2.2 %collective-permute-start.7 = (bf16[48,128]{1,0:T(8,128)(2,1)S(1)}, bf16[48,128]{1,0:T(8,128)(2,1)S(1)}, u32[]{:S(2)}, u32[]{:S(2)}) collective-permute-start(bf16[48,128]{1,0:T(8,128)(2,1)S(1)} %get-tuple-element.57), channel_id=1, source_target_pairs={{0,4},{4,0},{8,12},{12,8},{1,5},{5,1},{9,13},{13,9},{2,6},{6,2},{1... | collective-permute-start | bytes 36872 | tf_op jit(solution)/shard_map/ppermute | solution.py:347
  14.7 6.9 %collective-permute-start.2 = (bf16[256,128]{1,0:T(8,128)(2,1)S(1)}, bf16[256,128]{1,0:T(8,128)(2,1)S(1)}, u32[]{:S(2)}, u32[]{:S(2)}) collective-permute-start(bf16[256,128]{1,0:T(8,128)(2,1)S(1)} %get-tuple-element.55), channel_id=1, source_target_pairs={{0,12},{4,8},{8,4},{12,0},{1,13},{5,9},{9,5},{13,1},{2,14},{6,10},... | collective-permute-start | bytes 196616 | tf_op jit(solution)/shard_map/ppermute | solution.py:347
  16.0 5.9 %collective-permute-start.3 = (bf16[256,128]{1,0:T(8,128)(2,1)S(1)}, bf16[256,128]{1,0:T(8,128)(2,1)S(1)}, u32[]{:S(2)}, u32[]{:S(2)}) collective-permute-start(bf16[256,128]{1,0:T(8,128)(2,1)S(1)} %get-tuple-element.54), channel_id=1, source_target_pairs={{0,8},{4,12},{8,0},{12,4},{1,9},{5,13},{9,1},{13,5},{2,10},{6,14},... | collective-permute-start | bytes 196616 | tf_op jit(solution)/shard_map/ppermute | solution.py:347
  16.8 5.1 %collective-permute-start.4 = (bf16[256,128]{1,0:T(8,128)(2,1)S(1)}, bf16[256,128]{1,0:T(8,128)(2,1)S(1)}, u32[]{:S(2)}, u32[]{:S(2)}) collective-permute-start(bf16[256,128]{1,0:T(8,128)(2,1)S(1)} %get-tuple-element.53), channel_id=1, source_target_pairs={{0,4},{4,0},{8,12},{12,8},{1,5},{5,1},{9,13},{13,9},{2,6},{6,2},{1... | collective-permute-start | bytes 196616 | tf_op jit(solution)/shard_map/ppermute | solution.py:347
  17.2 5.7 %collective-permute-start.8 = (f32[16,128]{1,0:T(8,128)S(1)}, f32[16,128]{1,0:T(8,128)S(1)}, u32[]{:S(2)}, u32[]{:S(2)}) collective-permute-start(f32[16,128]{1,0:T(8,128)S(1)} %get-tuple-element.63), channel_id=1, source_target_pairs={{0,3},{1,2},{2,1},{3,0},{4,7},{5,6},{6,5},{7,4},{8,11},{9,10},{10,... | collective-permute-start | bytes 24584 | tf_op jit(solution)/shard_map/ppermute | solution.py:347
  20.8 4.5 %collective-permute-start.9 = (f32[16,128]{1,0:T(8,128)S(1)}, f32[16,128]{1,0:T(8,128)S(1)}, u32[]{:S(2)}, u32[]{:S(2)}) collective-permute-start(f32[16,128]{1,0:T(8,128)S(1)} %get-tuple-element.62), channel_id=1, source_target_pairs={{0,2},{1,3},{2,0},{3,1},{4,6},{5,7},{6,4},{7,5},{8,10},{9,11},{10,... | collective-permute-start | bytes 24584 | tf_op jit(solution)/shard_map/ppermute | solution.py:347
  21.6 3.8 %collective-permute-start.10 = (f32[16,128]{1,0:T(8,128)S(1)}, f32[16,128]{1,0:T(8,128)S(1)}, u32[]{:S(2)}, u32[]{:S(2)}) collective-permute-start(f32[16,128]{1,0:T(8,128)S(1)} %get-tuple-element.61), channel_id=1, source_target_pairs={{0,1},{1,0},{2,3},{3,2},{4,5},{5,4},{6,7},{7,6},{8,9},{9,8},{10,11... | collective-permute-start | bytes 24584 | tf_op jit(solution)/shard_map/ppermute | solution.py:347

commit v21 on v16

--- a/solution.py
+++ b/solution.py
@@ -225,7 +225,7 @@
             out_ref[step // tiles_dev, pl.ds(start, rows_dev), :] = estimate
         return carry
 
-    lax.fori_loop(0, n_frame * tiles_dev, columns_step, 0, unroll=2)
+    lax.fori_loop(0, n_frame * tiles_dev, columns_step, 0)
     lane_tiles = lax.broadcasted_iota(jnp.int32, (TILE, TILE), 1) % tiles_dev
     gathered = jnp.zeros((frames * n_frame * rows_dev, TILE), jnp.float32)
     for tile in range(tiles_dev):

time: 26.4 us -> 26.4 us (level)
  no operation moved by 1% of the time
where the time goes in v21:
time: 26.4 us; the launch traced here: 26.1 us
  starting transfers between devices  11.8 us (45%)
  Pallas kernels  5.7 us (22%)
  waiting for transfers between devices  5.35 us (20%)
  local copies, waits for them, and re-layouts  2.4 us (9%)
  between operations  0.75 us (3%)
    ppermute x9, starting transfers between devices, swapped(): lax.ppermute(part, axis, [(i, i ^ step) for i in range(count)])  8.63 us
    ppermute x1, starting transfers between devices, by_halo(): inner = lax.ppermute(inner.astype(jnp.float16), 'row', inner_swap)  3.09 us
    pallas_call x1, Pallas kernels, by_halo(): call(restore_kernel, 'restore', [vmem] * 6, (array(n_frame, frames * posi...  2.86 us
    ppermute x9, waiting for transfers between devices, swapped(): lax.ppermute(part, axis, [(i, i ^ step) for i in range(count)])  2.69 us
    ppermute x1, waiting for transfers between devices, by_halo(): inner = lax.ppermute(inner.astype(jnp.float16), 'row', inner_swap)  2.66 us
    unnamed x8, local copies, waits for them, and re-layouts  2.35 us
    pallas_call x1, Pallas kernels, by_halo(): call(functools.partial(temporal_kernel, frames=frames), 'temporal', [vmem...  0.91 us
    pallas_call x1, Pallas kernels, by_halo(): call(functools.partial(taps_kernel, height=rows_dev * n_row, rows_dev=row...  0.69 us
  transfers between devices with their start and end apart: 11, of which 2 were waited for; matrix products, arithmetic and copies ran while one was open for 0% of the time, Pallas kernels for 8%

profile of v21, /device:TPU:0, one launch (start us, length us, event | category | flops | bytes accessed | tf_op | source)
XLA Modules:
  0.0 26.1 jit_solution(5410558640756659937)
XLA Ops:
  0.6 1.0 %copy-done = f32[4,16,2048]{2,1,0:T(8,128)S(1)} copy-done((f32[4,16,2048]{2,1,0:T(8,128)S(1)}, f32[4,16,2048]{2,1,0:T(8,128)}, u32[]{:S(2)}) %copy-start) | copy-done | bytes 524312
  1.7 0.1 halo.1
  1.8 3.1 %collective-permute-start = (f16[48,2048]{1,0:T(8,128)(2,1)S(1)}, f16[48,2048]{1,0:T(8,128)(2,1)S(1)}, u32[]{:S(2)}, u32[]{:S(2)}) collective-permute-start(f16[48,2048]{1,0:T(8,128)(2,1)S(1)} %convert_element_type.12), channel_id=1, source_target_pairs={{0,1},{1,0},{2,3},{3,2},{4,5},{5,4},{6,7},{7,6},{8,9},{9,8},{10,11... | collective-permute-start | bytes 589832 | tf_op jit(solution)/shard_map/ppermute | solution.py:386
  4.9 0.1 collective-permute-start.1
  5.0 0.7 %copy-done.1 = s32[256,16,4]{0,2,1:T(4,128)S(1)} copy-done((s32[256,16,4]{0,2,1:T(4,128)S(1)}, s32[256,16,4]{0,2,1:T(4,128)}, u32[]{:S(2)}) %copy-start.1) | copy-done | bytes 65560
  5.8 0.1 feet.1.feet_ref
  5.9 0.6 %copy-done.2 = f32[8,5]{1,0:T(8,128)S(1)} copy-done((f32[8,5]{1,0:T(8,128)S(1)}, f32[8,5]{1,0:T(8,128)}, u32[]{:S(2)}) %copy-start.2) | copy-done | bytes 184
  6.4 0.7 %taps.1 = (f32[4,48,128]{2,1,0:T(8,128)S(1)}, f32[4,48,128]{2,1,0:T(8,128)S(1)}) custom-call(s32[8]{0:T(128)S(1)} %copy-done.3, f32[8,5]{1,0:T(8,128)S(1)} %copy-done.2), custom_call_target="tpu_custom_call" | custom-call | flops 1000 | bytes 1000 | tf_op jit(solution)/shard_map/taps/pallas_call | solution.py:389
  7.2 2.7 %collective-permute-done = f16[48,2048]{1,0:T(8,128)(2,1)S(1)} collective-permute-done((f16[48,2048]{1,0:T(8,128)(2,1)S(1)}, f16[48,2048]{1,0:T(8,128)(2,1)S(1)}, u32[]{:S(2)}, u32[]{:S(2)}) %collective-permute-start) | collective-permute-done | bytes 196640 | tf_op jit(solution)/shard_map/ppermute | solution.py:386
  9.8 0.0 collective-permute-done.1
  9.8 0.1 convert_select_fusion
  9.9 2.9 %restore.1 = (bf16[4,256,128]{2,1,0:T(8,128)(2,1)S(1)}, bf16[4,48,128]{2,1,0:T(8,128)(2,1)S(1)}) custom-call(f32[4,48,128]{2,1,0:T(8,128)S(1)} %get-tuple-element.25.taps_ref, f32[4,48,128]{2,1,0:T(8,128)S(1)} %get-tuple-element.26.back_ref, bf16[4,32,128]{2,1,0:T(8,128)(2,1)S(1)} %feet.1.feet_ref, f32[4,16,2048]{2,1,0:T(8,128)S(1)} %get-tuple-element.27.own_ref, ...), custom_call_target="tpu_custom_call" | custom-call | flops 1000 | bytes 1000 | tf_op jit(solution)/shard_map/restore/pallas_call | solution.py:405
  12.8 0.3 %collective-permute-start.5 = (bf16[48,128]{1,0:T(8,128)(2,1)S(1)}, bf16[48,128]{1,0:T(8,128)(2,1)S(1)}, u32[]{:S(2)}, u32[]{:S(2)}) collective-permute-start(bf16[48,128]{1,0:T(8,128)(2,1)S(1)} %get-tuple-element.57), channel_id=1, source_target_pairs={{0,12},{4,8},{8,4},{12,0},{1,13},{5,9},{9,5},{13,1},{2,14},{6,10},... | collective-permute-start | bytes 36872 | tf_op jit(solution)/shard_map/ppermute | solution.py:342
  13.1 1.5 %collective-permute-start.6 = (bf16[48,128]{1,0:T(8,128)(2,1)S(1)}, bf16[48,128]{1,0:T(8,128)(2,1)S(1)}, u32[]{:S(2)}, u32[]{:S(2)}) collective-permute-start(bf16[48,128]{1,0:T(8,128)(2,1)S(1)} %get-tuple-element.56), channel_id=1, source_target_pairs={{0,8},{4,12},{8,0},{12,4},{1,9},{5,13},{9,1},{13,5},{2,10},{6,14},... | collective-permute-start | bytes 36872 | tf_op jit(solution)/shard_map/ppermute | solution.py:342
  14.6 0.1 collective-permute-start.7
  14.8 1.3 %collective-permute-start.2 = (bf16[256,128]{1,0:T(8,128)(2,1)S(1)}, bf16[256,128]{1,0:T(8,128)(2,1)S(1)}, u32[]{:S(2)}, u32[]{:S(2)}) collective-permute-start(bf16[256,128]{1,0:T(8,128)(2,1)S(1)} %get-tuple-element.53), channel_id=1, source_target_pairs={{0,12},{4,8},{8,4},{12,0},{1,13},{5,9},{9,5},{13,1},{2,14},{6,10},... | collective-permute-start | bytes 196616 | tf_op jit(solution)/shard_map/ppermute | solution.py:342
  16.1 0.8 %collective-permute-start.3 = (bf16[256,128]{1,0:T(8,128)(2,1)S(1)}, bf16[256,128]{1,0:T(8,128)(2,1)S(1)}, u32[]{:S(2)}, u32[]{:S(2)}) collective-permute-start(bf16[256,128]{1,0:T(8,128)(2,1)S(1)} %get-tuple-element.52), channel_id=1, source_target_pairs={{0,8},{4,12},{8,0},{12,4},{1,9},{5,13},{9,1},{13,5},{2,10},{6,14},... | collective-permute-start | bytes 196616 | tf_op jit(solution)/shard_map/ppermute | solution.py:342
  16.8 0.0 collective-permute-done.5.refs_0_
  16.8 0.0 collective-permute-start.4
  16.8 0.0 collective-permute-done.6.refs_1_
  16.8 0.0 collective-permute-done.7.refs_2_
  16.8 0.3 %partial.1 = f32[4,16,128]{2,1,0:T(8,128)S(1)} custom-call(bf16[48,128]{1,0:T(8,128)(2,1)S(1)} %collective-permute-done.5.refs_0_, bf16[48,128]{1,0:T(8,128)(2,1)S(1)} %collective-permute-done.6.refs_1_, bf16[48,128]{1,0:T(8,128)(2,1)S(1)} %collective-permute-done.7.refs_2_, bf16[48,128]{1,0:T(8,128)(2,1)S(1)} %get-tuple-element.54.refs_3_), custom_call_target="tpu_custom_call" | custom-call | flops 1000 | bytes 1000 | tf_op jit(solution)/shard_map/partial/pallas_call | solution.py:417
  17.2 3.7 %collective-permute-start.8 = (f32[16,128]{1,0:T(8,128)S(1)}, f32[16,128]{1,0:T(8,128)S(1)}, u32[]{:S(2)}, u32[]{:S(2)}) collective-permute-start(f32[16,128]{1,0:T(8,128)S(1)} %get-tuple-element.61), channel_id=1, source_target_pairs={{0,3},{1,2},{2,1},{3,0},{4,7},{5,6},{6,5},{7,4},{8,11},{9,10},{10,... | collective-permute-start | bytes 24584 | tf_op jit(solution)/shard_map/ppermute | solution.py:342
  20.9 0.7 %collective-permute-start.9 = (f32[16,128]{1,0:T(8,128)S(1)}, f32[16,128]{1,0:T(8,128)S(1)}, u32[]{:S(2)}, u32[]{:S(2)}) collective-permute-start(f32[16,128]{1,0:T(8,128)S(1)} %get-tuple-element.60), channel_id=1, source_target_pairs={{0,2},{1,3},{2,0},{3,1},{4,6},{5,7},{6,4},{7,5},{8,10},{9,11},{10,... | collective-permute-start | bytes 24584 | tf_op jit(solution)/shard_map/ppermute | solution.py:342
  21.6 0.0 collective-permute-done.2.refs_0_
  21.6 0.3 %collective-permute-start.10 = (f32[16,128]{1,0:T(8,128)S(1)}, f32[16,128]{1,0:T(8,128)S(1)}, u32[]{:S(2)}, u32[]{:S(2)}) collective-permute-start(f32[16,128]{1,0:T(8,128)S(1)} %get-tuple-element.59), channel_id=1, source_target_pairs={{0,1},{1,0},{2,3},{3,2},{4,5},{5,4},{6,7},{7,6},{8,9},{9,8},{10,11... | collective-permute-start | bytes 24584 | tf_op jit(solution)/shard_map/ppermute | solution.py:342
  21.9 0.0 collective-permute-done.3.refs_1_
  21.9 0.0 collective-permute-done.4.refs_2_
  21.9 0.9 %temporal.1 = bf16[16,16,512]{2,1,0:T(8,128)(2,1)} custom-call(bf16[256,128]{1,0:T(8,128)(2,1)S(1)} %collective-permute-done.2.refs_0_, bf16[256,128]{1,0:T(8,128)(2,1)S(1)} %collective-permute-done.3.refs_1_, bf16[256,128]{1,0:T(8,128)(2,1)S(1)} %collective-permute-done.4.refs_2_, bf16[256,128]{1,0:T(8,128)(2,1)S(1)} %get-tuple-element.50.refs_3_), custom_call_target="tpu_custom_call" | custom-call | flops 1000 | bytes 1000 | tf_op jit(solution)/shard_map/temporal/pallas_call | solution.py:428
  22.8 0.0 collective-permute-done.8.refs_0_
  22.8 2.7 %collective-permute-done.9.refs_1_ = f32[16,128]{1,0:T(8,128)S(1)} collective-permute-done((f32[16,128]{1,0:T(8,128)S(1)}, f32[16,128]{1,0:T(8,128)S(1)}, u32[]{:S(2)}, u32[]{:S(2)}) %collective-permute-start.9) | collective-permute-done | bytes 8224 | tf_op jit(solution)/shard_map/ppermute | solution.py:342
  25.4 0.7 %means.1 = f32[16,16]{1,0:T(8,128)} custom-call(f32[16,128]{1,0:T(8,128)S(1)} %collective-permute-done.8.refs_0_, f32[16,128]{1,0:T(8,128)S(1)} %collective-permute-done.9.refs_1_, f32[16,128]{1,0:T(8,128)S(1)} %collective-permute-done.10.refs_2_, f32[16,128]{1,0:T(8,128)S(1)} %get-tuple-element.47.refs_3_), custom_call_target="tpu_custom_call" | custom-call | flops 1000 | bytes 1000 | tf_op jit(solution)/shard_map/means/pallas_call | solution.py:436
  (11 shorter events, 0.1 us)
Async XLA Ops:
  0.6 1.0 %copy-start = (f32[4,16,2048]{2,1,0:T(8,128)S(1)}, f32[4,16,2048]{2,1,0:T(8,128)}, u32[]{:S(2)}) copy-start(f32[4,16,2048]{2,1,0:T(8,128)} %observed_ref.1) | copy-start | bytes 1572868
  1.8 8.0 %collective-permute-start = (f16[48,2048]{1,0:T(8,128)(2,1)S(1)}, f16[48,2048]{1,0:T(8,128)(2,1)S(1)}, u32[]{:S(2)}, u32[]{:S(2)}) collective-permute-start(f16[48,2048]{1,0:T(8,128)(2,1)S(1)} %convert_element_type.12), channel_id=1, source_target_pairs={{0,1},{1,0},{2,3},{3,2},{4,5},{5,4},{6,7},{7,6},{8,9},{9,8},{10,11... | collective-permute-start | bytes 589832 | tf_op jit(solution)/shard_map/ppermute | solution.py:386
  4.9 0.8 %copy-start.1 = (s32[256,16,4]{0,2,1:T(4,128)S(1)}, s32[256,16,4]{0,2,1:T(4,128)}, u32[]{:S(2)}) copy-start(s32[256,16,4]{0,2,1:T(4,128)} %param.7) | copy-start | bytes 196612
  4.9 4.9 %collective-permute-start.1 = (f16[48,2048]{1,0:T(8,128)(2,1)S(1)}, f16[48,2048]{1,0:T(8,128)(2,1)S(1)}, u32[]{:S(2)}, u32[]{:S(2)}) collective-permute-start(f16[48,2048]{1,0:T(8,128)(2,1)S(1)} %convert_element_type.13), channel_id=1, source_target_pairs={{0,4},{1,2},{2,1},{3,7},{4,0},{5,6},{6,5},{7,3},{8,12},{9,10},{10,... | collective-permute-start | bytes 589832 | tf_op jit(solution)/shard_map/ppermute | solution.py:387
  5.8 0.7 %copy-start.2 = (f32[8,5]{1,0:T(8,128)S(1)}, f32[8,5]{1,0:T(8,128)}, u32[]{:S(2)}) copy-start(f32[8,5]{1,0:T(8,128)} %kernels_ref.1) | copy-start | bytes 484
  5.8 0.7 %copy-start.3 = (s32[8]{0:T(128)S(1)}, s32[8]{0:T(128)}, u32[]{:S(2)}) copy-start(s32[8]{0:T(128)} %band_ref.1) | copy-start | bytes 100
  12.8 4.0 %collective-permute-start.5 = (bf16[48,128]{1,0:T(8,128)(2,1)S(1)}, bf16[48,128]{1,0:T(8,128)(2,1)S(1)}, u32[]{:S(2)}, u32[]{:S(2)}) collective-permute-start(bf16[48,128]{1,0:T(8,128)(2,1)S(1)} %get-tuple-element.57), channel_id=1, source_target_pairs={{0,12},{4,8},{8,4},{12,0},{1,13},{5,9},{9,5},{13,1},{2,14},{6,10},... | collective-permute-start | bytes 36872 | tf_op jit(solution)/shard_map/ppermute | solution.py:342
  13.1 3.7 %collective-permute-start.6 = (bf16[48,128]{1,0:T(8,128)(2,1)S(1)}, bf16[48,128]{1,0:T(8,128)(2,1)S(1)}, u32[]{:S(2)}, u32[]{:S(2)}) collective-permute-start(bf16[48,128]{1,0:T(8,128)(2,1)S(1)} %get-tuple-element.56), channel_id=1, source_target_pairs={{0,8},{4,12},{8,0},{12,4},{1,9},{5,13},{9,1},{13,5},{2,10},{6,14},... | collective-permute-start | bytes 36872 | tf_op jit(solution)/shard_map/ppermute | solution.py:342
  14.6 2.2 %collective-permute-start.7 = (bf16[48,128]{1,0:T(8,128)(2,1)S(1)}, bf16[48,128]{1,0:T(8,128)(2,1)S(1)}, u32[]{:S(2)}, u32[]{:S(2)}) collective-permute-start(bf16[48,128]{1,0:T(8,128)(2,1)S(1)} %get-tuple-element.55), channel_id=1, source_target_pairs={{0,4},{4,0},{8,12},{12,8},{1,5},{5,1},{9,13},{13,9},{2,6},{6,2},{1... | collective-permute-start | bytes 36872 | tf_op jit(solution)/shard_map/ppermute | solution.py:342
  14.8 6.8 %collective-permute-start.2 = (bf16[256,128]{1,0:T(8,128)(2,1)S(1)}, bf16[256,128]{1,0:T(8,128)(2,1)S(1)}, u32[]{:S(2)}, u32[]{:S(2)}) collective-permute-start(bf16[256,128]{1,0:T(8,128)(2,1)S(1)} %get-tuple-element.53), channel_id=1, source_target_pairs={{0,12},{4,8},{8,4},{12,0},{1,13},{5,9},{9,5},{13,1},{2,14},{6,10},... | collective-permute-start | bytes 196616 | tf_op jit(solution)/shard_map/ppermute | solution.py:342
  16.1 5.8 %collective-permute-start.3 = (bf16[256,128]{1,0:T(8,128)(2,1)S(1)}, bf16[256,128]{1,0:T(8,128)(2,1)S(1)}, u32[]{:S(2)}, u32[]{:S(2)}) collective-permute-start(bf16[256,128]{1,0:T(8,128)(2,1)S(1)} %get-tuple-element.52), channel_id=1, source_target_pairs={{0,8},{4,12},{8,0},{12,4},{1,9},{5,13},{9,1},{13,5},{2,10},{6,14},... | collective-permute-start | bytes 196616 | tf_op jit(solution)/shard_map/ppermute | solution.py:342
  16.8 5.0 %collective-permute-start.4 = (bf16[256,128]{1,0:T(8,128)(2,1)S(1)}, bf16[256,128]{1,0:T(8,128)(2,1)S(1)}, u32[]{:S(2)}, u32[]{:S(2)}) collective-permute-start(bf16[256,128]{1,0:T(8,128)(2,1)S(1)} %get-tuple-element.51), channel_id=1, source_target_pairs={{0,4},{4,0},{8,12},{12,8},{1,5},{5,1},{9,13},{13,9},{2,6},{6,2},{1... | collective-permute-start | bytes 196616 | tf_op jit(solution)/shard_map/ppermute | solution.py:342
  17.2 5.6 %collective-permute-start.8 = (f32[16,128]{1,0:T(8,128)S(1)}, f32[16,128]{1,0:T(8,128)S(1)}, u32[]{:S(2)}, u32[]{:S(2)}) collective-permute-start(f32[16,128]{1,0:T(8,128)S(1)} %get-tuple-element.61), channel_id=1, source_target_pairs={{0,3},{1,2},{2,1},{3,0},{4,7},{5,6},{6,5},{7,4},{8,11},{9,10},{10,... | collective-permute-start | bytes 24584 | tf_op jit(solution)/shard_map/ppermute | solution.py:342
  20.9 4.5 %collective-permute-start.9 = (f32[16,128]{1,0:T(8,128)S(1)}, f32[16,128]{1,0:T(8,128)S(1)}, u32[]{:S(2)}, u32[]{:S(2)}) collective-permute-start(f32[16,128]{1,0:T(8,128)S(1)} %get-tuple-element.60), channel_id=1, source_target_pairs={{0,2},{1,3},{2,0},{3,1},{4,6},{5,7},{6,4},{7,5},{8,10},{9,11},{10,... | collective-permute-start | bytes 24584 | tf_op jit(solution)/shard_map/ppermute | solution.py:342
  21.6 3.9 %collective-permute-start.10 = (f32[16,128]{1,0:T(8,128)S(1)}, f32[16,128]{1,0:T(8,128)S(1)}, u32[]{:S(2)}, u32[]{:S(2)}) collective-permute-start(f32[16,128]{1,0:T(8,128)S(1)} %get-tuple-element.59), channel_id=1, source_target_pairs={{0,1},{1,0},{2,3},{3,2},{4,5},{5,4},{6,7},{7,6},{8,9},{9,8},{10,11... | collective-permute-start | bytes 24584 | tf_op jit(solution)/shard_map/ppermute | solution.py:342
